TPU v7x, 32 devices: a whole 2x2x4 slice. The times are simulated.
32 devices in a mesh: clip: 4 (over z), tm: 2 (over y), height: 4 (over x, core).
Axes of the slice: x: 2, y: 2, z: 4, core: 2. Of those that a mesh axis runs over, the one named last changes fastest.
Arguments:
- clip_input: bfloat16 [4, 8, 24, 24, 384], P('clip', 'tm', 'height'), may hold values from -6 to 6
- memory: bfloat16 [4, 2, 2, 8, 24, 24, 768], P('clip', None, None, 'tm', 'height'), may hold values from -8 to 8
- mem_len: int32 [4], P('clip'), may hold values from 0 to 2, as said below
- res_id: int32 [4], P('clip'), may hold values 0 or 1
- norm1_gain: float32 [384], replicated, may hold values from 0.5 to 1.5
- norm1_bias: float32 [384], replicated, may hold values from -1.75 to 1.75
- w_qkv: bfloat16 [2304, 384], replicated, may hold values from -0.5 to 0.5
- b_qkv: float32 [2304], replicated, may hold values from -1.75 to 1.75
- conv_kv: float32 [2, 3, 3, 3, 768], replicated, may hold values from -1.25 to 1.25
- compress: float32 [2, 2, 2, 768], replicated, may hold values from -3 to 3
- rel_t: float32 [15, 96], replicated, may hold values from -0.75 to 0.75
- rel_h: float32 [47, 96], replicated, may hold values from -0.75 to 0.75
- rel_w: float32 [47, 96], replicated, may hold values from -0.75 to 0.75
- w_proj: bfloat16 [768, 768], replicated, may hold values from -0.21875 to 0.21875
- b_proj: float32 [768], replicated, may hold values from -1.75 to 1.75
- w_short: bfloat16 [768, 384], replicated, may hold values from -0.3125 to 0.3125
- b_short: float32 [768], replicated, may hold values from -1.75 to 1.75
- norm2_gain: float32 [768], replicated, may hold values from 0.5 to 1.5
- norm2_bias: float32 [768], replicated, may hold values from -1.75 to 1.75
- w_fc1: bfloat16 [3072, 768], replicated, may hold values from -0.21875 to 0.21875
- b_fc1: float32 [3072], replicated, may hold values from -1.75 to 1.75
- w_fc2: bfloat16 [768, 3072], replicated, may hold values from -0.109375 to 0.109375
- b_fc2: float32 [768], replicated, may hold values from -1.75 to 1.75
- cotangent: bfloat16 [4, 8, 12, 12, 768], P('clip', 'tm', 'height'), may hold values from -6 to 6
Outputs:
- output: bfloat16 [4, 8, 12, 12, 768], P('clip', 'tm', 'height')
- input_grad: bfloat16 [4, 8, 24, 24, 384], P('clip', 'tm', 'height')
- grad_norm1_gain: float32 [384], replicated
- grad_norm1_bias: float32 [384], replicated
- grad_w_qkv: float32 [2304, 384], P('clip', ('tm', 'height'))
- grad_b_qkv: float32 [2304], replicated
- grad_conv_kv: float32 [2, 3, 3, 3, 768], replicated
- grad_compress: float32 [2, 2, 2, 768], replicated
- grad_rel_t: float32 [15, 96], replicated
- grad_rel_h: float32 [47, 96], replicated
- grad_rel_w: float32 [47, 96], replicated
- grad_w_proj: float32 [768, 768], P('clip', ('tm', 'height'))
- grad_b_proj: float32 [768], replicated
- grad_w_short: float32 [768, 384], P('clip', ('tm', 'height'))
- grad_b_short: float32 [768], replicated
- grad_norm2_gain: float32 [768], replicated
- grad_norm2_bias: float32 [768], replicated
- grad_w_fc1: float32 [3072, 768], P('clip', ('tm', 'height'))
- grad_b_fc1: float32 [3072], replicated
- grad_w_fc2: float32 [768, 3072], P('clip', ('tm', 'height'))
- grad_b_fc2: float32 [768], replicated
Inputs may be any that keep to these rules, and one draw needn't show every extreme that they name: `mem_len`: how many of a clip's 2 memory steps hold valid keys and values; some clip has all 2.
All inputs are finite; a program needn't handle non-finite values. No bound on the sum of `res_id` on one device may be relied on, other than what follows from the above.
Results may differ from a plain program's by a relative error of at most 0.019.
Values may be sent and summed in bfloat16 or wider, within the bound.
No kernel may reach another device: no remote copies, remote signals or barrier semaphores. Data moves between devices by JAX's collectives and lax.ppermute only.
A program may use at most 320 MiB of HBM per device.

v0:
```python
import jax
import jax.numpy as jnp
from jax import lax
from jax.sharding import PartitionSpec as P

HEADS = 8
SIDE_SMALL = 14
SIDE_BIG = 20
MEM = 2


HIGHEST_PREC = lax.Precision.HIGHEST
MASKED = -1e30
EPSILON = 1e-06
SQRT_HALF = 0.7071067811865476
ROOT_TWO_PI = 2.5066282746310002


def extended(block, sides, width):
    for axis, dim in sides:
        count = lax.axis_size(axis)
        forward = [(i, i + 1) for i in range(count - 1)]
        backward = [(target, source) for source, target in forward]
        low = lax.ppermute(
            lax.slice_in_dim(block, block.shape[dim] - width, None, axis=dim), axis, forward
        )
        high = lax.ppermute(lax.slice_in_dim(block, 0, width, axis=dim), axis, backward)
        block = jnp.concatenate([low, block, high], axis=dim)
    return block


def norm_rows(values, gain, shift):
    means = jnp.mean(values, axis=-1, keepdims=True)
    centred = values - means
    inverse = lax.rsqrt(jnp.mean(centred * centred, axis=-1, keepdims=True) + EPSILON)
    normed = centred * inverse
    return (normed * gain + shift, normed, inverse)


def norm_back(grad, normed, inverse, gain):
    leading = tuple(range(grad.ndim - 1))
    scaled = grad * gain
    inner = (
        scaled
        - jnp.mean(scaled, axis=-1, keepdims=True)
        - normed * jnp.mean(scaled * normed, axis=-1, keepdims=True)
    )
    return (inner * inverse, jnp.sum(grad * normed, axis=leading), jnp.sum(grad, axis=leading))


def gelu_slope(hidden):
    return (
        0.5 * (1.0 + lax.erf(hidden * SQRT_HALF))
        + hidden * jnp.exp(-0.5 * hidden * hidden) / ROOT_TWO_PI
    )


def query_tables(index, layout, tables):
    frames_dev, rows_dev, grid, n_height = layout
    half_rows = rows_dev // 2
    half_grid = grid // 2
    per_device = frames_dev * half_rows * half_grid
    device = index // per_device
    local = index % per_device
    places = (
        device // n_height * frames_dev + local // (half_rows * half_grid),
        2 * (device % n_height * half_rows + local // half_grid % half_rows),
        2 * (local % half_grid),
    )
    picks = []
    targets = []
    for place, table in zip(places, tables):
        count = (table.shape[0] + 1) // 2
        target = place[:, None] - jnp.arange(count)[None, :] + count - 1
        picks.append(table[target])
        targets.append(target)
    return (tuple(picks), tuple(targets))


def key_setup(index, layout, memory_steps, side, mem_len):
    frames_dev, rows_dev, grid, n_height = layout
    half_rows = rows_dev // 2
    half_grid = grid // 2
    current_count = frames_dev * rows_dev * grid
    per_device = current_count + memory_steps * current_count // 4
    local = index % per_device
    device = index // per_device
    current = local < current_count
    past = jnp.maximum(local - current_count, 0)
    row = device % n_height * rows_dev + jnp.where(
        current, local // grid % rows_dev, 2 * (past // half_grid % half_rows)
    )
    column = jnp.where(current, local % grid, 2 * (past % half_grid))
    step = past // (frames_dev * half_rows * half_grid)
    valid = (
        (row[None, :] < side[:, None])
        & (column[None, :] < side[:, None])
        & (current[None, :] | (step[None, :] < mem_len[:, None]))
    )
    return valid


def bias_forward(query_full, picks, devices, layout, keys_dev):
    frames_dev, rows_dev, grid, n_height = layout
    along = [
        jnp.einsum("bqhe,qke->bhqk", query_full, pick, precision=HIGHEST_PREC) for pick in picks
    ]

    def one_block(device):
        along_t = lax.dynamic_slice_in_dim(along[0], device // n_height * frames_dev, frames_dev, 3)
        along_h = lax.dynamic_slice_in_dim(along[1], device % n_height * rows_dev, rows_dev, 3)
        cells = (
            along_t[..., :, None, None] + along_h[..., None, :, None] + along[2][..., None, None, :]
        )
        flat = cells.reshape(cells.shape[:3] + (frames_dev * rows_dev * grid,))
        return jnp.pad(flat, ((0, 0), (0, 0), (0, 0), (0, keys_dev - flat.shape[-1])))

    stacked = jax.vmap(one_block)(devices)
    shards, batch, heads, queries = stacked.shape[:4]
    return jnp.moveaxis(stacked, 0, 3).reshape(batch, heads, queries, shards * keys_dev)


def bias_backward(score_low, query_full, picks, targets, devices, layout, keys_dev, tables):
    frames_dev, rows_dev, grid, n_height = layout
    batch, heads, queries, _ = score_low.shape
    shards = devices.shape[0]
    current_count = frames_dev * rows_dev * grid
    cells = score_low.reshape(batch, heads, queries, shards, keys_dev)[..., :current_count].astype(
        jnp.float32
    )
    cells = cells.reshape(batch, heads, queries, shards, frames_dev, rows_dev, grid)
    per_t = jnp.sum(cells, axis=(5, 6))
    per_h = jnp.sum(cells, axis=(4, 6))
    per_w = jnp.sum(cells, axis=(3, 4, 5))
    count_t = picks[0].shape[1]
    count_h = picks[1].shape[1]

    def spread(device, part_t, part_h):
        full_t = lax.dynamic_update_slice_in_dim(
            jnp.zeros((batch, heads, queries, count_t), jnp.float32),
            part_t,
            device // n_height * frames_dev,
            3,
        )
        full_h = lax.dynamic_update_slice_in_dim(
            jnp.zeros((batch, heads, queries, count_h), jnp.float32),
            part_h,
            device % n_height * rows_dev,
            3,
        )
        return (full_t, full_h)

    spread_t, spread_h = jax.vmap(spread, in_axes=(0, 3, 3))(devices, per_t, per_h)
    grads = (jnp.sum(spread_t, axis=0), jnp.sum(spread_h, axis=0), per_w)
    query_grad = 0.0
    table_grads = []
    for along_grad, pick, target, table in zip(grads, picks, targets, tables):
        query_grad = query_grad + jnp.einsum(
            "bhqk,qke->bqhe", along_grad, pick, precision=HIGHEST_PREC
        )
        weighted = jnp.einsum("bhqk,bqhe->qke", along_grad, query_full, precision=HIGHEST_PREC)
        table_grads.append(
            jax.ops.segment_sum(
                weighted.reshape(-1, weighted.shape[-1]),
                target.reshape(-1),
                num_segments=table.shape[0],
            )
        )
    return (query_grad, tuple(table_grads))


def scores_of(query_low, query_full, keys_low, picks, devices, layout, keys_dev, valid, scale):
    raw = (
        jnp.einsum("bqhe,bkhe->bhqk", query_low, keys_low, preferred_element_type=jnp.float32)
        * scale
    )
    raw = raw + bias_forward(query_full, picks, devices, layout, keys_dev)
    return jnp.where(valid[:, None, None, :], raw, MASKED)


def attend_back(
    query_low,
    query_full,
    keys_low,
    values_low,
    picks,
    targets,
    devices,
    layout,
    keys_dev,
    tables,
    valid,
    scale,
    dout_low,
    log_total,
    delta,
):
    scores = scores_of(
        query_low, query_full, keys_low, picks, devices, layout, keys_dev, valid, scale
    )
    shares = jnp.where(valid[:, None, None, :], jnp.exp(scores - log_total[..., None]), 0.0)
    value_grad = jnp.einsum(
        "bhqk,bqhe->bkhe", shares.astype(jnp.bfloat16), dout_low, preferred_element_type=jnp.float32
    )
    share_grad = jnp.einsum(
        "bqhe,bkhe->bhqk", dout_low, values_low, preferred_element_type=jnp.float32
    )
    score_low = (shares * (share_grad - delta[..., None])).astype(jnp.bfloat16)
    query_grad = (
        jnp.einsum("bhqk,bkhe->bqhe", score_low, keys_low, preferred_element_type=jnp.float32)
        * scale
    )
    key_grad = (
        jnp.einsum("bhqk,bqhe->bkhe", score_low, query_low, preferred_element_type=jnp.float32)
        * scale
    )
    bias_query, table_grads = bias_backward(
        score_low, query_full, picks, targets, devices, layout, keys_dev, tables
    )
    return (query_grad + bias_query, key_grad, value_grad, table_grads)


def body(
    clip_input,
    memory,
    mem_len,
    res_id,
    norm1_gain,
    norm1_bias,
    w_qkv,
    b_qkv,
    conv_kv,
    compress,
    rel_t,
    rel_h,
    rel_w,
    w_proj,
    b_proj,
    w_short,
    b_short,
    norm2_gain,
    norm2_bias,
    w_fc1,
    b_fc1,
    w_fc2,
    b_fc2,
    cotangent,
):
    batch, frames_dev, rows_dev, grid, channels = clip_input.shape
    width = w_proj.shape[0]
    head_size = width // HEADS
    scale = head_size ** (-0.5)
    half_rows = rows_dev // 2
    half_grid = grid // 2
    n_height = lax.axis_size("height")
    group = lax.axis_size("tm") * n_height
    member = lax.axis_index("tm") * n_height + lax.axis_index("height")
    layout = (frames_dev, rows_dev, grid, n_height)
    tables = (rel_t, rel_h, rel_w)
    queries_dev = frames_dev * half_rows * half_grid
    current_count = frames_dev * rows_dev * grid
    keys_dev = current_count + MEM * current_count // 4
    side = SIDE_SMALL + (SIDE_BIG - SIDE_SMALL) * res_id
    row_ids = lax.axis_index("height") * rows_dev + jnp.arange(rows_dev)
    inside = (
        (row_ids[None, :, None] < side[:, None, None])
        & (jnp.arange(grid)[None, None, :] < side[:, None, None])
    ).astype(jnp.float32)
    source = clip_input.astype(jnp.float32)
    norm1_out, norm1_unit, norm1_scale = norm_rows(source, norm1_gain, norm1_bias)
    normed1_low = norm1_out.astype(jnp.bfloat16)
    projected = (
        jnp.einsum("nthwc,oc->nthwo", normed1_low, w_qkv, preferred_element_type=jnp.float32)
        + b_qkv
    )
    pooled = (
        projected[..., :width]
        .reshape(batch, frames_dev, half_rows, 2, half_grid, 2, width)
        .mean(axis=(3, 5))
    )
    pooled_low = pooled.astype(jnp.bfloat16).reshape(batch, queries_dev, width)
    query_low = pooled_low.reshape(batch, queries_dev, HEADS, head_size)
    query_full = query_low.astype(jnp.float32)
    pair = jnp.stack([projected[..., width : 2 * width], projected[..., 2 * width :]], 1)
    masked_kv = (pair * inside[:, None, None, :, :, None]).astype(jnp.bfloat16)
    rimmed = extended(masked_kv, (("tm", 2), ("height", 3)), 1)
    framed = jnp.pad(rimmed, ((0, 0), (0, 0), (0, 0), (0, 0), (1, 1), (0, 0)))
    mixed = jnp.zeros(masked_kv.shape, jnp.float32)
    for tap_t in range(3):
        for tap_h in range(3):
            for tap_w in range(3):
                mixed = (
                    mixed
                    + framed[
                        :,
                        :,
                        tap_t : tap_t + frames_dev,
                        tap_h : tap_h + rows_dev,
                        tap_w : tap_w + grid,
                        :,
                    ]
                    * conv_kv[:, tap_t, tap_h, tap_w][None, :, None, None, None, :]
                )
    mixed_low = mixed.astype(jnp.bfloat16)
    past = memory.astype(jnp.float32).reshape(
        batch, MEM, 2, frames_dev, half_rows, 2, half_grid, 2, width
    )
    squeezed_low = jnp.einsum(
        "nsmtaicjd,mijd->nsmtacd", past, compress, precision=HIGHEST_PREC
    ).astype(jnp.bfloat16)
    key_rows = jnp.concatenate(
        [
            mixed_low[:, 0].reshape(batch, current_count, width),
            squeezed_low[:, :, 0].reshape(batch, keys_dev - current_count, width),
        ],
        1,
    )
    value_rows = jnp.concatenate(
        [
            mixed_low[:, 1].reshape(batch, current_count, width),
            squeezed_low[:, :, 1].reshape(batch, keys_dev - current_count, width),
        ],
        1,
    )
    kv_local = jnp.stack([key_rows, value_rows], 1)
    own_picks, own_targets = query_tables(
        member * queries_dev + jnp.arange(queries_dev), layout, tables
    )
    piece = lax.all_gather(kv_local, ("tm", "height"), axis=2, tiled=True)
    top = jnp.full((batch, HEADS, queries_dev), MASKED, jnp.float32)
    summed = jnp.zeros((batch, queries_dev, HEADS, head_size), jnp.float32)
    count = piece.shape[2]
    devices = jnp.arange(count // keys_dev)
    valid = key_setup(jnp.arange(count), layout, MEM, side, mem_len)
    scores = scores_of(
        query_low,
        query_full,
        piece[:, 0].reshape(batch, count, HEADS, head_size),
        own_picks,
        devices,
        layout,
        keys_dev,
        valid,
        scale,
    )
    newtop = jnp.maximum(top, jnp.max(scores, axis=-1))
    weights = jnp.where(valid[:, None, None, :], jnp.exp(scores - newtop[..., None]), 0.0)
    factor = jnp.exp(top - newtop)
    total = jnp.sum(weights, axis=-1)
    summed = summed * jnp.swapaxes(factor, 1, 2)[..., None] + jnp.einsum(
        "bhqk,bkhe->bqhe",
        weights.astype(jnp.bfloat16),
        piece[:, 1].reshape(batch, count, HEADS, head_size),
        preferred_element_type=jnp.float32,
    )
    top, total, summed = (newtop, total, summed)
    attention = summed / jnp.swapaxes(total, 1, 2)[..., None]
    log_own = top + jnp.log(total)
    joined = attention.reshape(batch, queries_dev, width) + pooled_low.astype(jnp.float32)
    joined_low = joined.astype(jnp.bfloat16)
    branch = (
        jnp.einsum("nqd,od->nqo", joined_low, w_proj, preferred_element_type=jnp.float32) + b_proj
    )
    maxima = clip_input.reshape(batch, frames_dev, half_rows, 2, half_grid, 2, channels).max(
        axis=(3, 5)
    )
    maxima_rows = maxima.reshape(batch, queries_dev, channels)
    shortcut = (
        jnp.einsum("nqc,oc->nqo", maxima_rows, w_short, preferred_element_type=jnp.float32)
        + b_short
    )
    resid = branch + shortcut
    norm2_out, norm2_unit, norm2_scale = norm_rows(resid, norm2_gain, norm2_bias)
    normed2_low = norm2_out.astype(jnp.bfloat16)
    hidden = (
        jnp.einsum("nqd,fd->nqf", normed2_low, w_fc1, preferred_element_type=jnp.float32) + b_fc1
    )
    activated_low = jax.nn.gelu(hidden, approximate=False).astype(jnp.bfloat16)
    result = (
        resid
        + jnp.einsum("nqf,of->nqo", activated_low, w_fc2, preferred_element_type=jnp.float32)
        + b_fc2
    )
    output = result.reshape(batch, frames_dev, half_rows, half_grid, width).astype(jnp.bfloat16)
    out_grad = cotangent.reshape(batch, queries_dev, width)
    out_full = out_grad.astype(jnp.float32)
    grad_fc2 = jnp.einsum(
        "nqo,nqf->of", out_grad, activated_low, preferred_element_type=jnp.float32
    )
    bias_fc2 = jnp.sum(out_full, axis=(0, 1))
    act_grad = jnp.einsum("nqo,of->nqf", out_grad, w_fc2, preferred_element_type=jnp.float32)
    hidden_grad = (act_grad * gelu_slope(hidden)).astype(jnp.bfloat16)
    grad_fc1 = jnp.einsum(
        "nqf,nqd->fd", hidden_grad, normed2_low, preferred_element_type=jnp.float32
    )
    bias_fc1 = jnp.sum(hidden_grad.astype(jnp.float32), axis=(0, 1))
    normed2_grad = jnp.einsum("nqf,fd->nqd", hidden_grad, w_fc1, preferred_element_type=jnp.float32)
    norm2_back, gain2_grad, shift2_grad = norm_back(
        normed2_grad, norm2_unit, norm2_scale, norm2_gain
    )
    resid_low = (out_full + norm2_back).astype(jnp.bfloat16)
    bias_resid = jnp.sum(resid_low.astype(jnp.float32), axis=(0, 1))
    grad_proj = jnp.einsum("nqo,nqd->od", resid_low, joined_low, preferred_element_type=jnp.float32)
    grad_short = jnp.einsum(
        "nqo,nqc->oc", resid_low, maxima_rows, preferred_element_type=jnp.float32
    )
    joined_grad_low = jnp.einsum(
        "nqo,od->nqd", resid_low, w_proj, preferred_element_type=jnp.float32
    ).astype(jnp.bfloat16)
    max_grad = jnp.einsum("nqo,oc->nqc", resid_low, w_short, preferred_element_type=jnp.float32)
    dout_heads = joined_grad_low.reshape(batch, queries_dev, HEADS, head_size)
    delta = jnp.swapaxes(jnp.sum(dout_heads.astype(jnp.float32) * attention, axis=-1), 1, 2)
    everything = lax.all_gather(kv_local[None], ("tm", "height"), axis=0, tiled=True)

    def piece_step(carry, item):
        piece, number = item
        valid = key_setup(number * keys_dev + jnp.arange(keys_dev), layout, MEM, side, mem_len)
        query_part, key_part, value_part, table_parts = attend_back(
            query_low,
            query_full,
            piece[:, 0].reshape(batch, keys_dev, HEADS, head_size),
            piece[:, 1].reshape(batch, keys_dev, HEADS, head_size),
            own_picks,
            own_targets,
            jnp.reshape(number, (1,)),
            layout,
            keys_dev,
            tables,
            valid,
            scale,
            dout_heads,
            log_own,
            delta,
        )
        carry = (
            carry[0] + query_part,
            carry[1] + table_parts[0],
            carry[2] + table_parts[1],
            carry[3] + table_parts[2],
        )
        return (
            carry,
            jnp.stack(
                [
                    key_part.reshape(batch, keys_dev, width),
                    value_part.reshape(batch, keys_dev, width),
                ],
                1,
            ),
        )

    start_scan = (
        jnp.zeros(query_full.shape, jnp.float32),
        jnp.zeros(rel_t.shape, jnp.float32),
        jnp.zeros(rel_h.shape, jnp.float32),
        jnp.zeros(rel_w.shape, jnp.float32),
    )
    (query_grad, table_t, table_h, table_w), pieces = lax.scan(
        piece_step, start_scan, (everything, jnp.arange(group))
    )
    kv_grad = lax.psum_scatter(
        pieces.astype(jnp.bfloat16), ("tm", "height"), scatter_dimension=0, tiled=True
    ).astype(jnp.float32)[0]
    pooled_grad = joined_grad_low.astype(jnp.float32) + query_grad.reshape(
        batch, queries_dev, width
    )
    query_cells = jnp.broadcast_to(
        pooled_grad.reshape(batch, frames_dev, half_rows, 1, half_grid, 1, width) * 0.25,
        (batch, frames_dev, half_rows, 2, half_grid, 2, width),
    ).reshape(batch, frames_dev, rows_dev, grid, width)
    mixed_grad = kv_grad[:, :, :current_count].reshape(batch, 2, frames_dev, rows_dev, grid, width)
    past_grad = kv_grad[:, :, current_count:].reshape(
        batch, 2, MEM, frames_dev, half_rows, half_grid, width
    )
    compress_grad = jnp.einsum("nsmtaicjd,nmstacd->mijd", past, past_grad, precision=HIGHEST_PREC)
    conv_taps = []
    for tap_t in range(3):
        for tap_h in range(3):
            for tap_w in range(3):
                conv_taps.append(
                    jnp.sum(
                        framed[
                            :,
                            :,
                            tap_t : tap_t + frames_dev,
                            tap_h : tap_h + rows_dev,
                            tap_w : tap_w + grid,
                            :,
                        ]
                        * mixed_grad,
                        axis=(0, 2, 3, 4),
                    )
                )
    conv_grad = jnp.stack(conv_taps).reshape(3, 3, 3, 2, width).transpose(3, 0, 1, 2, 4)
    rimmed_grad = extended(mixed_grad.astype(jnp.bfloat16), (("tm", 2), ("height", 3)), 1).astype(
        mixed_grad.dtype
    )
    framed_grad = jnp.pad(rimmed_grad, ((0, 0), (0, 0), (0, 0), (0, 0), (1, 1), (0, 0)))
    masked_grad = jnp.zeros(mixed_grad.shape, jnp.float32)
    for tap_t in range(3):
        for tap_h in range(3):
            for tap_w in range(3):
                masked_grad = (
                    masked_grad
                    + framed_grad[
                        :,
                        :,
                        2 - tap_t : 2 - tap_t + frames_dev,
                        2 - tap_h : 2 - tap_h + rows_dev,
                        2 - tap_w : 2 - tap_w + grid,
                        :,
                    ]
                    * conv_kv[:, tap_t, tap_h, tap_w][None, :, None, None, None, :]
                )
    masked_grad = masked_grad * inside[:, None, None, :, :, None]
    projected_grad = jnp.concatenate(
        [query_cells, masked_grad[:, 0], masked_grad[:, 1]], -1
    ).astype(jnp.bfloat16)
    grad_qkv = jnp.einsum(
        "nthwo,nthwc->oc", projected_grad, normed1_low, preferred_element_type=jnp.float32
    )
    bias_qkv = jnp.sum(projected_grad.astype(jnp.float32), axis=(0, 1, 2, 3))
    normed1_grad = jnp.einsum(
        "nthwo,oc->nthwc", projected_grad, w_qkv, preferred_element_type=jnp.float32
    )
    norm1_back, gain1_grad, shift1_grad = norm_back(
        normed1_grad, norm1_unit, norm1_scale, norm1_gain
    )
    window = source.reshape(batch, frames_dev, half_rows, 2, half_grid, 2, channels)
    hits = (window == maxima.astype(jnp.float32)[:, :, :, None, :, None, :]).astype(jnp.float32)
    spread = hits / jnp.sum(hits, axis=(3, 5), keepdims=True)
    pool_grad = (
        spread * max_grad.reshape(batch, frames_dev, half_rows, 1, half_grid, 1, channels)
    ).reshape(batch, frames_dev, rows_dev, grid, channels)
    input_grad = (norm1_back + pool_grad).astype(jnp.bfloat16)
    rows_qkv, rows_proj, rows_short, rows_fc1, rows_fc2 = (
        lax.psum_scatter(
            grad_qkv.astype(jnp.bfloat16), "clip", scatter_dimension=0, tiled=True
        ).astype(jnp.float32),
        lax.psum_scatter(
            grad_proj.astype(jnp.bfloat16), "clip", scatter_dimension=0, tiled=True
        ).astype(jnp.float32),
        lax.psum_scatter(
            grad_short.astype(jnp.bfloat16), "clip", scatter_dimension=0, tiled=True
        ).astype(jnp.float32),
        lax.psum_scatter(
            grad_fc1.astype(jnp.bfloat16), "clip", scatter_dimension=0, tiled=True
        ).astype(jnp.float32),
        lax.psum_scatter(
            grad_fc2.astype(jnp.bfloat16), "clip", scatter_dimension=0, tiled=True
        ).astype(jnp.float32),
    )
    part_qkv, part_proj, part_short, part_fc1, part_fc2 = (
        lax.psum_scatter(
            rows_qkv.astype(jnp.bfloat16), ("tm", "height"), scatter_dimension=1, tiled=True
        ).astype(jnp.float32),
        lax.psum_scatter(
            rows_proj.astype(jnp.bfloat16), ("tm", "height"), scatter_dimension=1, tiled=True
        ).astype(jnp.float32),
        lax.psum_scatter(
            rows_short.astype(jnp.bfloat16), ("tm", "height"), scatter_dimension=1, tiled=True
        ).astype(jnp.float32),
        lax.psum_scatter(
            rows_fc1.astype(jnp.bfloat16), ("tm", "height"), scatter_dimension=1, tiled=True
        ).astype(jnp.float32),
        lax.psum_scatter(
            rows_fc2.astype(jnp.bfloat16), ("tm", "height"), scatter_dimension=1, tiled=True
        ).astype(jnp.float32),
    )
    summed = lax.psum(
        (
            gain1_grad,
            shift1_grad,
            bias_qkv,
            conv_grad,
            compress_grad,
            table_t,
            table_h,
            table_w,
            bias_resid,
            gain2_grad,
            shift2_grad,
            bias_fc1,
            bias_fc2,
        ),
        ("clip", "tm", "height"),
    )
    return (
        output,
        input_grad,
        summed[0],
        summed[1],
        part_qkv,
        summed[2],
        summed[3],
        summed[4],
        summed[5],
        summed[6],
        summed[7],
        part_proj,
        summed[8],
        part_short,
        summed[8],
        summed[9],
        summed[10],
        part_fc1,
        summed[11],
        part_fc2,
        summed[12],
    )


def solution(mesh):
    placed = (
        P("clip", "tm", "height", None, None),
        P("clip", None, None, "tm", "height", None, None),
        P("clip"),
        P("clip"),
        P(),
        P(),
        P(),
        P(),
        P(),
        P(),
        P(),
        P(),
        P(),
        P(),
        P(),
        P(),
        P(),
        P(),
        P(),
        P(),
        P(),
        P(),
        P(),
        P("clip", "tm", "height", None, None),
    )
    return jax.shard_map(
        body,
        mesh=mesh,
        in_specs=placed,
        out_specs=(
            P("clip", "tm", "height", None, None),
            P("clip", "tm", "height", None, None),
            P(),
            P(),
            P("clip", ("tm", "height")),
            P(),
            P(),
            P(),
            P(),
            P(),
            P(),
            P("clip", ("tm", "height")),
            P(),
            P("clip", ("tm", "height")),
            P(),
            P(),
            P(),
            P("clip", ("tm", "height")),
            P(),
            P("clip", ("tm", "height")),
            P(),
        ),
        check_vma=False,
    )
```

profile of v0, /device:TPU:0, one launch (start us, length us, event | category | flops | bytes accessed | tf_op | source)
XLA Modules:
  0.0 2788.3 jit_solution(6828500100670024959)
XLA Ops:
  145.2 29.3 %broadcast_add_fusion.2 = f32[8,1,8,144,576]{3,4,2,0,1:T(8,128)} fusion(f32[8,1,8,144,576]{3,4,2,0,1:T(8,128)} %bitcast.579, f32[8,144,576]{1,2,0:T(8,128)} %bitcast.594), kind=kLoop, calls=%fused_computation.126 | loop fusion | flops 5308416 | bytes 45121536 | tf_op jit(solution)/shard_map/vmap()/add | solution.py:113
  174.5 32.0 %pad_bitcast_fusion = f32[1,8,144,8,864]{2,4,1,3,0:T(8,128)} fusion(f32[8,1,8,144,576]{3,4,2,0,1:T(8,128)} %broadcast_add_fusion.2), kind=kLoop, calls=%fused_computation.103 | loop fusion | bytes 53084160 | tf_op jit(solution)/shard_map/transpose | solution.py:120
  206.5 51.2 %copy.175 = f32[1,8,144,8,864]{4,3,2,1,0:T(8,128)} copy(f32[1,8,144,8,864]{2,4,1,3,0:T(8,128)} %pad_bitcast_fusion) | data formatting | bytes 63700992 | tf_op jit(solution)/shard_map/transpose | solution.py:120
  257.7 36.8 %reshape.2066 = f32[8,144,6912]{2,1,0:T(8,128)} reshape(f32[1,8,144,8,864]{4,3,2,1,0:T(8,128)} %copy.175) | data formatting | bytes 63700992 | tf_op jit(solution)/shard_map/reshape | solution.py:120
  298.9 41.5 %fusion.286 = (bf16[1,1,6912,768]{3,1,0,2:T(2,128)(2,1)}, bf16[1,1,6912,768]{3,1,0,2:T(2,128)(2,1)}) fusion(bf16[1,2,6912,768]{3,1,0,2:T(2,128)(2,1)} %all-gather.4.cloned.1.call-done), kind=kLoop, calls=%fused_computation.601 | loop fusion | bytes 42467328 | tf_op jit(solution)/shard_map/slice | solution.py:338
  340.5 42.1 %copy.168 = bf16[1,1,6912,768]{2,3,1,0:T(8,128)(2,1)} copy(bf16[1,1,6912,768]{3,1,0,2:T(2,128)(2,1)} %get-tuple-element.838) | data formatting | bytes 21233664 | tf_op jit(solution)/shard_map/slice | solution.py:338
  382.5 27.0 fusion.292
  424.1 42.1 %copy.176 = bf16[1,1,6912,768]{2,3,1,0:T(8,128)(2,1)} copy(bf16[1,1,6912,768]{3,1,0,2:T(2,128)(2,1)} %get-tuple-element.839) | data formatting | bytes 21233664 | tf_op jit(solution)/shard_map/slice | solution.py:353
  543.0 28.1 %reduce-scatter.26.cloned.1.call-done = bf16[192,768]{1,0:T(8,128)(2,1)} async-done(((bf16[768,768]{1,0:T(8,128)(2,1)}), bf16[192,768]{1,0:T(8,128)(2,1)}) %reduce-scatter.26.cloned.1.call-update) | async-done | bytes 294928 | tf_op jit(solution)/shard_map/reduce_scatter | solution.py:540
  573.0 84.2 %reduce-scatter.30.cloned.1.call-done = bf16[768,768]{1,0:T(8,128)(2,1)} async-done(((bf16[3072,768]{1,0:T(8,128)(2,1)}), bf16[768,768]{1,0:T(8,128)(2,1)}) %reduce-scatter.30.cloned.1.call-update) | async-done | bytes 1179664 | tf_op jit(solution)/shard_map/reduce_scatter | solution.py:546
  664.4 80.8 %reduce-scatter.42.cloned.1.call-done = bf16[192,3072]{1,0:T(8,128)(2,1)} async-done(((bf16[768,3072]{1,0:T(8,128)(2,1)}), bf16[192,3072]{1,0:T(8,128)(2,1)}) %reduce-scatter.42.cloned.1.call-update) | async-done | bytes 1179664
  747.8 108.4 %all-gather.6.cloned.1.call-done = bf16[8,2,864,768]{3,2,1,0:T(8,128)(2,1)} async-done(((bf16[1,2,864,768]{3,2,1,0:T(8,128)(2,1)}), bf16[8,2,864,768]{3,2,1,0:T(8,128)(2,1)}) %all-gather.6.cloned.1.call-update) | async-done | bytes 21233680 | tf_op jit(solution)/shard_map/all_gather | solution.py:413
  856.3 1298.2 %while.26 = (s32[]{:T(128)}, f32[1,144,8,96]{3,1,2,0:T(8,128)}, f32[15,96]{1,0:T(8,128)S(1)}, f32[47,96]{1,0:T(8,128)S(1)}, f32[47,96]{1,0:T(8,128)S(1)}, /*inde...) while((s32[]{:T(128)}, f32[1,144,8,96]{3,1,2,0:T(8,128)}, ...), condition=%wide.region_20.21_spmd.clone, body=%wide.region_11.20_spmd.clone.sunk | while | flops 1124585728 | bytes 119036352 | solution.py:458
  1069.2 25.6 scatter.17
  1235.0 25.6 scatter.17
  1400.9 25.6 scatter.17
  1713.7 25.6 scatter.17
  2045.3 25.6 scatter.17
  2193.1 102.3 %reduce-scatter.22.cloned.1.call-done = bf16[1,1,2,864,768]{3,4,2,1,0:T(8,128)(2,1)} async-done(((bf16[8,1,2,864,768]{3,4,2,1,0:T(8,128)(2,1)}), bf16[1,1,2,864,768]{3,4,2,1,0:T(8,128)(2,1)}) %reduce-scatter.22.cloned.1.call-update) | async-done | bytes 2654224 | tf_op jit(solution)/shard_map/reduce_scatter | solution.py:461
  2366.0 41.3 %fusion.166 = bf16[1,2,4,6,24,768]{5,4,3,2,1,0:T(8,128)(2,1)} fusion(f32[1,2,6,8,24,768]{5,4,3,2,1,0:T(8,128)} %maximum_convert_fusion, f32[2,768]{1,0:T(2,128)} %copy-done.81, f32[2,768]{1,0:T(2,128)} %copy-done.82, f32[2,768]{1,0:T(2,128)} %copy-done.84, f32[2,768]{1,0:T(2,128)} %copy-done.85, f32[2,768]{1,0:T(2,128)} %copy-done.86, ...), kind=kLoop, calls=%fused_computation.302 | loop fusion | flops 48660480 | bytes 40864320 | tf_op jit(solution)/shard_map/mul | solution.py:515
  2434.8 26.6 reduce-scatter.24.cloned.1.call-done
  2468.3 131.2 %all-reduce.10.cloned.1.call-done = (f32[384]{0:T(512)}, f32[384]{0:T(512)}, f32[2304]{0:T(1024)}, f32[2,2,2,768]{3,2,1,0:T(2,128)}, f32[15,96]{1,0:T(8,128)}, /...) async-done(((f32[384]{0:T(512)}, f32[384]{0:T(512)}, f32[2304]{0:T(1024)}, ...) | async-done | bytes 103312 | tf_op jit(solution)/shard_map/psum | solution.py:570
  2599.5 35.7 %reduce-scatter.34.cloned.1.call-done = bf16[48,576]{1,0:T(8,128)(2,1)} async-done(((bf16[384,576]{1,0:T(8,128)(2,1)}), bf16[48,576]{1,0:T(8,128)(2,1)}) %reduce-scatter.34.cloned.1.call-update) | async-done | bytes 55312
  2637.0 126.1 %all-reduce.8.cloned.1.call-done = f32[2,3,3,3,768]{4,0,3,2,1:T(2,128)} async-done(((f32[2,3,3,3,768]{4,0,3,2,1:T(2,128)}), f32[2,3,3,3,768]{4,0,3,2,1:T(2,128)}) %all-reduce.8.cloned.1.call-update) | async-done | bytes 165904 | tf_op jit(solution)/shard_map/psum | solution.py:570
  (1076 shorter events, 1538.4 us)
Async XLA Ops:
  7.2 291.7 %all-gather.4.cloned.1.call-start = ((), (), s32[]{:S(2)}) async-start(), calls=%async_computation.11 | async-start | bytes 23887872 | tf_op jit(solution)/shard_map/all_gather | solution.py:329
  21.2 29.1 %collective-permute-start = (bf16[1,2,1,6,24,768]{5,4,3,2,1,0:T(8,128)(2,1)}, bf16[1,2,1,6,24,768]{5,4,3,2,1,0:T(8,128)(2,1)}, u32[]{:S(2)}, u32[]{:S(2)}) collective-permute-start(bf16[1,2,1,6,24,768]{5,4,3,2,1,0:T(8,128)(2,1)} %get-tuple-element.859), channel_id=1, source_target_pairs={{0,4},{1,5},{2,6},{3,7},{8,12},{9,13},{10,14},{11,15},{16,20},{17,... | collective-permute-start | bytes 1327112 | tf_op jit(solution)/shard_map/ppermute | solution.py:24
  26.9 23.5 collective-permute-start.1
  51.5 3.3 collective-permute-start.2
  53.0 5.2 collective-permute-start.3
  89.7 451.5 %reduce-scatter.28.cloned.1.call-start = ((), (), s32[]{:S(2)}) async-start(), calls=%async_computation.16 | async-start | bytes 737280 | tf_op jit(solution)/shard_map/reduce_scatter | solution.py:543
  507.9 63.1 %reduce-scatter.26.cloned.1.call-start = ((), (), s32[]{:S(2)}) async-start(), calls=%async_computation.15 | async-start | bytes 1474560 | tf_op jit(solution)/shard_map/reduce_scatter | solution.py:540
  519.5 137.7 %reduce-scatter.30.cloned.1.call-start = ((), (), s32[]{:S(2)}) async-start(), calls=%async_computation.17 | async-start | bytes 5898240 | tf_op jit(solution)/shard_map/reduce_scatter | solution.py:546
  524.4 220.8 %reduce-scatter.42.cloned.1.call-start = ((), (), s32[]{:S(2)}) async-start(), calls=%async_computation.24 | async-start | bytes 5898240
  536.0 320.2 %all-gather.6.cloned.1.call-start = ((), (), s32[]{:S(2)}) async-start(), calls=%async_computation.19 | async-start | bytes 23887872 | tf_op jit(solution)/shard_map/all_gather | solution.py:413
  536.6 1649.7 %reduce-scatter.38.cloned.1.call-start = ((), (), s32[]{:S(2)}) async-start(), calls=%async_computation.22 | async-start | bytes 221184
  542.9 1644.9 %reduce-scatter.36.cloned.1.call-start = ((), (), s32[]{:S(2)}) async-start(), calls=%async_computation.21 | async-start | bytes 442368
  572.9 1616.5 %reduce-scatter.40.cloned.1.call-start = ((), (), s32[]{:S(2)}) async-start(), calls=%async_computation.23 | async-start | bytes 1327104
  659.6 1531.7 %reduce-scatter.32.cloned.1.call-start = ((), (), s32[]{:S(2)}) async-start(), calls=%async_computation.18 | async-start | bytes 1769472 | tf_op jit(solution)/shard_map/reduce_scatter | solution.py:566
  663.1 193.2 %copy-start.108 = (s32[144]{0:T(256)S(1)}, s32[144]{0:T(256)}, u32[]{:S(2)}) copy-start(s32[144]{0:T(256)} %copy-done.107) | copy-start | bytes 1732
  747.7 1547.7 %reduce-scatter.22.cloned.1.call-start = ((), (), s32[]{:S(2)}) async-start(), calls=%async_computation.12 | async-start | bytes 24772608 | tf_op jit(solution)/shard_map/reduce_scatter | solution.py:461
  2155.1 306.3 %reduce-scatter.24.cloned.1.call-start = ((), (), s32[]{:S(2)}) async-start(), calls=%async_computation.13 | async-start | bytes 2211840 | tf_op jit(solution)/shard_map/reduce_scatter | solution.py:537
  2325.8 28.8 %collective-permute-start.4 = (bf16[1,2,1,6,24,768]{5,4,3,2,1,0:T(8,128)(2,1)}, bf16[1,2,1,6,24,768]{5,4,3,2,1,0:T(8,128)(2,1)}, u32[]{:S(2)}, u32[]{:S(2)}) collective-permute-start(bf16[1,2,1,6,24,768]{5,4,3,2,1,0:T(8,128)(2,1)} %get-tuple-element.855), channel_id=1, source_target_pairs={{0,4},{1,5},{2,6},{3,7},{8,12},{9,13},{10,14},{11,15},{16,20},{17,... | collective-permute-start | bytes 1327112 | tf_op jit(solution)/shard_map/ppermute | solution.py:24
  2329.9 24.8 collective-permute-start.5
  2355.8 4.0 collective-permute-start.6
  2357.3 4.4 collective-permute-start.7
  2414.9 184.6 %all-reduce.10.cloned.1.call-start = ((), (), s32[]{:S(2)}) async-start(), calls=%async_computation.25 | async-start | bytes 253952 | tf_op jit(solution)/shard_map/psum | solution.py:570
  2434.2 201.1 %reduce-scatter.34.cloned.1.call-start = ((), (), s32[]{:S(2)}) async-start(), calls=%async_computation.20 | async-start | bytes 552960
  2463.4 299.7 %all-reduce.8.cloned.1.call-start = ((), (), s32[]{:S(2)}) async-start(), calls=%async_computation.14 | async-start | bytes 331776 | tf_op jit(solution)/shard_map/psum | solution.py:570
  (213 other events, 3935.1 us)
Sparse Core Ops, SparseCore 0:
  89.8 116.9 all-gather.3
  508.0 33.1 reduce-scatter.27
  543.5 27.4 reduce-scatter.25
  573.2 83.9 reduce-scatter.29
  659.4 85.7 reduce-scatter.41
  746.9 109.2 all-gather.5
  859.2 33.5 reduce-scatter.37
  896.1 33.8 reduce-scatter.35
  933.6 36.7 reduce-scatter.39
  973.5 38.4 reduce-scatter.31
  2154.7 140.7 reduce-scatter.21
  2415.0 46.3 reduce-scatter.23
  2470.7 128.7 all-reduce.9
  2602.4 32.7 reduce-scatter.33
  2641.2 121.8 all-reduce.7
where the time goes:
time: 2810 us; the launch traced here: 2790 us
  local copies, waits for them, and re-layouts  940 us (33%)
  waiting for transfers between devices  734 us (26%)
  other arithmetic  699 us (25%)
  matrix products  340 us (12%)
  loops' own time  37.9 us (1%)
    scatter-add x24, other arithmetic, bias_backward(): jax.ops.segment_sum(weighted.reshape(-1, weighted.shape[-1]), target.resh...  395 us
    psum x2, waiting for transfers between devices, body(): lax.psum((gain1_grad, shift1_grad, bias_qkv, conv_grad, compress_grad, ta...  257 us
    scatter x8, local copies, waits for them, and re-layouts, spread(): lax.dynamic_update_slice_in_dim(jnp.zeros((batch, heads, queries, count_h...  167 us
    unnamed x20, waiting for transfers between devices  117 us
    all_gather x1, waiting for transfers between devices, body(): lax.all_gather(kv_local[None], ('tm', 'height'), axis=0, tiled=True)  108 us
    reduce_scatter x1, waiting for transfers between devices, body(): lax.psum_scatter(pieces.astype(jnp.bfloat16), ('tm', 'height'), scatter_d...  102 us
    dot_general x24, matrix products, bias_backward(): jnp.einsum('bhqk,qke->bqhe', along_grad, pick, precision=HIGHEST_PREC)  93.5 us
    reduce_scatter x1, waiting for transfers between devices, body(): lax.psum_scatter(grad_fc1.astype(jnp.bfloat16), 'clip', scatter_dimension...  84.2 us
  transfers between devices with their start and end apart: 23, of which 12 were waited for; matrix products, arithmetic and copies ran while one was open for 58% of the time, Pallas kernels for 0%

commit v1 on v0

v1 whole, which is shorter than its diff:
```python
import functools

import jax
import jax.numpy as jnp
import numpy as np
from jax import lax
from jax.experimental import pallas as pl
from jax.experimental.pallas import tpu as pltpu
from jax.sharding import PartitionSpec as P

HEADS = 8
SIDE_SMALL = 14
SIDE_BIG = 20
MEM = 2
EPSILON = 1e-06
SQRT_HALF = 0.7071067811865476
ROOT_TWO_PI = 2.5066282746310002
LOG2E = 1.4426950408889634
FAR = -1e30

GRID = 24
FR = 8
HALF = GRID // 2
VW = SIDE_BIG
VH = VW // 2
LANE = 128
PLANE = (VW + 1) * GRID
FLAT = GRID + (FR + 2) * PLANE
CUR = FR * VW * VW
KEYS_USED = CUR + MEM * FR * VH * VH
KEYS = -(-KEYS_USED // 256) * 256
TAB = 8 * FR + 2 * GRID * HALF

bf = jnp.bfloat16
f32 = jnp.float32
HI = lax.Precision.HIGHEST
G = ("tm", "height")


def nn(a, b, **kw):
    return lax.dot_general(a, b, (((1,), (0,)), ((), ())), preferred_element_type=f32, **kw)


def nt(a, b, **kw):
    return lax.dot_general(a, b, (((1,), (1,)), ((), ())), preferred_element_type=f32, **kw)


def tn(a, b, **kw):
    return lax.dot_general(a, b, (((0,), (0,)), ((), ())), preferred_element_type=f32, **kw)


def shape(dims, dtype):
    return jax.ShapeDtypeStruct(dims, dtype)


def call(kernel, outs, args, scratch=(), smem=1, cost=None, **kw):
    specs = [pl.BlockSpec(memory_space=pltpu.SMEM)] * smem
    specs += [pl.BlockSpec(memory_space=pltpu.VMEM)] * (len(args) - smem)
    return pl.pallas_call(
        kernel,
        out_shape=outs,
        in_specs=specs,
        out_specs=jax.tree.map(lambda _: pl.BlockSpec(memory_space=pltpu.VMEM), outs),
        scratch_shapes=list(scratch),
        compiler_params=pltpu.CompilerParams(vmem_limit_bytes=56 << 20),
        cost_estimate=cost,
        **kw,
    )(*args)


def pad_lanes(x, lanes):
    return jnp.concatenate([x, jnp.zeros((x.shape[0], lanes - x.shape[1]), x.dtype)], axis=1)


def layer_unit(x):
    centred = x - jnp.mean(x, axis=-1, keepdims=True)
    inverse = lax.rsqrt(jnp.mean(centred * centred, axis=-1, keepdims=True) + EPSILON)
    return centred * inverse, inverse


def pair_reduce(value, scratch, op):
    rows, lanes = value.shape
    outs = []
    for j in range(lanes // LANE):
        scratch[j, 0:rows, :] = value[:, j * LANE : (j + 1) * LANE]
    for j in range(lanes // LANE):
        outs.append(op(scratch[j, pl.ds(0, rows // 2, 2), :], scratch[j, pl.ds(1, rows // 2, 2), :]))
    return jnp.concatenate(outs, axis=1)


def pair_spread(value, scratch):
    rows, lanes = value.shape
    for j in range(lanes // LANE):
        part = value[:, j * LANE : (j + 1) * LANE]
        scratch[j, pl.ds(0, rows, 2), :] = part
        scratch[j, pl.ds(1, rows, 2), :] = part
    return jnp.concatenate([scratch[j, 0 : 2 * rows, :] for j in range(lanes // LANE)], axis=1)


def qkv_kernel(dims, meta, x_ref, g_ref, b_ref, w_ref, bq_ref, bkv_ref, kv_ref, n1_ref, mx_ref, q_ref, x20, tiles):
    frames, rows, width, hd = dims
    half = rows // 2
    side, height = meta[0], meta[3]
    per = rows * GRID
    valid_rows = frames * rows * VW
    quarter = frames * half * HALF
    g = g_ref[...]
    b = b_ref[...]
    for t in range(frames):
        x = x_ref[t * per : (t + 1) * per, :].astype(f32)
        unit, _ = layer_unit(x)
        low = (unit * g + b).astype(bf)
        full = low.astype(f32)
        for h in range(rows):
            x20[(t * rows + h) * VW : (t * rows + h + 1) * VW, :] = full[h * GRID : h * GRID + VW]
        tall = jnp.concatenate(
            [
                jnp.maximum(x[2 * a * GRID : (2 * a + 1) * GRID], x[(2 * a + 1) * GRID : (2 * a + 2) * GRID])
                for a in range(half)
            ],
            axis=0,
        )
        mx_ref[t * half * HALF : (t + 1) * half * HALF, :] = pair_reduce(tall, tiles, jnp.maximum)
        sums = jnp.concatenate(
            [full[2 * a * GRID : (2 * a + 1) * GRID] + full[(2 * a + 1) * GRID : (2 * a + 2) * GRID] for a in range(half)],
            axis=0,
        )
        n1_ref[valid_rows + t * half * HALF : valid_rows + (t + 1) * half * HALF, :] = pair_reduce(sums, tiles, jnp.add).astype(f32)
        query = nt(low, w_ref[0:width, :])
        tall = jnp.concatenate(
            [query[2 * a * GRID : (2 * a + 1) * GRID] + query[(2 * a + 1) * GRID : (2 * a + 2) * GRID] for a in range(half)],
            axis=0,
        )
        pooled = pair_reduce(tall, tiles, jnp.add) * 0.25 + bq_ref[...]
        for n in range(HEADS):
            q_ref[n, t * half * HALF : (t + 1) * half * HALF, :] = pad_lanes(pooled[:, n * hd : (n + 1) * hd], LANE)
    n1_ref[0:valid_rows, :] = x20[...]
    low20 = x20[...].astype(bf)
    cells = valid_rows // 2
    index = lax.broadcasted_iota(jnp.int32, (cells, 1), 0)
    line = (index * 3277) >> 16
    row = height * rows + lax.rem(line, rows)
    inside = ((row < side) & (index - line * VW < side)).astype(f32)
    for n in range(HEADS):
        weight = jnp.concatenate(
            [w_ref[width + n * hd : width + (n + 1) * hd, :], w_ref[2 * width + n * hd : 2 * width + (n + 1) * hd, :]], axis=0
        )
        y = nt(low20, weight)
        packed = jnp.concatenate([y[0:cells], y[cells : 2 * cells]], axis=1)
        kv_ref[n] = ((packed + bkv_ref[n : n + 1, :]) * inside).astype(bf)


def squeeze_kernel(dims, mem_ref, c_ref, q_ref, out_ref, tiles, squeezed):
    frames, rows, width, hd = dims
    half = rows // 2
    count = half * frames * VH
    odd = lax.broadcasted_iota(jnp.int32, (GRID, 1), 0) % 2 == 1
    for m in range(2):
        taps = [jnp.where(odd, c_ref[m, i, 1:2, :], c_ref[m, i, 0:1, :]) for i in range(2)]
        for s in range(MEM):
            for t in range(frames):
                parts = [
                    mem_ref[s, m, t, 2 * a].astype(f32) * taps[0] + mem_ref[s, m, t, 2 * a + 1].astype(f32) * taps[1]
                    for a in range(half)
                ]
                for a in range(half):
                    done = pair_reduce(parts[a], tiles.at[(t * half + a) % 4], jnp.add)
                    squeezed[m, s, a * frames * VH + t * VH : a * frames * VH + (t + 1) * VH, :] = done[0:VH]
            squeezed[m, s, count:LANE, :] = jnp.zeros((LANE - count, width), f32)
    quarter = frames * half * HALF
    for n in range(HEADS):
        cut = slice(n * hd, (n + 1) * hd)
        out_ref[n, 0:LANE, :] = jnp.concatenate(
            [squeezed[0, 0, :, cut], squeezed[1, 0, :, cut], squeezed[0, 1, :, cut], squeezed[1, 1, :, cut]], axis=1
        ).astype(bf)
        third = quarter // 3
        out_ref[n, LANE : LANE + third, :] = jnp.concatenate(
            [q_ref[n, i * third : (i + 1) * third, :] for i in range(3)], axis=1
        ).astype(bf)


def flat_row(t, h):
    return GRID + (1 + t) * PLANE + h * GRID


def fill_grid(grid):
    zero = jnp.zeros((GRID, LANE), f32)
    grid[0 : GRID + PLANE, :] = jnp.zeros((GRID + PLANE, LANE), f32)
    grid[flat_row(FR, 0) :, :] = jnp.zeros((FLAT - flat_row(FR, 0), LANE), f32)
    for t in range(FR):
        grid[flat_row(t, VW) : flat_row(t, VW) + GRID, :] = zero


def taps9(w_ref, part):
    return [[[w_ref[(a * 3 + b) * 3 + c : (a * 3 + b) * 3 + c + 1, part * LANE : (part + 1) * LANE] for c in range(3)] for b in range(3)] for a in range(3)]


def four_rows(grid, weights, base, flip):
    acc = [[None] * 3 for _ in range(4)]
    for line in range(-1, 5):
        for a in range(3):
            shift = (1 - a if flip else a - 1) * PLANE + line * GRID
            cells = grid[pl.ds(pl.multiple_of(base + shift, 8), GRID), :]
            for h in range(4):
                b = (h - line + 1) if flip else (line - h + 1)
                if b < 0 or b > 2:
                    continue
                for c in range(3):
                    term = cells * weights[a][b][c]
                    acc[h][c] = term if acc[h][c] is None else acc[h][c] + term
    outs = []
    for h in range(4):
        left, mid, right = (acc[h][2], acc[h][1], acc[h][0]) if flip else (acc[h][0], acc[h][1], acc[h][2])
        outs.append((pltpu.roll(left, 1, 0) + mid + pltpu.roll(right, GRID - 1, 0))[0:VW])
    return jnp.concatenate(outs, axis=0)


def conv_kernel(dims, meta, y_ref, w_ref, k_ref, v_ref, gk, gv):
    frames, rows, n_height, hd = dims
    side = meta[0]
    for grid in (gk, gv):
        fill_grid(grid)
    for src in range(HEADS):
        part = y_ref[src].astype(f32)
        for g in range(2):
            for m, grid in ((0, gk), (1, gv)):
                lane = (2 * g + m) * hd
                cut = pad_lanes(part[:, lane : lane + hd], LANE)
                for t2 in range(frames // 2):
                    for h in range(rows):
                        row = src % n_height * rows + h
                        if row >= VW:
                            continue
                        t = src // n_height * frames + g * (frames // 2) + t2
                        at = (t2 * rows + h) * VW
                        grid[flat_row(t, row) : flat_row(t, row) + GRID, :] = jnp.concatenate(
                            [cut[at : at + VW], jnp.zeros((GRID - VW, LANE), f32)], axis=0
                        )
    local = lax.broadcasted_iota(jnp.int32, (4 * VW, LANE), 0)
    lane = lax.broadcasted_iota(jnp.int32, (4 * VW, LANE), 1)
    line = (local * 3277) >> 16
    column = local - line * VW
    fixed = [(lane + o == 143 - column) | (lane + o == 191 - column) for o in (0, LANE)]
    ones = (lane == hd).astype(f32)

    def step(it, carry):
        t = it // (VW // 4)
        quad = it % (VW // 4)
        base = GRID + (1 + t) * PLANE + quad * 4 * GRID
        out = pl.ds(pl.multiple_of(it * (4 * VW), 16), 4 * VW)
        mixed_k = four_rows(gk, taps9(w_ref, 0), base, False)
        mixed_v = four_rows(gv, taps9(w_ref, 1), base, False)
        h = quad * 4 + line
        bad = (h >= side) | (column >= side)
        for o in range(2):
            at = lane + o * LANE
            hit = fixed[o] | (at == 103 - t) | (at == 151 - t) | (at == 123 - h) | (at == 171 - h) | ((at == 192) & bad)
            marks = hit.astype(f32)
            k_ref[out, o * LANE : (o + 1) * LANE] = ((mixed_k + marks) if o == 0 else marks).astype(bf)
        v_ref[out, :] = (mixed_v + ones).astype(bf)
        return carry

    lax.fori_loop(0, FR * VW // 4, step, 0)


def build_table(tab, t_ref, h_ref, w_ref):
    tab[...] = jnp.zeros(tab.shape, f32)
    for v in range(FR):
        tab[8 * v : 8 * v + FR, :] = t_ref[v : v + FR, :]
    for n, ref in ((0, h_ref), (1, w_ref)):
        for a in range(HALF):
            at = 8 * FR + (n * HALF + a) * GRID
            first = 2 * a + GRID - VW
            tab[at : at + VW, :] = ref[first : first + VW, :]


def attend_kernel(dims, meta, kc_ref, vc_ref, y_ref, t_ref, h_ref, w_ref, place_ref, k_ref, kt_ref, v_ref, qt_ref, q_ref, o_ref, l_ref, j_ref, vt, qrow, tab, s_ref):
    frames, rows, n_height, hd = dims
    half = rows // 2
    side, length = meta[0], meta[1]
    queries = qrow.shape[0]
    scale = hd**-0.5
    k_ref[0:CUR, :] = kc_ref[...]
    v_ref[0:CUR, :] = vc_ref[...]
    count = half * frames * VH
    each = frames * VH
    per_q = queries // HEADS
    third = per_q // 3
    lane1 = lax.broadcasted_iota(jnp.int32, (1, LANE), 1)
    at = CUR
    for src in range(HEADS):
        packed = y_ref[src].astype(f32)
        first = src % n_height * half
        used = min(max(VH - first, 0), half) * each
        if used > 0:
            halves = []
            for m in range(2):
                halves.append(jnp.concatenate([packed[0:used, m * hd : (m + 1) * hd], packed[0:used, (2 + m) * hd : (3 + m) * hd]], axis=0))
            index = lax.broadcasted_iota(jnp.int32, (2 * used, LANE), 0)
            step = (index >= used).astype(jnp.int32)
            inner = index - step * used
            a = (inner >= each).astype(jnp.int32) + (inner >= 2 * each).astype(jnp.int32)
            inner = inner - a * each
            c = inner - ((inner * 6554) >> 16) * VH
            bad = (step >= length) | (2 * (first + a) >= side) | (2 * c >= side)
            mark = (bad & (lax.broadcasted_iota(jnp.int32, (2 * used, LANE), 1) == 64)).astype(f32)
            k_ref[at : at + 2 * used, 0:LANE] = pad_lanes(halves[0], LANE).astype(bf)
            k_ref[at : at + 2 * used, LANE:] = mark.astype(bf)
            v_ref[at : at + 2 * used, :] = (pad_lanes(halves[1], LANE) + (lane1 == hd).astype(f32)).astype(bf)
            at += 2 * used
        for i in range(3):
            qrow[src * per_q + i * third : src * per_q + (i + 1) * third, :] = packed[LANE : LANE + third, i * LANE : (i + 1) * LANE]
    rest = KEYS - at
    k_ref[at:, 0:LANE] = jnp.zeros((rest, LANE), bf)
    k_ref[at:, LANE:] = jnp.broadcast_to((lane1 == 64).astype(f32), (rest, LANE)).astype(bf)
    v_ref[at:, :] = jnp.zeros((rest, LANE), bf)
    for i in range(KEYS // 256):
        cut = slice(i * 256, (i + 1) * 256)
        kt_ref[:, cut] = k_ref[cut, :].T
        vt[:, cut] = v_ref[cut, :].T
    q_ref[...] = qrow[...].astype(bf)
    pt = qrow[...].T[0:hd]
    build_table(tab, t_ref, h_ref, w_ref)
    along = nn(tab[...], pt, precision=HI)
    tq, aq, cq = place_ref[0:1, :], place_ref[1:2, :], place_ref[2:3, :]
    part_t = jnp.zeros((FR, queries), f32)
    for v in range(FR):
        part_t = jnp.where(tq == v, along[8 * v : 8 * v + FR], part_t)
    parts = []
    for n, place in ((0, aq), (1, cq)):
        part = jnp.zeros((GRID, queries), f32)
        for a in range(HALF):
            row = 8 * FR + (n * HALF + a) * GRID
            part = jnp.where(place == a, along[row : row + GRID], part)
        parts.append(part[0:VW])
    bias = jnp.concatenate([part_t] + parts, axis=0) * hd**0.5
    high = bias.astype(bf)
    low = (bias - high.astype(f32)).astype(bf)
    qt_ref[0:hd, :] = pt.astype(bf)
    qt_ref[hd : hd + 48, :] = high
    qt_ref[hd + 48 : hd + 96, :] = low
    tail = lax.broadcasted_iota(jnp.int32, (64, queries), 0)
    qt_ref[192:256, :] = jnp.where(tail == 0, FAR, 0.0).astype(bf)
    factor = scale * LOG2E
    wide = s_ref.shape[1]
    blocks = [(i, min(i + 512, KEYS)) for i in range(0, KEYS, 512)]

    def one(block, carry):
        cols = pl.ds(pl.multiple_of(block * wide, LANE), wide)
        query = qt_ref[:, cols]
        top = jnp.full((8, wide), FAR, f32)
        for lo, hi in blocks:
            scores = nn(k_ref[lo:hi, :], query)
            s_ref[lo:hi, :] = scores
            top = jnp.maximum(top, jnp.max(scores.reshape((hi - lo) // 8, 8, wide), axis=0))
        top = jnp.max(top, axis=0, keepdims=True) * factor
        total = jnp.zeros((LANE, wide), f32)
        for lo, hi in blocks:
            weights = jnp.exp2(s_ref[lo:hi, :] * factor - top).astype(bf)
            total = total + nn(vt[:, lo:hi], weights)
        norm = total[hd : hd + 1]
        o_ref[:, cols] = total[0:hd] / norm
        l_ref[:, cols] = top + jnp.log2(norm)
        return carry

    lax.fori_loop(0, queries // wide, one, 0)
    j_ref[...] = pad_lanes((o_ref[...] + pt).T, LANE).astype(bf)


def mlp_kernel(dims, j_ref, mx_ref, cot_ref, wp_ref, ws_ref, bps_ref, g_ref, b_ref, w1_ref, b1_ref, w2_ref, b2_ref,
               out_ref, keep_ref, act_ref, hg_ref, dj_ref, mg_ref, gb1_ref, small_ref,
               resid, n2, acc, ngrad, joined):
    width, hd = dims
    i = pl.program_id(0)

    @pl.when(i == 0)
    def _():
        joined[...] = jnp.concatenate([j_ref[n][:, 0:hd] for n in range(HEADS)], axis=1)
        value = nt(joined[...], wp_ref[...]) + nt(mx_ref[...].astype(bf), ws_ref[...]) + bps_ref[...]
        resid[...] = value
        unit, _ = layer_unit(value)
        n2[...] = (unit * g_ref[...] + b_ref[...]).astype(bf)
        acc[...] = jnp.zeros(acc.shape, f32)
        ngrad[...] = jnp.zeros(ngrad.shape, f32)

    hidden = nt(n2[...], w1_ref[...]) + b1_ref[...]
    gate = 0.5 * (1.0 + lax.erf(hidden * SQRT_HALF))
    act = (hidden * gate).astype(bf)
    act_ref[0] = act
    acc[...] += nt(act, w2_ref[...])
    grad = nn(cot_ref[...], w2_ref[...])
    hgrad = (grad * (gate + hidden * jnp.exp(-0.5 * hidden * hidden) / ROOT_TWO_PI)).astype(bf)
    hg_ref[0] = hgrad
    gb1_ref[...] = jnp.sum(hgrad.astype(f32), axis=0, keepdims=True)
    ngrad[...] += nn(hgrad, w1_ref[...])

    @pl.when(i == pl.num_programs(0) - 1)
    def _():
        value = resid[...]
        out_ref[...] = (value + acc[...] + b2_ref[...]).astype(bf)
        unit, inverse = layer_unit(value)
        cot = cot_ref[...].astype(f32)
        grad = ngrad[...]
        scaled = grad * g_ref[...]
        back = inverse * (
            scaled - jnp.mean(scaled, axis=-1, keepdims=True) - unit * jnp.mean(scaled * unit, axis=-1, keepdims=True)
        )
        low = (cot + back).astype(bf)
        keep_ref[:, 0:width] = n2[...]
        keep_ref[:, width : 2 * width] = low
        keep_ref[:, 2 * width :] = mx_ref[...].astype(bf)
        joined_grad = nn(low, wp_ref[...])
        for n in range(HEADS):
            dj_ref[n] = pad_lanes(joined_grad[:, n * hd : (n + 1) * hd], LANE).astype(bf)
        mg_ref[...] = nn(low, ws_ref[...])
        small_ref[0:1, :] = jnp.sum(low.astype(f32), axis=0, keepdims=True)
        small_ref[1:2, :] = jnp.sum(grad * unit, axis=0, keepdims=True)
        small_ref[2:3, :] = jnp.sum(grad, axis=0, keepdims=True)
        small_ref[3:4, :] = jnp.sum(cot, axis=0, keepdims=True)
        small_ref[4:8, :] = jnp.zeros((4, width), f32)


def attend_back_kernel(dims, k_ref, kt_ref, v_ref, qt_ref, q_ref, o_ref, l_ref, dj_ref, t_ref, h_ref, w_ref, place_ref,
                       dk_ref, dv_ref, mem_ref, pq_ref, gt_ref, gh_ref, gw_ref,
                       dot_ref, dq, tab, dtab, dks, dvs, delta):
    frames, rows, n_height, hd = dims
    half = rows // 2
    queries = q_ref.shape[0]
    scale = hd**-0.5
    factor = scale * LOG2E
    turned = dj_ref[...].astype(f32).T
    dot_ref[...] = turned.astype(bf)
    delta[...] = jnp.sum(turned[0:hd] * o_ref[...], axis=0, keepdims=True)
    dq[...] = jnp.zeros(dq.shape, f32)
    wide = 384

    def chunk(i, carry):
        cut = pl.ds(pl.multiple_of(i * 256, 256), 256)
        dk = jnp.zeros((256, LANE), f32)
        dv = jnp.zeros((256, LANE), f32)
        for lo in range(0, queries, wide):
            cols = slice(lo, lo + wide)
            shares = jnp.exp2(nn(k_ref[cut, :], qt_ref[:, cols]) * factor - l_ref[:, cols])
            slope = nn(v_ref[cut, :], dot_ref[:, cols])
            score = (shares * (slope - delta[:, cols])).astype(bf)
            dv = dv + nn(shares.astype(bf), dj_ref[cols, :])
            dk = dk + nn(score, q_ref[cols, :])
            dq[:, cols] += nn(kt_ref[0 : dq.shape[0], cut], score)
        dks[cut, :] = dk * scale
        dvs[cut, :] = dv
        return carry

    lax.fori_loop(0, KEYS // 256, chunk, 0)
    dk_ref[...] = dks[0:CUR, :]
    dv_ref[...] = dvs[0:CUR, :]
    each = frames * VH
    at = CUR
    for dst in range(HEADS):
        first = dst % n_height * half
        used = min(max(VH - first, 0), half) * each
        if used > 0:
            parts = [ref[at + s * used : at + (s + 1) * used, 0:hd] for s in range(MEM) for ref in (dks, dvs)]
            packed = jnp.concatenate(parts, axis=1)
            at += 2 * used
        if used < LANE:
            zero = jnp.zeros((LANE - used, 4 * hd), f32)
            packed = jnp.concatenate([packed, zero], axis=0) if used > 0 else zero
        mem_ref[dst] = packed.astype(bf)
    build_table(tab, t_ref, h_ref, w_ref)
    tq, aq, cq = place_ref[0:1, :], place_ref[1:2, :], place_ref[2:3, :]
    grad_t = dq[hd : hd + FR, :]
    for v in range(FR):
        dtab[8 * v : 8 * v + FR, :] = jnp.where(tq == v, grad_t, 0.0)
    for n, place in ((0, aq), (1, cq)):
        part = jnp.concatenate(
            [dq[hd + FR + n * VW : hd + FR + (n + 1) * VW, :], jnp.zeros((GRID - VW, queries), f32)], axis=0
        )
        for a in range(HALF):
            row = 8 * FR + (n * HALF + a) * GRID
            dtab[row : row + GRID, :] = jnp.where(place == a, part, 0.0)
    pooled_grad = dq[0:hd, :] * scale + tn(tab[...], dtab[...], precision=HI) + dot_ref[0:hd, :].astype(f32)
    pq_ref[...] = pad_lanes(pooled_grad.T * 0.25, LANE)
    grads = nn(dtab[...], q_ref[...].astype(f32), precision=HI)
    gt_ref[...] = jnp.zeros(gt_ref.shape, f32)
    gh_ref[...] = jnp.zeros(gh_ref.shape, f32)
    gw_ref[...] = jnp.zeros(gw_ref.shape, f32)
    for v in range(FR):
        gt_ref[v : v + FR, :] += grads[8 * v : 8 * v + FR]
    for n, ref in ((0, gh_ref), (1, gw_ref)):
        for a in range(HALF):
            row = 8 * FR + (n * HALF + a) * GRID
            first = 2 * a + GRID - VW
            ref[first : first + VW, :] += grads[row : row + VW]


def conv_back_kernel(dims, meta, y_ref, dk_ref, dv_ref, pq_ref, w_ref, out_ref, gw_ref, pg_ref, mk, mv, gk, gv, acc):
    frames, rows, n_height, hd = dims
    side = meta[0]
    for grid in (gk, gv, mk, mv):
        fill_grid(grid)
    for src in range(HEADS):
        part = y_ref[src].astype(f32)
        for g in range(2):
            for m, grid in ((0, mk), (1, mv)):
                lane = (2 * g + m) * hd
                cut = pad_lanes(part[:, lane : lane + hd], LANE)
                for t2 in range(frames // 2):
                    for h in range(rows):
                        row = src % n_height * rows + h
                        if row >= VW:
                            continue
                        t = src // n_height * frames + g * (frames // 2) + t2
                        at = (t2 * rows + h) * VW
                        grid[flat_row(t, row) : flat_row(t, row) + GRID, :] = jnp.concatenate(
                            [cut[at : at + VW], jnp.zeros((GRID - VW, LANE), f32)], axis=0
                        )
    for ref, grid in ((dk_ref, gk), (dv_ref, gv)):
        for t in range(FR):
            for h in range(VW):
                at = (t * VW + h) * VW
                grid[flat_row(t, h) : flat_row(t, h) + GRID, :] = jnp.concatenate(
                    [ref[at : at + VW, :], jnp.zeros((GRID - VW, LANE), f32)], axis=0
                )
    acc[...] = jnp.zeros(acc.shape, f32)
    local = lax.broadcasted_iota(jnp.int32, (4 * VW, 1), 0)
    line = (local * 3277) >> 16
    column = local - line * VW

    def step(it, carry):
        t = it // (VW // 4)
        quad = it % (VW // 4)
        base = GRID + (1 + t) * PLANE + quad * 4 * GRID
        out = pl.ds(pl.multiple_of(it * (4 * VW), 16), 4 * VW)
        inside = ((quad * 4 + line < side) & (column < side)).astype(f32)
        for m, grid in ((0, gk), (1, gv)):
            back = four_rows(grid, taps9(w_ref, m), base, True)
            pg_ref[out, m * LANE : (m + 1) * LANE] = back * inside
        for m, grid, masked in ((0, gk, mk), (1, gv, mv)):
            for h in range(4):
                here = grid[pl.ds(pl.multiple_of(base + h * GRID, 8), GRID), :]
                turned = [pltpu.roll(here, GRID - 1, 0), here, pltpu.roll(here, 1, 0)]
                for a in range(3):
                    for b in range(3):
                        cells = masked[pl.ds(pl.multiple_of(base + (a - 1) * PLANE + (h + b - 1) * GRID, 8), GRID), :]
                        for c in range(3):
                            prod = cells * turned[c]
                            tap = m * 27 + (a * 3 + b) * 3 + c
                            acc[tap] += prod[0:8] + prod[8:16] + prod[16:24]
        return carry

    lax.fori_loop(0, FR * VW // 4, step, 0)
    for tap in range(54):
        gw_ref[tap : tap + 1, :] = jnp.sum(acc[tap], axis=0, keepdims=True)
    gw_ref[54:, :] = jnp.zeros((gw_ref.shape[0] - 54, LANE), f32)
    span = rows * VW
    for dst in range(HEADS):
        first = dst % n_height * rows
        used = min(max(VW - first, 0), rows) * VW
        lines = []
        for t2 in range(frames // 2):
            parts = []
            for g in range(2):
                t = dst // n_height * frames + g * (frames // 2) + t2
                at = (t * VW + first) * VW
                for m in range(2):
                    parts.append(pg_ref[at : at + used, m * LANE : m * LANE + hd])
            packed = jnp.concatenate(parts, axis=1)
            if used < span:
                packed = jnp.concatenate([packed, jnp.zeros((span - used, 4 * hd), f32)], axis=0)
            lines.append(packed)
        cells = span * (frames // 2)
        out_ref[dst, 0:cells, :] = jnp.concatenate(lines, axis=0).astype(bf)
        per_q = pq_ref.shape[0] // HEADS
        third = per_q // 3
        out_ref[dst, cells : cells + third, :] = jnp.concatenate(
            [pq_ref[dst * per_q + i * third : dst * per_q + (i + 1) * third, :] for i in range(3)], axis=1
        ).astype(bf)


def qkv_grad_kernel(dims, pg_ref, n1_ref, grad_ref, bias_ref):
    frames, rows, n_height, hd, channels = dims
    cells = rows * VW * (frames // 2)
    third = pg_ref.shape[1] - cells
    total_kv = jnp.zeros((2 * hd, channels), f32)
    total_q = jnp.zeros((LANE, channels), f32)
    sum_kv = jnp.zeros((1, 2 * hd), f32)
    sum_q = jnp.zeros((1, LANE), f32)
    for src in range(HEADS):
        packed = pg_ref[src]
        for g in range(2):
            part = packed[0:cells, g * 2 * hd : (g + 1) * 2 * hd]
            total_kv = total_kv + tn(part, n1_ref[src, g * cells : (g + 1) * cells, :])
            sum_kv = sum_kv + jnp.sum(part.astype(f32), axis=0, keepdims=True)
        for i in range(3):
            part = packed[cells:, i * LANE : (i + 1) * LANE]
            at = 2 * cells + i * third
            total_q = total_q + tn(part, n1_ref[src, at : at + third, :])
            sum_q = sum_q + jnp.sum(part.astype(f32), axis=0, keepdims=True)
    total = jnp.concatenate([total_q[0:hd], total_kv], axis=0)
    cols = channels // HEADS
    for n in range(HEADS):
        grad_ref[n] = pad_lanes(total[:, n * cols : (n + 1) * cols], LANE).astype(bf)
    bias_ref[0:1, :] = jnp.concatenate([sum_q[:, 0:hd] * 4.0, sum_kv, jnp.zeros((1, hd), f32)], axis=1)
    bias_ref[1:8, :] = jnp.zeros((7, 4 * hd), f32)


def weight_grad_kernel(dims, meta, keep_ref, cot_ref, act_ref, hg_ref, j_ref, fc2_ref, fc1_ref, rest_ref):
    width, hd, channels = dims
    member = meta[4]
    normed = keep_ref[:, 0:width]
    resid = keep_ref[:, width : 2 * width]
    fc2_ref[...] = tn(cot_ref[...], act_ref[...]).astype(bf)
    fc1 = tn(hg_ref[...], normed)
    for n in range(HEADS):
        fc1_ref[n] = pad_lanes(fc1[:, n * hd : (n + 1) * hd], LANE).astype(bf)
    cols = channels // HEADS
    pick = (
        lax.broadcasted_iota(jnp.int32, (channels, LANE), 0)
        == lax.broadcasted_iota(jnp.int32, (channels, LANE), 1) + member * cols
    ) & (lax.broadcasted_iota(jnp.int32, (channels, LANE), 1) < cols)
    maxima = nn(keep_ref[:, 2 * width :], pick.astype(f32).astype(bf)).astype(bf)
    both = tn(resid, jnp.concatenate([j_ref[...], maxima], axis=1))
    rest_ref[...] = both.astype(bf)


def last_kernel(dims, x_ref, g_ref, w_ref, pg_ref, mx_ref, mg_ref, out_ref, small_ref, full, tiles):
    frames, rows, width, hd = dims
    half = rows // 2
    cells = rows * VW * (frames // 2)
    third = pg_ref.shape[1] - cells
    channels = x_ref.shape[1]
    tops = jnp.zeros((cells, channels), f32)
    lows = jnp.zeros((cells, channels), f32)
    queries = []
    for n in range(HEADS):
        weight = jnp.concatenate(
            [w_ref[width + n * hd : width + (n + 1) * hd, :], w_ref[2 * width + n * hd : 2 * width + (n + 1) * hd, :]], axis=0
        )
        packed = pg_ref[n]
        tops = tops + nn(packed[0:cells, 0 : 2 * hd], weight)
        lows = lows + nn(packed[0:cells, 2 * hd :], weight)
        queries.append(
            jnp.concatenate([packed[cells:, i * LANE : i * LANE + hd] for i in range(3)], axis=0)
        )
    for part, value in ((0, tops), (1, lows)):
        for line in range(frames // 2 * rows):
            at = (part * (frames // 2) * rows + line) * GRID
            full[at : at + GRID, :] = jnp.concatenate(
                [value[line * VW : (line + 1) * VW], jnp.zeros((GRID - VW, channels), f32)], axis=0
            )
    query = nn(jnp.concatenate(queries, axis=1), w_ref[0:width, :])
    per = rows * GRID
    per_q = half * HALF
    g = g_ref[...]
    gain = jnp.zeros((1, channels), f32)
    shift = jnp.zeros((1, channels), f32)
    for t in range(frames):
        cut = slice(t * per_q, (t + 1) * per_q)
        x = x_ref[t * per : (t + 1) * per, :].astype(f32)

        def spread(value):
            wide = pair_spread(value, tiles)
            lines = []
            for a in range(half):
                lines += [wide[a * GRID : (a + 1) * GRID]] * 2
            return jnp.concatenate(lines, axis=0)

        grad = full[t * per : (t + 1) * per, :] + spread(query[cut])
        hits = (x == spread(mx_ref[cut, :])).astype(f32)
        sums = jnp.concatenate(
            [hits[2 * a * GRID : (2 * a + 1) * GRID] + hits[(2 * a + 1) * GRID : (2 * a + 2) * GRID] for a in range(half)], axis=0
        )
        number = pair_reduce(sums, tiles, jnp.add)
        pool = hits * spread(mg_ref[cut, :] / number)
        unit, inverse = layer_unit(x)
        scaled = grad * g
        back = inverse * (
            scaled - jnp.mean(scaled, axis=-1, keepdims=True) - unit * jnp.mean(scaled * unit, axis=-1, keepdims=True)
        )
        out_ref[t * per : (t + 1) * per, :] = (back + pool).astype(bf)
        gain = gain + jnp.sum(grad * unit, axis=0, keepdims=True)
        shift = shift + jnp.sum(grad, axis=0, keepdims=True)
    small_ref[0:1, :] = gain
    small_ref[1:2, :] = shift
    small_ref[2:8, :] = jnp.zeros((6, channels), f32)


def compress_kernel(dims, mem_ref, p_ref, out_ref, tiles):
    frames, rows, width, hd = dims
    half = rows // 2
    for m in range(2):
        sums = [jnp.zeros((GRID, width), f32) for _ in range(2)]
        for s in range(MEM):
            grads = jnp.concatenate([p_ref[n][:, (2 * s + m) * hd : (2 * s + m + 1) * hd] for n in range(HEADS)], axis=1).astype(f32)
            for t in range(frames):
                for a in range(half):
                    at = (a * frames + t) * VH
                    some = jnp.concatenate([grads[at : at + VH], jnp.zeros((HALF - VH, width), f32)], axis=0)
                    wide = pair_spread(some, tiles.at[(t * half + a) % 4])
                    for i in range(2):
                        sums[i] = sums[i] + mem_ref[s, m, t, 2 * a + i].astype(f32) * wide
        odd = (lax.broadcasted_iota(jnp.int32, (GRID, 1), 0) % 2 == 1).astype(f32)
        for i in range(2):
            out_ref[4 * m + 2 * i : 4 * m + 2 * i + 1, :] = jnp.sum(sums[i] * (1.0 - odd), axis=0, keepdims=True)
            out_ref[4 * m + 2 * i + 1 : 4 * m + 2 * i + 2, :] = jnp.sum(sums[i] * odd, axis=0, keepdims=True)


def everywhere(block):
    group = lax.axis_size("tm") * lax.axis_size("height")
    rows = block.shape[0]
    padded = -(-rows // (8 * group)) * 8 * group
    block = jnp.pad(block, ((0, padded - rows), (0, 0))).reshape(group, padded // group, LANE)
    part = jnp.sum(lax.all_to_all(block, G, 0, 0, tiled=True), axis=0)
    part = jnp.sum(lax.all_gather(part, "clip", axis=0), axis=0)
    return lax.all_gather(part, G, axis=0, tiled=True)[0:rows]


def body(clip_input, memory, mem_len, res_id, norm1_gain, norm1_bias, w_qkv, b_qkv, conv_kv, compress, rel_t, rel_h, rel_w,
         w_proj, b_proj, w_short, b_short, norm2_gain, norm2_bias, w_fc1, b_fc1, w_fc2, b_fc2, cotangent):
    _, frames, rows, grid, channels = clip_input.shape
    width = w_proj.shape[0]
    mlp = w_fc1.shape[0]
    hd = width // HEADS
    half = rows // 2
    n_clip = lax.axis_size("clip")
    n_height = lax.axis_size("height")
    tm, height = lax.axis_index("tm"), lax.axis_index("height")
    member = tm * n_height + height
    side = SIDE_SMALL + (SIDE_BIG - SIDE_SMALL) * res_id[0]
    meta = jnp.stack([side, mem_len[0], tm, height, member]).astype(jnp.int32)
    cells_all = frames * rows * GRID
    valid = frames * rows * VW
    per_q = frames * half * HALF
    third = per_q // 3
    queries = HEADS * per_q
    x = clip_input.reshape(cells_all, channels)
    mem = memory[0]
    cot = cotangent.reshape(per_q, width)

    split = b_qkv.reshape(3, HEADS, hd)
    bkv = jnp.concatenate([split[1], split[2], split[1], split[2]], axis=1)
    dims = (frames, rows, width, hd)
    kvp, n1, mx, qh = call(
        functools.partial(qkv_kernel, dims),
        (shape((HEADS, valid // 2, 4 * hd), bf), shape((valid + per_q, channels), f32), shape((per_q, channels), f32), shape((HEADS, per_q, LANE), f32)),
        (meta, x, norm1_gain[None], norm1_bias[None], w_qkv, b_qkv[None, :width], bkv),
        scratch=[pltpu.VMEM((valid, channels), f32), pltpu.VMEM((width // LANE, rows * GRID, LANE), f32)],
    )
    y1 = lax.all_to_all(kvp, G, 0, 0, tiled=True)
    pay2 = call(
        functools.partial(squeeze_kernel, dims),
        shape((HEADS, LANE + third, 4 * hd), bf),
        (mem, compress, qh),
        scratch=[pltpu.VMEM((4, width // LANE, GRID, LANE), f32), pltpu.VMEM((2, MEM, LANE, width), f32)],
        smem=0,
    )
    y2 = lax.all_to_all(pay2, G, 0, 0, tiled=True)
    taps = lax.dynamic_slice_in_dim(conv_kv.reshape(2, 27, width), member * hd, hd, 2)
    taps = jnp.pad(taps, ((0, 0), (0, 5), (0, LANE - hd)))
    taps = jnp.concatenate([taps[0], taps[1]], axis=1)
    hdims = (frames, rows, n_height, hd)
    kc, vc = call(
        functools.partial(conv_kernel, hdims),
        (shape((CUR, 2 * LANE), bf), shape((CUR, LANE), bf)),
        (meta, y1, taps),
        scratch=[pltpu.VMEM((FLAT, LANE), f32)] * 2,
    )
    index = np.arange(queries)
    src, local = index // per_q, index % per_q
    place = np.zeros((8, queries), np.int32)
    place[0] = src // n_height * frames + local // (half * HALF)
    place[1] = src % n_height * half + local // HALF % half
    place[2] = local % HALF
    place = jnp.asarray(place)
    wide = 384
    k_all, kt_all, v_all, qt_all, q_all, o_all, l_all, joined = call(
        functools.partial(attend_kernel, hdims),
        (
            shape((KEYS, 2 * LANE), bf),
            shape((2 * LANE, KEYS), bf),
            shape((KEYS, LANE), bf),
            shape((2 * LANE, queries), bf),
            shape((queries, LANE), bf),
            shape((hd, queries), f32),
            shape((1, queries), f32),
            shape((queries, LANE), bf),
        ),
        (meta, kc, vc, y2, rel_t, rel_h, rel_w, place),
        scratch=[
            pltpu.VMEM((LANE, KEYS), bf),
            pltpu.VMEM((queries, LANE), f32),
            pltpu.VMEM((TAB, hd), f32),
            pltpu.VMEM((KEYS, wide), f32),
        ],
    )
    joined_rows = lax.all_to_all(joined.reshape(HEADS, per_q, LANE), G, 0, 0, tiled=True)
    block = mlp // HEADS
    whole = lambda *dims: pl.BlockSpec(dims, lambda i: (0,) * len(dims))
    keep_width = 2 * width + channels
    output, keep, act, hgrad, dj, max_grad, gb1, small2 = pl.pallas_call(
        functools.partial(mlp_kernel, (width, hd)),
        grid=(HEADS,),
        out_shape=(
            shape((per_q, width), bf),
            shape((per_q, keep_width), bf),
            shape((HEADS, per_q, block), bf),
            shape((HEADS, per_q, block), bf),
            shape((HEADS, per_q, LANE), bf),
            shape((per_q, channels), f32),
            shape((1, mlp), f32),
            shape((8, width), f32),
        ),
        in_specs=[
            whole(HEADS, per_q, LANE),
            whole(per_q, channels),
            whole(per_q, width),
            whole(width, width),
            whole(width, channels),
            whole(1, width),
            whole(1, width),
            whole(1, width),
            pl.BlockSpec((block, width), lambda i: (i, 0)),
            pl.BlockSpec((1, block), lambda i: (0, i)),
            pl.BlockSpec((width, block), lambda i: (0, i)),
            whole(1, width),
        ],
        out_specs=(
            whole(per_q, width),
            whole(per_q, keep_width),
            pl.BlockSpec((1, per_q, block), lambda i: (i, 0, 0)),
            pl.BlockSpec((1, per_q, block), lambda i: (i, 0, 0)),
            whole(HEADS, per_q, LANE),
            whole(per_q, channels),
            pl.BlockSpec((1, block), lambda i: (0, i)),
            whole(8, width),
        ),
        scratch_shapes=[
            pltpu.VMEM((per_q, width), f32),
            pltpu.VMEM((per_q, width), bf),
            pltpu.VMEM((per_q, width), f32),
            pltpu.VMEM((per_q, width), f32),
            pltpu.VMEM((per_q, width), bf),
        ],
        compiler_params=pltpu.CompilerParams(vmem_limit_bytes=56 << 20),
    )(
        joined_rows, mx, cot, w_proj, w_short, (b_proj + b_short)[None], norm2_gain[None], norm2_bias[None],
        w_fc1, b_fc1[None], w_fc2, b_fc2[None],
    )
    dj_head = lax.all_to_all(dj, G, 0, 0, tiled=True).reshape(queries, LANE)
    n1_full = lax.all_gather(n1.astype(bf), G, axis=0)
    cot_full = lax.all_gather(cot, G, axis=0, tiled=True)
    keep_full = lax.all_gather(keep, G, axis=0, tiled=True)
    act_head = lax.all_to_all(act, G, 0, 0, tiled=True).reshape(queries, block)
    hg_head = lax.all_to_all(hgrad, G, 0, 0, tiled=True).reshape(queries, block)

    dk, dv, dmem, pq, gt, gh, gw = call(
        functools.partial(attend_back_kernel, hdims),
        (
            shape((CUR, LANE), f32),
            shape((CUR, LANE), f32),
            shape((HEADS, LANE, 4 * hd), bf),
            shape((queries, LANE), f32),
            shape((16, LANE), f32),
            shape((48, LANE), f32),
            shape((48, LANE), f32),
        ),
        (k_all, kt_all, v_all, qt_all, q_all, o_all, l_all, dj_head, rel_t, rel_h, rel_w, place),
        scratch=[
            pltpu.VMEM((LANE, queries), bf),
            pltpu.VMEM((hd + 48, queries), f32),
            pltpu.VMEM((TAB, hd), f32),
            pltpu.VMEM((TAB, queries), f32),
            pltpu.VMEM((KEYS, LANE), f32),
            pltpu.VMEM((KEYS, LANE), f32),
            pltpu.VMEM((1, queries), f32),
        ],
        smem=0,
    )
    mem_back = lax.all_to_all(dmem, G, 0, 0, tiled=True)
    pgp, gconv = pl.pallas_call(
        functools.partial(conv_back_kernel, hdims),
        out_shape=(shape((HEADS, valid // 2 + third, 4 * hd), bf), shape((64, LANE), f32)),
        in_specs=[pl.BlockSpec(memory_space=pltpu.SMEM)] + [pl.BlockSpec(memory_space=pltpu.VMEM)] * 5,
        out_specs=(pl.BlockSpec(memory_space=pltpu.VMEM),) * 2,
        scratch_shapes=[pltpu.VMEM((CUR, 2 * LANE), f32)] + [pltpu.VMEM((FLAT, LANE), f32)] * 4 + [pltpu.VMEM((54, 8, LANE), f32)],
        compiler_params=pltpu.CompilerParams(vmem_limit_bytes=56 << 20),
    )(meta, y1, dk, dv, pq, taps)
    pg_rows = lax.all_to_all(pgp, G, 0, 0, tiled=True)
    fc2p, fc1p, restp = call(
        functools.partial(weight_grad_kernel, (width, hd, channels)),
        (shape((width, block), bf), shape((HEADS, block, LANE), bf), shape((width, 2 * LANE), bf)),
        (meta, keep_full, cot_full, act_head, hg_head, joined),
    )
    qkvp, bqkv = call(
        functools.partial(qkv_grad_kernel, (frames, rows, n_height, hd, channels)),
        (shape((HEADS, 3 * hd, LANE), bf), shape((8, 4 * hd), f32)),
        (pgp, n1_full),
        smem=0,
    )
    fc1m = lax.all_to_all(fc1p, G, 0, 0, tiled=True)
    qkvm = lax.all_to_all(qkvp, G, 0, 0, tiled=True)

    def over_clips(value):
        value = value.reshape((n_clip, value.shape[0] // n_clip) + value.shape[1:])
        return jnp.sum(lax.all_to_all(value, "clip", 0, 0, tiled=True).astype(f32), axis=0)

    part_fc2 = over_clips(fc2p)
    rest = over_clips(restp)
    part_fc1 = over_clips(fc1m.reshape(mlp, LANE))[:, :hd]
    cols = channels // HEADS
    qkv_rows = qkvm.reshape(HEADS, 3, hd, LANE).transpose(1, 0, 2, 3).reshape(3 * width, LANE)
    part_qkv = over_clips(qkv_rows)[:, :cols]
    part_proj = rest[:, :hd]
    part_short = rest[:, LANE : LANE + cols]

    input_grad, small1 = call(
        functools.partial(last_kernel, dims),
        (shape((cells_all, channels), bf), shape((8, channels), f32)),
        (x, norm1_gain[None], w_qkv, pg_rows, mx, max_grad),
        scratch=[pltpu.VMEM((cells_all, channels), f32), pltpu.VMEM((width // LANE, rows * GRID, LANE), f32)],
        smem=0,
    )
    gcomp = call(
        functools.partial(compress_kernel, dims),
        shape((8, width), f32),
        (mem, mem_back),
        scratch=[pltpu.VMEM((4, width // LANE, GRID, LANE), f32)],
        smem=0,
    )
    head_part = jnp.concatenate([gconv[:54, :hd], bqkv[0, : 3 * hd].reshape(3, hd)], axis=0)
    head_part = lax.all_gather(head_part, G, axis=0)
    head_part = jnp.moveaxis(head_part, 0, 1).reshape(57, width)
    pieces = [head_part / (lax.axis_size("tm") * n_height), gcomp, small2[:4], gb1.reshape(-1, width)]
    flat = jnp.concatenate(pieces, axis=0).reshape(-1, LANE)
    tables = jnp.concatenate([gt, gh, gw], axis=0)
    norm1 = small1[:2].reshape(-1, LANE)
    flat_rows, table_rows = flat.shape[0], tables.shape[0]
    total = everywhere(jnp.concatenate([flat, tables, norm1], axis=0))
    wide_rows = total[:flat_rows].reshape(-1, width)
    tables = total[flat_rows : flat_rows + table_rows]
    norm1 = total[flat_rows + table_rows :].reshape(2, channels)
    bqkv = wide_rows[54:57].reshape(-1)
    base = 57
    gcomp = wide_rows[base : base + 8].reshape(2, 2, 2, width)
    small2 = wide_rows[base + 8 : base + 12]
    gb1 = wide_rows[base + 12 :].reshape(-1)
    return (
        output.reshape(1, frames, half, HALF, width),
        input_grad.reshape(clip_input.shape),
        norm1[0],
        norm1[1],
        part_qkv,
        bqkv,
        wide_rows[:54].reshape(2, 3, 3, 3, width),
        gcomp,
        tables[:15, :hd],
        tables[16 : 16 + 47, :hd],
        tables[64 : 64 + 47, :hd],
        part_proj,
        small2[0],
        part_short,
        small2[0],
        small2[1],
        small2[2],
        part_fc1,
        gb1,
        part_fc2,
        small2[3],
    )


def solution(mesh):
    split = P("clip", "tm", "height", None, None)
    shared = P()
    weight = P("clip", ("tm", "height"))
    placed = (split, P("clip", None, None, "tm", "height", None, None), P("clip"), P("clip")) + (shared,) * 19 + (split,)
    outs = (split, split, shared, shared, weight) + (shared,) * 6 + (weight, shared, weight, shared, shared, shared, weight, shared, weight, shared)
    return jax.shard_map(body, mesh=mesh, in_specs=placed, out_specs=outs, check_vma=False)
```

time: 2810 us -> 398 us (0.14)
  local copies, waits for them, and re-layouts: 940 us -> 23.6 us
  other arithmetic: 699 us -> 5.14 us
  waiting for transfers between devices: 734 us -> 64.6 us
  matrix products: 340 us -> 0 us
  Pallas kernels: 0 us -> 129 us
  blocking collectives: 0 us -> 115 us
  loops' own time: 37.9 us -> 0 us
    scatter-add x24 -> x0, other arithmetic: 395 us -> none  [bias_backward(): jax.ops.segment_sum(weighted.reshape(-1, weighted.shape[-1]), target.resh...]
    dot_general x108 -> x0, matrix products: 340 us -> none  [the longest x24 93.5 us: bias_backward(): jnp.einsum('bhqk,qke->bqhe', along_grad, pick, precision=HIGHEST_PREC)]
    psum x2 -> x0, waiting for transfers between devices: 257 us -> none  [body(): lax.psum((gain1_grad, shift1_grad, bias_qkv, conv_grad, compress_grad, ta...]
    reduce_scatter x6 -> x0, waiting for transfers between devices: 246 us -> none  [the longest x1 102 us: body(): lax.psum_scatter(pieces.astype(jnp.bfloat16), ('tm', 'height'), scatter_d...]
    scatter x16 -> x0, local copies, waits for them, and re-layouts: 227 us -> none  [the longest x8 167 us: spread(): lax.dynamic_update_slice_in_dim(jnp.zeros((batch, heads, queries, count_h...]
    slice x18 -> x11, local copies, waits for them, and re-layouts: 158 us -> 4.13 us  [the longest x1 0.78 us: body(): bkv = jnp.concatenate([split[1], split[2], split[1], split[2]], axis=1)]
    pallas_call x0 -> x11, Pallas kernels: none -> 129 us  [the longest x9 93.6 us: call(): pl.pallas_call(kernel, out_shape=outs, in_specs=specs, out_specs=jax.tree...]
    unnamed x20 -> x3, waiting for transfers between devices: 117 us -> 0.05 us
  transfers between devices with their start and end apart: 23 -> 14, of which waited for: 12 -> 6; matrix products, arithmetic and copies ran while one was open for 58% -> 5% of each run, Pallas kernels for 0% -> 31%
where the time goes in v1:
time: 398 us; the launch traced here: 396 us
  Pallas kernels  129 us (32%)
  blocking collectives  115 us (29%)
  waiting for transfers between devices  64.6 us (16%)
  starting transfers between devices  43.6 us (11%)
  local copies, waits for them, and re-layouts  23.6 us (6%)
  between operations  15.5 us (4%)
  other arithmetic  5.14 us (1%)
    pallas_call x9, Pallas kernels, call(): pl.pallas_call(kernel, out_shape=outs, in_specs=specs, out_specs=jax.tree...  93.6 us
    all_to_all x1, blocking collectives, body(): pg_rows = lax.all_to_all(pgp, G, 0, 0, tiled=True)  27.4 us
    pallas_call x1, Pallas kernels, body(): pl.pallas_call(functools.partial(conv_back_kernel, hdims), out_shape=(sha...  21 us
    all_gather x1, blocking collectives, everywhere(): part = jnp.sum(lax.all_gather(part, 'clip', axis=0), axis=0)  20.9 us
    all_to_all x1, waiting for transfers between devices, body(): y1 = lax.all_to_all(kvp, G, 0, 0, tiled=True)  20.5 us
    all_to_all x3, waiting for transfers between devices, over_clips(): lax.all_to_all(value, 'clip', 0, 0, tiled=True).astype(f32)  20.4 us
    all_to_all x1, blocking collectives, body(): fc1m = lax.all_to_all(fc1p, G, 0, 0, tiled=True)  16.7 us
    all_to_all x1, blocking collectives, over_clips(): lax.all_to_all(value, 'clip', 0, 0, tiled=True).astype(f32)  14.7 us
  transfers between devices with their start and end apart: 14, of which 6 were waited for; matrix products, arithmetic and copies ran while one was open for 5% of the time, Pallas kernels for 31%

profile of v1, /device:TPU:0, one launch (start us, length us, event | category | flops | bytes accessed | tf_op | source)
XLA Modules:
  0.0 396.2 jit_solution(17429227634543346288)
XLA Ops:
  13.9 5.2 %shard_map.400 = (bf16[8,240,384]{2,1,0:T(8,128)(2,1)}, f32[624,384]{1,0:T(8,128)}, f32[144,384]{1,0:T(8,128)}, f32[8,144,128]{2,1,0:T(8,128)}) custom-call(s32[5]{0:T(128)} %stack.16.meta, bf16[576,384]{1,0:T(8,128)(2,1)} %bitcast.55, f32[1,384]{1,0:T(1,128)} %broadcast_in_dim.25.g_ref, f32[1,384]{1,0:T(1,128)} %broadcast_in_dim.26.b_ref, ...), custom_call_target="tpu_custom_call" | custom-call | tf_op jit(solution)/shard_map/pallas_call | solution.py:59
  22.0 5.2 %all-to-all-start = ((bf16[8,240,384]{2,1,0:T(8,128)(2,1)}), bf16[8,240,384]{2,1,0:T(8,128)(2,1)S(1)}, u32[]{:S(2)}, u32[]{:S(2)}) async-start(bf16[8,240,384]{2,1,0:T(8,128)(2,1)} %get-tuple-element.59), calls=%async_computation | async-start | bytes 2949120 | tf_op jit(solution)/shard_map/all_to_all | solution.py:749
  31.7 20.5 %all-to-all-done.y_ref = bf16[8,240,384]{2,1,0:T(8,128)(2,1)S(1)} async-done(((bf16[8,240,384]{2,1,0:T(8,128)(2,1)}), bf16[8,240,384]{2,1,0:T(8,128)(2,1)S(1)}, u32[]{:S(2)}, u32[]{:S(2)}) %all-to-all-start) | async-done | bytes 1474592 | tf_op jit(solution)/shard_map/all_to_all | solution.py:749
  56.6 13.3 %shard_map.401 = (bf16[3200,256]{1,0:T(8,128)(2,1)}, bf16[3200,128]{1,0:T(8,128)(2,1)}) custom-call(s32[5]{0:T(128)} %stack.16.meta, bf16[8,240,384]{2,1,0:T(8,128)(2,1)} %copy-done.2, f32[32,256]{1,0:T(8,128)} %pad_maximum_fusion.1.w_ref), custom_call_target="tpu_custom_call" | custom-call | tf_op jit(solution)/shard_map/pallas_call | solution.py:59
  69.9 9.5 %all-to-all-done.1.y_ref = bf16[8,176,384]{2,1,0:T(8,128)(2,1)S(1)} async-done(((bf16[8,176,384]{2,1,0:T(8,128)(2,1)}), bf16[8,176,384]{2,1,0:T(8,128)(2,1)S(1)}, u32[]{:S(2)}, u32[]{:S(2)}) %all-to-all-start.1) | async-done | bytes 1081376 | tf_op jit(solution)/shard_map/all_to_all | solution.py:757
  80.4 15.9 %shard_map.403 = (bf16[4864,256]{1,0:T(8,128)(2,1)}, bf16[256,4864]{1,0:T(8,128)(2,1)}, bf16[4864,128]{1,0:T(8,128)(2,1)}, bf16[256,1152]{1,0:T(8,128)(2,1)}, bf...) custom-call(s32[5]{0:T(128)} %stack.16.meta, ...), custom_call_target="tpu_custom_call" | custom-call | tf_op jit(solution)/shard_map/pallas_call | solution.py:59
  102.4 7.7 %all-to-all-done.2.j_ref = bf16[8,144,128]{2,1,0:T(8,128)(2,1)S(1)} async-done(((bf16[8,144,128]{2,1,0:T(8,128)(2,1)}), bf16[8,144,128]{2,1,0:T(8,128)(2,1)S(1)}, u32[]{:S(2)}, u32[]{:S(2)}) %all-to-all-start.2) | async-done | bytes 294944 | tf_op jit(solution)/shard_map/all_to_all | solution.py:796
  110.8 14.3 %shard_map.404 = (bf16[144,768]{1,0:T(8,128)(2,1)}, bf16[144,1920]{1,0:T(8,128)(2,1)}, bf16[8,144,384]{2,1,0:T(8,128)(2,1)}, bf16[8,144,384]{2,1,0:T(8,128)(2,1)...) custom-call(bf16[8,144,128]{2,1,0:T(8,128)(2,1)} %copy-done.7, ...), custom_call_target="tpu_custom_call" | custom-call | tf_op jit(solution)/shard_map/pallas_call | solution.py:800
  125.1 12.5 %all_to_all.75 = bf16[8,144,128]{2,1,0:T(8,128)(2,1)} all-to-all(bf16[8,144,128]{2,1,0:T(8,128)(2,1)} %get-tuple-element.73), channel_id=1, replica_groups=mesh['clip'=4,'tm'=2,'height'=4] {'tm','height'}, dimensions={0} | all-to-all | bytes 589824 | tf_op jit(solution)/shard_map/all_to_all | solution.py:849
  141.2 31.9 %shard_map.405 = (f32[3200,128]{1,0:T(8,128)}, f32[3200,128]{1,0:T(8,128)}, bf16[8,128,384]{2,1,0:T(8,128)(2,1)}, f32[1152,128]{1,0:T(8,128)}, f32[16,128]{1,0:T...) custom-call(bf16[4864,256]{1,0:T(8,128)(2,1)} %get-tuple-element.66.k_ref, bf16[256,4864]{1,0:T(8,128)(2,1)} %get-tuple-element.67.kt_ref, ...), custom_call_target="tpu_custom_call" | custom-call | tf_op jit(solution)/shard_map/pallas_call | solution.py:59
  177.2 21.0 %shard_map.406 = (bf16[8,288,384]{2,1,0:T(8,128)(2,1)}, f32[64,128]{1,0:T(8,128)}) custom-call(s32[5]{0:T(128)} %stack.16.meta, bf16[8,240,384]{2,1,0:T(8,128)(2,1)} %copy-done.2, f32[3200,128]{1,0:T(8,128)} %get-tuple-element.74.dk_ref, f32[3200,128]{1,0:T(8,128)} %get-tuple-element.75.dv_ref, f32[1152,128]{1,0:T(8,128)} %get-tuple-element.76.pq_ref, ...), custom_call_target="tpu_custom_call" | custom-call | tf_op jit(solution)/shard_map/pallas_call | solution.py:880
  198.2 27.4 %all_to_all.76.pg_ref = bf16[8,288,384]{2,1,0:T(8,128)(2,1)} all-to-all(bf16[8,288,384]{2,1,0:T(8,128)(2,1)} %get-tuple-element.77.pg_ref), channel_id=1, replica_groups=mesh['clip'=4,'tm'=2,'height'=4] {'tm','height'}, dimensions={0} | all-to-all | bytes 3538944 | tf_op jit(solution)/shard_map/all_to_all | solution.py:888
  235.1 5.1 %shard_map.407 = (bf16[576,384]{1,0:T(8,128)(2,1)}, f32[8,384]{1,0:T(8,128)}) custom-call(bf16[576,384]{1,0:T(8,128)(2,1)} %bitcast.56, f32[1,384]{1,0:T(1,128)} %broadcast_in_dim.25.g_ref, bf16[2304,384]{1,0:T(8,128)(2,1)} %w_ref.7, bf16[8,288,384]{2,1,0:T(8,128)(2,1)} %all_to_all.76.pg_ref, f32[144,384]{1,0:T(8,128)} %get-tuple-element.64.mx_ref, ...), custom_call_target="tpu_custom_call" | custom-call | tf_op jit(solution)/shard_map/pallas_call | solution.py:59
  240.9 5.9 %shard_map.408 = (bf16[8,288,128]{2,1,0:T(8,128)(2,1)}, f32[8,384]{1,0:T(8,128)}) custom-call(bf16[8,288,384]{2,1,0:T(8,128)(2,1)} %get-tuple-element.77.pg_ref, bf16[8,624,384]{2,1,0:T(8,128)(2,1)} %bitcast.51), custom_call_target="tpu_custom_call" | custom-call | tf_op jit(solution)/shard_map/pallas_call | solution.py:59
  251.5 13.2 %all-gather.3 = f32[8,57,96]{2,1,0:T(8,128)S(1)} all-gather(f32[1,57,96]{2,1,0:T(8,128)S(1)} %maximum_bitcast_fusion), channel_id=3, replica_groups=mesh['clip'=4,'tm'=2,'height'=4] {'tm','height'}, dimensions={0}, use_global_device_ids=true | all-gather | bytes 196992 | tf_op jit(solution)/shard_map/all_gather | solution.py:931
  270.7 6.4 %all-to-all-done.6 = f32[8,72,128]{2,1,0:T(8,128)S(1)} async-done(((f32[8,72,128]{2,1,0:T(8,128)}), f32[8,72,128]{2,1,0:T(8,128)S(1)}, u32[]{:S(2)}, u32[]{:S(2)}) %all-to-all-start.6) | async-done | bytes 294944 | tf_op jit(solution)/shard_map/all_to_all | solution.py:713
  277.1 4.6 %all-to-all-start.8 = ((bf16[4,576,128]{2,1,0:T(8,128)(2,1)}), bf16[4,576,128]{2,1,0:T(8,128)(2,1)S(1)}, u32[]{:S(2)}, u32[]{:S(2)}) async-start(bf16[4,576,128]{2,1,0:T(8,128)(2,1)} %bitcast.21), calls=%async_computation.8 | async-start | bytes 1179648 | tf_op jit(solution)/shard_map/all_to_all | solution.py:905
  281.6 7.7 %shard_map.410 = (bf16[768,384]{1,0:T(8,128)(2,1)}, bf16[8,384,128]{2,1,0:T(8,128)(2,1)}, bf16[768,256]{1,0:T(8,128)(2,1)}) custom-call(s32[5]{0:T(128)} %stack.16.meta, bf16[1152,1920]{1,0:T(8,128)(2,1)} %all-gather.8.cloned.1.call-done.keep_ref, bf16[1152,768]{1,0:T(8,128)(2,1)} %all-gather.10.cloned.1.call-done.cot_ref, bf16[1152,384]{1,0:T(8,128)(2,1)} %bitcast.52, ...), custom_call_target="tpu_custom_call" | custom-call | tf_op jit(solution)/shard_map/pallas_call | solution.py:59
  289.3 7.4 %all-to-all-done.8 = bf16[4,576,128]{2,1,0:T(8,128)(2,1)S(1)} async-done(((bf16[4,576,128]{2,1,0:T(8,128)(2,1)}), bf16[4,576,128]{2,1,0:T(8,128)(2,1)S(1)}, u32[]{:S(2)}, u32[]{:S(2)}) %all-to-all-start.8) | async-done | bytes 589856 | tf_op jit(solution)/shard_map/all_to_all | solution.py:905
  296.7 14.7 %all_to_all.77 = bf16[4,192,256]{2,1,0:T(8,128)(2,1)S(1)} all-to-all(bf16[4,192,256]{2,1,0:T(8,128)(2,1)} %bitcast.62), channel_id=1, replica_groups=mesh['clip'=4,'tm'=2,'height'=4] {'clip'}, dimensions={0} | all-to-all | bytes 786432 | tf_op jit(solution)/shard_map/all_to_all | solution.py:905
  311.4 16.7 %all_to_all.78 = bf16[8,384,128]{2,1,0:T(8,128)(2,1)} all-to-all(bf16[8,384,128]{2,1,0:T(8,128)(2,1)} %get-tuple-element.95), channel_id=1, replica_groups=mesh['clip'=4,'tm'=2,'height'=4] {'tm','height'}, dimensions={0} | all-to-all | bytes 1572864 | tf_op jit(solution)/shard_map/all_to_all | solution.py:900
  332.6 20.9 %all-gather.2 = f32[288,128]{1,0:T(8,128)S(1)} all-gather(f32[72,128]{1,0:T(8,128)S(1)} %reduce_sum.54), channel_id=4, replica_groups=mesh['clip'=4,'tm'=2,'height'=4] {'clip'}, dimensions={0}, use_global_device_ids=true | all-gather | bytes 184320 | tf_op jit(solution)/shard_map/all_gather | solution.py:714
  353.5 9.2 %all_gather.33 = f32[576,128]{1,0:T(8,128)S(1)} all-gather(f32[72,128]{1,0:T(8,128)S(1)} %reduce_sum.55), channel_id=1, replica_groups=mesh['clip'=4,'tm'=2,'height'=4] {'tm','height'}, dimensions={0}, use_global_device_ids=true | all-gather | bytes 331776 | tf_op jit(solution)/shard_map/all_gather | solution.py:715
  375.0 13.1 %all-to-all-done.13 = bf16[4,768,128]{2,1,0:T(8,128)(2,1)S(1)} async-done(((bf16[4,768,128]{2,1,0:T(8,128)(2,1)}), bf16[4,768,128]{2,1,0:T(8,128)(2,1)S(1)}, u32[]{:S(2)}, u32[]{:S(2)}) %all-to-all-start.13) | async-done | bytes 786464 | tf_op jit(solution)/shard_map/all_to_all | solution.py:905
  (134 shorter events, 71.5 us)
Async XLA Ops:
  7.2 48.7 %copy-start = (f32[2,3,3,3,768]{4,0,3,2,1:T(2,128)S(1)}, f32[2,3,3,3,768]{4,0,3,2,1:T(2,128)}, u32[]{:S(2)}) copy-start(f32[2,3,3,3,768]{4,0,3,2,1:T(2,128)} %param.33) | copy-start | bytes 497668
  7.2 233.6 %all-gather.12.cloned.1.call-start = ((), (), s32[]{:S(2)}) async-start(), calls=%async_computation.17 | async-start | bytes 4313088 | tf_op jit(solution)/shard_map/all_gather | solution.py:850
  21.1 260.5 %all-gather.10.cloned.1.call-start = ((), (), s32[]{:S(2)}) async-start(), calls=%async_computation.16 | async-start | bytes 1990656 | tf_op jit(solution)/shard_map/all_gather | solution.py:851
  22.0 30.3 %all-to-all-start = ((bf16[8,240,384]{2,1,0:T(8,128)(2,1)}), bf16[8,240,384]{2,1,0:T(8,128)(2,1)S(1)}, u32[]{:S(2)}, u32[]{:S(2)}) async-start(bf16[8,240,384]{2,1,0:T(8,128)(2,1)} %get-tuple-element.59), calls=%async_computation | async-start | bytes 2949120 | tf_op jit(solution)/shard_map/all_to_all | solution.py:749
  52.3 27.2 %all-to-all-start.1 = ((bf16[8,176,384]{2,1,0:T(8,128)(2,1)}), bf16[8,176,384]{2,1,0:T(8,128)(2,1)S(1)}, u32[]{:S(2)}, u32[]{:S(2)}) async-start(bf16[8,176,384]{2,1,0:T(8,128)(2,1)} %shard_map.402), calls=%async_computation.1 | async-start | bytes 2162688 | tf_op jit(solution)/shard_map/all_to_all | solution.py:757
  80.4 19.6 %copy-start.18 = (f32[768]{0:T(1024)S(1)}, f32[768]{0:T(1024)}, u32[]{:S(2)}) copy-start(f32[768]{0:T(1024)} %param.39) | copy-start | bytes 9220
  80.4 19.6 %copy-start.19 = (f32[768]{0:T(1024)S(1)}, f32[768]{0:T(1024)}, u32[]{:S(2)}) copy-start(f32[768]{0:T(1024)} %param.41) | copy-start | bytes 9220
  80.4 20.2 %copy-start.20 = (f32[768]{0:T(1024)S(1)}, f32[768]{0:T(1024)}, u32[]{:S(2)}) copy-start(f32[768]{0:T(1024)} %param.42) | copy-start | bytes 9220
  80.4 20.8 %copy-start.21 = (f32[768]{0:T(1024)S(1)}, f32[768]{0:T(1024)}, u32[]{:S(2)}) copy-start(f32[768]{0:T(1024)} %param.43) | copy-start | bytes 9220
  80.4 21.3 %copy-start.22 = (f32[768]{0:T(1024)S(1)}, f32[768]{0:T(1024)}, u32[]{:S(2)}) copy-start(f32[768]{0:T(1024)} %param.47) | copy-start | bytes 9220
  96.3 13.8 %all-to-all-start.2 = ((bf16[8,144,128]{2,1,0:T(8,128)(2,1)}), bf16[8,144,128]{2,1,0:T(8,128)(2,1)S(1)}, u32[]{:S(2)}, u32[]{:S(2)}) async-start(bf16[8,144,128]{2,1,0:T(8,128)(2,1)} %bitcast.58), calls=%async_computation.2 | async-start | bytes 589824 | tf_op jit(solution)/shard_map/all_to_all | solution.py:796
  99.8 181.9 %all-gather.8.cloned.1.call-start = ((), (), s32[]{:S(2)}) async-start(), calls=%async_computation.15 | async-start | bytes 4976640 | tf_op jit(solution)/shard_map/all_gather | solution.py:852
  137.6 35.5 %all-to-all-start.9 = ((bf16[8,144,384]{2,1,0:T(8,128)(2,1)}), bf16[8,144,384]{2,1,0:T(8,128)(2,1)S(1)}, u32[]{:S(2)}, u32[]{:S(2)}) async-start(bf16[8,144,384]{2,1,0:T(8,128)(2,1)} %get-tuple-element.92), calls=%async_computation.9 | async-start | bytes 1769472 | tf_op jit(solution)/shard_map/all_to_all | solution.py:853
  173.1 25.1 %copy-start.4 = (bf16[8,144,384]{2,1,0:T(8,128)(2,1)}, bf16[8,144,384]{2,1,0:T(8,128)(2,1)S(1)}, u32[]{:S(2)}) copy-start(bf16[8,144,384]{2,1,0:T(8,128)(2,1)S(1)} %all-to-all-done.9) | copy-start | bytes 2654212
  173.1 25.1 %all-to-all-start.5 = ((bf16[8,128,384]{2,1,0:T(8,128)(2,1)}), bf16[8,128,384]{2,1,0:T(8,128)(2,1)S(1)}, u32[]{:S(2)}, u32[]{:S(2)}) async-start(bf16[8,128,384]{2,1,0:T(8,128)(2,1)} %get-tuple-element.83), calls=%async_computation.5 | async-start | bytes 1572864 | tf_op jit(solution)/shard_map/all_to_all | solution.py:879
  198.2 27.4 %copy-start.6 = (bf16[8,128,384]{2,1,0:T(8,128)(2,1)}, bf16[8,128,384]{2,1,0:T(8,128)(2,1)S(1)}, u32[]{:S(2)}) copy-start(bf16[8,128,384]{2,1,0:T(8,128)(2,1)S(1)} %all-to-all-done.5.p_ref) | copy-start | bytes 2359300
  225.7 21.0 %all-to-all-start.10 = ((bf16[8,144,384]{2,1,0:T(8,128)(2,1)}), bf16[8,144,384]{2,1,0:T(8,128)(2,1)S(1)}, u32[]{:S(2)}, u32[]{:S(2)}) async-start(bf16[8,144,384]{2,1,0:T(8,128)(2,1)} %get-tuple-element.93), calls=%async_computation.10 | async-start | bytes 1769472 | tf_op jit(solution)/shard_map/all_to_all | solution.py:854
  246.7 19.7 %all-to-all-start.7 = ((bf16[8,288,128]{2,1,0:T(8,128)(2,1)}), bf16[8,288,128]{2,1,0:T(8,128)(2,1)S(1)}, u32[]{:S(2)}, u32[]{:S(2)}) async-start(bf16[8,288,128]{2,1,0:T(8,128)(2,1)} %get-tuple-element.90), calls=%async_computation.7 | async-start | bytes 1179648 | tf_op jit(solution)/shard_map/all_to_all | solution.py:901
  266.4 10.6 %all-to-all-start.6 = ((f32[8,72,128]{2,1,0:T(8,128)}), f32[8,72,128]{2,1,0:T(8,128)S(1)}, u32[]{:S(2)}, u32[]{:S(2)}) async-start(f32[8,72,128]{2,1,0:T(8,128)} %bitcast.15), calls=%async_computation.6 | async-start | bytes 589824 | tf_op jit(solution)/shard_map/all_to_all | solution.py:713
  277.1 19.6 %all-to-all-start.8 = ((bf16[4,576,128]{2,1,0:T(8,128)(2,1)}), bf16[4,576,128]{2,1,0:T(8,128)(2,1)S(1)}, u32[]{:S(2)}, u32[]{:S(2)}) async-start(bf16[4,576,128]{2,1,0:T(8,128)(2,1)} %bitcast.21), calls=%async_computation.8 | async-start | bytes 1179648 | tf_op jit(solution)/shard_map/all_to_all | solution.py:905
  296.7 35.0 %copy-start.9 = (bf16[144,768]{1,0:T(8,128)(2,1)S(1)}, bf16[144,768]{1,0:T(8,128)(2,1)}, u32[]{:S(2)}) copy-start(bf16[144,768]{1,0:T(8,128)(2,1)} %get-tuple-element.65) | copy-start | bytes 663556
  328.2 35.2 %all-to-all-start.14 = ((bf16[4,192,384]{2,1,0:T(8,128)(2,1)}), bf16[4,192,384]{2,1,0:T(8,128)(2,1)S(1)}, u32[]{:S(2)}, u32[]{:S(2)}) async-start(bf16[4,192,384]{2,1,0:T(8,128)(2,1)} %bitcast.31), calls=%async_computation.14 | async-start | bytes 1179648 | tf_op jit(solution)/shard_map/all_to_all | solution.py:905
  363.3 25.7 %copy-start.14 = (f32[768]{0:T(1024)}, f32[768]{0:T(1024)S(1)}, u32[]{:S(2)}) copy-start(f32[768]{0:T(1024)S(1)} %get-tuple-element.229) | copy-start | bytes 9220
  363.3 24.7 %all-to-all-start.13 = ((bf16[4,768,128]{2,1,0:T(8,128)(2,1)}), bf16[4,768,128]{2,1,0:T(8,128)(2,1)S(1)}, u32[]{:S(2)}, u32[]{:S(2)}) async-start(bf16[4,768,128]{2,1,0:T(8,128)(2,1)} %bitcast.29), calls=%async_computation.13 | async-start | bytes 1572864 | tf_op jit(solution)/shard_map/all_to_all | solution.py:905
  (13 other events, 125.1 us)
Sparse Core Ops, SparseCore 0:
  21.2 56.0 all-gather.11
  79.2 32.5 all-gather.9
  125.2 42.1 all-gather.7

commit v2 on v1

v2 whole, which is shorter than its diff:
```python
import functools

import jax
import jax.numpy as jnp
import numpy as np
from jax import lax
from jax.experimental import pallas as pl
from jax.experimental.pallas import tpu as pltpu
from jax.sharding import PartitionSpec as P

HEADS = 8
SIDE_SMALL = 14
SIDE_BIG = 20
MEM = 2
EPSILON = 1e-06
SQRT_HALF = 0.7071067811865476
ROOT_TWO_PI = 2.5066282746310002
LOG2E = 1.4426950408889634
FAR = -1e30

GRID = 24
FR = 8
HALF = GRID // 2
VW = SIDE_BIG
VH = VW // 2
LANE = 128
PLANE = (VW + 1) * GRID
FLAT = GRID + (FR + 2) * PLANE
CUR = FR * VW * VW
KEYS_USED = CUR + MEM * FR * VH * VH
KEYS = -(-KEYS_USED // 256) * 256
LATE_COMP, LATE_SMALL, LATE_TABLE, LATE = 17, 33, 35, 40
TABLE_ROWS = 2 * FR + 4 * GRID
TAB = 8 * FR + 2 * GRID * HALF

bf = jnp.bfloat16
f32 = jnp.float32
HI = lax.Precision.HIGHEST
G = ("tm", "height")


def nn(a, b, **kw):
    return lax.dot_general(a, b, (((1,), (0,)), ((), ())), preferred_element_type=f32, **kw)


def nt(a, b, **kw):
    return lax.dot_general(a, b, (((1,), (1,)), ((), ())), preferred_element_type=f32, **kw)


def tn(a, b, **kw):
    return lax.dot_general(a, b, (((0,), (0,)), ((), ())), preferred_element_type=f32, **kw)


def shape(dims, dtype):
    return jax.ShapeDtypeStruct(dims, dtype)


def cost(us):
    return pl.CostEstimate(flops=int(us * 1e9), bytes_accessed=0, transcendentals=0)


def call(kernel, outs, args, scratch=(), smem=1, us=5, far=0):
    specs = [pl.BlockSpec(memory_space=pltpu.SMEM)] * smem
    specs += [pl.BlockSpec(memory_space=pltpu.VMEM)] * (len(args) - smem - far)
    specs += [pl.BlockSpec(memory_space=pl.ANY)] * far
    return pl.pallas_call(
        kernel,
        out_shape=outs,
        in_specs=specs,
        out_specs=jax.tree.map(lambda _: pl.BlockSpec(memory_space=pltpu.VMEM), outs),
        scratch_shapes=list(scratch),
        compiler_params=pltpu.CompilerParams(vmem_limit_bytes=56 << 20),
        cost_estimate=cost(us),
    )(*args)


def row_of(ref, lo, hi):
    return ref[lo:hi].reshape(1, hi - lo)


def pack_rows(value, scratch, groups):
    rows, lanes = value.shape
    scratch[0:rows, :] = pad_lanes(value, LANE)
    parts = [scratch[pl.ds(g, rows // groups, groups), :][:, 0:lanes] for g in range(groups)]
    return jnp.concatenate(parts, axis=1)


def pad_lanes(x, lanes):
    return jnp.concatenate([x, jnp.zeros((x.shape[0], lanes - x.shape[1]), x.dtype)], axis=1)


def layer_unit(x):
    centred = x - jnp.mean(x, axis=-1, keepdims=True)
    inverse = lax.rsqrt(jnp.mean(centred * centred, axis=-1, keepdims=True) + EPSILON)
    return centred * inverse, inverse


def pair_reduce(value, scratch, op):
    rows, lanes = value.shape
    outs = []
    for j in range(lanes // LANE):
        scratch[j, 0:rows, :] = value[:, j * LANE : (j + 1) * LANE]
    for j in range(lanes // LANE):
        outs.append(op(scratch[j, pl.ds(0, rows // 2, 2), :], scratch[j, pl.ds(1, rows // 2, 2), :]))
    return jnp.concatenate(outs, axis=1)


def join_lines(value, op):
    return jnp.concatenate(
        [op(value[a : a + GRID], value[a + GRID : a + 2 * GRID]) for a in range(0, value.shape[0], 2 * GRID)], axis=0
    )


def pair_spread(value, scratch):
    rows, lanes = value.shape
    for j in range(lanes // LANE):
        part = value[:, j * LANE : (j + 1) * LANE]
        scratch[j, pl.ds(0, rows, 2), :] = part
        scratch[j, pl.ds(1, rows, 2), :] = part
    return jnp.concatenate([scratch[j, 0 : 2 * rows, :] for j in range(lanes // LANE)], axis=1)


def norm_kernel(dims, x_ref, g_ref, b_ref, n1_ref, mx_ref, tiles):
    frames, rows = dims
    half = rows // 2
    channels = x_ref.shape[1]
    per = rows * GRID
    g = row_of(g_ref, 0, channels)
    b = row_of(b_ref, 0, channels)
    for t in range(frames):
        x = x_ref[t * per : (t + 1) * per, :].astype(f32)
        unit, _ = layer_unit(x)
        n1_ref[t * per : (t + 1) * per, :] = (unit * g + b).astype(bf)
        tall = join_lines(x, jnp.maximum)
        mx_ref[t * half * HALF : (t + 1) * half * HALF, :] = pair_reduce(tall, tiles, jnp.maximum)


def squeeze_kernel(dims, mem_ref, c_ref, out_ref, tiles, squeezed):
    frames, rows, width, hd = dims
    half = rows // 2
    count = half * frames * VH
    odd = lax.broadcasted_iota(jnp.int32, (GRID, 1), 0) % 2 == 1
    for m in range(2):
        taps = [jnp.where(odd, c_ref[m, i, 1:2, :], c_ref[m, i, 0:1, :]) for i in range(2)]
        for s in range(MEM):
            for t in range(frames):
                parts = [
                    mem_ref[s, m, t, 2 * a].astype(f32) * taps[0] + mem_ref[s, m, t, 2 * a + 1].astype(f32) * taps[1]
                    for a in range(half)
                ]
                for a in range(half):
                    done = pair_reduce(parts[a], tiles.at[(t * half + a) % 4], jnp.add)
                    squeezed[m, s, a * frames * VH + t * VH : a * frames * VH + (t + 1) * VH, :] = done[0:VH]
            squeezed[m, s, count:LANE, :] = jnp.zeros((LANE - count, width), f32)
    for n in range(HEADS):
        cut = slice(n * hd, (n + 1) * hd)
        out_ref[n] = jnp.concatenate(
            [squeezed[0, 0, :, cut], squeezed[1, 0, :, cut], squeezed[0, 1, :, cut], squeezed[1, 1, :, cut]], axis=1
        ).astype(bf)


def flat_row(t, h):
    return GRID + (1 + t) * PLANE + h * GRID


def fill_grid(grid):
    zero = jnp.zeros((GRID, LANE), f32)
    grid[0 : GRID + PLANE, :] = jnp.zeros((GRID + PLANE, LANE), f32)
    grid[flat_row(FR, 0) :, :] = jnp.zeros((FLAT - flat_row(FR, 0), LANE), f32)
    for t in range(FR):
        grid[flat_row(t, VW) : flat_row(t, VW) + GRID, :] = zero


def taps9(w_ref, part):
    return [[[w_ref[(a * 3 + b) * 3 + c : (a * 3 + b) * 3 + c + 1, part * LANE : (part + 1) * LANE] for c in range(3)] for b in range(3)] for a in range(3)]


def four_rows(grid, weights, base, flip, keep=VW):
    acc = [[None] * 3 for _ in range(4)]
    for line in range(-1, 5):
        for a in range(3):
            shift = (1 - a if flip else a - 1) * PLANE + line * GRID
            cells = grid[pl.ds(pl.multiple_of(base + shift, 8), GRID), :]
            for h in range(4):
                b = (h - line + 1) if flip else (line - h + 1)
                if b < 0 or b > 2:
                    continue
                for c in range(3):
                    term = cells * weights[a][b][c]
                    acc[h][c] = term if acc[h][c] is None else acc[h][c] + term
    outs = []
    for h in range(4):
        left, mid, right = (acc[h][2], acc[h][1], acc[h][0]) if flip else (acc[h][0], acc[h][1], acc[h][2])
        outs.append((pltpu.roll(left, 1, 0) + mid + pltpu.roll(right, GRID - 1, 0))[0:keep])
    return jnp.concatenate(outs, axis=0)


def gather_blocks(dims, meta, refs, out, sems):
    frames, rows, n_height = dims
    member = meta[4]
    per = rows * GRID
    x0, x2, x4, x6a, x6b, x1, x3, x5, x7a, x7b = refs
    copies = []
    for d, parts in enumerate([[x0], [x1], [x2], [x3], [x4], [x5], [x6a, x6b], [x7a, x7b]]):
        src = member ^ d
        t = lax.div(src, n_height) * frames
        at = pl.ds(pl.multiple_of(lax.rem(src, n_height) * per, 16), per)
        for ref in parts:
            for i in range(ref.shape[0] // per):
                copies.append(pltpu.make_async_copy(ref.at[i * per : (i + 1) * per, :], out.at[t, at, :], sems.at[len(copies)]))
                t = t + 1
    return copies


def conv_kernel(dims, meta, w_ref, qkv_ref, bias_ref, *refs):
    frames, rows, n_height, hd = dims
    half = rows // 2
    blocks, (k_ref, v_ref, q_ref, gk, gv, gather, tiles, qrow, sems) = refs[:10], refs[10:]
    copies = gather_blocks(dims[:3], meta, blocks, gather, sems)
    for copy in copies:
        copy.start()
    side, member = meta[0], meta[4]
    width = qkv_ref.shape[0] // 3
    channels = qkv_ref.shape[1]
    for grid in (gk, gv):
        fill_grid(grid)
    blank = jnp.zeros((LANE - hd, channels), bf)
    own = [qkv_ref[pl.ds(pl.multiple_of(p * width + member * hd, 32), hd), :] for p in range(3)]
    weight_q = jnp.concatenate([own[0], blank], axis=0)
    weight_kv = jnp.concatenate([own[1], blank, own[2], blank], axis=0)
    index = lax.broadcasted_iota(jnp.int32, (VW * GRID, 1), 0)
    line = (index * 2731) >> 16
    inside = ((line < side) & (index - line * GRID < side)).astype(f32)
    for copy in copies:
        copy.wait()
    piece = half * HALF
    for t in range(FR):
        query = pair_reduce(join_lines(nt(gather[t], weight_q), jnp.add), tiles.at[t % 2], jnp.add) * 0.25 + bias_ref[0:1, 0:LANE]
        for h in range(n_height):
            at = (t // frames * n_height + h) * frames * piece + t % frames * piece
            qrow[at : at + piece, :] = query[h * piece : (h + 1) * piece]
        pair = ((nt(gather[t, 0 : VW * GRID, :], weight_kv) + bias_ref[0:1, LANE:]) * inside).astype(bf).astype(f32)
        gk[flat_row(t, 0) : flat_row(t, VW), :] = pair[:, 0:LANE]
        gv[flat_row(t, 0) : flat_row(t, VW), :] = pair[:, LANE:]
    q_ref[...] = qrow[...].astype(bf)
    local = lax.broadcasted_iota(jnp.int32, (4 * VW, LANE), 0)
    lane = lax.broadcasted_iota(jnp.int32, (4 * VW, LANE), 1)
    line = (local * 3277) >> 16
    column = local - line * VW
    fixed = [(lane + o == 143 - column) | (lane + o == 191 - column) for o in (0, LANE)]
    ones = (lane == hd).astype(f32)

    def step(it, carry):
        t = it // (VW // 4)
        quad = it % (VW // 4)
        base = GRID + (1 + t) * PLANE + quad * 4 * GRID
        out = pl.ds(pl.multiple_of(it * (4 * VW), 16), 4 * VW)
        mixed_k = four_rows(gk, taps9(w_ref, 0), base, False)
        mixed_v = four_rows(gv, taps9(w_ref, 1), base, False)
        h = quad * 4 + line
        bad = (h >= side) | (column >= side)
        for o in range(2):
            at = lane + o * LANE
            hit = fixed[o] | (at == 103 - t) | (at == 151 - t) | (at == 123 - h) | (at == 171 - h) | ((at == 192) & bad)
            marks = hit.astype(f32)
            k_ref[out, o * LANE : (o + 1) * LANE] = ((mixed_k + marks) if o == 0 else marks).astype(bf)
        v_ref[out, :] = (mixed_v + ones).astype(bf)
        return carry

    lax.fori_loop(0, FR * VW // 4, step, 0)


def build_table(tab, t_ref, h_ref, w_ref):
    tab[...] = jnp.zeros(tab.shape, f32)
    for v in range(FR):
        tab[8 * v : 8 * v + FR, :] = t_ref[v : v + FR, :]
    for n, ref in ((0, h_ref), (1, w_ref)):
        for a in range(HALF):
            at = 8 * FR + (n * HALF + a) * GRID
            first = 2 * a + GRID - VW
            tab[at : at + VW, :] = ref[first : first + VW, :]


def attend_kernel(dims, meta, kc_ref, vc_ref, q_ref, y_ref, t_ref, h_ref, w_ref, place_ref, k_ref, kt_ref, v_ref, qt_ref, o_ref, l_ref, j_ref, vt, tab, s_ref):
    frames, rows, n_height, hd = dims
    half = rows // 2
    side, length = meta[0], meta[1]
    queries = q_ref.shape[0]
    scale = hd**-0.5
    k_ref[0:CUR, :] = kc_ref[...]
    v_ref[0:CUR, :] = vc_ref[...]
    count = half * frames * VH
    each = frames * VH
    lane1 = lax.broadcasted_iota(jnp.int32, (1, LANE), 1)
    at = CUR
    for src in range(HEADS):
        packed = y_ref[src].astype(f32)
        first = src % n_height * half
        used = min(max(VH - first, 0), half) * each
        if used > 0:
            halves = []
            for m in range(2):
                halves.append(jnp.concatenate([packed[0:used, m * hd : (m + 1) * hd], packed[0:used, (2 + m) * hd : (3 + m) * hd]], axis=0))
            index = lax.broadcasted_iota(jnp.int32, (2 * used, LANE), 0)
            step = (index >= used).astype(jnp.int32)
            inner = index - step * used
            a = (inner >= each).astype(jnp.int32) + (inner >= 2 * each).astype(jnp.int32)
            inner = inner - a * each
            c = inner - ((inner * 6554) >> 16) * VH
            bad = (step >= length) | (2 * (first + a) >= side) | (2 * c >= side)
            mark = (bad & (lax.broadcasted_iota(jnp.int32, (2 * used, LANE), 1) == 64)).astype(f32)
            k_ref[at : at + 2 * used, 0:LANE] = pad_lanes(halves[0], LANE).astype(bf)
            k_ref[at : at + 2 * used, LANE:] = mark.astype(bf)
            v_ref[at : at + 2 * used, :] = (pad_lanes(halves[1], LANE) + (lane1 == hd).astype(f32)).astype(bf)
            at += 2 * used
    rest = KEYS - at
    k_ref[at:, 0:LANE] = jnp.zeros((rest, LANE), bf)
    k_ref[at:, LANE:] = jnp.broadcast_to((lane1 == 64).astype(f32), (rest, LANE)).astype(bf)
    v_ref[at:, :] = jnp.zeros((rest, LANE), bf)
    for i in range(KEYS // 256):
        cut = slice(i * 256, (i + 1) * 256)
        kt_ref[:, cut] = k_ref[cut, :].T
        vt[:, cut] = v_ref[cut, :].T
    pt = q_ref[...].astype(f32).T[0:hd]
    build_table(tab, t_ref, h_ref, w_ref)
    along = nn(tab[...], pt, precision=HI)
    tq, aq, cq = place_ref[0:1, :], place_ref[1:2, :], place_ref[2:3, :]
    part_t = jnp.zeros((FR, queries), f32)
    for v in range(FR):
        part_t = jnp.where(tq == v, along[8 * v : 8 * v + FR], part_t)
    parts = []
    for n, place in ((0, aq), (1, cq)):
        part = jnp.zeros((GRID, queries), f32)
        for a in range(HALF):
            row = 8 * FR + (n * HALF + a) * GRID
            part = jnp.where(place == a, along[row : row + GRID], part)
        parts.append(part[0:VW])
    bias = jnp.concatenate([part_t] + parts, axis=0) * hd**0.5
    high = bias.astype(bf)
    low = (bias - high.astype(f32)).astype(bf)
    qt_ref[0:hd, :] = pt.astype(bf)
    qt_ref[hd : hd + 48, :] = high
    qt_ref[hd + 48 : hd + 96, :] = low
    tail = lax.broadcasted_iota(jnp.int32, (64, queries), 0)
    qt_ref[192:256, :] = jnp.where(tail == 0, FAR, 0.0).astype(bf)
    factor = scale * LOG2E
    wide = s_ref.shape[1]
    blocks = [(i, min(i + 512, KEYS)) for i in range(0, KEYS, 512)]

    def one(block, carry):
        cols = pl.ds(pl.multiple_of(block * wide, LANE), wide)
        query = qt_ref[:, cols]
        top = jnp.full((8, wide), FAR, f32)
        for lo, hi in blocks:
            scores = nn(k_ref[lo:hi, :], query)
            s_ref[lo:hi, :] = scores
            top = jnp.maximum(top, jnp.max(scores.reshape((hi - lo) // 8, 8, wide), axis=0))
        top = jnp.max(top, axis=0, keepdims=True) * factor
        total = jnp.zeros((LANE, wide), f32)
        for lo, hi in blocks:
            weights = jnp.exp2(s_ref[lo:hi, :] * factor - top).astype(bf)
            total = total + nn(vt[:, lo:hi], weights)
        norm = total[hd : hd + 1]
        o_ref[:, cols] = total[0:hd] / norm
        l_ref[:, cols] = top + jnp.log2(norm)
        return carry

    lax.fori_loop(0, queries // wide, one, 0)
    j_ref[...] = pad_lanes((o_ref[...] + pt).T, LANE).astype(bf)


def mlp_kernel(dims, j_ref, mx_ref, cot_ref, wp_ref, ws_ref, bp_ref, bs_ref, g_ref, b_ref, w1_ref, b1_ref, w2_ref, b2_ref,
               out_ref, keep_ref, act_ref, dj_ref, mg_ref,
               resid, n2, acc, ngrad, joined, gb1):
    width, hd = dims
    i = pl.program_id(0)
    per_q = cot_ref.shape[0]
    block = w1_ref.shape[0]

    @pl.when(i == 0)
    def _():
        joined[...] = jnp.concatenate([j_ref[n][:, 0:hd] for n in range(HEADS)], axis=1)
        shift = row_of(bp_ref, 0, width) + row_of(bs_ref, 0, width)
        value = nt(joined[...], wp_ref[...]) + nt(mx_ref[...].astype(bf), ws_ref[...]) + shift
        resid[...] = value
        unit, _ = layer_unit(value)
        n2[...] = (unit * row_of(g_ref, 0, width) + row_of(b_ref, 0, width)).astype(bf)
        acc[...] = jnp.zeros(acc.shape, f32)
        ngrad[...] = jnp.zeros(ngrad.shape, f32)

    here = pl.ds(pl.multiple_of(i * block, LANE), block)
    hidden = nt(n2[...], w1_ref[...]) + b1_ref[here].reshape(1, block)
    gate = 0.5 * (1.0 + lax.erf(hidden * SQRT_HALF))
    act = (hidden * gate).astype(bf)
    act_ref[0, 0:per_q, :] = act
    acc[...] += nt(act, w2_ref[...])
    grad = nn(cot_ref[...], w2_ref[...])
    hgrad = (grad * (gate + hidden * jnp.exp(-0.5 * hidden * hidden) / ROOT_TWO_PI)).astype(bf)
    act_ref[0, per_q:, :] = hgrad
    gb1[:, here] = jnp.sum(hgrad.astype(f32), axis=0, keepdims=True)
    ngrad[...] += nn(hgrad, w1_ref[...])

    @pl.when(i == pl.num_programs(0) - 1)
    def _():
        value = resid[...]
        out_ref[...] = (value + acc[...] + row_of(b2_ref, 0, width)).astype(bf)
        unit, inverse = layer_unit(value)
        cot = cot_ref[...].astype(f32)
        grad = ngrad[...]
        scaled = grad * row_of(g_ref, 0, width)
        back = inverse * (
            scaled - jnp.mean(scaled, axis=-1, keepdims=True) - unit * jnp.mean(scaled * unit, axis=-1, keepdims=True)
        )
        low = (cot + back).astype(bf)
        channels = mx_ref.shape[1]
        keep_ref[:, 0:width] = n2[...]
        keep_ref[:, width : 2 * width] = low
        keep_ref[:, 2 * width : 2 * width + channels] = mx_ref[...].astype(bf)
        joined_grad = nn(low, wp_ref[...])
        for n in range(HEADS):
            dj_ref[n] = pad_lanes(joined_grad[:, n * hd : (n + 1) * hd], LANE).astype(bf)
        mg_ref[...] = nn(low, ws_ref[...])
        sums = [jnp.sum(v, axis=0, keepdims=True) for v in (low.astype(f32), grad * unit, grad, cot)] + [gb1[...]]
        lines = [v[:, k : k + LANE] for v in sums for k in range(0, v.shape[1], LANE)]
        exact = jnp.concatenate(lines, axis=0)
        high = exact.astype(bf).astype(f32)
        lines = jnp.concatenate([high, exact - high, jnp.zeros((per_q - 2 * exact.shape[0], LANE), f32)], axis=0)
        keep_ref[:, 2 * width + channels :] = lines.astype(bf)


def attend_back_kernel(dims, k_ref, kt_ref, v_ref, qt_ref, q_ref, o_ref, l_ref, dj_ref, t_ref, h_ref, w_ref, place_ref,
                       dk_ref, dv_ref, mem_ref, pq_ref,
                       dot_ref, dq, tab, dtab, dks, dvs, delta, tables):
    frames, rows, n_height, hd = dims
    half = rows // 2
    queries = q_ref.shape[0]
    scale = hd**-0.5
    factor = scale * LOG2E
    turned = dj_ref[...].astype(f32).T
    dot_ref[...] = turned.astype(bf)
    delta[...] = jnp.sum(turned[0:hd] * o_ref[...], axis=0, keepdims=True)
    dq[...] = jnp.zeros(dq.shape, f32)
    wide = 384

    def chunk(i, carry):
        cut = pl.ds(pl.multiple_of(i * 256, 256), 256)
        dk = jnp.zeros((256, LANE), f32)
        dv = jnp.zeros((256, LANE), f32)
        for lo in range(0, queries, wide):
            cols = slice(lo, lo + wide)
            shares = jnp.exp2(nn(k_ref[cut, :], qt_ref[:, cols]) * factor - l_ref[:, cols])
            slope = nn(v_ref[cut, :], dot_ref[:, cols])
            score = (shares * (slope - delta[:, cols])).astype(bf)
            dv = dv + nn(shares.astype(bf), dj_ref[cols, :])
            dk = dk + nn(score, q_ref[cols, :])
            dq[:, cols] += nn(kt_ref[0 : dq.shape[0], cut], score)
        dks[cut, :] = dk * scale
        dvs[cut, :] = dv
        return carry

    lax.fori_loop(0, KEYS // 256, chunk, 0)
    dk_ref[...] = dks[0:CUR, :]
    dv_ref[...] = dvs[0:CUR, :]
    each = frames * VH
    at = CUR
    for dst in range(HEADS):
        first = dst % n_height * half
        used = min(max(VH - first, 0), half) * each
        if used > 0:
            parts = [ref[at + s * used : at + (s + 1) * used, 0:hd] for s in range(MEM) for ref in (dks, dvs)]
            packed = jnp.concatenate(parts, axis=1)
            at += 2 * used
        if used < LANE:
            zero = jnp.zeros((LANE - used, 4 * hd), f32)
            packed = jnp.concatenate([packed, zero], axis=0) if used > 0 else zero
        mem_ref[dst, 0:LANE, :] = packed.astype(bf)
    build_table(tab, t_ref, h_ref, w_ref)
    tq, aq, cq = place_ref[0:1, :], place_ref[1:2, :], place_ref[2:3, :]
    grad_t = dq[hd : hd + FR, :]
    for v in range(FR):
        dtab[8 * v : 8 * v + FR, :] = jnp.where(tq == v, grad_t, 0.0)
    for n, place in ((0, aq), (1, cq)):
        part = jnp.concatenate(
            [dq[hd + FR + n * VW : hd + FR + (n + 1) * VW, :], jnp.zeros((GRID - VW, queries), f32)], axis=0
        )
        for a in range(HALF):
            row = 8 * FR + (n * HALF + a) * GRID
            dtab[row : row + GRID, :] = jnp.where(place == a, part, 0.0)
    pooled_grad = dq[0:hd, :] * scale + tn(tab[...], dtab[...], precision=HI) + dot_ref[0:hd, :].astype(f32)
    pq_ref[...] = pad_lanes(pooled_grad.T * 0.25, LANE)
    grads = nn(dtab[...], q_ref[...].astype(f32), precision=HI)
    tables[...] = jnp.zeros(tables.shape, f32)
    for v in range(FR):
        tables[v : v + FR, :] += grads[8 * v : 8 * v + FR]
    for n in range(2):
        for a in range(HALF):
            row = 8 * FR + (n * HALF + a) * GRID
            first = 2 * FR + n * 2 * GRID + 2 * a + GRID - VW
            tables[first : first + VW, :] += grads[row : row + VW]
    share = TABLE_ROWS // HEADS
    for dst in range(HEADS):
        part = jnp.concatenate([tables[dst * share : (dst + 1) * share, :], jnp.zeros((16 - share, LANE), f32)], axis=0)
        high = part.astype(bf).astype(f32)
        mem_ref[dst, LANE:, :] = jnp.concatenate([high, part - high, jnp.zeros((16, LANE), f32)], axis=1).astype(bf)


def conv_back_kernel(dims, meta, mk, mv, dk_ref, dv_ref, pq_ref, w_ref, g_ref, b_ref, qkv_ref, *refs):
    frames, rows, n_height, hd = dims
    half = rows // 2
    blocks, (out_ref, gw_ref, stat_ref, pg, gk, gv, acc, wide, gather, tall, sems) = refs[:10], refs[10:]
    copies = gather_blocks(dims[:3], meta, blocks, gather, sems)
    for copy in copies:
        copy.start()
    side, member = meta[0], meta[4]
    width = qkv_ref.shape[0] // 3
    channels = qkv_ref.shape[1]
    for grid in (gk, gv):
        fill_grid(grid)
    for ref, grid in ((dk_ref, gk), (dv_ref, gv)):
        for t in range(FR):
            for h in range(VW):
                at = (t * VW + h) * VW
                grid[flat_row(t, h) : flat_row(t, h) + GRID, :] = jnp.concatenate(
                    [ref[at : at + VW, :], jnp.zeros((GRID - VW, LANE), f32)], axis=0
                )
    acc[...] = jnp.zeros(acc.shape, f32)
    local = lax.broadcasted_iota(jnp.int32, (4 * GRID, 1), 0)
    line = (local * 2731) >> 16
    column = local - line * GRID
    empty = jnp.zeros(((GRID - VW) * GRID, 2 * LANE), bf)
    for t in range(FR):
        pg[t * GRID * GRID + VW * GRID : (t + 1) * GRID * GRID, LANE:] = empty

    def step(it, carry):
        t = it // (VW // 4)
        quad = it % (VW // 4)
        base = GRID + (1 + t) * PLANE + quad * 4 * GRID
        out = pl.ds(pl.multiple_of((t * GRID + quad * 4) * GRID, 32), 4 * GRID)
        inside = ((quad * 4 + line < side) & (column < side)).astype(f32)
        for m, grid in ((0, gk), (1, gv)):
            back = four_rows(grid, taps9(w_ref, m), base, True, GRID)
            pg[out, (1 + m) * LANE : (2 + m) * LANE] = (back * inside).astype(bf)
        for m, grid, masked in ((0, gk, mk), (1, gv, mv)):
            for h in range(4):
                here = grid[pl.ds(pl.multiple_of(base + h * GRID, 8), GRID), :]
                turned = [pltpu.roll(here, GRID - 1, 0), here, pltpu.roll(here, 1, 0)]
                for a in range(3):
                    for b in range(3):
                        cells = masked[pl.ds(pl.multiple_of(base + (a - 1) * PLANE + (h + b - 1) * GRID, 8), GRID), :]
                        for c in range(3):
                            prod = cells * turned[c]
                            tap = m * 27 + (a * 3 + b) * 3 + c
                            acc[tap] += prod[0:8] + prod[8:16] + prod[16:24]
        return carry

    lax.fori_loop(0, FR * VW // 4, step, 0)
    for tap in range(54):
        gw_ref[tap : tap + 1, :] = jnp.sum(acc[tap], axis=0, keepdims=True)
    gw_ref[54:, :] = jnp.zeros((gw_ref.shape[0] - 54, LANE), f32)
    queries = pq_ref.shape[0]
    wide[pl.ds(0, queries, 2), :] = pq_ref[...]
    wide[pl.ds(1, queries, 2), :] = pq_ref[...]
    per_q = queries // HEADS
    for src in range(HEADS):
        for t in range(frames):
            for a in range(half):
                at = ((src * frames + t) * half + a) * GRID
                lines = wide[at : at + GRID, :]
                row = ((src // n_height * frames + t) * GRID + src % n_height * rows + 2 * a) * GRID
                pg[row : row + 2 * GRID, 0:LANE] = jnp.concatenate([lines, lines], axis=0).astype(bf)
    span = rows * VW
    cells = span * (frames // 2)
    third = per_q // 3
    for dst in range(HEADS):
        first = dst % n_height * rows
        lines = []
        for t2 in range(frames // 2):
            parts = []
            for g in range(2):
                t = dst // n_height * frames + g * (frames // 2) + t2
                at = (t * GRID + first) * GRID
                block = pg[at : at + rows * GRID, LANE:].astype(f32)
                block = jnp.concatenate([block[h * GRID : h * GRID + VW] for h in range(rows)], axis=0)
                parts += [block[:, 0:hd], block[:, LANE : LANE + hd]]
            lines.append(jnp.concatenate(parts, axis=1))
        out_ref[dst, 0:cells, :] = jnp.concatenate(lines, axis=0).astype(bf)
        out_ref[dst, cells : cells + third, :] = jnp.concatenate(
            [pq_ref[dst * per_q + i * third : dst * per_q + (i + 1) * third, :] for i in range(3)], axis=1
        ).astype(bf)
    for copy in copies:
        copy.wait()
    total = jnp.zeros((3 * LANE, channels), f32)
    sums = jnp.zeros((1, 3 * LANE), f32)
    for t in range(FR):
        part = pg[t * GRID * GRID : (t + 1) * GRID * GRID, :]
        total = total + tn(part, gather[t])
        sums = sums + jnp.sum(part.astype(f32), axis=0, keepdims=True)
    total = jnp.concatenate([total[p * LANE : p * LANE + hd] for p in range(3)], axis=0)
    sums = jnp.concatenate([sums[:, p * LANE : p * LANE + hd] for p in range(3)], axis=1)
    cols = channels // HEADS
    packed = 3 * hd // HEADS
    rest = out_ref.shape[1] - cells - third
    for n in range(HEADS):
        value = pack_rows(total[:, n * cols : (n + 1) * cols], tall.at[n % 2], HEADS)
        out_ref[n, cells + third :, :] = jnp.concatenate([value, jnp.zeros((rest - packed, channels), f32)], axis=0).astype(bf)
    weight = jnp.concatenate(
        [qkv_ref[pl.ds(pl.multiple_of(p * width + member * hd, 32), hd), :].astype(f32) for p in range(3)], axis=0
    )
    shift = nn(jnp.broadcast_to(sums, (8, 3 * hd)), weight, precision=HI)[0:1]
    gain = jnp.sum(total * weight, axis=0, keepdims=True)
    gain = (gain - shift * row_of(b_ref, 0, channels)) / row_of(g_ref, 0, channels)
    stat_ref[0:1, :] = pad_lanes(sums, channels)
    stat_ref[1:2, :] = gain
    stat_ref[2:3, :] = shift
    stat_ref[3:8, :] = jnp.zeros((5, channels), f32)


def weight_grad_kernel(dims, meta, keep_ref, ah_ref, j_ref, cot_ref, dmem_ref, fc2_ref, fc1_ref, proj_ref, short_ref, small_ref,
                       act, hgrad, tall, parts):
    width, hd, channels, per_q = dims
    member = meta[4]
    for src in range(HEADS):
        cut = slice(src * per_q, (src + 1) * per_q)
        act[cut, :] = ah_ref[src, 0:per_q, :]
        hgrad[cut, :] = ah_ref[src, per_q:, :]
    normed = keep_ref[:, 0:width]
    resid = keep_ref[:, width : 2 * width]
    fc1 = tn(hgrad[...], normed)
    for n in range(HEADS):
        fc1_ref[n, 0 : dmem_ref.shape[1], :] = dmem_ref[n]
        fc1_ref[n, dmem_ref.shape[1] :, :] = pack_rows(fc1[:, n * hd : (n + 1) * hd], parts.at[n % 2], channels // hd).astype(bf)
    cols = channels // HEADS
    lane = lax.broadcasted_iota(jnp.int32, (channels, LANE), 1)
    pick = (lax.broadcasted_iota(jnp.int32, (channels, LANE), 0) == lane + member * cols) & (lane < cols)
    maxima = nn(keep_ref[:, 2 * width : 2 * width + channels], pick.astype(f32).astype(bf)).astype(bf)
    both = tn(resid, jnp.concatenate([j_ref[...], maxima], axis=1))
    proj_ref[...] = pack_rows(both[:, 0:hd], tall.at[0], channels // hd).astype(bf)
    short_ref[...] = pack_rows(both[:, LANE : LANE + cols], tall.at[1], channels // cols).astype(bf)
    sums = jnp.zeros((per_q, LANE), f32)
    for src in range(HEADS):
        sums = sums + keep_ref[src * per_q : (src + 1) * per_q, 2 * width + channels :].astype(f32)
    lines = HEADS * width // LANE
    sums = sums[0:lines] + sums[lines : 2 * lines]
    each = lines // HEADS
    own = jnp.zeros((each, LANE), f32)
    for n in range(HEADS):
        own = jnp.where(member == n, sums[n * each : (n + 1) * each], own)
    small_ref[...] = jnp.concatenate([own, jnp.zeros((8 - each, LANE), f32)], axis=0)
    fc2_ref[...] = tn(cot_ref[...], act[...]).astype(bf)


def last_kernel(dims, x_ref, g_ref, w_ref, pg_ref, mx_ref, mg_ref, out_ref, full, tiles):
    frames, rows, width, hd = dims
    half = rows // 2
    cells = rows * VW * (frames // 2)
    third = frames * half * HALF // 3
    channels = x_ref.shape[1]
    tops = jnp.zeros((cells, channels), f32)
    lows = jnp.zeros((cells, channels), f32)
    queries = []
    for n in range(HEADS):
        weight = jnp.concatenate(
            [w_ref[width + n * hd : width + (n + 1) * hd, :], w_ref[2 * width + n * hd : 2 * width + (n + 1) * hd, :]], axis=0
        )
        packed = pg_ref[n]
        tops = tops + nn(packed[0:cells, 0 : 2 * hd], weight)
        lows = lows + nn(packed[0:cells, 2 * hd :], weight)
        queries.append(
            jnp.concatenate([packed[cells : cells + third, i * LANE : i * LANE + hd] for i in range(3)], axis=0)
        )
    for part, value in ((0, tops), (1, lows)):
        for line in range(frames // 2 * rows):
            at = (part * (frames // 2) * rows + line) * GRID
            full[at : at + GRID, :] = jnp.concatenate(
                [value[line * VW : (line + 1) * VW], jnp.zeros((GRID - VW, channels), f32)], axis=0
            )
    query = nn(jnp.concatenate(queries, axis=1), w_ref[0:width, :])
    per = rows * GRID
    per_q = half * HALF
    g = row_of(g_ref, 0, channels)
    for t in range(frames):
        cut = slice(t * per_q, (t + 1) * per_q)
        x = x_ref[t * per : (t + 1) * per, :].astype(f32)

        def spread(value):
            wide = pair_spread(value, tiles)
            lines = []
            for a in range(half):
                lines += [wide[a * GRID : (a + 1) * GRID]] * 2
            return jnp.concatenate(lines, axis=0)

        grad = full[t * per : (t + 1) * per, :] + spread(query[cut])
        hits = (x == spread(mx_ref[cut, :])).astype(f32)
        sums = jnp.concatenate(
            [hits[2 * a * GRID : (2 * a + 1) * GRID] + hits[(2 * a + 1) * GRID : (2 * a + 2) * GRID] for a in range(half)], axis=0
        )
        number = pair_reduce(sums, tiles, jnp.add)
        pool = hits * spread(mg_ref[cut, :] / number)
        unit, inverse = layer_unit(x)
        scaled = grad * g
        back = inverse * (
            scaled - jnp.mean(scaled, axis=-1, keepdims=True) - unit * jnp.mean(scaled * unit, axis=-1, keepdims=True)
        )
        out_ref[t * per : (t + 1) * per, :] = (back + pool).astype(bf)


def compress_kernel(dims, mem_ref, p_ref, conv_ref, stat_ref, small_ref, late_ref, tiles, lines):
    frames, rows, width, hd = dims
    half = rows // 2
    channels = late_ref.shape[1]
    for m in range(2):
        sums = [jnp.zeros((GRID, width), f32) for _ in range(2)]
        for s in range(MEM):
            grads = jnp.concatenate(
                [p_ref[n][0:LANE, (2 * s + m) * hd : (2 * s + m + 1) * hd] for n in range(HEADS)], axis=1
            ).astype(f32)
            for t in range(frames):
                for a in range(half):
                    at = (a * frames + t) * VH
                    some = jnp.concatenate([grads[at : at + VH], jnp.zeros((HALF - VH, width), f32)], axis=0)
                    wide = pair_spread(some, tiles.at[(t * half + a) % 4])
                    for i in range(2):
                        sums[i] = sums[i] + mem_ref[s, m, t, 2 * a + i].astype(f32) * wide
        odd = (lax.broadcasted_iota(jnp.int32, (GRID, 1), 0) % 2 == 1).astype(f32)
        for i in range(2):
            for j, keep in ((0, 1.0 - odd), (1, odd)):
                done = jnp.sum(sums[i] * keep, axis=0, keepdims=True)
                for k in range(width // channels):
                    at = LATE_COMP + 8 * k + 4 * m + 2 * i + j
                    lines[at : at + 1, :] = done[:, k * channels : (k + 1) * channels]
    conv = jnp.concatenate([conv_ref[14 * g : 14 * (g + 1), 0:hd] for g in range(4)], axis=1)
    lines[0:14, :] = conv
    lines[14:17, :] = stat_ref[0:3, :]
    for k in range(2):
        lines[LATE_SMALL + k : LATE_SMALL + k + 1, :] = jnp.concatenate([small_ref[3 * k + i : 3 * k + i + 1, :] for i in range(3)], axis=1)
    tables = jnp.zeros((16, LANE), f32)
    for n in range(HEADS):
        part = p_ref[n][LANE:, :].astype(f32)
        tables = tables + part[:, 0:LANE] + part[:, LANE : 2 * LANE]
    lines[LATE_TABLE : LATE_TABLE + 5, :] = jnp.concatenate([tables[5 * g : 5 * (g + 1), :] for g in range(3)], axis=1)
    late_ref[...] = lines[...].astype(bf)


def sums_kernel(dims, late_ref, g1_ref, b1_ref, bqkv_ref, conv_ref, comp_ref, t_ref, h_ref, w_ref, bp_ref, bs_ref, g2_ref, b2_ref, bf1_ref, bf2_ref, lines):
    width, hd, channels = dims
    parts = []
    for n in range(HEADS):
        parts.append(late_ref[n])
    total = parts[0]
    for n in range(1, HEADS):
        total = total + parts[n]
    for g in range(4):
        conv = jnp.concatenate([parts[n][0:14, g * hd : (g + 1) * hd] for n in range(HEADS)], axis=1)
        for r in range(14):
            i = 14 * g + r
            if i < 54:
                conv_ref[i // 27, i % 27 // 9, i % 9 // 3, i % 3 : i % 3 + 1, :] = conv[r : r + 1]
    for p in range(3):
        value = jnp.concatenate([parts[n][14:15, p * hd : (p + 1) * hd] for n in range(HEADS)], axis=1)
        bqkv_ref[p * width : (p + 1) * width] = value.reshape(width)
    g1_ref[...] = total[15:16].reshape(channels)
    b1_ref[...] = total[16:17].reshape(channels)
    for i in range(8):
        value = jnp.concatenate([total[LATE_COMP + 8 * k + i : LATE_COMP + 8 * k + i + 1] for k in range(2)], axis=1)
        comp_ref[i // 4, i % 4 // 2, i % 2 : i % 2 + 1, :] = value
    for n in range(HEADS):
        value = jnp.concatenate([parts[n][LATE_SMALL + k : LATE_SMALL + k + 1] for k in range(2)], axis=1).reshape(width)
        if n == 0:
            bp_ref[...] = value
            bs_ref[...] = value
        elif n < 4:
            (g2_ref, b2_ref, bf2_ref)[n - 1][...] = value
        else:
            bf1_ref[(n - 4) * width : (n - 3) * width] = value
    share = TABLE_ROWS // HEADS
    for n in range(HEADS):
        part = parts[n][LATE_TABLE : LATE_TABLE + 5]
        value = jnp.concatenate([part[:, g * LANE : (g + 1) * LANE] for g in range(3)], axis=0)
        lines[n * share : (n + 1) * share, :] = value[0:share]
    at = 0
    for ref, step in ((t_ref, 2 * FR), (h_ref, 2 * GRID), (w_ref, 2 * GRID)):
        ref[...] = lines[at : at + ref.shape[0], 0:hd]
        at += step


def body(clip_input, memory, mem_len, res_id, norm1_gain, norm1_bias, w_qkv, b_qkv, conv_kv, compress, rel_t, rel_h, rel_w,
         w_proj, b_proj, w_short, b_short, norm2_gain, norm2_bias, w_fc1, b_fc1, w_fc2, b_fc2, cotangent):
    _, frames, rows, grid, channels = clip_input.shape
    width = w_proj.shape[0]
    mlp = w_fc1.shape[0]
    hd = width // HEADS
    half = rows // 2
    n_clip = lax.axis_size("clip")
    n_height = lax.axis_size("height")
    tm, height = lax.axis_index("tm"), lax.axis_index("height")
    member = tm * n_height + height
    side = SIDE_SMALL + (SIDE_BIG - SIDE_SMALL) * res_id[0]
    meta = jnp.stack([side, mem_len[0], tm, height, member]).astype(jnp.int32)
    cells_all = frames * rows * GRID
    valid = frames * rows * VW
    per_q = frames * half * HALF
    third = per_q // 3
    queries = HEADS * per_q
    x = clip_input.reshape(cells_all, channels)
    mem = memory[0]
    cot = cotangent.reshape(per_q, width)

    dims = (frames, rows, width, hd)
    n1, mx = call(
        functools.partial(norm_kernel, (frames, rows)),
        (shape((cells_all, channels), bf), shape((per_q, channels), f32)),
        (x, norm1_gain, norm1_bias),
        scratch=[pltpu.VMEM((channels // LANE, rows * GRID, LANE), f32)],
        smem=0,
        us=3,
    )

    def swap(value, bit):
        if bit == 4:
            return lax.ppermute(value, "tm", [(i, i ^ 1) for i in range(lax.axis_size("tm"))])
        return lax.ppermute(value, "height", [(i, i ^ bit) for i in range(n_height)])

    x2, x4, x1 = swap(n1, 2), swap(n1, 4), swap(n1, 1)
    pay2 = call(
        functools.partial(squeeze_kernel, dims),
        shape((HEADS, LANE, 4 * hd), bf),
        (mem, compress),
        scratch=[pltpu.VMEM((4, width // LANE, GRID, LANE), f32), pltpu.VMEM((2, MEM, LANE, width), f32)],
        smem=0,
        us=5,
    )
    x2, x4, pay2 = lax.optimization_barrier((x2, x4, pay2))
    cut = cells_all // 2
    x6a, x6b = swap(x2[:cut], 4), swap(x4[cut:], 2)
    x3, x5 = swap(x2, 1), swap(x4, 1)
    x7a, x7b = swap(x6a, 1), swap(x6b, 1)
    y2 = lax.all_to_all(pay2, G, 0, 0, tiled=True)
    cot_late, x7a = lax.optimization_barrier((cot, x7a))
    cot_full = lax.all_gather(cot_late, G, axis=0, tiled=True)
    taps = lax.dynamic_slice_in_dim(conv_kv.reshape(2, 27, width), member * hd, hd, 2)
    taps = jnp.pad(taps, ((0, 0), (0, 5), (0, LANE - hd)))
    taps = jnp.concatenate([taps[0], taps[1]], axis=1)
    hdims = (frames, rows, n_height, hd)
    bias = lax.dynamic_slice_in_dim(b_qkv.reshape(3, width), member * hd, hd, 1)
    bias = jnp.pad(bias, ((0, 0), (0, LANE - hd))).reshape(1, 3 * LANE)
    vmem = pl.BlockSpec(memory_space=pltpu.VMEM)
    blocks = (n1, x2, x4, x6a, x6b, x1, x3, x5, x7a, x7b)
    kc, vc, q_all, mk, mv = pl.pallas_call(
        functools.partial(conv_kernel, hdims),
        out_shape=(
            shape((CUR, 2 * LANE), bf),
            shape((CUR, LANE), bf),
            shape((queries, LANE), bf),
            shape((FLAT, LANE), f32),
            shape((FLAT, LANE), f32),
        ),
        in_specs=[pl.BlockSpec(memory_space=pltpu.SMEM)] + [vmem] * 3 + [pl.BlockSpec(memory_space=pl.ANY)] * 10,
        out_specs=(vmem,) * 5,
        scratch_shapes=[
            pltpu.VMEM((FR, GRID * GRID, channels), bf),
            pltpu.VMEM((2, 1, GRID * HALF, LANE), f32),
            pltpu.VMEM((queries, LANE), f32),
            pltpu.SemaphoreType.DMA((HEADS * frames,)),
        ],
        compiler_params=pltpu.CompilerParams(vmem_limit_bytes=56 << 20),
        cost_estimate=cost(18),
    )(meta, taps, w_qkv, bias, *blocks)
    index = np.arange(queries)
    src, local = index // per_q, index % per_q
    place = np.zeros((8, queries), np.int32)
    place[0] = src // n_height * frames + local // (half * HALF)
    place[1] = src % n_height * half + local // HALF % half
    place[2] = local % HALF
    place = jnp.asarray(place)
    wide = 384
    k_all, kt_all, v_all, qt_all, o_all, l_all, joined = call(
        functools.partial(attend_kernel, hdims),
        (
            shape((KEYS, 2 * LANE), bf),
            shape((2 * LANE, KEYS), bf),
            shape((KEYS, LANE), bf),
            shape((2 * LANE, queries), bf),
            shape((hd, queries), f32),
            shape((1, queries), f32),
            shape((queries, LANE), bf),
        ),
        (meta, kc, vc, q_all, y2, rel_t, rel_h, rel_w, place),
        scratch=[
            pltpu.VMEM((LANE, KEYS), bf),
            pltpu.VMEM((TAB, hd), f32),
            pltpu.VMEM((KEYS, wide), f32),
        ],
        us=16,
    )
    joined_rows = lax.all_to_all(joined.reshape(HEADS, per_q, LANE), G, 0, 0, tiled=True)
    block = mlp // HEADS
    whole = lambda *dims: pl.BlockSpec(dims, lambda i: (0,) * len(dims))
    keep_width = 2 * width + channels
    keep_width = keep_width + LANE
    output, keep, acthg, dj, max_grad = pl.pallas_call(
        functools.partial(mlp_kernel, (width, hd)),
        grid=(HEADS,),
        out_shape=(
            shape((per_q, width), bf),
            shape((per_q, keep_width), bf),
            shape((HEADS, 2 * per_q, block), bf),
            shape((HEADS, per_q, LANE), bf),
            shape((per_q, channels), f32),
        ),
        in_specs=[
            whole(HEADS, per_q, LANE),
            whole(per_q, channels),
            whole(per_q, width),
            whole(width, width),
            whole(width, channels),
            whole(width),
            whole(width),
            whole(width),
            whole(width),
            pl.BlockSpec((block, width), lambda i: (i, 0)),
            whole(mlp),
            pl.BlockSpec((width, block), lambda i: (0, i)),
            whole(width),
        ],
        out_specs=(
            whole(per_q, width),
            whole(per_q, keep_width),
            pl.BlockSpec((1, 2 * per_q, block), lambda i: (i, 0, 0)),
            whole(HEADS, per_q, LANE),
            whole(per_q, channels),
        ),
        scratch_shapes=[
            pltpu.VMEM((per_q, width), f32),
            pltpu.VMEM((per_q, width), bf),
            pltpu.VMEM((per_q, width), f32),
            pltpu.VMEM((per_q, width), f32),
            pltpu.VMEM((per_q, width), bf),
            pltpu.VMEM((1, mlp), f32),
        ],
        compiler_params=pltpu.CompilerParams(vmem_limit_bytes=56 << 20),
        cost_estimate=cost(14),
    )(joined_rows, mx, cot, w_proj, w_short, b_proj, b_short, norm2_gain, norm2_bias, w_fc1, b_fc1, w_fc2, b_fc2)
    dj_head = lax.all_to_all(dj, G, 0, 0, tiled=True).reshape(queries, LANE)
    keep_full = lax.all_gather(keep, G, axis=0, tiled=True)
    acthg, dj_head = lax.optimization_barrier((acthg, dj_head))
    ah_head = lax.all_to_all(acthg, G, 0, 0, tiled=True)

    dk, dv, dmem, pq = call(
        functools.partial(attend_back_kernel, hdims),
        (
            shape((CUR, LANE), f32),
            shape((CUR, LANE), f32),
            shape((HEADS, LANE + 16, 4 * hd), bf),
            shape((queries, LANE), f32),
        ),
        (k_all, kt_all, v_all, qt_all, q_all, o_all, l_all, dj_head, rel_t, rel_h, rel_w, place),
        scratch=[
            pltpu.VMEM((LANE, queries), bf),
            pltpu.VMEM((hd + 48, queries), f32),
            pltpu.VMEM((TAB, hd), f32),
            pltpu.VMEM((TAB, queries), f32),
            pltpu.VMEM((KEYS, LANE), f32),
            pltpu.VMEM((KEYS, LANE), f32),
            pltpu.VMEM((1, queries), f32),
            pltpu.VMEM((TABLE_ROWS, LANE), f32),
        ],
        smem=0,
        us=32,
    )
    cols = channels // HEADS
    taken = dmem.shape[1]
    fc2p, fc1p, projp, shortp, small2 = call(
        functools.partial(weight_grad_kernel, (width, hd, channels, per_q)),
        (
            shape((width, block), bf),
            shape((HEADS, taken + block * hd // channels, channels), bf),
            shape((width * hd // channels, channels), bf),
            shape((width // HEADS, channels), bf),
            shape((8, LANE), f32),
        ),
        (meta, keep_full, ah_head, joined, cot_full, dmem),
        scratch=[
            pltpu.VMEM((queries, block), bf),
            pltpu.VMEM((queries, block), bf),
            pltpu.VMEM((2, width, LANE), f32),
            pltpu.VMEM((2, block, LANE), f32),
        ],
        us=9,
    )

    def over_clips(parts, permute):
        parts = [v.reshape(n_clip, v.shape[0] // n_clip, v.shape[1]) for v in parts]
        ends = np.cumsum([0] + [v.shape[1] for v in parts])
        value = jnp.concatenate(parts, axis=1) if len(parts) > 1 else parts[0]
        if permute and n_clip <= 4:
            clip = lax.axis_index("clip")
            total = lax.dynamic_index_in_dim(value, clip, 0, keepdims=False).astype(f32)
            for k in range(1, n_clip):
                sent = lax.dynamic_index_in_dim(value, lax.rem(clip + k, n_clip), 0, keepdims=False)
                total = total + lax.ppermute(sent, "clip", [(i, (i + k) % n_clip) for i in range(n_clip)]).astype(f32)
        else:
            total = jnp.sum(lax.all_to_all(value, "clip", 0, 0, tiled=True).astype(f32), axis=0)
        return [total[lo:hi] for lo, hi in zip(ends, ends[1:])]

    dk, fc1p = lax.optimization_barrier((dk, fc1p))
    first_back = lax.all_to_all(fc1p, G, 0, 0, tiled=True)
    part_fc2, part_proj, part_short = over_clips([fc2p, projp, shortp], True)
    sent = valid // 2 + third
    pgp, gconv, stats = pl.pallas_call(
        functools.partial(conv_back_kernel, hdims),
        out_shape=(shape((HEADS, sent + 48, 4 * hd), bf), shape((64, LANE), f32), shape((8, channels), f32)),
        in_specs=[pl.BlockSpec(memory_space=pltpu.SMEM)] + [vmem] * 9 + [pl.BlockSpec(memory_space=pl.ANY)] * 10,
        out_specs=(vmem,) * 3,
        scratch_shapes=[
            pltpu.VMEM((FR * GRID * GRID, 3 * LANE), bf),
            pltpu.VMEM((FLAT, LANE), f32),
            pltpu.VMEM((FLAT, LANE), f32),
            pltpu.VMEM((54, 8, LANE), f32),
            pltpu.VMEM((2 * queries, LANE), f32),
            pltpu.VMEM((FR, GRID * GRID, channels), bf),
            pltpu.VMEM((2, 3 * hd, LANE), f32),
            pltpu.SemaphoreType.DMA((HEADS * frames,)),
        ],
        compiler_params=pltpu.CompilerParams(vmem_limit_bytes=56 << 20),
        cost_estimate=cost(28),
    )(meta, mk, mv, dk, dv, pq, taps, norm1_gain, norm1_bias, w_qkv, *blocks)
    pgp, first_back = lax.optimization_barrier((pgp, first_back))
    pg_rows = lax.all_to_all(pgp, G, 0, 0, tiled=True)
    mem_back = first_back[:, :taken]
    [part_fc1] = over_clips([first_back[:, taken:].reshape(-1, channels)], True)
    late = call(
        functools.partial(compress_kernel, dims),
        shape((LATE, channels), bf),
        (mem, mem_back, gconv, stats, small2),
        scratch=[pltpu.VMEM((4, width // LANE, GRID, LANE), f32), pltpu.VMEM((LATE, channels), f32)],
        smem=0,
        us=6,
    )
    late = jnp.sum(lax.all_gather(late, "clip", axis=0).astype(f32), axis=0)
    late_full = lax.all_gather(late, G, axis=0)
    vector = lambda n: shape((n,), f32)
    g1, b1, gbq, gconv, gcomp, gt, gh, gw, gbp, gbs, g2, b2, gb1, gb2 = call(
        functools.partial(sums_kernel, (width, hd, channels)),
        (
            vector(channels), vector(channels), vector(3 * width), shape(conv_kv.shape, f32), shape(compress.shape, f32),
            shape(rel_t.shape, f32), shape(rel_h.shape, f32), shape(rel_w.shape, f32),
            vector(width), vector(width), vector(width), vector(width), vector(mlp), vector(width),
        ),
        (late_full,),
        scratch=[pltpu.VMEM((TABLE_ROWS, LANE), f32)],
        smem=0,
        us=3,
    )
    pg_rows, gb1 = lax.optimization_barrier((pg_rows, gb1))
    qkv_rows = pg_rows[:, sent : sent + 3 * hd // HEADS]
    qkv_rows = qkv_rows.reshape(HEADS, 3, hd // HEADS, channels).transpose(1, 0, 2, 3).reshape(-1, channels)
    [part_qkv] = over_clips([qkv_rows], False)
    input_grad = call(
        functools.partial(last_kernel, dims),
        shape((cells_all, channels), bf),
        (x, norm1_gain, w_qkv, pg_rows, mx, max_grad),
        scratch=[pltpu.VMEM((cells_all, channels), f32), pltpu.VMEM((width // LANE, rows * GRID, LANE), f32)],
        smem=0,
        us=8,
    )
    return (
        output.reshape(1, frames, half, HALF, width),
        input_grad.reshape(clip_input.shape),
        g1,
        b1,
        part_qkv.reshape(-1, cols),
        gbq,
        gconv,
        gcomp,
        gt,
        gh,
        gw,
        part_proj.reshape(-1, hd),
        gbp,
        part_short.reshape(-1, cols),
        gbs,
        g2,
        b2,
        part_fc1.reshape(-1, hd),
        gb1,
        part_fc2,
        gb2,
    )


def solution(mesh):
    split = P("clip", "tm", "height", None, None)
    shared = P()
    weight = P("clip", ("tm", "height"))
    placed = (split, P("clip", None, None, "tm", "height", None, None), P("clip"), P("clip")) + (shared,) * 19 + (split,)
    outs = (split, split, shared, shared, weight) + (shared,) * 6 + (weight, shared, weight, shared, shared, shared, weight, shared, weight, shared)
    return jax.shard_map(body, mesh=mesh, in_specs=placed, out_specs=outs, check_vma=False)
```

time: 398 us -> 270 us (0.68)
  blocking collectives: 115 us -> 38.5 us
  waiting for transfers between devices: 64.6 us -> 24.7 us
  local copies, waits for them, and re-layouts: 23.6 us -> 16.3 us
  starting transfers between devices: 43.6 us -> 38.3 us
  Pallas kernels: 129 us -> 133 us
    all_to_all x4 -> x1, blocking collectives: 71.4 us -> 11.5 us  [body(): lax.all_to_all(joined.reshape(HEADS, per_q, LANE), G, 0, 0, tiled=True)]
    all_to_all x7 -> x4, waiting for transfers between devices: 34.6 us -> 11 us  [the longest x1 7.23 us: body(): dj_head = lax.all_to_all(dj, G, 0, 0, tiled=True).reshape(queries, LANE)]
    pallas_call x9 -> x8, Pallas kernels: 93.6 us -> 74.2 us  [call(): pl.pallas_call(kernel, out_shape=outs, in_specs=specs, out_specs=jax.tree...]
    pallas_call x0 -> x1, Pallas kernels: none -> 18.7 us  [body(): pl.pallas_call(functools.partial(conv_kernel, hdims), out_shape=(shape((C...]
    all_to_all x3 -> x1, waiting for transfers between devices: 20.4 us -> 3.67 us  [over_clips(): lax.all_to_all(value, 'clip', 0, 0, tiled=True).astype(f32)]
    all_gather x3 -> x2, blocking collectives: 43.4 us -> 27.1 us  [the longest x1 16.1 us: body(): late = jnp.sum(lax.all_gather(late, 'clip', axis=0).astype(f32), axis=0)]
    ppermute x0 -> x15, starting transfers between devices: none -> 16.1 us  [the longest x6 8.92 us: over_clips(): lax.ppermute(sent, 'clip', [(i, (i + k) % n_clip) for i in range(n_clip)])]
    all_to_all x7 -> x4, starting transfers between devices: 27.5 us -> 15.2 us  [the longest x1 4.5 us: body(): pg_rows = lax.all_to_all(pgp, G, 0, 0, tiled=True)]
  transfers between devices with their start and end apart: 14 -> 23, of which waited for: 6 -> 8; matrix products, arithmetic and copies ran while one was open for 5% -> 4% of each run, Pallas kernels for 31% -> 46%
where the time goes in v2:
time: 270 us; the launch traced here: 269 us
  Pallas kernels  133 us (49%)
  blocking collectives  38.5 us (14%)
  starting transfers between devices  38.3 us (14%)
  waiting for transfers between devices  24.7 us (9%)
  local copies, waits for them, and re-layouts  16.3 us (6%)
  between operations  15.8 us (6%)
    pallas_call x8, Pallas kernels, call(): pl.pallas_call(kernel, out_shape=outs, in_specs=specs, out_specs=jax.tree...  74.2 us
    pallas_call x1, Pallas kernels, body(): pl.pallas_call(functools.partial(conv_back_kernel, hdims), out_shape=(sha...  26 us
    pallas_call x1, Pallas kernels, body(): pl.pallas_call(functools.partial(conv_kernel, hdims), out_shape=(shape((C...  18.7 us
    all_gather x1, blocking collectives, body(): late = jnp.sum(lax.all_gather(late, 'clip', axis=0).astype(f32), axis=0)  16.1 us
    pallas_call x1, Pallas kernels, body(): pl.pallas_call(functools.partial(mlp_kernel, (width, hd)), grid=(HEADS,),...  14.2 us
    all_to_all x1, blocking collectives, body(): lax.all_to_all(joined.reshape(HEADS, per_q, LANE), G, 0, 0, tiled=True)  11.5 us
    all_gather x1, blocking collectives, body(): late_full = lax.all_gather(late, G, axis=0)  10.9 us
    unnamed x43, local copies, waits for them, and re-layouts  9.14 us
  transfers between devices with their start and end apart: 23, of which 8 were waited for; matrix products, arithmetic and copies ran while one was open for 4% of the time, Pallas kernels for 46%

profile of v2, /device:TPU:0, one launch (start us, length us, event | category | flops | bytes accessed | tf_op | source)
XLA Modules:
  0.0 268.9 jit_solution(15771021356284490631)
XLA Ops:
  15.3 4.4 %shard_map.401 = bf16[8,128,384]{2,1,0:T(8,128)(2,1)} custom-call(bf16[2,2,4,6,24,768]{5,4,3,2,1,0:T(8,128)(2,1)} %bitcast.59, f32[2,2,2,768]{3,2,1,0:T(2,128)} %c_ref.1), custom_call_target="tpu_custom_call" | custom-call | flops 5000000000 | tf_op jit(solution)/shard_map/pallas_call | solution.py:66
  19.7 3.0 %collective-permute-done.refs_1_ = bf16[576,384]{1,0:T(8,128)(2,1)S(1)} collective-permute-done((bf16[576,384]{1,0:T(8,128)(2,1)}, bf16[576,384]{1,0:T(8,128)(2,1)S(1)}, u32[]{:S(2)}, u32[]{:S(2)}) %collective-permute-start) | collective-permute-done | bytes 442400 | tf_op jit(solution)/shard_map/ppermute | solution.py:821
  29.0 3.3 %collective-permute-done.2.refs_3_ = bf16[288,384]{1,0:T(8,128)(2,1)S(1)} collective-permute-done((bf16[288,384]{1,0:T(8,128)(2,1)S(1)}, bf16[288,384]{1,0:T(8,128)(2,1)S(1)}, u32[]{:S(2)}, u32[]{:S(2)}) %collective-permute-start.2) | collective-permute-done | bytes 221216 | tf_op jit(solution)/shard_map/ppermute | solution.py:820
  34.3 3.5 %all-to-all-start = ((bf16[8,128,384]{2,1,0:T(8,128)(2,1)}), bf16[8,128,384]{2,1,0:T(8,128)(2,1)S(1)}, u32[]{:S(2)}, u32[]{:S(2)}) async-start(bf16[8,128,384]{2,1,0:T(8,128)(2,1)} %shard_map.401), calls=%async_computation | async-start | bytes 1572864 | tf_op jit(solution)/shard_map/all_to_all | solution.py:837
  39.7 18.7 %shard_map.402 = (bf16[3200,256]{1,0:T(8,128)(2,1)}, bf16[3200,128]{1,0:T(8,128)(2,1)}, bf16[1152,128]{1,0:T(8,128)(2,1)}, f32[5064,128]{1,0:T(8,128)}, f32[5064,128]{1,0:T(8,128)}) custom-call(s32[5]{0:T(128)} %stack.16.meta, f32[32,256]{1,0:T(8,128)} %pad_maximum_fusion.1.w_ref, bf16[2304,384]{1,0:T(8,128)(2,1)} %w_ref.5, f32[1,384]{1,0:T(1,128)} %bitcast.58, ...), custom_call_target="tpu_custom_call" | custom-call | flops 17999998976 | tf_op jit(solution)/shard_map/pallas_call | solution.py:848
  59.3 16.1 %shard_map.403 = (bf16[4864,256]{1,0:T(8,128)(2,1)}, bf16[256,4864]{1,0:T(8,128)(2,1)}, bf16[4864,128]{1,0:T(8,128)(2,1)}, bf16[256,1152]{1,0:T(8,128)(2,1)}, f3...) custom-call(s32[5]{0:T(128)} %stack.16.meta, bf16[3200,256]{1,0:T(8,128)(2,1)} %get-tuple-element.83.kc_ref, ...), custom_call_target="tpu_custom_call" | custom-call | flops 16000000000 | tf_op jit(solution)/shard_map/pallas_call | solution.py:66
  75.4 11.5 %all_to_all.35.j_ref = bf16[8,144,128]{2,1,0:T(8,128)(2,1)} all-to-all(bf16[8,144,128]{2,1,0:T(8,128)(2,1)} %bitcast.54), channel_id=1, replica_groups=mesh['clip'=4,'tm'=2,'height'=4] {'tm','height'}, dimensions={0} | all-to-all | bytes 589824 | tf_op jit(solution)/shard_map/all_to_all | solution.py:895
  86.9 14.2 %shard_map.404 = (bf16[144,768]{1,0:T(8,128)(2,1)}, bf16[144,2048]{1,0:T(8,128)(2,1)}, bf16[8,288,384]{2,1,0:T(8,128)(2,1)}, bf16[8,144,128]{2,1,0:T(8,128)(2,1)}, f32[144,384]{1,0:T(8,128)}) custom-call(bf16[8,144,128]{2,1,0:T(8,128)(2,1)} %all_to_all.35.j_ref, f32[144,384]{1,0:T(8,128)} %get-tuple-element.88.mx_ref, bf16[144,768]{1,0:T(8,128)(2,1)} %reshape.106.cot_ref, ...), custom_call_target="tpu_custom_call" | custom-call | flops 14000000000 | tf_op jit(solution)/shard_map/pallas_call | solution.py:900
  101.1 3.4 %all-to-all-start.2 = ((bf16[8,144,128]{2,1,0:T(8,128)(2,1)}), bf16[8,144,128]{2,1,0:T(8,128)(2,1)S(1)}, u32[]{:S(2)}, u32[]{:S(2)}) async-start(bf16[8,144,128]{2,1,0:T(8,128)(2,1)} %get-tuple-element.99), calls=%async_computation.2 | async-start | bytes 589824 | tf_op jit(solution)/shard_map/all_to_all | solution.py:943
  104.5 7.2 %all-to-all-done.2 = bf16[8,144,128]{2,1,0:T(8,128)(2,1)S(1)} async-done(((bf16[8,144,128]{2,1,0:T(8,128)(2,1)}), bf16[8,144,128]{2,1,0:T(8,128)(2,1)S(1)}, u32[]{:S(2)}, u32[]{:S(2)}) %all-to-all-start.2) | async-done | bytes 294944 | tf_op jit(solution)/shard_map/all_to_all | solution.py:943
  112.5 3.6 %all-to-all-start.3 = ((bf16[8,288,384]{2,1,0:T(8,128)(2,1)}), bf16[8,288,384]{2,1,0:T(8,128)(2,1)S(1)}, u32[]{:S(2)}, u32[]{:S(2)}) async-start(bf16[8,288,384]{2,1,0:T(8,128)(2,1)} %get-tuple-element.103), calls=%async_computation.3 | async-start | bytes 3538944 | tf_op jit(solution)/shard_map/all_to_all | solution.py:946
  116.1 31.9 %shard_map.405 = (f32[3200,128]{1,0:T(8,128)}, f32[3200,128]{1,0:T(8,128)}, bf16[8,144,384]{2,1,0:T(8,128)(2,1)}, f32[1152,128]{1,0:T(8,128)}) custom-call(bf16[4864,256]{1,0:T(8,128)(2,1)} %get-tuple-element.92.k_ref, bf16[256,4864]{1,0:T(8,128)(2,1)} %get-tuple-element.93.kt_ref, bf16[4864,128]{1,0:T(8,128)(2,1)} %get-tuple-element.94.v_ref, ...), custom_call_target="tpu_custom_call" | custom-call | flops 32000000000 | tf_op jit(solution)/shard_map/pallas_call | solution.py:66
  148.0 3.8 %all-to-all-done.3.ah_ref = bf16[8,288,384]{2,1,0:T(8,128)(2,1)S(1)} async-done(((bf16[8,288,384]{2,1,0:T(8,128)(2,1)}), bf16[8,288,384]{2,1,0:T(8,128)(2,1)S(1)}, u32[]{:S(2)}, u32[]{:S(2)}) %all-to-all-start.3) | async-done | bytes 1769504 | tf_op jit(solution)/shard_map/all_to_all | solution.py:946
  153.0 8.4 %shard_map.406 = (bf16[768,384]{1,0:T(8,128)(2,1)}, bf16[8,240,384]{2,1,0:T(8,128)(2,1)}, bf16[192,384]{1,0:T(8,128)(2,1)}, bf16[96,384]{1,0:T(8,128)(2,1)}, f32[8,128]{1,0:T(8,128)}) custom-call(s32[5]{0:T(128)} %stack.16.meta, bf16[1152,2048]{1,0:T(8,128)(2,1)} %all-gather.5.cloned.1.call-done.keep_ref, bf16[8,288,384]{2,1,0:T(8,128)(2,1)} %copy-done.2, ...), custom_call_target="tpu_custom_call" | custom-call | flops 8999999488 | tf_op jit(solution)/shard_map/pallas_call | solution.py:66
  161.3 3.7 %all-to-all-start.4 = ((bf16[8,240,384]{2,1,0:T(8,128)(2,1)}), bf16[8,240,384]{2,1,0:T(8,128)(2,1)S(1)}, u32[]{:S(2)}, u32[]{:S(2)}) async-start(bf16[8,240,384]{2,1,0:T(8,128)(2,1)} %get-tuple-element.111), calls=%async_computation.4 | async-start | bytes 2949120 | tf_op jit(solution)/shard_map/all_to_all | solution.py:1006
  165.9 3.9 %collective-permute-start.11 = (bf16[264,384]{1,0:T(8,128)(2,1)}, bf16[264,384]{1,0:T(8,128)(2,1)}, u32[]{:S(2)}, u32[]{:S(2)}) collective-permute-start(bf16[264,384]{1,0:T(8,128)(2,1)} %get-tuple-element.180), channel_id=1, source_target_pairs={{0,24},{8,0},{16,8},{24,16},{1,25},{9,1},{17,9},{25,17},{2,26},{10... | collective-permute-start | bytes 608264 | tf_op jit(solution)/shard_map/ppermute | solution.py:1000
  170.9 26.0 %shard_map.407 = (bf16[8,336,384]{2,1,0:T(8,128)(2,1)}, f32[64,128]{1,0:T(8,128)}, f32[8,384]{1,0:T(8,128)}) custom-call(s32[5]{0:T(128)} %stack.16.meta, f32[5064,128]{1,0:T(8,128)} %get-tuple-element.90.mk, f32[5064,128]{1,0:T(8,128)} %get-tuple-element.91.mv, f32[3200,128]{1,0:T(8,128)} %get-tuple-element.107.dk_ref, ...), custom_call_target="tpu_custom_call" | custom-call | flops 28000000000 | tf_op jit(solution)/shard_map/pallas_call | solution.py:1009
  196.9 4.5 %all-to-all-start.5 = ((bf16[8,336,384]{2,1,0:T(8,128)(2,1)}), bf16[8,336,384]{2,1,0:T(8,128)(2,1)}, u32[]{:S(2)}, u32[]{:S(2)}) async-start(bf16[8,336,384]{2,1,0:T(8,128)(2,1)} %get-tuple-element.112), calls=%async_computation.5 | async-start | bytes 4128768 | tf_op jit(solution)/shard_map/all_to_all | solution.py:1028
  211.0 4.4 %shard_map.408 = bf16[40,384]{1,0:T(8,128)(2,1)} custom-call(bf16[2,2,4,6,24,768]{5,4,3,2,1,0:T(8,128)(2,1)} %bitcast.60, bf16[8,144,384]{2,1,0:T(8,128)(2,1)} %slice.34.p_ref, f32[64,128]{1,0:T(8,128)} %get-tuple-element.114.conv_ref, f32[8,384]{1,0:T(8,128)} %get-tuple-element.115.stat_ref, f32[8,128]{1,0:T(8,128)} %get-tuple-element.116.small_ref), custom_call_target="tpu_custom_call" | custom-call | flops 6000000000 | tf_op jit(solution)/shard_map/pallas_call | solution.py:66
  215.3 16.1 %all-gather = bf16[160,384]{1,0:T(8,128)(2,1)S(1)} all-gather(bf16[40,384]{1,0:T(8,128)(2,1)} %shard_map.408), channel_id=2, replica_groups=mesh['clip'=4,'tm'=2,'height'=4] {'clip'}, dimensions={0}, use_global_device_ids=true | all-gather | bytes 153600 | tf_op jit(solution)/shard_map/all_gather | solution.py:1039
  231.5 10.9 %all-gather.1 = f32[320,384]{1,0:T(8,128)} all-gather(f32[40,384]{1,0:T(8,128)S(1)} %convert_reduce_fusion.1), channel_id=3, replica_groups=mesh['clip'=4,'tm'=2,'height'=4] {'tm','height'}, dimensions={0}, use_global_device_ids=true | all-gather | bytes 552960 | tf_op jit(solution)/shard_map/all_gather | solution.py:1040
  248.9 3.4 %all-to-all-start.6 = ((bf16[4,72,384]{2,1,0:T(8,128)(2,1)}), bf16[4,72,384]{2,1,0:T(8,128)(2,1)S(1)}, u32[]{:S(2)}, u32[]{:S(2)}) async-start(bf16[4,72,384]{2,1,0:T(8,128)(2,1)} %reshape_reshape.6), calls=%async_computation.6 | async-start | bytes 442368 | tf_op jit(solution)/shard_map/all_to_all | solution.py:1002
  252.3 5.1 %shard_map.410 = bf16[576,384]{1,0:T(8,128)(2,1)} custom-call(bf16[576,384]{1,0:T(8,128)(2,1)} %bitcast.62, f32[384]{0:T(512)} %g_ref.7, bf16[2304,384]{1,0:T(8,128)(2,1)} %w_ref.5, bf16[8,336,384]{2,1,0:T(8,128)(2,1)} %all-to-all-done.5.pg_ref, f32[144,384]{1,0:T(8,128)} %get-tuple-element.88.mx_ref, f32[144,384]{1,0:T(8,128)} %get-tuple-element.119.mg_ref), custom_call_target="tpu_custom_call" | custom-call | flops 8000000000 | tf_op jit(solution)/shard_map/pallas_call | solution.py:66
  257.4 3.7 %all-to-all-done.6 = bf16[4,72,384]{2,1,0:T(8,128)(2,1)S(1)} async-done(((bf16[4,72,384]{2,1,0:T(8,128)(2,1)}), bf16[4,72,384]{2,1,0:T(8,128)(2,1)S(1)}, u32[]{:S(2)}, u32[]{:S(2)}) %all-to-all-start.6) | async-done | bytes 221216 | tf_op jit(solution)/shard_map/all_to_all | solution.py:1002
  (111 shorter events, 38.4 us)
Async XLA Ops:
  9.4 13.3 %collective-permute-start = (bf16[576,384]{1,0:T(8,128)(2,1)}, bf16[576,384]{1,0:T(8,128)(2,1)S(1)}, u32[]{:S(2)}, u32[]{:S(2)}) collective-permute-start(bf16[576,384]{1,0:T(8,128)(2,1)} %get-tuple-element.79.refs_0_), channel_id=1, source_target_pairs={{0,2},{1,3},{2,0},{3,1},{4,6},{5,7},{6,4},{7,5},{8,10},{9,11},{10,... | collective-permute-start | bytes 1327112 | tf_op jit(solution)/shard_map/ppermute | solution.py:821
  12.3 11.8 %collective-permute-start.1 = (bf16[576,384]{1,0:T(8,128)(2,1)}, bf16[576,384]{1,0:T(8,128)(2,1)S(1)}, u32[]{:S(2)}, u32[]{:S(2)}) collective-permute-start(bf16[576,384]{1,0:T(8,128)(2,1)} %get-tuple-element.79.refs_0_), channel_id=1, source_target_pairs={{0,4},{4,0},{1,5},{5,1},{2,6},{6,2},{3,7},{7,3},{8,12},{12,8},{9,1... | collective-permute-start | bytes 1327112 | tf_op jit(solution)/shard_map/ppermute | solution.py:820
  13.9 24.8 %collective-permute-start.4 = (bf16[576,384]{1,0:T(8,128)(2,1)}, bf16[576,384]{1,0:T(8,128)(2,1)S(1)}, u32[]{:S(2)}, u32[]{:S(2)}) collective-permute-start(bf16[576,384]{1,0:T(8,128)(2,1)} %get-tuple-element.79.refs_0_), channel_id=1, source_target_pairs={{0,1},{1,0},{2,3},{3,2},{4,5},{5,4},{6,7},{7,6},{8,9},{9,8},{10,11... | collective-permute-start | bytes 1327112 | tf_op jit(solution)/shard_map/ppermute | solution.py:821
  15.3 12.3 %copy-start.6 = (bf16[1,4,3,12,768]{4,1,3,2,0:T(4,128)(2,1)S(1)}, bf16[1,4,3,12,768]{4,1,3,2,0:T(4,128)(2,1)}, u32[]{:S(2)}) copy-start(bf16[1,4,3,12,768]{4,1,3,2,0:T(4,128)(2,1)} %param.48) | copy-start | bytes 663556
  24.2 14.4 %collective-permute-start.5 = (bf16[576,384]{1,0:T(8,128)(2,1)S(1)}, bf16[576,384]{1,0:T(8,128)(2,1)S(1)}, u32[]{:S(2)}, u32[]{:S(2)}) collective-permute-start(bf16[576,384]{1,0:T(8,128)(2,1)S(1)} %collective-permute-done.refs_1_), channel_id=1, source_target_pairs={{0,1},{1,0},{2,3},{3,2},{4,5},{5,4},{6,7},{7,6},{8,9},{9,8},{10,11... | collective-permute-start | bytes 1327112 | tf_op jit(solution)/shard_map/ppermute | solution.py:821
  24.3 14.3 %collective-permute-start.6 = (bf16[576,384]{1,0:T(8,128)(2,1)S(1)}, bf16[576,384]{1,0:T(8,128)(2,1)S(1)}, u32[]{:S(2)}, u32[]{:S(2)}) collective-permute-start(bf16[576,384]{1,0:T(8,128)(2,1)S(1)} %collective-permute-done.1.refs_2_), channel_id=1, source_target_pairs={{0,1},{1,0},{2,3},{3,2},{4,5},{5,4},{6,7},{7,6},{8,9},{9,8},{10,11... | collective-permute-start | bytes 1327112 | tf_op jit(solution)/shard_map/ppermute | solution.py:821
  24.9 7.4 %collective-permute-start.2 = (bf16[288,384]{1,0:T(8,128)(2,1)S(1)}, bf16[288,384]{1,0:T(8,128)(2,1)S(1)}, u32[]{:S(2)}, u32[]{:S(2)}) collective-permute-start(bf16[288,384]{1,0:T(8,128)(2,1)S(1)} %slice.32), channel_id=1, source_target_pairs={{0,4},{4,0},{1,5},{5,1},{2,6},{6,2},{3,7},{7,3},{8,12},{12,8},{9,1... | collective-permute-start | bytes 663560 | tf_op jit(solution)/shard_map/ppermute | solution.py:820
  26.4 7.2 %collective-permute-start.3 = (bf16[288,384]{1,0:T(8,128)(2,1)S(1)}, bf16[288,384]{1,0:T(8,128)(2,1)}, u32[]{:S(2)}, u32[]{:S(2)}) collective-permute-start(bf16[288,384]{1,0:T(8,128)(2,1)S(1)} %slice.33), channel_id=1, source_target_pairs={{0,2},{1,3},{2,0},{3,1},{4,6},{5,7},{6,4},{7,5},{8,10},{9,11},{10,... | collective-permute-start | bytes 663560 | tf_op jit(solution)/shard_map/ppermute | solution.py:821
  32.3 5.6 %collective-permute-start.7 = (bf16[288,384]{1,0:T(8,128)(2,1)S(1)}, bf16[288,384]{1,0:T(8,128)(2,1)}, u32[]{:S(2)}, u32[]{:S(2)}) collective-permute-start(bf16[288,384]{1,0:T(8,128)(2,1)S(1)} %collective-permute-done.2.refs_3_), channel_id=1, source_target_pairs={{0,1},{1,0},{2,3},{3,2},{4,5},{5,4},{6,7},{7,6},{8,9},{9,8},{10,11... | collective-permute-start | bytes 663560 | tf_op jit(solution)/shard_map/ppermute | solution.py:821
  33.6 5.0 %collective-permute-start.8 = (bf16[288,384]{1,0:T(8,128)(2,1)}, bf16[288,384]{1,0:T(8,128)(2,1)}, u32[]{:S(2)}, u32[]{:S(2)}) collective-permute-start(bf16[288,384]{1,0:T(8,128)(2,1)} %collective-permute-done.3.refs_4_), channel_id=1, source_target_pairs={{0,1},{1,0},{2,3},{3,2},{4,5},{5,4},{6,7},{7,6},{8,9},{9,8},{10,11... | collective-permute-start | bytes 663560 | tf_op jit(solution)/shard_map/ppermute | solution.py:821
  34.3 24.1 %all-to-all-start = ((bf16[8,128,384]{2,1,0:T(8,128)(2,1)}), bf16[8,128,384]{2,1,0:T(8,128)(2,1)S(1)}, u32[]{:S(2)}, u32[]{:S(2)}) async-start(bf16[8,128,384]{2,1,0:T(8,128)(2,1)} %shard_map.401), calls=%async_computation | async-start | bytes 1572864 | tf_op jit(solution)/shard_map/all_to_all | solution.py:837
  37.8 113.9 %all-gather.7.cloned.1.call-start = ((), (), s32[]{:S(2)}) async-start(), calls=%async_computation.8 | async-start | bytes 1990656 | tf_op jit(solution)/shard_map/all_gather | solution.py:839
  38.6 113.4 %all-gather.5.cloned.1.call-start = ((), (), s32[]{:S(2)}) async-start(), calls=%async_computation.7 | async-start | bytes 5308416 | tf_op jit(solution)/shard_map/all_gather | solution.py:944
  101.1 10.7 %all-to-all-start.2 = ((bf16[8,144,128]{2,1,0:T(8,128)(2,1)}), bf16[8,144,128]{2,1,0:T(8,128)(2,1)S(1)}, u32[]{:S(2)}, u32[]{:S(2)}) async-start(bf16[8,144,128]{2,1,0:T(8,128)(2,1)} %get-tuple-element.99), calls=%async_computation.2 | async-start | bytes 589824 | tf_op jit(solution)/shard_map/all_to_all | solution.py:943
  112.5 39.3 %all-to-all-start.3 = ((bf16[8,288,384]{2,1,0:T(8,128)(2,1)}), bf16[8,288,384]{2,1,0:T(8,128)(2,1)S(1)}, u32[]{:S(2)}, u32[]{:S(2)}) async-start(bf16[8,288,384]{2,1,0:T(8,128)(2,1)} %get-tuple-element.103), calls=%async_computation.3 | async-start | bytes 3538944 | tf_op jit(solution)/shard_map/all_to_all | solution.py:946
  161.3 35.6 %all-to-all-start.4 = ((bf16[8,240,384]{2,1,0:T(8,128)(2,1)}), bf16[8,240,384]{2,1,0:T(8,128)(2,1)S(1)}, u32[]{:S(2)}, u32[]{:S(2)}) async-start(bf16[8,240,384]{2,1,0:T(8,128)(2,1)} %get-tuple-element.111), calls=%async_computation.4 | async-start | bytes 2949120 | tf_op jit(solution)/shard_map/all_to_all | solution.py:1006
  165.9 36.4 %collective-permute-start.11 = (bf16[264,384]{1,0:T(8,128)(2,1)}, bf16[264,384]{1,0:T(8,128)(2,1)}, u32[]{:S(2)}, u32[]{:S(2)}) collective-permute-start(bf16[264,384]{1,0:T(8,128)(2,1)} %get-tuple-element.180), channel_id=1, source_target_pairs={{0,24},{8,0},{16,8},{24,16},{1,25},{9,1},{17,9},{25,17},{2,26},{10... | collective-permute-start | bytes 608264 | tf_op jit(solution)/shard_map/ppermute | solution.py:1000
  169.8 32.5 %collective-permute-start.10 = (bf16[264,384]{1,0:T(8,128)(2,1)S(1)}, bf16[264,384]{1,0:T(8,128)(2,1)}, u32[]{:S(2)}, u32[]{:S(2)}) collective-permute-start(bf16[264,384]{1,0:T(8,128)(2,1)S(1)} %get-tuple-element.181), channel_id=1, source_target_pairs={{0,16},{8,24},{16,0},{24,8},{1,17},{9,25},{17,1},{25,9},{2,18},{10... | collective-permute-start | bytes 608264 | tf_op jit(solution)/shard_map/ppermute | solution.py:1000
  169.8 32.5 %collective-permute-start.9 = (bf16[264,384]{1,0:T(8,128)(2,1)S(1)}, bf16[264,384]{1,0:T(8,128)(2,1)}, u32[]{:S(2)}, u32[]{:S(2)}) collective-permute-start(bf16[264,384]{1,0:T(8,128)(2,1)S(1)} %get-tuple-element.179), channel_id=1, source_target_pairs={{0,8},{8,16},{16,24},{24,0},{1,9},{9,17},{17,25},{25,1},{2,10},{10... | collective-permute-start | bytes 608264 | tf_op jit(solution)/shard_map/ppermute | solution.py:1000
  196.9 50.2 %all-to-all-start.5 = ((bf16[8,336,384]{2,1,0:T(8,128)(2,1)}), bf16[8,336,384]{2,1,0:T(8,128)(2,1)}, u32[]{:S(2)}, u32[]{:S(2)}) async-start(bf16[8,336,384]{2,1,0:T(8,128)(2,1)} %get-tuple-element.112), calls=%async_computation.5 | async-start | bytes 4128768 | tf_op jit(solution)/shard_map/all_to_all | solution.py:1028
  207.0 39.0 %collective-permute-start.14 = (bf16[192,384]{1,0:T(8,128)(2,1)S(1)}, bf16[192,384]{1,0:T(8,128)(2,1)S(1)}, u32[]{:S(2)}, u32[]{:S(2)}) collective-permute-start(bf16[192,384]{1,0:T(8,128)(2,1)S(1)} %get-tuple-element.183), channel_id=1, source_target_pairs={{0,24},{8,0},{16,8},{24,16},{1,25},{9,1},{17,9},{25,17},{2,26},{10... | collective-permute-start | bytes 442376 | tf_op jit(solution)/shard_map/ppermute | solution.py:1000
  209.8 36.2 %collective-permute-start.13 = (bf16[192,384]{1,0:T(8,128)(2,1)S(1)}, bf16[192,384]{1,0:T(8,128)(2,1)S(1)}, u32[]{:S(2)}, u32[]{:S(2)}) collective-permute-start(bf16[192,384]{1,0:T(8,128)(2,1)S(1)} %get-tuple-element.184), channel_id=1, source_target_pairs={{0,16},{8,24},{16,0},{24,8},{1,17},{9,25},{17,1},{25,9},{2,18},{10... | collective-permute-start | bytes 442376 | tf_op jit(solution)/shard_map/ppermute | solution.py:1000
  211.0 35.0 %collective-permute-start.12 = (bf16[192,384]{1,0:T(8,128)(2,1)S(1)}, bf16[192,384]{1,0:T(8,128)(2,1)S(1)}, u32[]{:S(2)}, u32[]{:S(2)}) collective-permute-start(bf16[192,384]{1,0:T(8,128)(2,1)S(1)} %get-tuple-element.182), channel_id=1, source_target_pairs={{0,8},{8,16},{16,24},{24,0},{1,9},{9,17},{17,25},{25,1},{2,10},{10... | collective-permute-start | bytes 442376 | tf_op jit(solution)/shard_map/ppermute | solution.py:1000
  248.9 12.1 %all-to-all-start.6 = ((bf16[4,72,384]{2,1,0:T(8,128)(2,1)}), bf16[4,72,384]{2,1,0:T(8,128)(2,1)S(1)}, u32[]{:S(2)}, u32[]{:S(2)}) async-start(bf16[4,72,384]{2,1,0:T(8,128)(2,1)} %reshape_reshape.6), calls=%async_computation.6 | async-start | bytes 442368 | tf_op jit(solution)/shard_map/all_to_all | solution.py:1002
  (16 other events, 75.2 us)
Sparse Core Ops, SparseCore 0:
  40.6 28.1 all-gather.6
  101.2 50.7 all-gather.4

commit v3 on v2

--- a/solution.py
+++ b/solution.py
@@ -135,7 +135,7 @@
         mx_ref[t * half * HALF : (t + 1) * half * HALF, :] = pair_reduce(tall, tiles, jnp.maximum)
 
 
-def squeeze_kernel(dims, mem_ref, c_ref, out_ref, tiles, squeezed):
+def squeeze_kernel(dims, mem_ref, c_ref, cot_ref, mx_ref, out_ref, early_ref, tiles, squeezed):
     frames, rows, width, hd = dims
     half = rows // 2
     count = half * frames * VH
@@ -157,6 +157,9 @@
         out_ref[n] = jnp.concatenate(
             [squeezed[0, 0, :, cut], squeezed[1, 0, :, cut], squeezed[0, 1, :, cut], squeezed[1, 1, :, cut]], axis=1
         ).astype(bf)
+    cot = jnp.concatenate([cot_ref[t, a].astype(f32) for t in range(frames) for a in range(half)], axis=0)
+    early_ref[:, 0:width] = cot.astype(bf)
+    early_ref[:, width:] = mx_ref[...].astype(bf)
 
 
 def flat_row(t, h):
@@ -281,7 +284,7 @@
             tab[at : at + VW, :] = ref[first : first + VW, :]
 
 
-def attend_kernel(dims, meta, kc_ref, vc_ref, q_ref, y_ref, t_ref, h_ref, w_ref, place_ref, k_ref, kt_ref, v_ref, qt_ref, o_ref, l_ref, j_ref, vt, tab, s_ref):
+def attend_kernel(dims, meta, kc_ref, vc_ref, q_ref, y_ref, t_ref, h_ref, w_ref, place_ref, k_ref, v_ref, qt_ref, o_ref, l_ref, j_ref, vt, tab):
     frames, rows, n_height, hd = dims
     half = rows // 2
     side, length = meta[0], meta[1]
@@ -319,11 +322,13 @@
     v_ref[at:, :] = jnp.zeros((rest, LANE), bf)
     for i in range(KEYS // 256):
         cut = slice(i * 256, (i + 1) * 256)
-        kt_ref[:, cut] = k_ref[cut, :].T
         vt[:, cut] = v_ref[cut, :].T
     pt = q_ref[...].astype(f32).T[0:hd]
     build_table(tab, t_ref, h_ref, w_ref)
-    along = nn(tab[...], pt, precision=HI)
+    table = tab[...]
+    coarse = table.astype(bf)
+    turned = pt.astype(bf)
+    along = nn(coarse, turned) + nn((table - coarse.astype(f32)).astype(bf), turned)
     tq, aq, cq = place_ref[0:1, :], place_ref[1:2, :], place_ref[2:3, :]
     part_t = jnp.zeros((FR, queries), f32)
     for v in range(FR):
@@ -344,44 +349,42 @@
     tail = lax.broadcasted_iota(jnp.int32, (64, queries), 0)
     qt_ref[192:256, :] = jnp.where(tail == 0, FAR, 0.0).astype(bf)
     factor = scale * LOG2E
-    wide = s_ref.shape[1]
-    blocks = [(i, min(i + 512, KEYS)) for i in range(0, KEYS, 512)]
-
-    def one(block, carry):
-        cols = pl.ds(pl.multiple_of(block * wide, LANE), wide)
-        query = qt_ref[:, cols]
-        top = jnp.full((8, wide), FAR, f32)
-        for lo, hi in blocks:
-            scores = nn(k_ref[lo:hi, :], query)
-            s_ref[lo:hi, :] = scores
-            top = jnp.maximum(top, jnp.max(scores.reshape((hi - lo) // 8, 8, wide), axis=0))
-        top = jnp.max(top, axis=0, keepdims=True) * factor
-        total = jnp.zeros((LANE, wide), f32)
-        for lo, hi in blocks:
-            weights = jnp.exp2(s_ref[lo:hi, :] * factor - top).astype(bf)
-            total = total + nn(vt[:, lo:hi], weights)
-        norm = total[hd : hd + 1]
-        o_ref[:, cols] = total[0:hd] / norm
-        l_ref[:, cols] = top + jnp.log2(norm)
-        return carry
-
-    lax.fori_loop(0, queries // wide, one, 0)
+    query = qt_ref[...]
+    top = None
+    for lo in range(0, KEYS, 1024):
+        cut = slice(lo, min(lo + 1024, KEYS))
+        scores = nn(k_ref[cut, :], query)
+        here = jnp.max(scores.reshape(scores.shape[0] // 8, 8, queries), axis=0)
+        here = jnp.max(here, axis=0, keepdims=True) * factor
+        new = here if top is None else jnp.maximum(top, here)
+        part = nn(vt[:, cut], jnp.exp2(scores * factor - new).astype(bf))
+        total = part if top is None else total * jnp.exp2(top - new) + part
+        top = new
+    norm = total[hd : hd + 1]
+    o_ref[...] = total[0:hd] / norm
+    l_ref[...] = top + jnp.log2(norm)
     j_ref[...] = pad_lanes((o_ref[...] + pt).T, LANE).astype(bf)
 
 
-def mlp_kernel(dims, j_ref, mx_ref, cot_ref, wp_ref, ws_ref, bp_ref, bs_ref, g_ref, b_ref, w1_ref, b1_ref, w2_ref, b2_ref,
+def turn_kernel(k_ref, kt_ref):
+    for i in range(KEYS // 256):
+        cut = slice(i * 256, (i + 1) * 256)
+        kt_ref[:, cut] = k_ref[cut, :].T
+
+
+def mlp_kernel(dims, j_ref, early_ref, wp_ref, ws_ref, bp_ref, bs_ref, g_ref, b_ref, w1_ref, b1_ref, w2_ref, b2_ref,
                out_ref, keep_ref, act_ref, dj_ref, mg_ref,
                resid, n2, acc, ngrad, joined, gb1):
     width, hd = dims
     i = pl.program_id(0)
-    per_q = cot_ref.shape[0]
+    per_q = early_ref.shape[0]
     block = w1_ref.shape[0]
 
     @pl.when(i == 0)
     def _():
         joined[...] = jnp.concatenate([j_ref[n][:, 0:hd] for n in range(HEADS)], axis=1)
         shift = row_of(bp_ref, 0, width) + row_of(bs_ref, 0, width)
-        value = nt(joined[...], wp_ref[...]) + nt(mx_ref[...].astype(bf), ws_ref[...]) + shift
+        value = nt(joined[...], wp_ref[...]) + nt(early_ref[:, width:], ws_ref[...]) + shift
         resid[...] = value
         unit, _ = layer_unit(value)
         n2[...] = (unit * row_of(g_ref, 0, width) + row_of(b_ref, 0, width)).astype(bf)
@@ -394,7 +397,7 @@
     act = (hidden * gate).astype(bf)
     act_ref[0, 0:per_q, :] = act
     acc[...] += nt(act, w2_ref[...])
-    grad = nn(cot_ref[...], w2_ref[...])
+    grad = nn(early_ref[:, 0:width], w2_ref[...])
     hgrad = (grad * (gate + hidden * jnp.exp(-0.5 * hidden * hidden) / ROOT_TWO_PI)).astype(bf)
     act_ref[0, per_q:, :] = hgrad
     gb1[:, here] = jnp.sum(hgrad.astype(f32), axis=0, keepdims=True)
@@ -403,33 +406,35 @@
     @pl.when(i == pl.num_programs(0) - 1)
     def _():
         value = resid[...]
-        out_ref[...] = (value + acc[...] + row_of(b2_ref, 0, width)).astype(bf)
+        result = value + acc[...] + row_of(b2_ref, 0, width)
+        for t in range(out_ref.shape[0]):
+            for a in range(out_ref.shape[1]):
+                at = (t * out_ref.shape[1] + a) * HALF
+                out_ref[t, a] = result[at : at + HALF].astype(bf)
         unit, inverse = layer_unit(value)
-        cot = cot_ref[...].astype(f32)
+        cot = early_ref[:, 0:width].astype(f32)
         grad = ngrad[...]
         scaled = grad * row_of(g_ref, 0, width)
         back = inverse * (
             scaled - jnp.mean(scaled, axis=-1, keepdims=True) - unit * jnp.mean(scaled * unit, axis=-1, keepdims=True)
         )
         low = (cot + back).astype(bf)
-        channels = mx_ref.shape[1]
         keep_ref[:, 0:width] = n2[...]
-        keep_ref[:, width : 2 * width] = low
-        keep_ref[:, 2 * width : 2 * width + channels] = mx_ref[...].astype(bf)
+        keep_ref[:, width:] = low
         joined_grad = nn(low, wp_ref[...])
-        for n in range(HEADS):
-            dj_ref[n] = pad_lanes(joined_grad[:, n * hd : (n + 1) * hd], LANE).astype(bf)
         mg_ref[...] = nn(low, ws_ref[...])
         sums = [jnp.sum(v, axis=0, keepdims=True) for v in (low.astype(f32), grad * unit, grad, cot)] + [gb1[...]]
-        lines = [v[:, k : k + LANE] for v in sums for k in range(0, v.shape[1], LANE)]
-        exact = jnp.concatenate(lines, axis=0)
-        high = exact.astype(bf).astype(f32)
-        lines = jnp.concatenate([high, exact - high, jnp.zeros((per_q - 2 * exact.shape[0], LANE), f32)], axis=0)
-        keep_ref[:, 2 * width + channels :] = lines.astype(bf)
+        flat = [v[:, k : k + width] for v in sums for k in range(0, v.shape[1], width)]
+        spare = LANE - hd
+        for n in range(HEADS):
+            exact = jnp.concatenate([flat[n][:, k : k + spare] for k in range(0, width, spare)], axis=0)
+            high = exact.astype(bf).astype(f32)
+            side = jnp.concatenate([high, exact - high, jnp.zeros((per_q - 2 * exact.shape[0], spare), f32)], axis=0)
+            dj_ref[n] = jnp.concatenate([joined_grad[:, n * hd : (n + 1) * hd], side], axis=1).astype(bf)
 
 
 def attend_back_kernel(dims, k_ref, kt_ref, v_ref, qt_ref, q_ref, o_ref, l_ref, dj_ref, t_ref, h_ref, w_ref, place_ref,
-                       dk_ref, dv_ref, mem_ref, pq_ref,
+                       dk_ref, dv_ref, mem_ref, pq_ref, small_ref,
                        dot_ref, dq, tab, dtab, dks, dvs, delta, tables):
     frames, rows, n_height, hd = dims
     half = rows // 2
@@ -437,28 +442,29 @@
     scale = hd**-0.5
     factor = scale * LOG2E
     turned = dj_ref[...].astype(f32).T
-    dot_ref[...] = turned.astype(bf)
+    per_q = queries // HEADS
+    spare = jnp.zeros((per_q, LANE - hd), f32)
+    for src in range(HEADS):
+        spare = spare + dj_ref[src * per_q : (src + 1) * per_q, hd:].astype(f32)
+    lines = small_ref.shape[0]
+    small_ref[...] = spare[0:lines] + spare[lines : 2 * lines]
+    dot_ref[0:hd, :] = turned[0:hd].astype(bf)
+    dot_ref[hd:, :] = jnp.zeros((LANE - hd, queries), bf)
     delta[...] = jnp.sum(turned[0:hd] * o_ref[...], axis=0, keepdims=True)
     dq[...] = jnp.zeros(dq.shape, f32)
-    wide = 384
+    half_keys = KEYS // 2
 
     def chunk(i, carry):
-        cut = pl.ds(pl.multiple_of(i * 256, 256), 256)
-        dk = jnp.zeros((256, LANE), f32)
-        dv = jnp.zeros((256, LANE), f32)
-        for lo in range(0, queries, wide):
-            cols = slice(lo, lo + wide)
-            shares = jnp.exp2(nn(k_ref[cut, :], qt_ref[:, cols]) * factor - l_ref[:, cols])
-            slope = nn(v_ref[cut, :], dot_ref[:, cols])
-            score = (shares * (slope - delta[:, cols])).astype(bf)
-            dv = dv + nn(shares.astype(bf), dj_ref[cols, :])
-            dk = dk + nn(score, q_ref[cols, :])
-            dq[:, cols] += nn(kt_ref[0 : dq.shape[0], cut], score)
-        dks[cut, :] = dk * scale
-        dvs[cut, :] = dv
+        cut = pl.ds(pl.multiple_of(i * half_keys, LANE), half_keys)
+        shares = jnp.exp2(nn(k_ref[cut, :], qt_ref[...]) * factor - l_ref[...])
+        slope = nn(v_ref[cut, :], dot_ref[...])
+        score = (shares * (slope - delta[...])).astype(bf)
+        dvs[cut, :] = nn(shares.astype(bf), dj_ref[...])
+        dks[cut, :] = nn(score, q_ref[...]) * scale
+        dq[...] += nn(kt_ref[0 : dq.shape[0], cut], score)
         return carry
 
-    lax.fori_loop(0, KEYS // 256, chunk, 0)
+    lax.fori_loop(0, 2, chunk, 0)
     dk_ref[...] = dks[0:CUR, :]
     dv_ref[...] = dvs[0:CUR, :]
     each = frames * VH
@@ -486,9 +492,10 @@
         for a in range(HALF):
             row = 8 * FR + (n * HALF + a) * GRID
             dtab[row : row + GRID, :] = jnp.where(place == a, part, 0.0)
-    pooled_grad = dq[0:hd, :] * scale + tn(tab[...], dtab[...], precision=HI) + dot_ref[0:hd, :].astype(f32)
+    spread = dtab[...].astype(bf)
+    pooled_grad = dq[0:hd, :] * scale + tn(tab[...].astype(bf), spread) + dot_ref[0:hd, :].astype(f32)
     pq_ref[...] = pad_lanes(pooled_grad.T * 0.25, LANE)
-    grads = nn(dtab[...], q_ref[...].astype(f32), precision=HI)
+    grads = nn(spread, q_ref[...])
     tables[...] = jnp.zeros(tables.shape, f32)
     for v in range(FR):
         tables[v : v + FR, :] += grads[8 * v : 8 * v + FR]
@@ -504,10 +511,10 @@
         mem_ref[dst, LANE:, :] = jnp.concatenate([high, part - high, jnp.zeros((16, LANE), f32)], axis=1).astype(bf)
 
 
-def conv_back_kernel(dims, meta, mk, mv, dk_ref, dv_ref, pq_ref, w_ref, g_ref, b_ref, qkv_ref, *refs):
+def conv_back_kernel(dims, meta, dk_ref, dv_ref, pq_ref, w_ref, g_ref, b_ref, qkv_ref, *refs):
     frames, rows, n_height, hd = dims
     half = rows // 2
-    blocks, (out_ref, gw_ref, stat_ref, pg, gk, gv, acc, wide, gather, tall, sems) = refs[:10], refs[10:]
+    blocks, (out_ref, stat_ref, pg, gk, gv, wide, gather, tall, sems) = refs[:10], refs[10:]
     copies = gather_blocks(dims[:3], meta, blocks, gather, sems)
     for copy in copies:
         copy.start()
@@ -523,7 +530,6 @@
                 grid[flat_row(t, h) : flat_row(t, h) + GRID, :] = jnp.concatenate(
                     [ref[at : at + VW, :], jnp.zeros((GRID - VW, LANE), f32)], axis=0
                 )
-    acc[...] = jnp.zeros(acc.shape, f32)
     local = lax.broadcasted_iota(jnp.int32, (4 * GRID, 1), 0)
     line = (local * 2731) >> 16
     column = local - line * GRID
@@ -540,23 +546,9 @@
         for m, grid in ((0, gk), (1, gv)):
             back = four_rows(grid, taps9(w_ref, m), base, True, GRID)
             pg[out, (1 + m) * LANE : (2 + m) * LANE] = (back * inside).astype(bf)
-        for m, grid, masked in ((0, gk, mk), (1, gv, mv)):
-            for h in range(4):
-                here = grid[pl.ds(pl.multiple_of(base + h * GRID, 8), GRID), :]
-                turned = [pltpu.roll(here, GRID - 1, 0), here, pltpu.roll(here, 1, 0)]
-                for a in range(3):
-                    for b in range(3):
-                        cells = masked[pl.ds(pl.multiple_of(base + (a - 1) * PLANE + (h + b - 1) * GRID, 8), GRID), :]
-                        for c in range(3):
-                            prod = cells * turned[c]
-                            tap = m * 27 + (a * 3 + b) * 3 + c
-                            acc[tap] += prod[0:8] + prod[8:16] + prod[16:24]
         return carry
 
     lax.fori_loop(0, FR * VW // 4, step, 0)
-    for tap in range(54):
-        gw_ref[tap : tap + 1, :] = jnp.sum(acc[tap], axis=0, keepdims=True)
-    gw_ref[54:, :] = jnp.zeros((gw_ref.shape[0] - 54, LANE), f32)
     queries = pq_ref.shape[0]
     wide[pl.ds(0, queries, 2), :] = pq_ref[...]
     wide[pl.ds(1, queries, 2), :] = pq_ref[...]
@@ -615,14 +607,36 @@
     stat_ref[3:8, :] = jnp.zeros((5, channels), f32)
 
 
-def weight_grad_kernel(dims, meta, keep_ref, ah_ref, j_ref, cot_ref, dmem_ref, fc2_ref, fc1_ref, proj_ref, short_ref, small_ref,
-                       act, hgrad, tall, parts):
+def gather_rows(meta, refs, out, sems):
+    x0, x2, x4, x6a, x6b, x1, x3, x5, x7a, x7b = refs
+    copies = []
+    for d, parts in enumerate([[x0], [x1], [x2], [x3], [x4], [x5], [x6a, x6b], [x7a, x7b]]):
+        at = (meta[4] ^ d) * (out.shape[0] // HEADS)
+        for ref in parts:
+            size = ref.shape[0]
+            copies.append(pltpu.make_async_copy(ref, out.at[pl.ds(pl.multiple_of(at, 16), size), :], sems.at[len(copies)]))
+            at = at + size
+    return copies
+
+
+def weight_grad_kernel(dims, meta, ah_ref, j_ref, dmem_ref, *refs):
     width, hd, channels, per_q = dims
+    early, kept = refs[:10], refs[10:20]
+    fc2_ref, fc1_ref, proj_ref, short_ref, act, hgrad, tall, parts, cot_ref, keep_ref, sems = refs[20:]
     member = meta[4]
+    first = gather_rows(meta, early, cot_ref, sems.at[0])
+    second = gather_rows(meta, kept, keep_ref, sems.at[1])
+    for copy in first + second:
+        copy.start()
     for src in range(HEADS):
         cut = slice(src * per_q, (src + 1) * per_q)
         act[cut, :] = ah_ref[src, 0:per_q, :]
         hgrad[cut, :] = ah_ref[src, per_q:, :]
+    for copy in first:
+        copy.wait()
+    fc2_ref[...] = tn(cot_ref[:, 0:width], act[...]).astype(bf)
+    for copy in second:
+        copy.wait()
     normed = keep_ref[:, 0:width]
     resid = keep_ref[:, width : 2 * width]
     fc1 = tn(hgrad[...], normed)
@@ -632,21 +646,10 @@
     cols = channels // HEADS
     lane = lax.broadcasted_iota(jnp.int32, (channels, LANE), 1)
     pick = (lax.broadcasted_iota(jnp.int32, (channels, LANE), 0) == lane + member * cols) & (lane < cols)
-    maxima = nn(keep_ref[:, 2 * width : 2 * width + channels], pick.astype(f32).astype(bf)).astype(bf)
+    maxima = nn(cot_ref[:, width:], pick.astype(f32).astype(bf)).astype(bf)
     both = tn(resid, jnp.concatenate([j_ref[...], maxima], axis=1))
     proj_ref[...] = pack_rows(both[:, 0:hd], tall.at[0], channels // hd).astype(bf)
     short_ref[...] = pack_rows(both[:, LANE : LANE + cols], tall.at[1], channels // cols).astype(bf)
-    sums = jnp.zeros((per_q, LANE), f32)
-    for src in range(HEADS):
-        sums = sums + keep_ref[src * per_q : (src + 1) * per_q, 2 * width + channels :].astype(f32)
-    lines = HEADS * width // LANE
-    sums = sums[0:lines] + sums[lines : 2 * lines]
-    each = lines // HEADS
-    own = jnp.zeros((each, LANE), f32)
-    for n in range(HEADS):
-        own = jnp.where(member == n, sums[n * each : (n + 1) * each], own)
-    small_ref[...] = jnp.concatenate([own, jnp.zeros((8 - each, LANE), f32)], axis=0)
-    fc2_ref[...] = tn(cot_ref[...], act[...]).astype(bf)
 
 
 def last_kernel(dims, x_ref, g_ref, w_ref, pg_ref, mx_ref, mg_ref, out_ref, full, tiles):
@@ -704,7 +707,34 @@
         out_ref[t * per : (t + 1) * per, :] = (back + pool).astype(bf)
 
 
-def compress_kernel(dims, mem_ref, p_ref, conv_ref, stat_ref, small_ref, late_ref, tiles, lines):
+def conv_grad_kernel(hd, mk, mv, dk_ref, dv_ref, out_ref, acc):
+    acc[...] = jnp.zeros(acc.shape, f32)
+    blank = jnp.zeros((GRID - VW, LANE), f32)
+
+    def step(it, carry):
+        t = it // (VW // 4)
+        base = GRID + (1 + t) * PLANE + it % (VW // 4) * 4 * GRID
+        for m, ref, masked in ((0, dk_ref, mk), (1, dv_ref, mv)):
+            quad = ref[pl.ds(pl.multiple_of(it * (4 * VW), 16), 4 * VW), :]
+            for h in range(4):
+                here = jnp.concatenate([quad[h * VW : (h + 1) * VW], blank], axis=0)
+                turned = [pltpu.roll(here, GRID - 1, 0), here, pltpu.roll(here, 1, 0)]
+                for a in range(3):
+                    for b in range(3):
+                        cells = masked[pl.ds(pl.multiple_of(base + (a - 1) * PLANE + (h + b - 1) * GRID, 8), GRID), :]
+                        for c in range(3):
+                            prod = cells * turned[c]
+                            acc[m * 27 + (a * 3 + b) * 3 + c] += prod[0:8] + prod[8:16] + prod[16:24]
+        return carry
+
+    lax.fori_loop(0, FR * VW // 4, step, 0)
+    sums = [jnp.sum(acc[tap], axis=0, keepdims=True) for tap in range(54)] + [jnp.zeros((1, LANE), f32)] * 2
+    sums = jnp.concatenate(sums, axis=0)
+    out_ref[0:14, :] = jnp.concatenate([sums[14 * g : 14 * (g + 1), 0:hd] for g in range(4)], axis=1)
+    out_ref[14:16, :] = jnp.zeros((2, 4 * hd), f32)
+
+
+def late_kernel(dims, mem_ref, p_ref, conv_ref, stat_ref, small_ref, late_ref, tiles, lines):
     frames, rows, width, hd = dims
     half = rows // 2
     channels = late_ref.shape[1]
@@ -728,14 +758,16 @@
                 for k in range(width // channels):
                     at = LATE_COMP + 8 * k + 4 * m + 2 * i + j
                     lines[at : at + 1, :] = done[:, k * channels : (k + 1) * channels]
-    conv = jnp.concatenate([conv_ref[14 * g : 14 * (g + 1), 0:hd] for g in range(4)], axis=1)
-    lines[0:14, :] = conv
+    lines[0:14, :] = conv_ref[0:14, :]
     lines[14:17, :] = stat_ref[0:3, :]
+    count = small_ref.shape[0] // 2
     for k in range(2):
-        lines[LATE_SMALL + k : LATE_SMALL + k + 1, :] = jnp.concatenate([small_ref[3 * k + i : 3 * k + i + 1, :] for i in range(3)], axis=1)
+        lines[LATE_SMALL + k : LATE_SMALL + k + 1, :] = jnp.concatenate(
+            [small_ref[k * count + i : k * count + i + 1, :] for i in range(count)], axis=1
+        )
     tables = jnp.zeros((16, LANE), f32)
     for n in range(HEADS):
-        part = p_ref[n][LANE:, :].astype(f32)
+        part = p_ref[n][LANE : LANE + 16, :].astype(f32)
         tables = tables + part[:, 0:LANE] + part[:, LANE : 2 * LANE]
     lines[LATE_TABLE : LATE_TABLE + 5, :] = jnp.concatenate([tables[5 * g : 5 * (g + 1), :] for g in range(3)], axis=1)
     late_ref[...] = lines[...].astype(bf)
@@ -754,7 +786,7 @@
         for r in range(14):
             i = 14 * g + r
             if i < 54:
-                conv_ref[i // 27, i % 27 // 9, i % 9 // 3, i % 3 : i % 3 + 1, :] = conv[r : r + 1]
+                conv_ref[i % 27 // 9, i % 9 // 3, i % 3, i // 27 : i // 27 + 1, :] = conv[r : r + 1]
     for p in range(3):
         value = jnp.concatenate([parts[n][14:15, p * hd : (p + 1) * hd] for n in range(HEADS)], axis=1)
         bqkv_ref[p * width : (p + 1) * width] = value.reshape(width)
@@ -803,7 +835,6 @@
     queries = HEADS * per_q
     x = clip_input.reshape(cells_all, channels)
     mem = memory[0]
-    cot = cotangent.reshape(per_q, width)
 
     dims = (frames, rows, width, hd)
     n1, mx = call(
@@ -820,23 +851,31 @@
             return lax.ppermute(value, "tm", [(i, i ^ 1) for i in range(lax.axis_size("tm"))])
         return lax.ppermute(value, "height", [(i, i ^ bit) for i in range(n_height)])
 
-    x2, x4, x1 = swap(n1, 2), swap(n1, 4), swap(n1, 1)
-    pay2 = call(
+    def near(value):
+        return swap(value, 2), swap(value, 4), swap(value, 1)
+
+    def across(x2, x4, cut):
+        return swap(x2[:cut], 4), swap(x4[cut:], 2), swap(x2, 1), swap(x4, 1)
+
+    def last(x6a, x6b):
+        return swap(x6a, 1), swap(x6b, 1)
+
+    x2, x4, x1 = near(n1)
+    pay2, early = call(
         functools.partial(squeeze_kernel, dims),
-        shape((HEADS, LANE, 4 * hd), bf),
-        (mem, compress),
+        (shape((HEADS, LANE, 4 * hd), bf), shape((per_q, width + channels), bf)),
+        (mem, compress, cotangent[0], mx),
         scratch=[pltpu.VMEM((4, width // LANE, GRID, LANE), f32), pltpu.VMEM((2, MEM, LANE, width), f32)],
         smem=0,
         us=5,
     )
     x2, x4, pay2 = lax.optimization_barrier((x2, x4, pay2))
-    cut = cells_all // 2
-    x6a, x6b = swap(x2[:cut], 4), swap(x4[cut:], 2)
-    x3, x5 = swap(x2, 1), swap(x4, 1)
-    x7a, x7b = swap(x6a, 1), swap(x6b, 1)
+    x6a, x6b, x3, x5 = across(x2, x4, cells_all // 2)
+    x7a, x7b = last(x6a, x6b)
     y2 = lax.all_to_all(pay2, G, 0, 0, tiled=True)
-    cot_late, x7a = lax.optimization_barrier((cot, x7a))
-    cot_full = lax.all_gather(cot_late, G, axis=0, tiled=True)
+    early, x7a = lax.optimization_barrier((early, x7a))
+    e2, e4, e1 = near(early)
+    cut = -(-per_q // 32) * 16
     taps = lax.dynamic_slice_in_dim(conv_kv.reshape(2, 27, width), member * hd, hd, 2)
     taps = jnp.pad(taps, ((0, 0), (0, 5), (0, LANE - hd)))
     taps = jnp.concatenate([taps[0], taps[1]], axis=1)
@@ -873,11 +912,12 @@
     place[2] = local % HALF
     place = jnp.asarray(place)
     wide = 384
-    k_all, kt_all, v_all, qt_all, o_all, l_all, joined = call(
+    kc, e2, e4, e1 = lax.optimization_barrier((kc, e2, e4, e1))
+    e6a, e6b, e3, e5 = across(e2, e4, cut)
+    k_all, v_all, qt_all, o_all, l_all, joined = call(
         functools.partial(attend_kernel, hdims),
         (
             shape((KEYS, 2 * LANE), bf),
-            shape((2 * LANE, KEYS), bf),
             shape((KEYS, LANE), bf),
             shape((2 * LANE, queries), bf),
             shape((hd, queries), f32),
@@ -888,20 +928,21 @@
         scratch=[
             pltpu.VMEM((LANE, KEYS), bf),
             pltpu.VMEM((TAB, hd), f32),
-            pltpu.VMEM((KEYS, wide), f32),
         ],
         us=16,
     )
     joined_rows = lax.all_to_all(joined.reshape(HEADS, per_q, LANE), G, 0, 0, tiled=True)
+    kt_all = call(turn_kernel, shape((2 * LANE, KEYS), bf), (k_all,), smem=0, us=4)
+    joined_rows, kt_all, e6a, e6b, e3, e5 = lax.optimization_barrier((joined_rows, kt_all, e6a, e6b, e3, e5))
+    e7a, e7b = last(e6a, e6b)
     block = mlp // HEADS
     whole = lambda *dims: pl.BlockSpec(dims, lambda i: (0,) * len(dims))
-    keep_width = 2 * width + channels
-    keep_width = keep_width + LANE
+    keep_width = 2 * width
     output, keep, acthg, dj, max_grad = pl.pallas_call(
         functools.partial(mlp_kernel, (width, hd)),
         grid=(HEADS,),
         out_shape=(
-            shape((per_q, width), bf),
+            shape((frames, half, HALF, width), bf),
             shape((per_q, keep_width), bf),
             shape((HEADS, 2 * per_q, block), bf),
             shape((HEADS, per_q, LANE), bf),
@@ -909,8 +950,7 @@
         ),
         in_specs=[
             whole(HEADS, per_q, LANE),
-            whole(per_q, channels),
-            whole(per_q, width),
+            whole(per_q, width + channels),
             whole(width, width),
             whole(width, channels),
             whole(width),
@@ -923,7 +963,7 @@
             whole(width),
         ],
         out_specs=(
-            whole(per_q, width),
+            whole(frames, half, HALF, width),
             whole(per_q, keep_width),
             pl.BlockSpec((1, 2 * per_q, block), lambda i: (i, 0, 0)),
             whole(HEADS, per_q, LANE),
@@ -939,19 +979,20 @@
         ],
         compiler_params=pltpu.CompilerParams(vmem_limit_bytes=56 << 20),
         cost_estimate=cost(14),
-    )(joined_rows, mx, cot, w_proj, w_short, b_proj, b_short, norm2_gain, norm2_bias, w_fc1, b_fc1, w_fc2, b_fc2)
+    )(joined_rows, early, w_proj, w_short, b_proj, b_short, norm2_gain, norm2_bias, w_fc1, b_fc1, w_fc2, b_fc2)
     dj_head = lax.all_to_all(dj, G, 0, 0, tiled=True).reshape(queries, LANE)
-    keep_full = lax.all_gather(keep, G, axis=0, tiled=True)
-    acthg, dj_head = lax.optimization_barrier((acthg, dj_head))
+    k2, k4, k1 = near(keep)
+    acthg, dj_head, e7a, e7b = lax.optimization_barrier((acthg, dj_head, e7a, e7b))
     ah_head = lax.all_to_all(acthg, G, 0, 0, tiled=True)
 
-    dk, dv, dmem, pq = call(
+    dk, dv, dmem, pq, small2 = call(
         functools.partial(attend_back_kernel, hdims),
         (
             shape((CUR, LANE), f32),
             shape((CUR, LANE), f32),
             shape((HEADS, LANE + 16, 4 * hd), bf),
             shape((queries, LANE), f32),
+            shape((width // (LANE - hd), LANE - hd), f32),
         ),
         (k_all, kt_all, v_all, qt_all, q_all, o_all, l_all, dj_head, rel_t, rel_h, rel_w, place),
         scratch=[
@@ -965,39 +1006,57 @@
             pltpu.VMEM((TABLE_ROWS, LANE), f32),
         ],
         smem=0,
-        us=32,
+        us=25,
     )
     cols = channels // HEADS
     taken = dmem.shape[1]
-    fc2p, fc1p, projp, shortp, small2 = call(
+    mk, k2, k4, k1 = lax.optimization_barrier((mk, k2, k4, k1))
+    k6a, k6b, k3, k5 = across(k2, k4, cut)
+    k7a, k7b = last(k6a, k6b)
+    gconv = call(
+        functools.partial(conv_grad_kernel, hd),
+        shape((16, 4 * hd), f32),
+        (mk, mv, dk, dv),
+        scratch=[pltpu.VMEM((54, 8, LANE), f32)],
+        smem=0,
+        us=12,
+    )
+    dmem, gconv = lax.optimization_barrier((dmem, gconv))
+    outs = (
+        shape((width, block), bf),
+        shape((HEADS, taken + block * hd // channels, channels), bf),
+        shape((width * hd // channels, channels), bf),
+        shape((width // HEADS, channels), bf),
+    )
+    fc2p, fc1p, projp, shortp = call(
         functools.partial(weight_grad_kernel, (width, hd, channels, per_q)),
-        (
-            shape((width, block), bf),
-            shape((HEADS, taken + block * hd // channels, channels), bf),
-            shape((width * hd // channels, channels), bf),
-            shape((width // HEADS, channels), bf),
-            shape((8, LANE), f32),
-        ),
-        (meta, keep_full, ah_head, joined, cot_full, dmem),
+        outs,
+        (meta, ah_head, joined, dmem, early, e2, e4, e6a, e6b, e1, e3, e5, e7a, e7b, keep, k2, k4, k6a, k6b, k1, k3, k5, k7a, k7b),
         scratch=[
             pltpu.VMEM((queries, block), bf),
             pltpu.VMEM((queries, block), bf),
             pltpu.VMEM((2, width, LANE), f32),
             pltpu.VMEM((2, block, LANE), f32),
+            pltpu.VMEM((queries, width + channels), bf),
+            pltpu.VMEM((queries, 2 * width), bf),
+            pltpu.SemaphoreType.DMA((2, 10)),
         ],
         us=9,
-    )
+        far=20,
+    )
+
+    def over_four(sent):
+        got = [lax.ppermute(sent[k], "clip", [(i, i ^ k) for i in range(n_clip)]) for k in range(1, n_clip)]
+        first, second, third_, fourth = [v.astype(f32) for v in [sent[0]] + got]
+        return (first + second) + (third_ + fourth)
 
     def over_clips(parts, permute):
         parts = [v.reshape(n_clip, v.shape[0] // n_clip, v.shape[1]) for v in parts]
         ends = np.cumsum([0] + [v.shape[1] for v in parts])
         value = jnp.concatenate(parts, axis=1) if len(parts) > 1 else parts[0]
-        if permute and n_clip <= 4:
+        if permute and n_clip == 4:
             clip = lax.axis_index("clip")
-            total = lax.dynamic_index_in_dim(value, clip, 0, keepdims=False).astype(f32)
-            for k in range(1, n_clip):
-                sent = lax.dynamic_index_in_dim(value, lax.rem(clip + k, n_clip), 0, keepdims=False)
-                total = total + lax.ppermute(sent, "clip", [(i, (i + k) % n_clip) for i in range(n_clip)]).astype(f32)
+            total = over_four([lax.dynamic_index_in_dim(value, clip ^ k, 0, keepdims=False) for k in range(n_clip)])
         else:
             total = jnp.sum(lax.all_to_all(value, "clip", 0, 0, tiled=True).astype(f32), axis=0)
         return [total[lo:hi] for lo, hi in zip(ends, ends[1:])]
@@ -1006,43 +1065,44 @@
     first_back = lax.all_to_all(fc1p, G, 0, 0, tiled=True)
     part_fc2, part_proj, part_short = over_clips([fc2p, projp, shortp], True)
     sent = valid // 2 + third
-    pgp, gconv, stats = pl.pallas_call(
+    pgp, stats = pl.pallas_call(
         functools.partial(conv_back_kernel, hdims),
-        out_shape=(shape((HEADS, sent + 48, 4 * hd), bf), shape((64, LANE), f32), shape((8, channels), f32)),
-        in_specs=[pl.BlockSpec(memory_space=pltpu.SMEM)] + [vmem] * 9 + [pl.BlockSpec(memory_space=pl.ANY)] * 10,
-        out_specs=(vmem,) * 3,
+        out_shape=(shape((HEADS, sent + 48, 4 * hd), bf), shape((8, channels), f32)),
+        in_specs=[pl.BlockSpec(memory_space=pltpu.SMEM)] + [vmem] * 7 + [pl.BlockSpec(memory_space=pl.ANY)] * 10,
+        out_specs=(vmem,) * 2,
         scratch_shapes=[
             pltpu.VMEM((FR * GRID * GRID, 3 * LANE), bf),
             pltpu.VMEM((FLAT, LANE), f32),
             pltpu.VMEM((FLAT, LANE), f32),
-            pltpu.VMEM((54, 8, LANE), f32),
             pltpu.VMEM((2 * queries, LANE), f32),
             pltpu.VMEM((FR, GRID * GRID, channels), bf),
             pltpu.VMEM((2, 3 * hd, LANE), f32),
             pltpu.SemaphoreType.DMA((HEADS * frames,)),
         ],
         compiler_params=pltpu.CompilerParams(vmem_limit_bytes=56 << 20),
-        cost_estimate=cost(28),
-    )(meta, mk, mv, dk, dv, pq, taps, norm1_gain, norm1_bias, w_qkv, *blocks)
+        cost_estimate=cost(18),
+    )(meta, dk, dv, pq, taps, norm1_gain, norm1_bias, w_qkv, *blocks)
     pgp, first_back = lax.optimization_barrier((pgp, first_back))
     pg_rows = lax.all_to_all(pgp, G, 0, 0, tiled=True)
-    mem_back = first_back[:, :taken]
     [part_fc1] = over_clips([first_back[:, taken:].reshape(-1, channels)], True)
     late = call(
-        functools.partial(compress_kernel, dims),
+        functools.partial(late_kernel, dims),
         shape((LATE, channels), bf),
-        (mem, mem_back, gconv, stats, small2),
+        (mem, first_back, gconv, stats, small2),
         scratch=[pltpu.VMEM((4, width // LANE, GRID, LANE), f32), pltpu.VMEM((LATE, channels), f32)],
         smem=0,
-        us=6,
-    )
-    late = jnp.sum(lax.all_gather(late, "clip", axis=0).astype(f32), axis=0)
+        us=5,
+    )
+    if n_clip == 4:
+        late = over_four([late] * n_clip)
+    else:
+        late = jnp.sum(lax.all_gather(late, "clip", axis=0).astype(f32), axis=0)
     late_full = lax.all_gather(late, G, axis=0)
     vector = lambda n: shape((n,), f32)
     g1, b1, gbq, gconv, gcomp, gt, gh, gw, gbp, gbs, g2, b2, gb1, gb2 = call(
         functools.partial(sums_kernel, (width, hd, channels)),
         (
-            vector(channels), vector(channels), vector(3 * width), shape(conv_kv.shape, f32), shape(compress.shape, f32),
+            vector(channels), vector(channels), vector(3 * width), shape((3, 3, 3, 2, width), f32), shape(compress.shape, f32),
             shape(rel_t.shape, f32), shape(rel_h.shape, f32), shape(rel_w.shape, f32),
             vector(width), vector(width), vector(width), vector(width), vector(mlp), vector(width),
         ),
@@ -1051,7 +1111,7 @@
         smem=0,
         us=3,
     )
-    pg_rows, gb1 = lax.optimization_barrier((pg_rows, gb1))
+    pg_rows, gb1, part_fc1 = lax.optimization_barrier((pg_rows, gb1, part_fc1))
     qkv_rows = pg_rows[:, sent : sent + 3 * hd // HEADS]
     qkv_rows = qkv_rows.reshape(HEADS, 3, hd // HEADS, channels).transpose(1, 0, 2, 3).reshape(-1, channels)
     [part_qkv] = over_clips([qkv_rows], False)
@@ -1061,16 +1121,16 @@
         (x, norm1_gain, w_qkv, pg_rows, mx, max_grad),
         scratch=[pltpu.VMEM((cells_all, channels), f32), pltpu.VMEM((width // LANE, rows * GRID, LANE), f32)],
         smem=0,
-        us=8,
+        us=5,
     )
     return (
-        output.reshape(1, frames, half, HALF, width),
+        output[None],
         input_grad.reshape(clip_input.shape),
         g1,
         b1,
         part_qkv.reshape(-1, cols),
         gbq,
-        gconv,
+        jnp.moveaxis(gconv, 3, 0),
         gcomp,
         gt,
         gh,

time: 270 us -> 257 us (0.952); the launches traced: 269 us -> 253 us
  blocking collectives: 38.5 us -> 12.4 us
  starting transfers between devices: 38.3 us -> 62.6 us
  between operations: 15.8 us -> 2.9 us
  Pallas kernels: 133 us -> 128 us
    all_gather x1 -> x0, blocking collectives: 16.1 us -> none  [body(): late = jnp.sum(lax.all_gather(late, 'clip', axis=0).astype(f32), axis=0)]
    all_to_all x1 -> x0, blocking collectives: 11.5 us -> none  [body(): lax.all_to_all(joined.reshape(HEADS, per_q, LANE), G, 0, 0, tiled=True)]
    ppermute x7 -> x21, starting transfers between devices: 4.11 us -> 12.9 us  [swap(): lax.ppermute(value, 'height', [(i, i ^ bit) for i in range(n_height)])]
    pallas_call x1, Pallas kernels: 26 us -> 17.4 us  [body(): pl.pallas_call(functools.partial(conv_back_kernel, hdims), out_shape=(sha...]
    ppermute x2 -> x6, starting transfers between devices: 3.04 us -> 8.9 us  [swap(): lax.ppermute(value, 'tm', [(i, i ^ 1) for i in range(lax.axis_size('tm'))])]
    ppermute x6 -> x9, starting transfers between devices: 8.92 us -> 13.3 us  [over_four(): lax.ppermute(sent[k], 'clip', [(i, i ^ k) for i in range(n_clip)])]
    all_to_all x0 -> x1, starting transfers between devices: none -> 3.84 us  [body(): lax.all_to_all(joined.reshape(HEADS, per_q, LANE), G, 0, 0, tiled=True)]
    all_to_all x1, waiting for transfers between devices: 3.76 us -> 0.01 us  [body(): ah_head = lax.all_to_all(acthg, G, 0, 0, tiled=True)]
  transfers between devices with their start and end apart: 23 -> 43, of which waited for: 8 -> 11; matrix products, arithmetic and copies ran while one was open for 4% -> 4% of each run, Pallas kernels for 46% -> 41%
where the time goes in v3:
time: 257 us; the launch traced here: 253 us
  Pallas kernels  128 us (50%)
  starting transfers between devices  62.6 us (24%)
  waiting for transfers between devices  26.3 us (10%)
  local copies, waits for them, and re-layouts  18.2 us (7%)
  blocking collectives  12.4 us (5%)
  between operations  2.9 us (1%)
    pallas_call x10, Pallas kernels, call(): pl.pallas_call(kernel, out_shape=outs, in_specs=specs, out_specs=jax.tree...  77.6 us
    pallas_call x1, Pallas kernels, body(): pl.pallas_call(functools.partial(conv_kernel, hdims), out_shape=(shape((C...  18.7 us
    pallas_call x1, Pallas kernels, body(): pl.pallas_call(functools.partial(conv_back_kernel, hdims), out_shape=(sha...  17.4 us
    pallas_call x1, Pallas kernels, body(): pl.pallas_call(functools.partial(mlp_kernel, (width, hd)), grid=(HEADS,),...  14.6 us
    ppermute x9, starting transfers between devices, over_four(): lax.ppermute(sent[k], 'clip', [(i, i ^ k) for i in range(n_clip)])  13.3 us
    ppermute x21, starting transfers between devices, swap(): lax.ppermute(value, 'height', [(i, i ^ bit) for i in range(n_height)])  12.9 us
    all_gather x1, blocking collectives, body(): late_full = lax.all_gather(late, G, axis=0)  12.4 us
    unnamed x82, local copies, waits for them, and re-layouts  12.4 us
  transfers between devices with their start and end apart: 43, of which 11 were waited for; matrix products, arithmetic and copies ran while one was open for 4% of the time, Pallas kernels for 41%

profile of v3, /device:TPU:0, one launch (start us, length us, event | category | flops | bytes accessed | tf_op | source)
XLA Modules:
  0.0 252.7 jit_solution(4323219212492848710)
XLA Ops:
  9.6 4.6 %shard_map.401 = (bf16[8,128,384]{2,1,0:T(8,128)(2,1)}, bf16[144,1152]{1,0:T(8,128)(2,1)}) custom-call(bf16[2,2,4,6,24,768]{5,4,3,2,1,0:T(8,128)(2,1)} %bitcast.63, f32[2,2,2,768]{3,2,1,0:T(2,128)} %c_ref.1, bf16[4,3,12,768]{3,2,1,0:T(8,128)(2,1)} %bitcast.59, f32[144,384]{1,0:T(8,128)} %get-tuple-element.99.mx_ref), custom_call_target="tpu_custom_call" | custom-call | flops 5000000000 | tf_op jit(solution)/shard_map/pallas_call | solution.py:66
  21.7 4.1 %collective-permute-done.2.refs_3_ = bf16[288,384]{1,0:T(8,128)(2,1)S(1)} collective-permute-done((bf16[288,384]{1,0:T(8,128)(2,1)S(1)}, bf16[288,384]{1,0:T(8,128)(2,1)S(1)}, u32[]{:S(2)}, u32[]{:S(2)}) %collective-permute-start.2) | collective-permute-done | bytes 221216 | tf_op jit(solution)/shard_map/ppermute | solution.py:851
  27.8 3.7 %all-to-all-start = ((bf16[8,128,384]{2,1,0:T(8,128)(2,1)}), bf16[8,128,384]{2,1,0:T(8,128)(2,1)S(1)}, u32[]{:S(2)}, u32[]{:S(2)}) async-start(bf16[8,128,384]{2,1,0:T(8,128)(2,1)} %get-tuple-element.110), calls=%async_computation | async-start | bytes 1572864 | tf_op jit(solution)/shard_map/all_to_all | solution.py:875
  35.7 18.7 %shard_map.402 = (bf16[3200,256]{1,0:T(8,128)(2,1)}, bf16[3200,128]{1,0:T(8,128)(2,1)}, bf16[1152,128]{1,0:T(8,128)(2,1)}, f32[5064,128]{1,0:T(8,128)}, f32[5064,128]{1,0:T(8,128)}) custom-call(s32[5]{0:T(128)} %stack.16.meta, f32[32,256]{1,0:T(8,128)} %pad_maximum_fusion.1.w_ref, bf16[2304,384]{1,0:T(8,128)(2,1)} %w_ref.5, f32[1,384]{1,0:T(1,128)} %bitcast.62, ...), custom_call_target="tpu_custom_call" | custom-call | flops 17999998976 | tf_op jit(solution)/shard_map/pallas_call | solution.py:887
  56.7 12.1 %shard_map.403 = (bf16[4864,256]{1,0:T(8,128)(2,1)}, bf16[4864,128]{1,0:T(8,128)(2,1)}, bf16[256,1152]{1,0:T(8,128)(2,1)}, f32[96,1152]{1,0:T(8,128)}, f32[1,1152]{1,0:T(1,128)}, /*index=5*/bf16[1152,128]{1,0:T(8,128)(2,1)}) custom-call(s32[5]{0:T(128)} %stack.16.meta, bf16[3200,256]{1,0:T(8,128)(2,1)} %get-tuple-element.107.kc_ref, ...), custom_call_target="tpu_custom_call" | custom-call | flops 16000000000 | tf_op jit(solution)/shard_map/pallas_call | solution.py:66
  68.8 3.8 %all-to-all-start.1 = ((bf16[8,144,128]{2,1,0:T(8,128)(2,1)}), bf16[8,144,128]{2,1,0:T(8,128)(2,1)S(1)}, u32[]{:S(2)}, u32[]{:S(2)}) async-start(bf16[8,144,128]{2,1,0:T(8,128)(2,1)} %bitcast.56), calls=%async_computation.1 | async-start | bytes 589824 | tf_op jit(solution)/shard_map/all_to_all | solution.py:934
  76.2 3.8 %shard_map.404.kt_ref = bf16[256,4864]{1,0:T(8,128)(2,1)} custom-call(bf16[4864,256]{1,0:T(8,128)(2,1)} %get-tuple-element.112.k_ref), custom_call_target="tpu_custom_call" | custom-call | flops 4000000000 | tf_op jit(solution)/shard_map/pallas_call | solution.py:66
  83.7 14.6 %shard_map.405 = (bf16[4,3,12,768]{3,2,1,0:T(8,128)(2,1)}, bf16[144,1536]{1,0:T(8,128)(2,1)}, bf16[8,288,384]{2,1,0:T(8,128)(2,1)}, bf16[8,144,128]{2,1,0:T(8,128)(2,1)}, f32[144,384]{1,0:T(8,128)}) custom-call(bf16[8,144,128]{2,1,0:T(8,128)(2,1)} %copy-done.7, bf16[144,1152]{1,0:T(8,128)(2,1)} %get-tuple-element.106.early_ref.refs_0_, ...), custom_call_target="tpu_custom_call" | custom-call | flops 14000000000 | tf_op jit(solution)/shard_map/pallas_call | solution.py:941
  100.1 3.4 %all-to-all-start.2 = ((bf16[8,144,128]{2,1,0:T(8,128)(2,1)}), bf16[8,144,128]{2,1,0:T(8,128)(2,1)S(1)}, u32[]{:S(2)}, u32[]{:S(2)}) async-start(bf16[8,144,128]{2,1,0:T(8,128)(2,1)} %get-tuple-element.123), calls=%async_computation.2 | async-start | bytes 589824 | tf_op jit(solution)/shard_map/all_to_all | solution.py:983
  105.5 9.4 %all-to-all-done.2 = bf16[8,144,128]{2,1,0:T(8,128)(2,1)S(1)} async-done(((bf16[8,144,128]{2,1,0:T(8,128)(2,1)}), bf16[8,144,128]{2,1,0:T(8,128)(2,1)S(1)}, u32[]{:S(2)}, u32[]{:S(2)}) %all-to-all-start.2) | async-done | bytes 294944 | tf_op jit(solution)/shard_map/all_to_all | solution.py:983
  115.6 3.6 %all-to-all-start.3 = ((bf16[8,288,384]{2,1,0:T(8,128)(2,1)}), bf16[8,288,384]{2,1,0:T(8,128)(2,1)S(1)}, u32[]{:S(2)}, u32[]{:S(2)}) async-start(bf16[8,288,384]{2,1,0:T(8,128)(2,1)} %get-tuple-element.128), calls=%async_computation.3 | async-start | bytes 3538944 | tf_op jit(solution)/shard_map/all_to_all | solution.py:986
  122.9 22.0 %shard_map.406 = (f32[3200,128]{1,0:T(8,128)}, f32[3200,128]{1,0:T(8,128)}, bf16[8,144,384]{2,1,0:T(8,128)(2,1)}, f32[1152,128]{1,0:T(8,128)}, f32[24,32]{1,0:T(8,128)}) custom-call(bf16[4864,256]{1,0:T(8,128)(2,1)} %get-tuple-element.112.k_ref, bf16[256,4864]{1,0:T(8,128)(2,1)} %shard_map.404.kt_ref, bf16[4864,128]{1,0:T(8,128)(2,1)} %get-tuple-element.118.v_ref, ...), custom_call_target="tpu_custom_call" | custom-call | flops 24999999488 | tf_op jit(solution)/shard_map/pallas_call | solution.py:66
  146.6 12.4 %shard_map.407.conv_ref = f32[16,384]{1,0:T(8,128)} custom-call(f32[5064,128]{1,0:T(8,128)} %get-tuple-element.132.mk, f32[5064,128]{1,0:T(8,128)} %get-tuple-element.133.mv, f32[3200,128]{1,0:T(8,128)} %get-tuple-element.145.dk_ref, f32[3200,128]{1,0:T(8,128)} %get-tuple-element.134.dv_ref), custom_call_target="tpu_custom_call" | custom-call | flops 12000000000 | tf_op jit(solution)/shard_map/pallas_call | solution.py:66
  162.5 9.0 %shard_map.408 = (bf16[768,384]{1,0:T(8,128)(2,1)}, bf16[8,240,384]{2,1,0:T(8,128)(2,1)}, bf16[192,384]{1,0:T(8,128)(2,1)}, bf16[96,384]{1,0:T(8,128)(2,1)}) custom-call(s32[5]{0:T(128)} %stack.16.meta, bf16[8,288,384]{2,1,0:T(8,128)(2,1)} %copy-done.3, bf16[1152,128]{1,0:T(8,128)(2,1)} %get-tuple-element.111.j_ref, ...), custom_call_target="tpu_custom_call" | custom-call | flops 8999999488 | tf_op jit(solution)/shard_map/pallas_call | solution.py:66
  171.5 3.7 %all-to-all-start.4 = ((bf16[8,240,384]{2,1,0:T(8,128)(2,1)}), bf16[8,240,384]{2,1,0:T(8,128)(2,1)S(1)}, u32[]{:S(2)}, u32[]{:S(2)}) async-start(bf16[8,240,384]{2,1,0:T(8,128)(2,1)} %get-tuple-element.148), calls=%async_computation.4 | async-start | bytes 2949120 | tf_op jit(solution)/shard_map/all_to_all | solution.py:1065
  175.5 3.7 %collective-permute-start.35 = (bf16[264,384]{1,0:T(8,128)(2,1)S(1)}, bf16[264,384]{1,0:T(8,128)(2,1)}, u32[]{:S(2)}, u32[]{:S(2)}) collective-permute-start(bf16[264,384]{1,0:T(8,128)(2,1)S(1)} %get-tuple-element.218), channel_id=1, source_target_pairs={{0,24},{8,16},{16,8},{24,0},{1,25},{9,17},{17,9},{25,1},{2,26},{10... | collective-permute-start | bytes 608264 | tf_op jit(solution)/shard_map/ppermute | solution.py:1049
  180.0 17.4 %shard_map.409 = (bf16[8,336,384]{2,1,0:T(8,128)(2,1)}, f32[8,384]{1,0:T(8,128)}) custom-call(s32[5]{0:T(128)} %stack.16.meta, f32[3200,128]{1,0:T(8,128)} %get-tuple-element.145.dk_ref, f32[3200,128]{1,0:T(8,128)} %get-tuple-element.134.dv_ref, f32[1152,128]{1,0:T(8,128)} %get-tuple-element.146.pq_ref, f32[32,256]{1,0:T(8,128)} %pad_maximum_fusion.1.w_ref, ...), custom_call_target="tpu_custom_call" | custom-call | flops 17999998976 | tf_op jit(solution)/shard_map/pallas_call | solution.py:1068
  198.6 4.3 %all-to-all-start.5 = ((bf16[8,336,384]{2,1,0:T(8,128)(2,1)}), bf16[8,336,384]{2,1,0:T(8,128)(2,1)}, u32[]{:S(2)}, u32[]{:S(2)}) async-start(bf16[8,336,384]{2,1,0:T(8,128)(2,1)} %get-tuple-element.149), calls=%async_computation.5 | async-start | bytes 4128768 | tf_op jit(solution)/shard_map/all_to_all | solution.py:1086
  207.2 4.5 %shard_map.410 = bf16[40,384]{1,0:T(8,128)(2,1)} custom-call(bf16[2,2,4,6,24,768]{5,4,3,2,1,0:T(8,128)(2,1)} %bitcast.64, bf16[8,240,384]{2,1,0:T(8,128)(2,1)} %copy-done.2, f32[16,384]{1,0:T(8,128)} %shard_map.407.conv_ref, f32[8,384]{1,0:T(8,128)} %get-tuple-element.152.stat_ref, f32[24,32]{1,0:T(8,128)} %get-tuple-element.153.small_ref), custom_call_target="tpu_custom_call" | custom-call | flops 5000000000 | tf_op jit(solution)/shard_map/pallas_call | solution.py:66
  211.8 3.6 %collective-permute-start.29 = (bf16[40,384]{1,0:T(8,128)(2,1)}, bf16[40,384]{1,0:T(8,128)(2,1)S(1)}, u32[]{:S(2)}, u32[]{:S(2)}) collective-permute-start(bf16[40,384]{1,0:T(8,128)(2,1)} %shard_map.410), channel_id=1, source_target_pairs={{0,24},{8,16},{16,8},{24,0},{1,25},{9,17},{17,9},{25,1},{2,26},{10... | collective-permute-start | bytes 92168 | tf_op jit(solution)/shard_map/ppermute | solution.py:1049
  217.4 3.7 %collective-permute-start.32 = (bf16[192,384]{1,0:T(8,128)(2,1)S(1)}, bf16[192,384]{1,0:T(8,128)(2,1)S(1)}, u32[]{:S(2)}, u32[]{:S(2)}) collective-permute-start(bf16[192,384]{1,0:T(8,128)(2,1)S(1)} %get-tuple-element.221), channel_id=1, source_target_pairs={{0,24},{8,16},{16,8},{24,0},{1,25},{9,17},{17,9},{25,1},{2,26},{10... | collective-permute-start | bytes 442376 | tf_op jit(solution)/shard_map/ppermute | solution.py:1049
  221.9 12.4 %all-gather = f32[320,384]{1,0:T(8,128)} all-gather(f32[40,384]{1,0:T(8,128)S(1)} %add_add_fusion), channel_id=2, replica_groups=mesh['clip'=4,'tm'=2,'height'=4] {'tm','height'}, dimensions={0}, use_global_device_ids=true | all-gather | bytes 552960 | tf_op jit(solution)/shard_map/all_gather | solution.py:1100
  238.1 4.9 %all-to-all-start.6 = ((bf16[4,72,384]{2,1,0:T(8,128)(2,1)}), bf16[4,72,384]{2,1,0:T(8,128)(2,1)S(1)}, u32[]{:S(2)}, u32[]{:S(2)}) async-start(bf16[4,72,384]{2,1,0:T(8,128)(2,1)} %reshape_reshape.7), calls=%async_computation.6 | async-start | bytes 442368 | tf_op jit(solution)/shard_map/all_to_all | solution.py:1061
  244.0 5.1 %shard_map.412 = bf16[576,384]{1,0:T(8,128)(2,1)} custom-call(bf16[576,384]{1,0:T(8,128)(2,1)} %bitcast.66, f32[384]{0:T(512)} %g_ref.7, bf16[2304,384]{1,0:T(8,128)(2,1)} %w_ref.5, bf16[8,336,384]{2,1,0:T(8,128)(2,1)} %all-to-all-done.5.pg_ref, f32[144,384]{1,0:T(8,128)} %get-tuple-element.99.mx_ref, f32[144,384]{1,0:T(8,128)} %get-tuple-element.156.mg_ref), custom_call_target="tpu_custom_call" | custom-call | flops 5000000000 | tf_op jit(solution)/shard_map/pallas_call | solution.py:66
  (189 shorter events, 61.1 us)
Async XLA Ops:
  7.4 26.8 %collective-permute-start.4 = (bf16[576,384]{1,0:T(8,128)(2,1)}, bf16[576,384]{1,0:T(8,128)(2,1)S(1)}, u32[]{:S(2)}, u32[]{:S(2)}) collective-permute-start(bf16[576,384]{1,0:T(8,128)(2,1)} %get-tuple-element.98.refs_0_), channel_id=1, source_target_pairs={{0,1},{1,0},{2,3},{3,2},{4,5},{5,4},{6,7},{7,6},{8,9},{9,8},{10,11... | collective-permute-start | bytes 1327112 | tf_op jit(solution)/shard_map/ppermute | solution.py:852
  17.7 18.0 %collective-permute-start.5 = (bf16[576,384]{1,0:T(8,128)(2,1)S(1)}, bf16[576,384]{1,0:T(8,128)(2,1)}, u32[]{:S(2)}, u32[]{:S(2)}) collective-permute-start(bf16[576,384]{1,0:T(8,128)(2,1)S(1)} %collective-permute-done.refs_1_), channel_id=1, source_target_pairs={{0,1},{1,0},{2,3},{3,2},{4,5},{5,4},{6,7},{7,6},{8,9},{9,8},{10,11... | collective-permute-start | bytes 1327112 | tf_op jit(solution)/shard_map/ppermute | solution.py:852
  17.8 17.9 %collective-permute-start.6 = (bf16[576,384]{1,0:T(8,128)(2,1)S(1)}, bf16[576,384]{1,0:T(8,128)(2,1)}, u32[]{:S(2)}, u32[]{:S(2)}) collective-permute-start(bf16[576,384]{1,0:T(8,128)(2,1)S(1)} %collective-permute-done.1.refs_2_), channel_id=1, source_target_pairs={{0,1},{1,0},{2,3},{3,2},{4,5},{5,4},{6,7},{7,6},{8,9},{9,8},{10,11... | collective-permute-start | bytes 1327112 | tf_op jit(solution)/shard_map/ppermute | solution.py:852
  27.8 28.0 %all-to-all-start = ((bf16[8,128,384]{2,1,0:T(8,128)(2,1)}), bf16[8,128,384]{2,1,0:T(8,128)(2,1)S(1)}, u32[]{:S(2)}, u32[]{:S(2)}) async-start(bf16[8,128,384]{2,1,0:T(8,128)(2,1)} %get-tuple-element.110), calls=%async_computation | async-start | bytes 1572864 | tf_op jit(solution)/shard_map/all_to_all | solution.py:875
  32.2 22.2 %collective-permute-start.9 = (bf16[144,1152]{1,0:T(8,128)(2,1)S(1)}, bf16[144,1152]{1,0:T(8,128)(2,1)S(1)}, u32[]{:S(2)}, u32[]{:S(2)}) collective-permute-start(bf16[144,1152]{1,0:T(8,128)(2,1)S(1)} %copy-done.23), channel_id=1, source_target_pairs={{0,2},{1,3},{2,0},{3,1},{4,6},{5,7},{6,4},{7,5},{8,10},{9,11},{10,... | collective-permute-start | bytes 995336 | tf_op jit(solution)/shard_map/ppermute | solution.py:852
  34.2 20.3 %collective-permute-start.10 = (bf16[144,1152]{1,0:T(8,128)(2,1)S(1)}, bf16[144,1152]{1,0:T(8,128)(2,1)S(1)}, u32[]{:S(2)}, u32[]{:S(2)}) collective-permute-start(bf16[144,1152]{1,0:T(8,128)(2,1)S(1)} %copy-done.23), channel_id=1, source_target_pairs={{0,4},{4,0},{1,5},{5,1},{2,6},{6,2},{3,7},{7,3},{8,12},{12,8},{9,1... | collective-permute-start | bytes 995336 | tf_op jit(solution)/shard_map/ppermute | solution.py:851
  35.7 18.8 %collective-permute-start.11 = (bf16[144,1152]{1,0:T(8,128)(2,1)S(1)}, bf16[144,1152]{1,0:T(8,128)(2,1)S(1)}, u32[]{:S(2)}, u32[]{:S(2)}) collective-permute-start(bf16[144,1152]{1,0:T(8,128)(2,1)S(1)} %copy-done.23), channel_id=1, source_target_pairs={{0,1},{1,0},{2,3},{3,2},{4,5},{5,4},{6,7},{7,6},{8,9},{9,8},{10,11... | collective-permute-start | bytes 995336 | tf_op jit(solution)/shard_map/ppermute | solution.py:852
  54.5 28.4 %collective-permute-start.14 = (bf16[144,1152]{1,0:T(8,128)(2,1)S(1)}, bf16[144,1152]{1,0:T(8,128)(2,1)S(1)}, u32[]{:S(2)}, u32[]{:S(2)}) collective-permute-start(bf16[144,1152]{1,0:T(8,128)(2,1)S(1)} %collective-permute-done.9.refs_1_), channel_id=1, source_target_pairs={{0,1},{1,0},{2,3},{3,2},{4,5},{5,4},{6,7},{7,6},{8,9},{9,8},{10,11... | collective-permute-start | bytes 995336 | tf_op jit(solution)/shard_map/ppermute | solution.py:852
  55.3 27.7 %collective-permute-start.15 = (bf16[144,1152]{1,0:T(8,128)(2,1)S(1)}, bf16[144,1152]{1,0:T(8,128)(2,1)S(1)}, u32[]{:S(2)}, u32[]{:S(2)}) collective-permute-start(bf16[144,1152]{1,0:T(8,128)(2,1)S(1)} %collective-permute-done.10.refs_2_), channel_id=1, source_target_pairs={{0,1},{1,0},{2,3},{3,2},{4,5},{5,4},{6,7},{7,6},{8,9},{9,8},{10,11... | collective-permute-start | bytes 995336 | tf_op jit(solution)/shard_map/ppermute | solution.py:852
  98.2 21.0 %collective-permute-start.18 = (bf16[144,1536]{1,0:T(8,128)(2,1)}, bf16[144,1536]{1,0:T(8,128)(2,1)S(1)}, u32[]{:S(2)}, u32[]{:S(2)}) collective-permute-start(bf16[144,1536]{1,0:T(8,128)(2,1)} %get-tuple-element.131.refs_10_), channel_id=1, source_target_pairs={{0,2},{1,3},{2,0},{3,1},{4,6},{5,7},{6,4},{7,5},{8,10},{9,11},{10,... | collective-permute-start | bytes 1327112 | tf_op jit(solution)/shard_map/ppermute | solution.py:852
  99.8 19.5 %collective-permute-start.19 = (bf16[144,1536]{1,0:T(8,128)(2,1)}, bf16[144,1536]{1,0:T(8,128)(2,1)S(1)}, u32[]{:S(2)}, u32[]{:S(2)}) collective-permute-start(bf16[144,1536]{1,0:T(8,128)(2,1)} %get-tuple-element.131.refs_10_), channel_id=1, source_target_pairs={{0,4},{4,0},{1,5},{5,1},{2,6},{6,2},{3,7},{7,3},{8,12},{12,8},{9,1... | collective-permute-start | bytes 1327112 | tf_op jit(solution)/shard_map/ppermute | solution.py:851
  100.1 19.1 %collective-permute-start.20 = (bf16[144,1536]{1,0:T(8,128)(2,1)}, bf16[144,1536]{1,0:T(8,128)(2,1)}, u32[]{:S(2)}, u32[]{:S(2)}) collective-permute-start(bf16[144,1536]{1,0:T(8,128)(2,1)} %get-tuple-element.131.refs_10_), channel_id=1, source_target_pairs={{0,1},{1,0},{2,3},{3,2},{4,5},{5,4},{6,7},{7,6},{8,9},{9,8},{10,11... | collective-permute-start | bytes 1327112 | tf_op jit(solution)/shard_map/ppermute | solution.py:852
  100.1 14.8 %all-to-all-start.2 = ((bf16[8,144,128]{2,1,0:T(8,128)(2,1)}), bf16[8,144,128]{2,1,0:T(8,128)(2,1)S(1)}, u32[]{:S(2)}, u32[]{:S(2)}) async-start(bf16[8,144,128]{2,1,0:T(8,128)(2,1)} %get-tuple-element.123), calls=%async_computation.2 | async-start | bytes 589824 | tf_op jit(solution)/shard_map/all_to_all | solution.py:983
  115.6 45.0 %all-to-all-start.3 = ((bf16[8,288,384]{2,1,0:T(8,128)(2,1)}), bf16[8,288,384]{2,1,0:T(8,128)(2,1)S(1)}, u32[]{:S(2)}, u32[]{:S(2)}) async-start(bf16[8,288,384]{2,1,0:T(8,128)(2,1)} %get-tuple-element.128), calls=%async_computation.3 | async-start | bytes 3538944 | tf_op jit(solution)/shard_map/all_to_all | solution.py:986
  119.3 27.3 %collective-permute-start.21 = (bf16[80,1536]{1,0:T(8,128)(2,1)S(1)}, bf16[80,1536]{1,0:T(8,128)(2,1)S(1)}, u32[]{:S(2)}, u32[]{:S(2)}) collective-permute-start(bf16[80,1536]{1,0:T(8,128)(2,1)S(1)} %slice.45), channel_id=1, source_target_pairs={{0,4},{4,0},{1,5},{5,1},{2,6},{6,2},{3,7},{7,3},{8,12},{12,8},{9,1... | collective-permute-start | bytes 737288 | tf_op jit(solution)/shard_map/ppermute | solution.py:851
  121.3 24.3 %collective-permute-start.22 = (bf16[64,1536]{1,0:T(8,128)(2,1)S(1)}, bf16[64,1536]{1,0:T(8,128)(2,1)S(1)}, u32[]{:S(2)}, u32[]{:S(2)}) collective-permute-start(bf16[64,1536]{1,0:T(8,128)(2,1)S(1)} %slice.46), channel_id=1, source_target_pairs={{0,2},{1,3},{2,0},{3,1},{4,6},{5,7},{6,4},{7,5},{8,10},{9,11},{10,... | collective-permute-start | bytes 589832 | tf_op jit(solution)/shard_map/ppermute | solution.py:852
  171.5 25.9 %all-to-all-start.4 = ((bf16[8,240,384]{2,1,0:T(8,128)(2,1)}), bf16[8,240,384]{2,1,0:T(8,128)(2,1)S(1)}, u32[]{:S(2)}, u32[]{:S(2)}) async-start(bf16[8,240,384]{2,1,0:T(8,128)(2,1)} %get-tuple-element.148), calls=%async_computation.4 | async-start | bytes 2949120 | tf_op jit(solution)/shard_map/all_to_all | solution.py:1065
  175.5 28.2 %collective-permute-start.35 = (bf16[264,384]{1,0:T(8,128)(2,1)S(1)}, bf16[264,384]{1,0:T(8,128)(2,1)}, u32[]{:S(2)}, u32[]{:S(2)}) collective-permute-start(bf16[264,384]{1,0:T(8,128)(2,1)S(1)} %get-tuple-element.218), channel_id=1, source_target_pairs={{0,24},{8,16},{16,8},{24,0},{1,25},{9,17},{17,9},{25,1},{2,26},{10... | collective-permute-start | bytes 608264 | tf_op jit(solution)/shard_map/ppermute | solution.py:1049
  179.2 24.5 %collective-permute-start.34 = (bf16[264,384]{1,0:T(8,128)(2,1)S(1)}, bf16[264,384]{1,0:T(8,128)(2,1)}, u32[]{:S(2)}, u32[]{:S(2)}) collective-permute-start(bf16[264,384]{1,0:T(8,128)(2,1)S(1)} %get-tuple-element.219), channel_id=1, source_target_pairs={{0,16},{8,24},{16,0},{24,8},{1,17},{9,25},{17,1},{25,9},{2,18},{10... | collective-permute-start | bytes 608264 | tf_op jit(solution)/shard_map/ppermute | solution.py:1049
  179.2 24.5 %collective-permute-start.33 = (bf16[264,384]{1,0:T(8,128)(2,1)S(1)}, bf16[264,384]{1,0:T(8,128)(2,1)}, u32[]{:S(2)}, u32[]{:S(2)}) collective-permute-start(bf16[264,384]{1,0:T(8,128)(2,1)S(1)} %get-tuple-element.217), channel_id=1, source_target_pairs={{0,8},{8,0},{16,24},{24,16},{1,9},{9,1},{17,25},{25,17},{2,10},{10... | collective-permute-start | bytes 608264 | tf_op jit(solution)/shard_map/ppermute | solution.py:1049
  198.6 37.7 %all-to-all-start.5 = ((bf16[8,336,384]{2,1,0:T(8,128)(2,1)}), bf16[8,336,384]{2,1,0:T(8,128)(2,1)}, u32[]{:S(2)}, u32[]{:S(2)}) async-start(bf16[8,336,384]{2,1,0:T(8,128)(2,1)} %get-tuple-element.149), calls=%async_computation.5 | async-start | bytes 4128768 | tf_op jit(solution)/shard_map/all_to_all | solution.py:1086
  217.4 18.8 %collective-permute-start.32 = (bf16[192,384]{1,0:T(8,128)(2,1)S(1)}, bf16[192,384]{1,0:T(8,128)(2,1)S(1)}, u32[]{:S(2)}, u32[]{:S(2)}) collective-permute-start(bf16[192,384]{1,0:T(8,128)(2,1)S(1)} %get-tuple-element.221), channel_id=1, source_target_pairs={{0,24},{8,16},{16,8},{24,0},{1,25},{9,17},{17,9},{25,1},{2,26},{10... | collective-permute-start | bytes 442376 | tf_op jit(solution)/shard_map/ppermute | solution.py:1049
  221.0 15.1 %collective-permute-start.31 = (bf16[192,384]{1,0:T(8,128)(2,1)S(1)}, bf16[192,384]{1,0:T(8,128)(2,1)S(1)}, u32[]{:S(2)}, u32[]{:S(2)}) collective-permute-start(bf16[192,384]{1,0:T(8,128)(2,1)S(1)} %get-tuple-element.222), channel_id=1, source_target_pairs={{0,16},{8,24},{16,0},{24,8},{1,17},{9,25},{17,1},{25,9},{2,18},{10... | collective-permute-start | bytes 442376 | tf_op jit(solution)/shard_map/ppermute | solution.py:1049
  221.0 15.1 %collective-permute-start.30 = (bf16[192,384]{1,0:T(8,128)(2,1)S(1)}, bf16[192,384]{1,0:T(8,128)(2,1)S(1)}, u32[]{:S(2)}, u32[]{:S(2)}) collective-permute-start(bf16[192,384]{1,0:T(8,128)(2,1)S(1)} %get-tuple-element.220), channel_id=1, source_target_pairs={{0,8},{8,0},{16,24},{24,16},{1,9},{9,1},{17,25},{25,17},{2,10},{10... | collective-permute-start | bytes 442376 | tf_op jit(solution)/shard_map/ppermute | solution.py:1049
  (56 other events, 508.8 us)

commit v4 on v3

--- a/solution.py
+++ b/solution.py
@@ -29,7 +29,9 @@
 CUR = FR * VW * VW
 KEYS_USED = CUR + MEM * FR * VH * VH
 KEYS = -(-KEYS_USED // 256) * 256
+BACK = 144
 LATE_COMP, LATE_SMALL, LATE_TABLE, LATE = 17, 33, 35, 40
+STEP = 4
 TABLE_ROWS = 2 * FR + 4 * GRID
 TAB = 8 * FR + 2 * GRID * HALF
 
@@ -59,7 +61,7 @@
     return pl.CostEstimate(flops=int(us * 1e9), bytes_accessed=0, transcendentals=0)
 
 
-def call(kernel, outs, args, scratch=(), smem=1, us=5, far=0):
+def call(kernel, outs, args, scratch=(), smem=1, us=5, far=0, away=()):
     specs = [pl.BlockSpec(memory_space=pltpu.SMEM)] * smem
     specs += [pl.BlockSpec(memory_space=pltpu.VMEM)] * (len(args) - smem - far)
     specs += [pl.BlockSpec(memory_space=pl.ANY)] * far
@@ -67,7 +69,11 @@
         kernel,
         out_shape=outs,
         in_specs=specs,
-        out_specs=jax.tree.map(lambda _: pl.BlockSpec(memory_space=pltpu.VMEM), outs),
+        out_specs=(
+            tuple(pl.BlockSpec(memory_space=pl.ANY if i in away else pltpu.VMEM) for i in range(len(outs)))
+            if isinstance(outs, tuple)
+            else pl.BlockSpec(memory_space=pltpu.VMEM)
+        ),
         scratch_shapes=list(scratch),
         compiler_params=pltpu.CompilerParams(vmem_limit_bytes=56 << 20),
         cost_estimate=cost(us),
@@ -215,27 +221,31 @@
     return copies
 
 
-def conv_kernel(dims, meta, w_ref, qkv_ref, bias_ref, *refs):
+def own_weights(meta, qkv_ref, out, sems):
+    width, hd = qkv_ref.shape[0] // 3, out.shape[1]
+    rows = [pl.ds(pl.multiple_of(p * width + meta[4] * hd, 32), hd) for p in range(3)]
+    return [pltpu.make_async_copy(qkv_ref.at[rows[p], :], out.at[p], sems.at[p]) for p in range(3)]
+
+
+def conv_kernel(dims, meta, w_ref, bias_ref, *refs):
     frames, rows, n_height, hd = dims
     half = rows // 2
-    blocks, (k_ref, v_ref, q_ref, gk, gv, gather, tiles, qrow, sems) = refs[:10], refs[10:]
-    copies = gather_blocks(dims[:3], meta, blocks, gather, sems)
+    blocks, qkv_ref, (k_ref, v_ref, q_ref, mk, mv, gk, gv, gather, tiles, qrow, wide, sems, more) = refs[:10], refs[10], refs[11:]
+    copies = own_weights(meta, qkv_ref, wide, more) + gather_blocks(dims[:3], meta, blocks, gather, sems)
     for copy in copies:
         copy.start()
-    side, member = meta[0], meta[4]
-    width = qkv_ref.shape[0] // 3
+    side = meta[0]
     channels = qkv_ref.shape[1]
     for grid in (gk, gv):
         fill_grid(grid)
     blank = jnp.zeros((LANE - hd, channels), bf)
-    own = [qkv_ref[pl.ds(pl.multiple_of(p * width + member * hd, 32), hd), :] for p in range(3)]
-    weight_q = jnp.concatenate([own[0], blank], axis=0)
-    weight_kv = jnp.concatenate([own[1], blank, own[2], blank], axis=0)
     index = lax.broadcasted_iota(jnp.int32, (VW * GRID, 1), 0)
     line = (index * 2731) >> 16
     inside = ((line < side) & (index - line * GRID < side)).astype(f32)
     for copy in copies:
         copy.wait()
+    weight_q = jnp.concatenate([wide[0], blank], axis=0)
+    weight_kv = jnp.concatenate([wide[1], blank, wide[2], blank], axis=0)
     piece = half * HALF
     for t in range(FR):
         query = pair_reduce(join_lines(nt(gather[t], weight_q), jnp.add), tiles.at[t % 2], jnp.add) * 0.25 + bias_ref[0:1, 0:LANE]
@@ -246,6 +256,9 @@
         gk[flat_row(t, 0) : flat_row(t, VW), :] = pair[:, 0:LANE]
         gv[flat_row(t, 0) : flat_row(t, VW), :] = pair[:, LANE:]
     q_ref[...] = qrow[...].astype(bf)
+    sent = [pltpu.make_async_copy(gk, mk, more.at[3]), pltpu.make_async_copy(gv, mv, more.at[4])]
+    for copy in sent:
+        copy.start()
     local = lax.broadcasted_iota(jnp.int32, (4 * VW, LANE), 0)
     lane = lax.broadcasted_iota(jnp.int32, (4 * VW, LANE), 1)
     line = (local * 3277) >> 16
@@ -271,6 +284,8 @@
         return carry
 
     lax.fori_loop(0, FR * VW // 4, step, 0)
+    for copy in sent:
+        copy.wait()
 
 
 def build_table(tab, t_ref, h_ref, w_ref):
@@ -284,7 +299,7 @@
             tab[at : at + VW, :] = ref[first : first + VW, :]
 
 
-def attend_kernel(dims, meta, kc_ref, vc_ref, q_ref, y_ref, t_ref, h_ref, w_ref, place_ref, k_ref, v_ref, qt_ref, o_ref, l_ref, j_ref, vt, tab):
+def attend_kernel(dims, meta, kc_ref, vc_ref, q_ref, y_ref, t_ref, h_ref, w_ref, place_ref, k_out, v_out, qt_ref, o_ref, l_ref, j_ref, vt, tab, k_ref, v_ref, sems):
     frames, rows, n_height, hd = dims
     half = rows // 2
     side, length = meta[0], meta[1]
@@ -323,6 +338,9 @@
     for i in range(KEYS // 256):
         cut = slice(i * 256, (i + 1) * 256)
         vt[:, cut] = v_ref[cut, :].T
+    sent = [pltpu.make_async_copy(k_ref, k_out, sems.at[0]), pltpu.make_async_copy(v_ref, v_out, sems.at[1])]
+    for copy in sent:
+        copy.start()
     pt = q_ref[...].astype(f32).T[0:hd]
     build_table(tab, t_ref, h_ref, w_ref)
     table = tab[...]
@@ -364,12 +382,15 @@
     o_ref[...] = total[0:hd] / norm
     l_ref[...] = top + jnp.log2(norm)
     j_ref[...] = pad_lanes((o_ref[...] + pt).T, LANE).astype(bf)
+    for copy in sent:
+        copy.wait()
 
 
 def turn_kernel(k_ref, kt_ref):
     for i in range(KEYS // 256):
         cut = slice(i * 256, (i + 1) * 256)
-        kt_ref[:, cut] = k_ref[cut, :].T
+        kt_ref[0:LANE, cut] = k_ref[cut, 0:LANE].T
+        kt_ref[LANE:BACK, cut] = k_ref[cut, LANE:].T[0 : BACK - LANE]
 
 
 def mlp_kernel(dims, j_ref, early_ref, wp_ref, ws_ref, bp_ref, bs_ref, g_ref, b_ref, w1_ref, b1_ref, w2_ref, b2_ref,
@@ -395,11 +416,14 @@
     hidden = nt(n2[...], w1_ref[...]) + b1_ref[here].reshape(1, block)
     gate = 0.5 * (1.0 + lax.erf(hidden * SQRT_HALF))
     act = (hidden * gate).astype(bf)
-    act_ref[0, 0:per_q, :] = act
+    each = act_ref.shape[2]
+    for n in range(act_ref.shape[0]):
+        act_ref[n, 0:per_q, :] = act[:, n * each : (n + 1) * each]
     acc[...] += nt(act, w2_ref[...])
     grad = nn(early_ref[:, 0:width], w2_ref[...])
     hgrad = (grad * (gate + hidden * jnp.exp(-0.5 * hidden * hidden) / ROOT_TWO_PI)).astype(bf)
-    act_ref[0, per_q:, :] = hgrad
+    for n in range(act_ref.shape[0]):
+        act_ref[n, per_q:, :] = hgrad[:, n * each : (n + 1) * each]
     gb1[:, here] = jnp.sum(hgrad.astype(f32), axis=0, keepdims=True)
     ngrad[...] += nn(hgrad, w1_ref[...])
 
@@ -433,15 +457,27 @@
             dj_ref[n] = jnp.concatenate([joined_grad[:, n * hd : (n + 1) * hd], side], axis=1).astype(bf)
 
 
-def attend_back_kernel(dims, k_ref, kt_ref, v_ref, qt_ref, q_ref, o_ref, l_ref, dj_ref, t_ref, h_ref, w_ref, place_ref,
+def attend_back_kernel(dims, qt_ref, q_ref, o_ref, l_ref, dj_ref, t_ref, h_ref, w_ref, place_ref, k_in, kt_in, v_in,
                        dk_ref, dv_ref, mem_ref, pq_ref, small_ref,
-                       dot_ref, dq, tab, dtab, dks, dvs, delta, tables):
+                       dot_ref, dq, tab, dtab, dks, dvs, delta, tables, k_ref, kt_ref, v_ref, sems):
     frames, rows, n_height, hd = dims
     half = rows // 2
     queries = q_ref.shape[0]
     scale = hd**-0.5
     factor = scale * LOG2E
     turned = dj_ref[...].astype(f32).T
+    half_keys = KEYS // 2
+
+    def brought(i):
+        cut = pl.ds(pl.multiple_of(i * half_keys, LANE), half_keys)
+        return [
+            pltpu.make_async_copy(k_in.at[cut, :], k_ref.at[cut, :], sems.at[0, i]),
+            pltpu.make_async_copy(v_in.at[cut, :], v_ref.at[cut, :], sems.at[1, i]),
+            pltpu.make_async_copy(kt_in.at[:, cut], kt_ref.at[:, cut], sems.at[2, i]),
+        ]
+
+    for copy in brought(0) + brought(1):
+        copy.start()
     per_q = queries // HEADS
     spare = jnp.zeros((per_q, LANE - hd), f32)
     for src in range(HEADS):
@@ -452,21 +488,25 @@
     dot_ref[hd:, :] = jnp.zeros((LANE - hd, queries), bf)
     delta[...] = jnp.sum(turned[0:hd] * o_ref[...], axis=0, keepdims=True)
     dq[...] = jnp.zeros(dq.shape, f32)
-    half_keys = KEYS // 2
-
     def chunk(i, carry):
         cut = pl.ds(pl.multiple_of(i * half_keys, LANE), half_keys)
+        for copy in brought(i):
+            copy.wait()
         shares = jnp.exp2(nn(k_ref[cut, :], qt_ref[...]) * factor - l_ref[...])
         slope = nn(v_ref[cut, :], dot_ref[...])
         score = (shares * (slope - delta[...])).astype(bf)
         dvs[cut, :] = nn(shares.astype(bf), dj_ref[...])
         dks[cut, :] = nn(score, q_ref[...]) * scale
-        dq[...] += nn(kt_ref[0 : dq.shape[0], cut], score)
+        dq[...] += nn(kt_ref[:, cut], score)
         return carry
 
     lax.fori_loop(0, 2, chunk, 0)
-    dk_ref[...] = dks[0:CUR, :]
-    dv_ref[...] = dvs[0:CUR, :]
+    sent = [
+        pltpu.make_async_copy(dks.at[0:CUR, :], dk_ref, sems.at[3, 0]),
+        pltpu.make_async_copy(dvs.at[0:CUR, :], dv_ref, sems.at[3, 1]),
+    ]
+    for copy in sent:
+        copy.start()
     each = frames * VH
     at = CUR
     for dst in range(HEADS):
@@ -509,17 +549,18 @@
         part = jnp.concatenate([tables[dst * share : (dst + 1) * share, :], jnp.zeros((16 - share, LANE), f32)], axis=0)
         high = part.astype(bf).astype(f32)
         mem_ref[dst, LANE:, :] = jnp.concatenate([high, part - high, jnp.zeros((16, LANE), f32)], axis=1).astype(bf)
-
-
-def conv_back_kernel(dims, meta, dk_ref, dv_ref, pq_ref, w_ref, g_ref, b_ref, qkv_ref, *refs):
+    for copy in sent:
+        copy.wait()
+
+
+def conv_back_kernel(dims, meta, dk_ref, dv_ref, pq_ref, w_ref, g_ref, b_ref, *refs):
     frames, rows, n_height, hd = dims
     half = rows // 2
-    blocks, (out_ref, stat_ref, pg, gk, gv, wide, gather, tall, sems) = refs[:10], refs[10:]
-    copies = gather_blocks(dims[:3], meta, blocks, gather, sems)
+    blocks, qkv_ref, (out_ref, stat_ref, pg, gk, gv, wide, gather, tall, own, sems, more) = refs[:10], refs[10], refs[11:]
+    copies = gather_blocks(dims[:3], meta, blocks, gather, sems) + own_weights(meta, qkv_ref, own, more)
     for copy in copies:
         copy.start()
-    side, member = meta[0], meta[4]
-    width = qkv_ref.shape[0] // 3
+    side = meta[0]
     channels = qkv_ref.shape[1]
     for grid in (gk, gv):
         fill_grid(grid)
@@ -595,9 +636,7 @@
     for n in range(HEADS):
         value = pack_rows(total[:, n * cols : (n + 1) * cols], tall.at[n % 2], HEADS)
         out_ref[n, cells + third :, :] = jnp.concatenate([value, jnp.zeros((rest - packed, channels), f32)], axis=0).astype(bf)
-    weight = jnp.concatenate(
-        [qkv_ref[pl.ds(pl.multiple_of(p * width + member * hd, 32), hd), :].astype(f32) for p in range(3)], axis=0
-    )
+    weight = jnp.concatenate([own[p].astype(f32) for p in range(3)], axis=0)
     shift = nn(jnp.broadcast_to(sums, (8, 3 * hd)), weight, precision=HI)[0:1]
     gain = jnp.sum(total * weight, axis=0, keepdims=True)
     gain = (gain - shift * row_of(b_ref, 0, channels)) / row_of(g_ref, 0, channels)
@@ -652,12 +691,18 @@
     short_ref[...] = pack_rows(both[:, LANE : LANE + cols], tall.at[1], channels // cols).astype(bf)
 
 
-def last_kernel(dims, x_ref, g_ref, w_ref, pg_ref, mx_ref, mg_ref, out_ref, full, tiles):
+def last_kernel(dims, x_ref, g_ref, mx_ref, mg_ref, w_in, pg_in, out_ref, full, tiles, w_ref, pg_ref, sems):
     frames, rows, width, hd = dims
     half = rows // 2
     cells = rows * VW * (frames // 2)
     third = frames * half * HALF // 3
     channels = x_ref.shape[1]
+    rows_in = pg_ref.shape[1]
+    copies = [pltpu.make_async_copy(w_in, w_ref, sems.at[HEADS])]
+    copies += [pltpu.make_async_copy(pg_in.at[n, 0:rows_in, :], pg_ref.at[n], sems.at[n]) for n in range(HEADS)]
+    for copy in copies:
+        copy.start()
+    copies[0].wait()
     tops = jnp.zeros((cells, channels), f32)
     lows = jnp.zeros((cells, channels), f32)
     queries = []
@@ -665,6 +710,7 @@
         weight = jnp.concatenate(
             [w_ref[width + n * hd : width + (n + 1) * hd, :], w_ref[2 * width + n * hd : 2 * width + (n + 1) * hd, :]], axis=0
         )
+        copies[1 + n].wait()
         packed = pg_ref[n]
         tops = tops + nn(packed[0:cells, 0 : 2 * hd], weight)
         lows = lows + nn(packed[0:cells, 2 * hd :], weight)
@@ -707,14 +753,29 @@
         out_ref[t * per : (t + 1) * per, :] = (back + pool).astype(bf)
 
 
-def conv_grad_kernel(hd, mk, mv, dk_ref, dv_ref, out_ref, acc):
+def conv_grad_kernel(hd, mk_in, mv_in, dk_in, dv_in, out_ref, acc, mk, mv, dks, dvs, sems):
+    groups = FR // 2
+    lead = GRID + 4 * PLANE
+
+    def brought(g, first):
+        if first:
+            cut = pl.ds(0, lead)
+        else:
+            cut = pl.ds(pl.multiple_of(lead + (g - 1) * 2 * PLANE, 8), 2 * PLANE)
+        rows = pl.ds(pl.multiple_of(g * (CUR // groups), 16), CUR // groups)
+        pairs = [(mk_in, mk, cut), (mv_in, mv, cut), (dk_in, dks, rows), (dv_in, dvs, rows)]
+        return [pltpu.make_async_copy(a.at[c, :], b.at[c, :], sems.at[i, g]) for i, (a, b, c) in enumerate(pairs)]
+
+    for g in range(groups):
+        for copy in brought(g, g == 0):
+            copy.start()
     acc[...] = jnp.zeros(acc.shape, f32)
     blank = jnp.zeros((GRID - VW, LANE), f32)
 
     def step(it, carry):
         t = it // (VW // 4)
         base = GRID + (1 + t) * PLANE + it % (VW // 4) * 4 * GRID
-        for m, ref, masked in ((0, dk_ref, mk), (1, dv_ref, mv)):
+        for m, ref, masked in ((0, dks, mk), (1, dvs, mv)):
             quad = ref[pl.ds(pl.multiple_of(it * (4 * VW), 16), 4 * VW), :]
             for h in range(4):
                 here = jnp.concatenate([quad[h * VW : (h + 1) * VW], blank], axis=0)
@@ -727,20 +788,40 @@
                             acc[m * 27 + (a * 3 + b) * 3 + c] += prod[0:8] + prod[8:16] + prod[16:24]
         return carry
 
-    lax.fori_loop(0, FR * VW // 4, step, 0)
+    def group(g, carry):
+        @pl.when(g == 0)
+        def _():
+            for copy in brought(0, True):
+                copy.wait()
+
+        @pl.when(g > 0)
+        def _():
+            for copy in brought(g, False):
+                copy.wait()
+
+        each = 2 * VW // 4
+        return lax.fori_loop(g * each, (g + 1) * each, step, carry)
+
+    lax.fori_loop(0, groups, group, 0)
     sums = [jnp.sum(acc[tap], axis=0, keepdims=True) for tap in range(54)] + [jnp.zeros((1, LANE), f32)] * 2
     sums = jnp.concatenate(sums, axis=0)
     out_ref[0:14, :] = jnp.concatenate([sums[14 * g : 14 * (g + 1), 0:hd] for g in range(4)], axis=1)
     out_ref[14:16, :] = jnp.zeros((2, 4 * hd), f32)
 
 
-def late_kernel(dims, mem_ref, p_ref, conv_ref, stat_ref, small_ref, late_ref, tiles, lines):
+def late_kernel(dims, conv_ref, stat_ref, small_ref, mem_in, p_in, late_ref, tiles, lines, mem_ref, p_ref, sems):
     frames, rows, width, hd = dims
     half = rows // 2
     channels = late_ref.shape[1]
+    first = pltpu.make_async_copy(p_in.at[:, 0 : p_ref.shape[1], :], p_ref, sems.at[2 * MEM])
+    copies = [pltpu.make_async_copy(mem_in.at[s, m], mem_ref.at[s, m], sems.at[m * MEM + s]) for m in range(2) for s in range(MEM)]
+    for copy in [first] + copies:
+        copy.start()
+    first.wait()
     for m in range(2):
         sums = [jnp.zeros((GRID, width), f32) for _ in range(2)]
         for s in range(MEM):
+            copies[m * MEM + s].wait()
             grads = jnp.concatenate(
                 [p_ref[n][0:LANE, (2 * s + m) * hd : (2 * s + m + 1) * hd] for n in range(HEADS)], axis=1
             ).astype(f32)
@@ -893,17 +974,21 @@
             shape((FLAT, LANE), f32),
             shape((FLAT, LANE), f32),
         ),
-        in_specs=[pl.BlockSpec(memory_space=pltpu.SMEM)] + [vmem] * 3 + [pl.BlockSpec(memory_space=pl.ANY)] * 10,
-        out_specs=(vmem,) * 5,
+        in_specs=[pl.BlockSpec(memory_space=pltpu.SMEM)] + [vmem] * 2 + [pl.BlockSpec(memory_space=pl.ANY)] * 11,
+        out_specs=(vmem,) * 3 + (pl.BlockSpec(memory_space=pl.ANY),) * 2,
         scratch_shapes=[
+            pltpu.VMEM((FLAT, LANE), f32),
+            pltpu.VMEM((FLAT, LANE), f32),
             pltpu.VMEM((FR, GRID * GRID, channels), bf),
             pltpu.VMEM((2, 1, GRID * HALF, LANE), f32),
             pltpu.VMEM((queries, LANE), f32),
+            pltpu.VMEM((3, hd, channels), bf),
             pltpu.SemaphoreType.DMA((HEADS * frames,)),
+            pltpu.SemaphoreType.DMA((5,)),
         ],
         compiler_params=pltpu.CompilerParams(vmem_limit_bytes=56 << 20),
         cost_estimate=cost(18),
-    )(meta, taps, w_qkv, bias, *blocks)
+    )(meta, taps, bias, *blocks, w_qkv)
     index = np.arange(queries)
     src, local = index // per_q, index % per_q
     place = np.zeros((8, queries), np.int32)
@@ -928,19 +1013,22 @@
         scratch=[
             pltpu.VMEM((LANE, KEYS), bf),
             pltpu.VMEM((TAB, hd), f32),
+            pltpu.VMEM((KEYS, 2 * LANE), bf),
+            pltpu.VMEM((KEYS, LANE), bf),
+            pltpu.SemaphoreType.DMA((2,)),
         ],
         us=16,
+        away=(0, 1),
     )
     joined_rows = lax.all_to_all(joined.reshape(HEADS, per_q, LANE), G, 0, 0, tiled=True)
-    kt_all = call(turn_kernel, shape((2 * LANE, KEYS), bf), (k_all,), smem=0, us=4)
-    joined_rows, kt_all, e6a, e6b, e3, e5 = lax.optimization_barrier((joined_rows, kt_all, e6a, e6b, e3, e5))
-    e7a, e7b = last(e6a, e6b)
+    kt_all = call(turn_kernel, shape((BACK, KEYS), bf), (k_all,), smem=0, us=4)
+    joined_rows, kt_all = lax.optimization_barrier((joined_rows, kt_all))
     block = mlp // HEADS
     whole = lambda *dims: pl.BlockSpec(dims, lambda i: (0,) * len(dims))
     keep_width = 2 * width
     output, keep, acthg, dj, max_grad = pl.pallas_call(
         functools.partial(mlp_kernel, (width, hd)),
-        grid=(HEADS,),
+        grid=(HEADS // STEP,),
         out_shape=(
             shape((frames, half, HALF, width), bf),
             shape((per_q, keep_width), bf),
@@ -957,15 +1045,15 @@
             whole(width),
             whole(width),
             whole(width),
-            pl.BlockSpec((block, width), lambda i: (i, 0)),
+            pl.BlockSpec((STEP * block, width), lambda i: (i, 0)),
             whole(mlp),
-            pl.BlockSpec((width, block), lambda i: (0, i)),
+            pl.BlockSpec((width, STEP * block), lambda i: (0, i)),
             whole(width),
         ],
         out_specs=(
             whole(frames, half, HALF, width),
             whole(per_q, keep_width),
-            pl.BlockSpec((1, 2 * per_q, block), lambda i: (i, 0, 0)),
+            pl.BlockSpec((STEP, 2 * per_q, block), lambda i: (i, 0, 0)),
             whole(HEADS, per_q, LANE),
             whole(per_q, channels),
         ),
@@ -981,8 +1069,10 @@
         cost_estimate=cost(14),
     )(joined_rows, early, w_proj, w_short, b_proj, b_short, norm2_gain, norm2_bias, w_fc1, b_fc1, w_fc2, b_fc2)
     dj_head = lax.all_to_all(dj, G, 0, 0, tiled=True).reshape(queries, LANE)
+    keep, e6a, e6b = lax.optimization_barrier((keep, e6a, e6b))
     k2, k4, k1 = near(keep)
-    acthg, dj_head, e7a, e7b = lax.optimization_barrier((acthg, dj_head, e7a, e7b))
+    e7a, e7b = last(e6a, e6b)
+    acthg, dj_head = lax.optimization_barrier((acthg, dj_head))
     ah_head = lax.all_to_all(acthg, G, 0, 0, tiled=True)
 
     dk, dv, dmem, pq, small2 = call(
@@ -994,7 +1084,7 @@
             shape((queries, LANE), f32),
             shape((width // (LANE - hd), LANE - hd), f32),
         ),
-        (k_all, kt_all, v_all, qt_all, q_all, o_all, l_all, dj_head, rel_t, rel_h, rel_w, place),
+        (qt_all, q_all, o_all, l_all, dj_head, rel_t, rel_h, rel_w, place, k_all, kt_all, v_all),
         scratch=[
             pltpu.VMEM((LANE, queries), bf),
             pltpu.VMEM((hd + 48, queries), f32),
@@ -1004,9 +1094,15 @@
             pltpu.VMEM((KEYS, LANE), f32),
             pltpu.VMEM((1, queries), f32),
             pltpu.VMEM((TABLE_ROWS, LANE), f32),
+            pltpu.VMEM((KEYS, 2 * LANE), bf),
+            pltpu.VMEM((BACK, KEYS), bf),
+            pltpu.VMEM((KEYS, LANE), bf),
+            pltpu.SemaphoreType.DMA((4, 2)),
         ],
         smem=0,
         us=25,
+        far=3,
+        away=(0, 1),
     )
     cols = channels // HEADS
     taken = dmem.shape[1]
@@ -1017,9 +1113,13 @@
         functools.partial(conv_grad_kernel, hd),
         shape((16, 4 * hd), f32),
         (mk, mv, dk, dv),
-        scratch=[pltpu.VMEM((54, 8, LANE), f32)],
+        scratch=[pltpu.VMEM((54, 8, LANE), f32)]
+        + [pltpu.VMEM((FLAT, LANE), f32)] * 2
+        + [pltpu.VMEM((CUR, LANE), f32)] * 2
+        + [pltpu.SemaphoreType.DMA((4, FR // 2))],
         smem=0,
         us=12,
+        far=4,
     )
     dmem, gconv = lax.optimization_barrier((dmem, gconv))
     outs = (
@@ -1050,25 +1150,27 @@
         first, second, third_, fourth = [v.astype(f32) for v in [sent[0]] + got]
         return (first + second) + (third_ + fourth)
 
-    def over_clips(parts, permute):
-        parts = [v.reshape(n_clip, v.shape[0] // n_clip, v.shape[1]) for v in parts]
-        ends = np.cumsum([0] + [v.shape[1] for v in parts])
-        value = jnp.concatenate(parts, axis=1) if len(parts) > 1 else parts[0]
-        if permute and n_clip == 4:
-            clip = lax.axis_index("clip")
-            total = over_four([lax.dynamic_index_in_dim(value, clip ^ k, 0, keepdims=False) for k in range(n_clip)])
-        else:
-            total = jnp.sum(lax.all_to_all(value, "clip", 0, 0, tiled=True).astype(f32), axis=0)
-        return [total[lo:hi] for lo, hi in zip(ends, ends[1:])]
+    clip = lax.axis_index("clip")
+
+    def send_four(block):
+        return [block(clip)] + [lax.ppermute(block(clip ^ k), "clip", [(i, i ^ k) for i in range(n_clip)]) for k in range(1, n_clip)]
+
+    def add(got):
+        return (got[0].astype(f32) + got[1].astype(f32)) + (got[2].astype(f32) + got[3].astype(f32))
 
     dk, fc1p = lax.optimization_barrier((dk, fc1p))
     first_back = lax.all_to_all(fc1p, G, 0, 0, tiled=True)
-    part_fc2, part_proj, part_short = over_clips([fc2p, projp, shortp], True)
+    own = [v.reshape(n_clip, v.shape[0] // n_clip, channels) for v in (fc2p, projp, shortp)]
+    if n_clip == 4:
+        together = jnp.concatenate(own, axis=1)
+        got2 = send_four(lambda c: lax.dynamic_index_in_dim(together, c, 0, keepdims=False))
+    else:
+        got2 = lax.all_to_all(jnp.concatenate(own, axis=1), "clip", 0, 0, tiled=True)
     sent = valid // 2 + third
     pgp, stats = pl.pallas_call(
         functools.partial(conv_back_kernel, hdims),
         out_shape=(shape((HEADS, sent + 48, 4 * hd), bf), shape((8, channels), f32)),
-        in_specs=[pl.BlockSpec(memory_space=pltpu.SMEM)] + [vmem] * 7 + [pl.BlockSpec(memory_space=pl.ANY)] * 10,
+        in_specs=[pl.BlockSpec(memory_space=pltpu.SMEM)] + [vmem] * 6 + [pl.BlockSpec(memory_space=pl.ANY)] * 11,
         out_specs=(vmem,) * 2,
         scratch_shapes=[
             pltpu.VMEM((FR * GRID * GRID, 3 * LANE), bf),
@@ -1077,21 +1179,36 @@
             pltpu.VMEM((2 * queries, LANE), f32),
             pltpu.VMEM((FR, GRID * GRID, channels), bf),
             pltpu.VMEM((2, 3 * hd, LANE), f32),
+            pltpu.VMEM((3, hd, channels), bf),
             pltpu.SemaphoreType.DMA((HEADS * frames,)),
+            pltpu.SemaphoreType.DMA((3,)),
         ],
         compiler_params=pltpu.CompilerParams(vmem_limit_bytes=56 << 20),
         cost_estimate=cost(18),
-    )(meta, dk, dv, pq, taps, norm1_gain, norm1_bias, w_qkv, *blocks)
-    pgp, first_back = lax.optimization_barrier((pgp, first_back))
+    )(meta, dk, dv, pq, taps, norm1_gain, norm1_bias, *blocks, w_qkv)
+    pgp, first_back, got2 = lax.optimization_barrier((pgp, first_back, got2))
     pg_rows = lax.all_to_all(pgp, G, 0, 0, tiled=True)
-    [part_fc1] = over_clips([first_back[:, taken:].reshape(-1, channels)], True)
+    if n_clip == 4:
+        each = HEADS // n_clip
+        got1 = send_four(
+            lambda c: lax.dynamic_slice(first_back, (c * each, taken, 0), (each, first_back.shape[1] - taken, channels))
+        )
+    else:
+        got1 = lax.all_to_all(first_back[:, taken:].reshape(n_clip, -1, channels), "clip", 0, 0, tiled=True)
     late = call(
         functools.partial(late_kernel, dims),
         shape((LATE, channels), bf),
-        (mem, first_back, gconv, stats, small2),
-        scratch=[pltpu.VMEM((4, width // LANE, GRID, LANE), f32), pltpu.VMEM((LATE, channels), f32)],
+        (gconv, stats, small2, mem, first_back),
+        scratch=[
+            pltpu.VMEM((4, width // LANE, GRID, LANE), f32),
+            pltpu.VMEM((LATE, channels), f32),
+            pltpu.VMEM(mem.shape, bf),
+            pltpu.VMEM((HEADS, taken, channels), bf),
+            pltpu.SemaphoreType.DMA((2 * MEM + 1,)),
+        ],
         smem=0,
         us=5,
+        far=2,
     )
     if n_clip == 4:
         late = over_four([late] * n_clip)
@@ -1111,18 +1228,32 @@
         smem=0,
         us=3,
     )
-    pg_rows, gb1, part_fc1 = lax.optimization_barrier((pg_rows, gb1, part_fc1))
+    pg_rows, gb1, got1 = lax.optimization_barrier((pg_rows, gb1, got1))
     qkv_rows = pg_rows[:, sent : sent + 3 * hd // HEADS]
     qkv_rows = qkv_rows.reshape(HEADS, 3, hd // HEADS, channels).transpose(1, 0, 2, 3).reshape(-1, channels)
-    [part_qkv] = over_clips([qkv_rows], False)
+    got = lax.all_to_all(qkv_rows.reshape(n_clip, -1, channels), "clip", 0, 0, tiled=True)
     input_grad = call(
         functools.partial(last_kernel, dims),
         shape((cells_all, channels), bf),
-        (x, norm1_gain, w_qkv, pg_rows, mx, max_grad),
-        scratch=[pltpu.VMEM((cells_all, channels), f32), pltpu.VMEM((width // LANE, rows * GRID, LANE), f32)],
+        (x, norm1_gain, mx, max_grad, w_qkv, pg_rows),
+        scratch=[
+            pltpu.VMEM((cells_all, channels), f32),
+            pltpu.VMEM((width // LANE, rows * GRID, LANE), f32),
+            pltpu.VMEM(w_qkv.shape, bf),
+            pltpu.VMEM((HEADS, sent, channels), bf),
+            pltpu.SemaphoreType.DMA((HEADS + 1,)),
+        ],
         smem=0,
         us=5,
+        far=2,
     )
+    if n_clip == 4:
+        part_fc1, part2 = add(got1), add(got2)
+    else:
+        part_fc1, part2 = (jnp.sum(v.astype(f32), axis=0) for v in (got1, got2))
+    part_qkv = jnp.sum(got.astype(f32), axis=0)
+    ends = np.cumsum([v.shape[1] for v in own])
+    part_fc2, part_proj, part_short = part2[: ends[0]], part2[ends[0] : ends[1]], part2[ends[1] :]
     return (
         output[None],
         input_grad.reshape(clip_input.shape),

time: 257 us -> 248 us (0.965)
  waiting for transfers between devices: 26.3 us -> 19.6 us
  Pallas kernels: 128 us -> 122 us
  local copies, waits for them, and re-layouts: 18.2 us -> 22.7 us
    ppermute x9 -> x3, starting transfers between devices: 13.3 us -> 4.47 us  [over_four(): lax.ppermute(sent[k], 'clip', [(i, i ^ k) for i in range(n_clip)])]
    ppermute x0 -> x6, starting transfers between devices: none -> 8.8 us  [send_four(): lax.ppermute(block(clip ^ k), 'clip', [(i, i ^ k) for i in range(n_clip)])]
    ppermute x21, waiting for transfers between devices: 7.03 us -> 3.37 us  [swap(): lax.ppermute(value, 'height', [(i, i ^ bit) for i in range(n_height)])]
    pallas_call x11, Pallas kernels: 92.1 us -> 88.6 us  [the longest x10 77.1 us: call(): pl.pallas_call(kernel, out_shape=outs, in_specs=specs, out_specs=tuple((p...]
    unnamed x82 -> x94, local copies, waits for them, and re-layouts: 12.4 us -> 15.3 us
  transfers between devices with their start and end apart: 43 -> 43, of which waited for: 11 -> 6; matrix products, arithmetic and copies ran while one was open for 4% -> 6% of each run, Pallas kernels for 41% -> 40%
where the time goes in v4:
time: 248 us; the launch traced here: 244 us
  Pallas kernels  122 us (49%)
  starting transfers between devices  61.7 us (25%)
  local copies, waits for them, and re-layouts  22.7 us (9%)
  waiting for transfers between devices  19.6 us (8%)
  blocking collectives  11.8 us (5%)
  between operations  3.03 us (1%)
  other arithmetic  2.76 us (1%)
    pallas_call x10, Pallas kernels, call(): pl.pallas_call(kernel, out_shape=outs, in_specs=specs, out_specs=tuple((p...  77.1 us
    pallas_call x1, Pallas kernels, body(): pl.pallas_call(functools.partial(conv_back_kernel, hdims), out_shape=(sha...  16.9 us
    pallas_call x1, Pallas kernels, body(): pl.pallas_call(functools.partial(conv_kernel, hdims), out_shape=(shape((C...  16.7 us
    unnamed x94, local copies, waits for them, and re-layouts  15.3 us
    ppermute x21, starting transfers between devices, swap(): lax.ppermute(value, 'height', [(i, i ^ bit) for i in range(n_height)])  11.9 us
    all_gather x1, blocking collectives, body(): late_full = lax.all_gather(late, G, axis=0)  11.8 us
    pallas_call x1, Pallas kernels, body(): pl.pallas_call(functools.partial(mlp_kernel, (width, hd)), grid=(HEADS //...  11.5 us
    all_to_all x1, waiting for transfers between devices, body(): dj_head = lax.all_to_all(dj, G, 0, 0, tiled=True).reshape(queries, LANE)  9.91 us
  transfers between devices with their start and end apart: 43, of which 6 were waited for; matrix products, arithmetic and copies ran while one was open for 6% of the time, Pallas kernels for 40%

profile of v4, /device:TPU:0, one launch (start us, length us, event | category | flops | bytes accessed | tf_op | source)
XLA Modules:
  0.0 243.6 jit_solution(6350512688559066237)
XLA Ops:
  2.9 2.9 %collective-permute-start = (bf16[576,384]{1,0:T(8,128)(2,1)}, bf16[576,384]{1,0:T(8,128)(2,1)S(1)}, u32[]{:S(2)}, u32[]{:S(2)}) collective-permute-start(bf16[576,384]{1,0:T(8,128)(2,1)} %get-tuple-element.102.refs_0_), channel_id=1, source_target_pairs={{0,2},{1,3},{2,0},{3,1},{4,6},{5,7},{6,4},{7,5},{8,10},{9,11},{10,... | collective-permute-start | bytes 1327112 | tf_op jit(solution)/shard_map/ppermute | solution.py:933
  9.6 4.6 %shard_map.401 = (bf16[8,128,384]{2,1,0:T(8,128)(2,1)}, bf16[144,1152]{1,0:T(8,128)(2,1)}) custom-call(bf16[2,2,4,6,24,768]{5,4,3,2,1,0:T(8,128)(2,1)} %bitcast.50, f32[2,2,2,768]{3,2,1,0:T(2,128)} %c_ref.1, bf16[4,3,12,768]{3,2,1,0:T(8,128)(2,1)} %bitcast.46, f32[144,384]{1,0:T(8,128)} %get-tuple-element.103.mx_ref), custom_call_target="tpu_custom_call" | custom-call | flops 5000000000 | tf_op jit(solution)/shard_map/pallas_call | solution.py:68
  21.7 4.2 %collective-permute-done.2.refs_3_ = bf16[288,384]{1,0:T(8,128)(2,1)} collective-permute-done((bf16[288,384]{1,0:T(8,128)(2,1)S(1)}, bf16[288,384]{1,0:T(8,128)(2,1)}, u32[]{:S(2)}, u32[]{:S(2)}) %collective-permute-start.2) | collective-permute-done | bytes 221216 | tf_op jit(solution)/shard_map/ppermute | solution.py:932
  27.8 3.7 %all-to-all-start = ((bf16[8,128,384]{2,1,0:T(8,128)(2,1)}), bf16[8,128,384]{2,1,0:T(8,128)(2,1)S(1)}, u32[]{:S(2)}, u32[]{:S(2)}) async-start(bf16[8,128,384]{2,1,0:T(8,128)(2,1)} %get-tuple-element.114), calls=%async_computation | async-start | bytes 1572864 | tf_op jit(solution)/shard_map/all_to_all | solution.py:956
  36.0 16.7 %shard_map.402 = (bf16[3200,256]{1,0:T(8,128)(2,1)}, bf16[3200,128]{1,0:T(8,128)(2,1)}, bf16[1152,128]{1,0:T(8,128)(2,1)}, f32[5064,128]{1,0:T(8,128)}, f32[5064,128]{1,0:T(8,128)}) custom-call(s32[5]{0:T(128)} %stack.16.meta, f32[32,256]{1,0:T(8,128)} %pad_maximum_fusion.1.w_ref, f32[1,384]{1,0:T(1,128)} %bitcast.49, ...), custom_call_target="tpu_custom_call" | custom-call | flops 17999998976 | tf_op jit(solution)/shard_map/pallas_call | solution.py:968
  54.3 12.3 %shard_map.403 = (bf16[4864,256]{1,0:T(8,128)(2,1)}, bf16[4864,128]{1,0:T(8,128)(2,1)}, bf16[256,1152]{1,0:T(8,128)(2,1)}, f32[96,1152]{1,0:T(8,128)}, f32[1,1152]{1,0:T(1,128)}, /*index=5*/bf16[1152,128]{1,0:T(8,128)(2,1)}) custom-call(s32[5]{0:T(128)} %stack.16.meta, bf16[3200,256]{1,0:T(8,128)(2,1)} %get-tuple-element.111.kc_ref, ...), custom_call_target="tpu_custom_call" | custom-call | flops 16000000000 | tf_op jit(solution)/shard_map/pallas_call | solution.py:68
  66.6 3.8 %all-to-all-start.1 = ((bf16[8,144,128]{2,1,0:T(8,128)(2,1)}), bf16[8,144,128]{2,1,0:T(8,128)(2,1)S(1)}, u32[]{:S(2)}, u32[]{:S(2)}) async-start(bf16[8,144,128]{2,1,0:T(8,128)(2,1)} %bitcast.43), calls=%async_computation.1 | async-start | bytes 589824 | tf_op jit(solution)/shard_map/all_to_all | solution.py:1023
  75.9 3.5 %shard_map.404.kt_in = bf16[144,4864]{1,0:T(8,128)(2,1)} custom-call(bf16[4864,256]{1,0:T(8,128)(2,1)} %get-tuple-element.116.k_ref.k_in), custom_call_target="tpu_custom_call" | custom-call | flops 4000000000 | tf_op jit(solution)/shard_map/pallas_call | solution.py:68
  80.2 11.5 %shard_map.405 = (bf16[4,3,12,768]{3,2,1,0:T(8,128)(2,1)}, bf16[144,1536]{1,0:T(8,128)(2,1)}, bf16[8,288,384]{2,1,0:T(8,128)(2,1)}, bf16[8,144,128]{2,1,0:T(8,128)(2,1)}, f32[144,384]{1,0:T(8,128)}) custom-call(bf16[8,144,128]{2,1,0:T(8,128)(2,1)} %copy-done.9, bf16[144,1152]{1,0:T(8,128)(2,1)} %get-tuple-element.110.early_ref.refs_0_, ...), custom_call_target="tpu_custom_call" | custom-call | flops 14000000000 | tf_op jit(solution)/shard_map/pallas_call | solution.py:1029
  92.4 4.3 %all-to-all-start.2 = ((bf16[8,144,128]{2,1,0:T(8,128)(2,1)}), bf16[8,144,128]{2,1,0:T(8,128)(2,1)S(1)}, u32[]{:S(2)}, u32[]{:S(2)}) async-start(bf16[8,144,128]{2,1,0:T(8,128)(2,1)} %get-tuple-element.124), calls=%async_computation.2 | async-start | bytes 589824 | tf_op jit(solution)/shard_map/all_to_all | solution.py:1071
  97.1 9.9 %all-to-all-done.2 = bf16[8,144,128]{2,1,0:T(8,128)(2,1)S(1)} async-done(((bf16[8,144,128]{2,1,0:T(8,128)(2,1)}), bf16[8,144,128]{2,1,0:T(8,128)(2,1)S(1)}, u32[]{:S(2)}, u32[]{:S(2)}) %all-to-all-start.2) | async-done | bytes 294944 | tf_op jit(solution)/shard_map/all_to_all | solution.py:1071
  107.8 3.6 %all-to-all-start.3 = ((bf16[8,288,384]{2,1,0:T(8,128)(2,1)}), bf16[8,288,384]{2,1,0:T(8,128)(2,1)S(1)}, u32[]{:S(2)}, u32[]{:S(2)}) async-start(bf16[8,288,384]{2,1,0:T(8,128)(2,1)} %get-tuple-element.129), calls=%async_computation.3 | async-start | bytes 3538944 | tf_op jit(solution)/shard_map/all_to_all | solution.py:1076
  115.3 21.8 %shard_map.406 = (f32[3200,128]{1,0:T(8,128)}, f32[3200,128]{1,0:T(8,128)}, bf16[8,144,384]{2,1,0:T(8,128)(2,1)}, f32[1152,128]{1,0:T(8,128)}, f32[24,32]{1,0:T(8,128)}) custom-call(bf16[256,1152]{1,0:T(8,128)(2,1)} %get-tuple-element.120.qt_ref, bf16[1152,128]{1,0:T(8,128)(2,1)} %get-tuple-element.113.q_ref, f32[96,1152]{1,0:T(8,128)} %get-tuple-element.121.o_ref, ...), custom_call_target="tpu_custom_call" | custom-call | flops 24999999488 | tf_op jit(solution)/shard_map/pallas_call | solution.py:68
  138.8 10.9 %shard_map.407.conv_ref = f32[16,384]{1,0:T(8,128)} custom-call(f32[5064,128]{1,0:T(8,128)} %get-tuple-element.136.mk_in, f32[5064,128]{1,0:T(8,128)} %get-tuple-element.137.mv_in, f32[3200,128]{1,0:T(8,128)} %get-tuple-element.147.dk_in.dk_ref, f32[3200,128]{1,0:T(8,128)} %get-tuple-element.138.dv_in.dv_ref), custom_call_target="tpu_custom_call" | custom-call | flops 12000000000 | tf_op jit(solution)/shard_map/pallas_call | solution.py:68
  152.4 9.0 %shard_map.408 = (bf16[768,384]{1,0:T(8,128)(2,1)}, bf16[8,240,384]{2,1,0:T(8,128)(2,1)}, bf16[192,384]{1,0:T(8,128)(2,1)}, bf16[96,384]{1,0:T(8,128)(2,1)}) custom-call(s32[5]{0:T(128)} %stack.16.meta, bf16[8,288,384]{2,1,0:T(8,128)(2,1)} %copy-done.4, bf16[1152,128]{1,0:T(8,128)(2,1)} %get-tuple-element.115.j_ref, ...), custom_call_target="tpu_custom_call" | custom-call | flops 8999999488 | tf_op jit(solution)/shard_map/pallas_call | solution.py:68
  161.4 3.7 %all-to-all-start.4 = ((bf16[8,240,384]{2,1,0:T(8,128)(2,1)}), bf16[8,240,384]{2,1,0:T(8,128)(2,1)S(1)}, u32[]{:S(2)}, u32[]{:S(2)}) async-start(bf16[8,240,384]{2,1,0:T(8,128)(2,1)} %get-tuple-element.150), calls=%async_computation.4 | async-start | bytes 2949120 | tf_op jit(solution)/shard_map/all_to_all | solution.py:1162
  170.4 16.9 %shard_map.409 = (bf16[8,336,384]{2,1,0:T(8,128)(2,1)}, f32[8,384]{1,0:T(8,128)}) custom-call(s32[5]{0:T(128)} %stack.16.meta, f32[3200,128]{1,0:T(8,128)} %get-tuple-element.147.dk_in.dk_ref, f32[3200,128]{1,0:T(8,128)} %get-tuple-element.138.dv_in.dv_ref, f32[1152,128]{1,0:T(8,128)} %get-tuple-element.148.pq_ref, f32[32,256]{1,0:T(8,128)} %pad_maximum_fusion.1.w_ref, ...), custom_call_target="tpu_custom_call" | custom-call | flops 17999998976 | tf_op jit(solution)/shard_map/pallas_call | solution.py:1170
  189.9 4.1 %all-to-all-start.5 = ((bf16[8,336,384]{2,1,0:T(8,128)(2,1)}), bf16[8,336,384]{2,1,0:T(8,128)(2,1)S(1)}, u32[]{:S(2)}, u32[]{:S(2)}) async-start(bf16[8,336,384]{2,1,0:T(8,128)(2,1)} %get-tuple-element.154), calls=%async_computation.5 | async-start | bytes 4128768 | tf_op jit(solution)/shard_map/all_to_all | solution.py:1190
  195.7 4.4 %shard_map.410 = bf16[40,384]{1,0:T(8,128)(2,1)} custom-call(f32[16,384]{1,0:T(8,128)} %shard_map.407.conv_ref, f32[8,384]{1,0:T(8,128)} %get-tuple-element.156.stat_ref, f32[24,32]{1,0:T(8,128)} %get-tuple-element.157.small_ref, bf16[2,2,4,6,24,768]{5,4,3,2,1,0:T(8,128)(2,1)} %bitcast.51, bf16[8,240,384]{2,1,0:T(8,128)(2,1)} %copy-done.2), custom_call_target="tpu_custom_call" | custom-call | flops 5000000000 | tf_op jit(solution)/shard_map/pallas_call | solution.py:68
  200.1 3.7 %collective-permute-start.32 = (bf16[40,384]{1,0:T(8,128)(2,1)}, bf16[40,384]{1,0:T(8,128)(2,1)S(1)}, u32[]{:S(2)}, u32[]{:S(2)}) collective-permute-start(bf16[40,384]{1,0:T(8,128)(2,1)} %shard_map.410), channel_id=1, source_target_pairs={{0,24},{8,16},{16,8},{24,0},{1,25},{9,17},{17,9},{25,1},{2,26},{10... | collective-permute-start | bytes 92168 | tf_op jit(solution)/shard_map/ppermute | solution.py:1149
  208.9 2.9 %collective-permute-start.34 = (bf16[2,96,384]{2,1,0:T(8,128)(2,1)S(1)}, bf16[2,96,384]{2,1,0:T(8,128)(2,1)S(1)}, u32[]{:S(2)}, u32[]{:S(2)}) collective-permute-start(bf16[2,96,384]{2,1,0:T(8,128)(2,1)S(1)} %get-tuple-element.226), channel_id=1, source_target_pairs={{0,16},{8,24},{16,0},{24,8},{1,17},{9,25},{17,1},{25,9},{2,18},{10... | collective-permute-start | bytes 442376 | tf_op jit(solution)/shard_map/ppermute | solution.py:1156
  213.6 11.8 %all-gather = f32[320,384]{1,0:T(8,128)} all-gather(f32[40,384]{1,0:T(8,128)S(1)} %add_add_fusion.2), channel_id=2, replica_groups=mesh['clip'=4,'tm'=2,'height'=4] {'tm','height'}, dimensions={0}, use_global_device_ids=true | all-gather | bytes 552960 | tf_op jit(solution)/shard_map/all_gather | solution.py:1217
  228.9 4.9 %all-to-all-start.6 = ((bf16[4,72,384]{2,1,0:T(8,128)(2,1)}), bf16[4,72,384]{2,1,0:T(8,128)(2,1)S(1)}, u32[]{:S(2)}, u32[]{:S(2)}) async-start(bf16[4,72,384]{2,1,0:T(8,128)(2,1)} %reshape_reshape.3), calls=%async_computation.6 | async-start | bytes 442368 | tf_op jit(solution)/shard_map/all_to_all | solution.py:1234
  235.8 6.6 %shard_map.412 = bf16[576,384]{1,0:T(8,128)(2,1)} custom-call(bf16[576,384]{1,0:T(8,128)(2,1)} %bitcast.53, f32[384]{0:T(512)} %g_ref.7, f32[144,384]{1,0:T(8,128)} %get-tuple-element.103.mx_ref, f32[144,384]{1,0:T(8,128)} %get-tuple-element.119.mg_ref, bf16[2304,384]{1,0:T(8,128)(2,1)} %w_in.1, bf16[8,336,384]{2,1,0:T(8,128)(2,1)} %copy-done.3), custom_call_target="tpu_custom_call" | custom-call | flops 5000000000 | tf_op jit(solution)/shard_map/pallas_call | solution.py:68
  (200 shorter events, 59.0 us)
Async XLA Ops:
  7.4 26.2 %collective-permute-start.4 = (bf16[576,384]{1,0:T(8,128)(2,1)}, bf16[576,384]{1,0:T(8,128)(2,1)S(1)}, u32[]{:S(2)}, u32[]{:S(2)}) collective-permute-start(bf16[576,384]{1,0:T(8,128)(2,1)} %get-tuple-element.102.refs_0_), channel_id=1, source_target_pairs={{0,1},{1,0},{2,3},{3,2},{4,5},{5,4},{6,7},{7,6},{8,9},{9,8},{10,11... | collective-permute-start | bytes 1327112 | tf_op jit(solution)/shard_map/ppermute | solution.py:933
  17.7 17.3 %collective-permute-start.5 = (bf16[576,384]{1,0:T(8,128)(2,1)S(1)}, bf16[576,384]{1,0:T(8,128)(2,1)S(1)}, u32[]{:S(2)}, u32[]{:S(2)}) collective-permute-start(bf16[576,384]{1,0:T(8,128)(2,1)S(1)} %collective-permute-done.refs_1_), channel_id=1, source_target_pairs={{0,1},{1,0},{2,3},{3,2},{4,5},{5,4},{6,7},{7,6},{8,9},{9,8},{10,11... | collective-permute-start | bytes 1327112 | tf_op jit(solution)/shard_map/ppermute | solution.py:933
  27.8 25.6 %all-to-all-start = ((bf16[8,128,384]{2,1,0:T(8,128)(2,1)}), bf16[8,128,384]{2,1,0:T(8,128)(2,1)S(1)}, u32[]{:S(2)}, u32[]{:S(2)}) async-start(bf16[8,128,384]{2,1,0:T(8,128)(2,1)} %get-tuple-element.114), calls=%async_computation | async-start | bytes 1572864 | tf_op jit(solution)/shard_map/all_to_all | solution.py:956
  31.5 21.1 %collective-permute-start.9 = (bf16[144,1152]{1,0:T(8,128)(2,1)S(1)}, bf16[144,1152]{1,0:T(8,128)(2,1)}, u32[]{:S(2)}, u32[]{:S(2)}) collective-permute-start(bf16[144,1152]{1,0:T(8,128)(2,1)S(1)} %copy-done.34), channel_id=1, source_target_pairs={{0,2},{1,3},{2,0},{3,1},{4,6},{5,7},{6,4},{7,5},{8,10},{9,11},{10,... | collective-permute-start | bytes 995336 | tf_op jit(solution)/shard_map/ppermute | solution.py:933
  33.5 19.1 %collective-permute-start.10 = (bf16[144,1152]{1,0:T(8,128)(2,1)S(1)}, bf16[144,1152]{1,0:T(8,128)(2,1)}, u32[]{:S(2)}, u32[]{:S(2)}) collective-permute-start(bf16[144,1152]{1,0:T(8,128)(2,1)S(1)} %copy-done.34), channel_id=1, source_target_pairs={{0,4},{4,0},{1,5},{5,1},{2,6},{6,2},{3,7},{7,3},{8,12},{12,8},{9,1... | collective-permute-start | bytes 995336 | tf_op jit(solution)/shard_map/ppermute | solution.py:932
  35.0 17.6 %collective-permute-start.11 = (bf16[144,1152]{1,0:T(8,128)(2,1)S(1)}, bf16[144,1152]{1,0:T(8,128)(2,1)S(1)}, u32[]{:S(2)}, u32[]{:S(2)}) collective-permute-start(bf16[144,1152]{1,0:T(8,128)(2,1)S(1)} %copy-done.34), channel_id=1, source_target_pairs={{0,1},{1,0},{2,3},{3,2},{4,5},{5,4},{6,7},{7,6},{8,9},{9,8},{10,11... | collective-permute-start | bytes 995336 | tf_op jit(solution)/shard_map/ppermute | solution.py:933
  71.4 20.3 %collective-permute-start.12 = (bf16[80,1152]{1,0:T(8,128)(2,1)S(1)}, bf16[80,1152]{1,0:T(8,128)(2,1)S(1)}, u32[]{:S(2)}, u32[]{:S(2)}) collective-permute-start(bf16[80,1152]{1,0:T(8,128)(2,1)S(1)} %slice.40), channel_id=1, source_target_pairs={{0,4},{4,0},{1,5},{5,1},{2,6},{6,2},{3,7},{7,3},{8,12},{12,8},{9,1... | collective-permute-start | bytes 552968 | tf_op jit(solution)/shard_map/ppermute | solution.py:932
  74.4 17.3 %collective-permute-start.13 = (bf16[64,1152]{1,0:T(8,128)(2,1)S(1)}, bf16[64,1152]{1,0:T(8,128)(2,1)S(1)}, u32[]{:S(2)}, u32[]{:S(2)}) collective-permute-start(bf16[64,1152]{1,0:T(8,128)(2,1)S(1)} %slice.41), channel_id=1, source_target_pairs={{0,2},{1,3},{2,0},{3,1},{4,6},{5,7},{6,4},{7,5},{8,10},{9,11},{10,... | collective-permute-start | bytes 442376 | tf_op jit(solution)/shard_map/ppermute | solution.py:933
  91.7 19.7 %collective-permute-start.14 = (bf16[144,1536]{1,0:T(8,128)(2,1)}, bf16[144,1536]{1,0:T(8,128)(2,1)S(1)}, u32[]{:S(2)}, u32[]{:S(2)}) collective-permute-start(bf16[144,1536]{1,0:T(8,128)(2,1)} %get-tuple-element.135.refs_10_), channel_id=1, source_target_pairs={{0,2},{1,3},{2,0},{3,1},{4,6},{5,7},{6,4},{7,5},{8,10},{9,11},{10,... | collective-permute-start | bytes 1327112 | tf_op jit(solution)/shard_map/ppermute | solution.py:933
  92.3 19.6 %collective-permute-start.15 = (bf16[144,1536]{1,0:T(8,128)(2,1)}, bf16[144,1536]{1,0:T(8,128)(2,1)S(1)}, u32[]{:S(2)}, u32[]{:S(2)}) collective-permute-start(bf16[144,1536]{1,0:T(8,128)(2,1)} %get-tuple-element.135.refs_10_), channel_id=1, source_target_pairs={{0,4},{4,0},{1,5},{5,1},{2,6},{6,2},{3,7},{7,3},{8,12},{12,8},{9,1... | collective-permute-start | bytes 1327112 | tf_op jit(solution)/shard_map/ppermute | solution.py:932
  92.4 19.5 %collective-permute-start.16 = (bf16[144,1536]{1,0:T(8,128)(2,1)}, bf16[144,1536]{1,0:T(8,128)(2,1)S(1)}, u32[]{:S(2)}, u32[]{:S(2)}) collective-permute-start(bf16[144,1536]{1,0:T(8,128)(2,1)} %get-tuple-element.135.refs_10_), channel_id=1, source_target_pairs={{0,1},{1,0},{2,3},{3,2},{4,5},{5,4},{6,7},{7,6},{8,9},{9,8},{10,11... | collective-permute-start | bytes 1327112 | tf_op jit(solution)/shard_map/ppermute | solution.py:933
  96.6 40.4 %collective-permute-start.17 = (bf16[144,1152]{1,0:T(8,128)(2,1)}, bf16[144,1152]{1,0:T(8,128)(2,1)}, u32[]{:S(2)}, u32[]{:S(2)}) collective-permute-start(bf16[144,1152]{1,0:T(8,128)(2,1)} %collective-permute-done.9.refs_1_), channel_id=1, source_target_pairs={{0,1},{1,0},{2,3},{3,2},{4,5},{5,4},{6,7},{7,6},{8,9},{9,8},{10,11... | collective-permute-start | bytes 995336 | tf_op jit(solution)/shard_map/ppermute | solution.py:933
  97.1 40.0 %collective-permute-start.18 = (bf16[144,1152]{1,0:T(8,128)(2,1)}, bf16[144,1152]{1,0:T(8,128)(2,1)}, u32[]{:S(2)}, u32[]{:S(2)}) collective-permute-start(bf16[144,1152]{1,0:T(8,128)(2,1)} %collective-permute-done.10.refs_2_), channel_id=1, source_target_pairs={{0,1},{1,0},{2,3},{3,2},{4,5},{5,4},{6,7},{7,6},{8,9},{9,8},{10,11... | collective-permute-start | bytes 995336 | tf_op jit(solution)/shard_map/ppermute | solution.py:933
  107.8 43.4 %all-to-all-start.3 = ((bf16[8,288,384]{2,1,0:T(8,128)(2,1)}), bf16[8,288,384]{2,1,0:T(8,128)(2,1)S(1)}, u32[]{:S(2)}, u32[]{:S(2)}) async-start(bf16[8,288,384]{2,1,0:T(8,128)(2,1)} %get-tuple-element.129), calls=%async_computation.3 | async-start | bytes 3538944 | tf_op jit(solution)/shard_map/all_to_all | solution.py:1076
  111.4 26.3 %collective-permute-start.20 = (bf16[64,1152]{1,0:T(8,128)(2,1)S(1)}, bf16[64,1152]{1,0:T(8,128)(2,1)}, u32[]{:S(2)}, u32[]{:S(2)}) collective-permute-start(bf16[64,1152]{1,0:T(8,128)(2,1)S(1)} %collective-permute-done.13.refs_4_), channel_id=1, source_target_pairs={{0,1},{1,0},{2,3},{3,2},{4,5},{5,4},{6,7},{7,6},{8,9},{9,8},{10,11... | collective-permute-start | bytes 442376 | tf_op jit(solution)/shard_map/ppermute | solution.py:933
  111.9 26.8 %collective-permute-start.21 = (bf16[80,1536]{1,0:T(8,128)(2,1)S(1)}, bf16[80,1536]{1,0:T(8,128)(2,1)S(1)}, u32[]{:S(2)}, u32[]{:S(2)}) collective-permute-start(bf16[80,1536]{1,0:T(8,128)(2,1)S(1)} %slice.42), channel_id=1, source_target_pairs={{0,4},{4,0},{1,5},{5,1},{2,6},{6,2},{3,7},{7,3},{8,12},{12,8},{9,1... | collective-permute-start | bytes 737288 | tf_op jit(solution)/shard_map/ppermute | solution.py:932
  113.7 24.1 %collective-permute-start.22 = (bf16[64,1536]{1,0:T(8,128)(2,1)S(1)}, bf16[64,1536]{1,0:T(8,128)(2,1)S(1)}, u32[]{:S(2)}, u32[]{:S(2)}) collective-permute-start(bf16[64,1536]{1,0:T(8,128)(2,1)S(1)} %slice.43), channel_id=1, source_target_pairs={{0,2},{1,3},{2,0},{3,1},{4,6},{5,7},{6,4},{7,5},{8,10},{9,11},{10,... | collective-permute-start | bytes 589832 | tf_op jit(solution)/shard_map/ppermute | solution.py:933
  161.4 27.3 %all-to-all-start.4 = ((bf16[8,240,384]{2,1,0:T(8,128)(2,1)}), bf16[8,240,384]{2,1,0:T(8,128)(2,1)S(1)}, u32[]{:S(2)}, u32[]{:S(2)}) async-start(bf16[8,240,384]{2,1,0:T(8,128)(2,1)} %get-tuple-element.150), calls=%async_computation.4 | async-start | bytes 2949120 | tf_op jit(solution)/shard_map/all_to_all | solution.py:1162
  166.0 21.3 %collective-permute-start.27 = (bf16[264,384]{1,0:T(8,128)(2,1)S(1)}, bf16[264,384]{1,0:T(8,128)(2,1)S(1)}, u32[]{:S(2)}, u32[]{:S(2)}) collective-permute-start(bf16[264,384]{1,0:T(8,128)(2,1)S(1)} %get-tuple-element.231), channel_id=1, source_target_pairs={{0,8},{8,0},{16,24},{24,16},{1,9},{9,1},{17,25},{25,17},{2,10},{10... | collective-permute-start | bytes 608264 | tf_op jit(solution)/shard_map/ppermute | solution.py:1156
  167.6 19.7 %collective-permute-start.28 = (bf16[264,384]{1,0:T(8,128)(2,1)S(1)}, bf16[264,384]{1,0:T(8,128)(2,1)S(1)}, u32[]{:S(2)}, u32[]{:S(2)}) collective-permute-start(bf16[264,384]{1,0:T(8,128)(2,1)S(1)} %get-tuple-element.230), channel_id=1, source_target_pairs={{0,16},{8,24},{16,0},{24,8},{1,17},{9,25},{17,1},{25,9},{2,18},{10... | collective-permute-start | bytes 608264 | tf_op jit(solution)/shard_map/ppermute | solution.py:1156
  170.2 18.5 %collective-permute-start.29 = (bf16[264,384]{1,0:T(8,128)(2,1)S(1)}, bf16[264,384]{1,0:T(8,128)(2,1)}, u32[]{:S(2)}, u32[]{:S(2)}) collective-permute-start(bf16[264,384]{1,0:T(8,128)(2,1)S(1)} %get-tuple-element.229), channel_id=1, source_target_pairs={{0,24},{8,16},{16,8},{24,0},{1,25},{9,17},{17,9},{25,1},{2,26},{10... | collective-permute-start | bytes 608264 | tf_op jit(solution)/shard_map/ppermute | solution.py:1156
  189.9 37.4 %all-to-all-start.5 = ((bf16[8,336,384]{2,1,0:T(8,128)(2,1)}), bf16[8,336,384]{2,1,0:T(8,128)(2,1)S(1)}, u32[]{:S(2)}, u32[]{:S(2)}) async-start(bf16[8,336,384]{2,1,0:T(8,128)(2,1)} %get-tuple-element.154), calls=%async_computation.5 | async-start | bytes 4128768 | tf_op jit(solution)/shard_map/all_to_all | solution.py:1190
  207.6 19.6 %collective-permute-start.33 = (bf16[2,96,384]{2,1,0:T(8,128)(2,1)S(1)}, bf16[2,96,384]{2,1,0:T(8,128)(2,1)S(1)}, u32[]{:S(2)}, u32[]{:S(2)}) collective-permute-start(bf16[2,96,384]{2,1,0:T(8,128)(2,1)S(1)} %get-tuple-element.227), channel_id=1, source_target_pairs={{0,8},{8,0},{16,24},{24,16},{1,9},{9,1},{17,25},{25,17},{2,10},{10... | collective-permute-start | bytes 442376 | tf_op jit(solution)/shard_map/ppermute | solution.py:1156
  208.9 18.4 %collective-permute-start.34 = (bf16[2,96,384]{2,1,0:T(8,128)(2,1)S(1)}, bf16[2,96,384]{2,1,0:T(8,128)(2,1)S(1)}, u32[]{:S(2)}, u32[]{:S(2)}) collective-permute-start(bf16[2,96,384]{2,1,0:T(8,128)(2,1)S(1)} %get-tuple-element.226), channel_id=1, source_target_pairs={{0,16},{8,24},{16,0},{24,8},{1,17},{9,25},{17,1},{25,9},{2,18},{10... | collective-permute-start | bytes 442376 | tf_op jit(solution)/shard_map/ppermute | solution.py:1156
  (62 other events, 547.9 us)

commit v5 on v4

--- a/solution.py
+++ b/solution.py
@@ -854,6 +854,35 @@
     late_ref[...] = lines[...].astype(bf)
 
 
+def add_four(got, lo, hi):
+    a, b, c, d = [v[lo:hi, :].astype(f32) for v in got]
+    return (a + b) + (c + d)
+
+
+def unpack_rows(value, rows, lanes):
+    groups = value.shape[1] // lanes
+    for g in range(groups):
+        rows[pl.ds(g, value.shape[0], groups), :] = pad_lanes(value[:, g * lanes : (g + 1) * lanes], LANE)
+
+
+def second_kernel(dims, *refs):
+    hd, cols, channels = dims
+    got, (fc2_ref, proj_ref, short_ref, rows) = refs[0:4], refs[4:]
+    count = proj_ref.shape[0]
+    ends = np.cumsum([0, fc2_ref.shape[0], count * hd // channels, count * cols // channels])
+    fc2_ref[...] = add_four(got, ends[0], ends[1])
+    unpack_rows(add_four(got, ends[1], ends[2]), rows, hd)
+    proj_ref[...] = rows[0:count, 0:hd]
+    unpack_rows(add_four(got, ends[2], ends[3]), rows, cols)
+    short_ref[...] = rows[...].T[0:cols, 0:count]
+
+
+def first_kernel(hd, *refs):
+    got, (fc1_ref, rows) = refs[0:4], refs[4:]
+    unpack_rows(add_four(got, 0, got[0].shape[0]), rows, hd)
+    fc1_ref[...] = rows[...].T[0:hd]
+
+
 def sums_kernel(dims, late_ref, g1_ref, b1_ref, bqkv_ref, conv_ref, comp_ref, t_ref, h_ref, w_ref, bp_ref, bs_ref, g2_ref, b2_ref, bf1_ref, bf2_ref, lines):
     width, hd, channels = dims
     parts = []
@@ -894,6 +923,18 @@
     for ref, step in ((t_ref, 2 * FR), (h_ref, 2 * GRID), (w_ref, 2 * GRID)):
         ref[...] = lines[at : at + ref.shape[0], 0:hd]
         at += step
+
+
+def tail_kernel(dims, sums_dims, four, *refs):
+    ins, refs = refs[: 7 + four], refs[7 + four :]
+    x, gain, mx, mg, late = ins[0:5]
+    got, (w_in, pg_in) = ins[5 : 5 + four], ins[5 + four :]
+    outs, refs = refs[: 15 + four // 4], refs[15 + four // 4 :]
+    full, tiles, w_ref, pg_ref, sems, lines = refs[:6]
+    last_kernel(dims, x, gain, mx, mg, w_in, pg_in, outs[0], full, tiles, w_ref, pg_ref, sems)
+    sums_kernel(sums_dims, late, *outs[1:15], lines)
+    if four:
+        first_kernel(sums_dims[1], *got, outs[15], refs[6])
 
 
 def body(clip_input, memory, mem_len, res_id, norm1_gain, norm1_bias, w_qkv, b_qkv, conv_kv, compress, rel_t, rel_h, rel_w,
@@ -1021,8 +1062,8 @@
         away=(0, 1),
     )
     joined_rows = lax.all_to_all(joined.reshape(HEADS, per_q, LANE), G, 0, 0, tiled=True)
+    k_all, joined_rows = lax.optimization_barrier((k_all, joined_rows))
     kt_all = call(turn_kernel, shape((BACK, KEYS), bf), (k_all,), smem=0, us=4)
-    joined_rows, kt_all = lax.optimization_barrier((joined_rows, kt_all))
     block = mlp // HEADS
     whole = lambda *dims: pl.BlockSpec(dims, lambda i: (0,) * len(dims))
     keep_width = 2 * width
@@ -1072,7 +1113,8 @@
     keep, e6a, e6b = lax.optimization_barrier((keep, e6a, e6b))
     k2, k4, k1 = near(keep)
     e7a, e7b = last(e6a, e6b)
-    acthg, dj_head = lax.optimization_barrier((acthg, dj_head))
+    output = output.transpose(1, 2, 0, 3)
+    acthg, dj_head, kt_all, output = lax.optimization_barrier((acthg, dj_head, kt_all, output))
     ah_head = lax.all_to_all(acthg, G, 0, 0, tiled=True)
 
     dk, dv, dmem, pq, small2 = call(
@@ -1214,65 +1256,78 @@
         late = over_four([late] * n_clip)
     else:
         late = jnp.sum(lax.all_gather(late, "clip", axis=0).astype(f32), axis=0)
+    if n_clip == 4:
+        count = width // n_clip
+        part_fc2, part_proj, part_short = call(
+            functools.partial(second_kernel, (hd, cols, channels)),
+            (shape((count, block), f32), shape((count, hd), f32), shape((cols, count), f32)),
+            tuple(got2),
+            scratch=[pltpu.VMEM((-(-count // LANE) * LANE, LANE), f32)],
+            smem=0,
+            us=2,
+        )
+        late, part_fc2 = lax.optimization_barrier((late, part_fc2))
     late_full = lax.all_gather(late, G, axis=0)
+    pg_rows, late_full, got1 = lax.optimization_barrier((pg_rows, late_full, got1))
     vector = lambda n: shape((n,), f32)
-    g1, b1, gbq, gconv, gcomp, gt, gh, gw, gbp, gbs, g2, b2, gb1, gb2 = call(
-        functools.partial(sums_kernel, (width, hd, channels)),
+    qkv_rows = pg_rows[:, sent : sent + 3 * hd // HEADS]
+    qkv_rows = qkv_rows.reshape(HEADS, 3, hd // HEADS, channels).transpose(1, 0, 2, 3).reshape(-1, channels)
+    got = lax.all_to_all(qkv_rows.reshape(n_clip, -1, channels), "clip", 0, 0, tiled=True)
+    four = 4 if n_clip == 4 else 0
+    results = call(
+        functools.partial(tail_kernel, dims, (width, hd, channels), four),
         (
+            shape((cells_all, channels), bf),
             vector(channels), vector(channels), vector(3 * width), shape((3, 3, 3, 2, width), f32), shape(compress.shape, f32),
             shape(rel_t.shape, f32), shape(rel_h.shape, f32), shape(rel_w.shape, f32),
             vector(width), vector(width), vector(width), vector(width), vector(mlp), vector(width),
-        ),
-        (late_full,),
-        scratch=[pltpu.VMEM((TABLE_ROWS, LANE), f32)],
-        smem=0,
-        us=3,
-    )
-    pg_rows, gb1, got1 = lax.optimization_barrier((pg_rows, gb1, got1))
-    qkv_rows = pg_rows[:, sent : sent + 3 * hd // HEADS]
-    qkv_rows = qkv_rows.reshape(HEADS, 3, hd // HEADS, channels).transpose(1, 0, 2, 3).reshape(-1, channels)
-    got = lax.all_to_all(qkv_rows.reshape(n_clip, -1, channels), "clip", 0, 0, tiled=True)
-    input_grad = call(
-        functools.partial(last_kernel, dims),
-        shape((cells_all, channels), bf),
-        (x, norm1_gain, mx, max_grad, w_qkv, pg_rows),
+        )
+        + ((shape((hd, mlp // n_clip), f32),) if four else ()),
+        (x, norm1_gain, mx, max_grad, late_full)
+        + (tuple(v.reshape(-1, channels) for v in got1) if four else ())
+        + (w_qkv, pg_rows),
         scratch=[
             pltpu.VMEM((cells_all, channels), f32),
             pltpu.VMEM((width // LANE, rows * GRID, LANE), f32),
             pltpu.VMEM(w_qkv.shape, bf),
             pltpu.VMEM((HEADS, sent, channels), bf),
             pltpu.SemaphoreType.DMA((HEADS + 1,)),
-        ],
+            pltpu.VMEM((TABLE_ROWS, LANE), f32),
+        ]
+        + ([pltpu.VMEM((mlp // n_clip, LANE), f32)] if four else []),
         smem=0,
-        us=5,
+        us=9,
         far=2,
     )
+    input_grad, g1, b1, gbq, gconv, gcomp, gt, gh, gw, gbp, gbs, g2, b2, gb1, gb2 = results[:15]
+    part_qkv = jnp.sum(got.astype(f32), axis=0).reshape(-1, cols)
     if n_clip == 4:
-        part_fc1, part2 = add(got1), add(got2)
+        part_fc1 = results[15].T
+        part_short = part_short.T
     else:
         part_fc1, part2 = (jnp.sum(v.astype(f32), axis=0) for v in (got1, got2))
-    part_qkv = jnp.sum(got.astype(f32), axis=0)
-    ends = np.cumsum([v.shape[1] for v in own])
-    part_fc2, part_proj, part_short = part2[: ends[0]], part2[ends[0] : ends[1]], part2[ends[1] :]
+        ends = np.cumsum([v.shape[1] for v in own])
+        part_fc2, part_proj, part_short = part2[: ends[0]], part2[ends[0] : ends[1]], part2[ends[1] :]
+        part_fc1, part_proj, part_short = part_fc1.reshape(-1, hd), part_proj.reshape(-1, hd), part_short.reshape(-1, cols)
     return (
-        output[None],
+        output.transpose(2, 0, 1, 3)[None],
         input_grad.reshape(clip_input.shape),
         g1,
         b1,
-        part_qkv.reshape(-1, cols),
+        part_qkv,
         gbq,
         jnp.moveaxis(gconv, 3, 0),
         gcomp,
         gt,
         gh,
         gw,
-        part_proj.reshape(-1, hd),
+        part_proj,
         gbp,
-        part_short.reshape(-1, cols),
+        part_short,
         gbs,
         g2,
         b2,
-        part_fc1.reshape(-1, hd),
+        part_fc1,
         gb1,
         part_fc2,
         gb2,

time: 248 us -> 244 us (0.984)
  local copies, waits for them, and re-layouts: 22.7 us -> 19.6 us
    all_to_all x1, waiting for transfers between devices: 9.91 us -> 6.39 us  [body(): dj_head = lax.all_to_all(dj, G, 0, 0, tiled=True).reshape(queries, LANE)]
    unnamed x94 -> x82, local copies, waits for them, and re-layouts: 15.3 us -> 13.1 us
  transfers between devices with their start and end apart: 43 -> 43, of which waited for: 6 -> 8; matrix products, arithmetic and copies ran while one was open for 6% -> 4% of each run, Pallas kernels for 40% -> 42%
where the time goes in v5:
time: 244 us; the launch traced here: 240 us
  Pallas kernels  123 us (50%)
  starting transfers between devices  61.6 us (25%)
  local copies, waits for them, and re-layouts  19.6 us (8%)
  waiting for transfers between devices  19.2 us (8%)
  blocking collectives  12.4 us (5%)
  between operations  2.92 us (1%)
    pallas_call x10, Pallas kernels, call(): pl.pallas_call(kernel, out_shape=outs, in_specs=specs, out_specs=tuple((p...  78.3 us
    pallas_call x1, Pallas kernels, body(): pl.pallas_call(functools.partial(conv_back_kernel, hdims), out_shape=(sha...  16.9 us
    pallas_call x1, Pallas kernels, body(): pl.pallas_call(functools.partial(conv_kernel, hdims), out_shape=(shape((C...  16.7 us
    unnamed x82, local copies, waits for them, and re-layouts  13.1 us
    all_gather x1, blocking collectives, body(): late_full = lax.all_gather(late, G, axis=0)  12.4 us
    ppermute x21, starting transfers between devices, swap(): lax.ppermute(value, 'height', [(i, i ^ bit) for i in range(n_height)])  11.5 us
    pallas_call x1, Pallas kernels, body(): pl.pallas_call(functools.partial(mlp_kernel, (width, hd)), grid=(HEADS //...  11.5 us
    ppermute x6, starting transfers between devices, send_four(): lax.ppermute(block(clip ^ k), 'clip', [(i, i ^ k) for i in range(n_clip)])  8.8 us
  transfers between devices with their start and end apart: 43, of which 8 were waited for; matrix products, arithmetic and copies ran while one was open for 4% of the time, Pallas kernels for 42%

profile of v5, /device:TPU:0, one launch (start us, length us, event | category | flops | bytes accessed | tf_op | source)
XLA Modules:
  0.0 239.9 jit_solution(9445600144783712177)
XLA Ops:
  2.9 2.9 %collective-permute-start = (bf16[576,384]{1,0:T(8,128)(2,1)}, bf16[576,384]{1,0:T(8,128)(2,1)S(1)}, u32[]{:S(2)}, u32[]{:S(2)}) collective-permute-start(bf16[576,384]{1,0:T(8,128)(2,1)} %get-tuple-element.111.refs_0_), channel_id=1, source_target_pairs={{0,2},{1,3},{2,0},{3,1},{4,6},{5,7},{6,4},{7,5},{8,10},{9,11},{10,... | collective-permute-start | bytes 1327112 | tf_op jit(solution)/shard_map/ppermute | solution.py:974
  9.6 4.6 %shard_map.401 = (bf16[8,128,384]{2,1,0:T(8,128)(2,1)}, bf16[144,1152]{1,0:T(8,128)(2,1)}) custom-call(bf16[2,2,4,6,24,768]{5,4,3,2,1,0:T(8,128)(2,1)} %bitcast.60, f32[2,2,2,768]{3,2,1,0:T(2,128)} %c_ref.1, bf16[4,3,12,768]{3,2,1,0:T(8,128)(2,1)} %bitcast.55, f32[144,384]{1,0:T(8,128)} %get-tuple-element.112.mx_ref.refs_2_), custom_call_target="tpu_custom_call" | custom-call | flops 5000000000 | tf_op jit(solution)/shard_map/pallas_call | solution.py:68
  21.7 4.2 %collective-permute-done.2.refs_3_ = bf16[288,384]{1,0:T(8,128)(2,1)} collective-permute-done((bf16[288,384]{1,0:T(8,128)(2,1)S(1)}, bf16[288,384]{1,0:T(8,128)(2,1)}, u32[]{:S(2)}, u32[]{:S(2)}) %collective-permute-start.2) | collective-permute-done | bytes 221216 | tf_op jit(solution)/shard_map/ppermute | solution.py:973
  27.8 3.7 %all-to-all-start = ((bf16[8,128,384]{2,1,0:T(8,128)(2,1)}), bf16[8,128,384]{2,1,0:T(8,128)(2,1)S(1)}, u32[]{:S(2)}, u32[]{:S(2)}) async-start(bf16[8,128,384]{2,1,0:T(8,128)(2,1)} %get-tuple-element.123), calls=%async_computation | async-start | bytes 1572864 | tf_op jit(solution)/shard_map/all_to_all | solution.py:997
  36.0 16.7 %shard_map.402 = (bf16[3200,256]{1,0:T(8,128)(2,1)}, bf16[3200,128]{1,0:T(8,128)(2,1)}, bf16[1152,128]{1,0:T(8,128)(2,1)}, f32[5064,128]{1,0:T(8,128)}, f32[5064,128]{1,0:T(8,128)}) custom-call(s32[5]{0:T(128)} %stack.16.meta, f32[32,256]{1,0:T(8,128)} %pad_maximum_fusion.1.w_ref, f32[1,384]{1,0:T(1,128)} %bitcast.59, ...), custom_call_target="tpu_custom_call" | custom-call | flops 17999998976 | tf_op jit(solution)/shard_map/pallas_call | solution.py:1009
  54.3 12.3 %shard_map.403 = (bf16[4864,256]{1,0:T(8,128)(2,1)}, bf16[4864,128]{1,0:T(8,128)(2,1)}, bf16[256,1152]{1,0:T(8,128)(2,1)}, f32[96,1152]{1,0:T(8,128)}, f32[1,1152]{1,0:T(1,128)}, /*index=5*/bf16[1152,128]{1,0:T(8,128)(2,1)}) custom-call(s32[5]{0:T(128)} %stack.16.meta, bf16[3200,256]{1,0:T(8,128)(2,1)} %get-tuple-element.120.kc_ref, ...), custom_call_target="tpu_custom_call" | custom-call | flops 16000000000 | tf_op jit(solution)/shard_map/pallas_call | solution.py:68
  66.7 3.8 %all-to-all-start.1 = ((bf16[8,144,128]{2,1,0:T(8,128)(2,1)}), bf16[8,144,128]{2,1,0:T(8,128)(2,1)S(1)}, u32[]{:S(2)}, u32[]{:S(2)}) async-start(bf16[8,144,128]{2,1,0:T(8,128)(2,1)} %bitcast.52), calls=%async_computation.1 | async-start | bytes 589824 | tf_op jit(solution)/shard_map/all_to_all | solution.py:1064
  78.9 11.5 %shard_map.404 = (bf16[4,3,12,768]{3,2,1,0:T(8,128)(2,1)}, bf16[144,1536]{1,0:T(8,128)(2,1)}, bf16[8,288,384]{2,1,0:T(8,128)(2,1)}, bf16[8,144,128]{2,1,0:T(8,128)(2,1)}, f32[144,384]{1,0:T(8,128)}) custom-call(bf16[8,144,128]{2,1,0:T(8,128)(2,1)} %copy-done.8, bf16[144,1152]{1,0:T(8,128)(2,1)} %get-tuple-element.119.early_ref.refs_0_, ...), custom_call_target="tpu_custom_call" | custom-call | flops 14000000000 | tf_op jit(solution)/shard_map/pallas_call | solution.py:1070
  91.7 4.2 %all-to-all-start.2 = ((bf16[8,144,128]{2,1,0:T(8,128)(2,1)}), bf16[8,144,128]{2,1,0:T(8,128)(2,1)S(1)}, u32[]{:S(2)}, u32[]{:S(2)}) async-start(bf16[8,144,128]{2,1,0:T(8,128)(2,1)} %get-tuple-element.128), calls=%async_computation.2 | async-start | bytes 589824 | tf_op jit(solution)/shard_map/all_to_all | solution.py:1112
  95.9 3.5 %shard_map.405.kt_in = bf16[144,4864]{1,0:T(8,128)(2,1)} custom-call(bf16[4864,256]{1,0:T(8,128)(2,1)} %get-tuple-element.129.k_ref.k_in), custom_call_target="tpu_custom_call" | custom-call | flops 4000000000 | tf_op jit(solution)/shard_map/pallas_call | solution.py:68
  99.4 6.4 %all-to-all-done.2 = bf16[8,144,128]{2,1,0:T(8,128)(2,1)S(1)} async-done(((bf16[8,144,128]{2,1,0:T(8,128)(2,1)}), bf16[8,144,128]{2,1,0:T(8,128)(2,1)S(1)}, u32[]{:S(2)}, u32[]{:S(2)}) %all-to-all-start.2) | async-done | bytes 294944 | tf_op jit(solution)/shard_map/all_to_all | solution.py:1112
  106.5 3.6 %all-to-all-start.3 = ((bf16[8,288,384]{2,1,0:T(8,128)(2,1)}), bf16[8,288,384]{2,1,0:T(8,128)(2,1)S(1)}, u32[]{:S(2)}, u32[]{:S(2)}) async-start(bf16[8,288,384]{2,1,0:T(8,128)(2,1)} %get-tuple-element.140), calls=%async_computation.3 | async-start | bytes 3538944 | tf_op jit(solution)/shard_map/all_to_all | solution.py:1118
  114.0 21.8 %shard_map.406 = (f32[3200,128]{1,0:T(8,128)}, f32[3200,128]{1,0:T(8,128)}, bf16[8,144,384]{2,1,0:T(8,128)(2,1)}, f32[1152,128]{1,0:T(8,128)}, f32[24,32]{1,0:T(8,128)}) custom-call(bf16[256,1152]{1,0:T(8,128)(2,1)} %get-tuple-element.133.qt_ref, bf16[1152,128]{1,0:T(8,128)(2,1)} %get-tuple-element.122.q_ref, f32[96,1152]{1,0:T(8,128)} %get-tuple-element.134.o_ref, ...), custom_call_target="tpu_custom_call" | custom-call | flops 24999999488 | tf_op jit(solution)/shard_map/pallas_call | solution.py:68
  137.5 10.9 %shard_map.407.conv_ref = f32[16,384]{1,0:T(8,128)} custom-call(f32[5064,128]{1,0:T(8,128)} %get-tuple-element.147.mk_in, f32[5064,128]{1,0:T(8,128)} %get-tuple-element.148.mv_in, f32[3200,128]{1,0:T(8,128)} %get-tuple-element.158.dk_in.dk_ref, f32[3200,128]{1,0:T(8,128)} %get-tuple-element.149.dv_in.dv_ref), custom_call_target="tpu_custom_call" | custom-call | flops 12000000000 | tf_op jit(solution)/shard_map/pallas_call | solution.py:68
  151.1 9.0 %shard_map.408 = (bf16[768,384]{1,0:T(8,128)(2,1)}, bf16[8,240,384]{2,1,0:T(8,128)(2,1)}, bf16[192,384]{1,0:T(8,128)(2,1)}, bf16[96,384]{1,0:T(8,128)(2,1)}) custom-call(s32[5]{0:T(128)} %stack.16.meta, bf16[8,288,384]{2,1,0:T(8,128)(2,1)} %copy-done.4, bf16[1152,128]{1,0:T(8,128)(2,1)} %get-tuple-element.125.j_ref, ...), custom_call_target="tpu_custom_call" | custom-call | flops 8999999488 | tf_op jit(solution)/shard_map/pallas_call | solution.py:68
  160.1 3.7 %all-to-all-start.4 = ((bf16[8,240,384]{2,1,0:T(8,128)(2,1)}), bf16[8,240,384]{2,1,0:T(8,128)(2,1)S(1)}, u32[]{:S(2)}, u32[]{:S(2)}) async-start(bf16[8,240,384]{2,1,0:T(8,128)(2,1)} %get-tuple-element.161), calls=%async_computation.4 | async-start | bytes 2949120 | tf_op jit(solution)/shard_map/all_to_all | solution.py:1204
  169.2 16.9 %shard_map.409 = (bf16[8,336,384]{2,1,0:T(8,128)(2,1)}, f32[8,384]{1,0:T(8,128)}) custom-call(s32[5]{0:T(128)} %stack.16.meta, f32[3200,128]{1,0:T(8,128)} %get-tuple-element.158.dk_in.dk_ref, f32[3200,128]{1,0:T(8,128)} %get-tuple-element.149.dv_in.dv_ref, f32[1152,128]{1,0:T(8,128)} %get-tuple-element.159.pq_ref, f32[32,256]{1,0:T(8,128)} %pad_maximum_fusion.1.w_ref, ...), custom_call_target="tpu_custom_call" | custom-call | flops 17999998976 | tf_op jit(solution)/shard_map/pallas_call | solution.py:1212
  188.6 4.1 %all-to-all-start.5 = ((bf16[8,336,384]{2,1,0:T(8,128)(2,1)}), bf16[8,336,384]{2,1,0:T(8,128)(2,1)S(1)}, u32[]{:S(2)}, u32[]{:S(2)}) async-start(bf16[8,336,384]{2,1,0:T(8,128)(2,1)} %get-tuple-element.165), calls=%async_computation.5 | async-start | bytes 4128768 | tf_op jit(solution)/shard_map/all_to_all | solution.py:1232
  194.4 4.3 %shard_map.410 = bf16[40,384]{1,0:T(8,128)(2,1)} custom-call(f32[16,384]{1,0:T(8,128)} %shard_map.407.conv_ref, f32[8,384]{1,0:T(8,128)} %get-tuple-element.167.stat_ref, f32[24,32]{1,0:T(8,128)} %get-tuple-element.168.small_ref, bf16[2,2,4,6,24,768]{5,4,3,2,1,0:T(8,128)(2,1)} %bitcast.61, bf16[8,240,384]{2,1,0:T(8,128)(2,1)} %copy-done.2), custom_call_target="tpu_custom_call" | custom-call | flops 5000000000 | tf_op jit(solution)/shard_map/pallas_call | solution.py:68
  198.8 3.7 %collective-permute-start.32 = (bf16[40,384]{1,0:T(8,128)(2,1)}, bf16[40,384]{1,0:T(8,128)(2,1)S(1)}, u32[]{:S(2)}, u32[]{:S(2)}) collective-permute-start(bf16[40,384]{1,0:T(8,128)(2,1)} %shard_map.410), channel_id=1, source_target_pairs={{0,24},{8,16},{16,8},{24,0},{1,25},{9,17},{17,9},{25,1},{2,26},{10... | collective-permute-start | bytes 92168 | tf_op jit(solution)/shard_map/ppermute | solution.py:1191
  206.4 2.9 %collective-permute-start.34 = (bf16[2,96,384]{2,1,0:T(8,128)(2,1)S(1)}, bf16[2,96,384]{2,1,0:T(8,128)(2,1)S(1)}, u32[]{:S(2)}, u32[]{:S(2)}) collective-permute-start(bf16[2,96,384]{2,1,0:T(8,128)(2,1)S(1)} %get-tuple-element.244), channel_id=1, source_target_pairs={{0,16},{8,24},{16,0},{24,8},{1,17},{9,25},{17,1},{25,9},{2,18},{10... | collective-permute-start | bytes 442376 | tf_op jit(solution)/shard_map/ppermute | solution.py:1198
  211.7 12.4 %all-gather = f32[320,384]{1,0:T(8,128)} all-gather(f32[40,384]{1,0:T(8,128)S(1)} %add_add_fusion), channel_id=2, replica_groups=mesh['clip'=4,'tm'=2,'height'=4] {'tm','height'}, dimensions={0}, use_global_device_ids=true | all-gather | bytes 552960 | tf_op jit(solution)/shard_map/all_gather | solution.py:1270
  225.2 4.9 %all-to-all-start.6 = ((bf16[4,72,384]{2,1,0:T(8,128)(2,1)}), bf16[4,72,384]{2,1,0:T(8,128)(2,1)S(1)}, u32[]{:S(2)}, u32[]{:S(2)}) async-start(bf16[4,72,384]{2,1,0:T(8,128)(2,1)} %reshape_reshape.3), calls=%async_computation.6 | async-start | bytes 442368 | tf_op jit(solution)/shard_map/all_to_all | solution.py:1275
  230.2 7.6 %shard_map.412 = (bf16[576,384]{1,0:T(8,128)(2,1)}, f32[384]{0:T(512)}, f32[384]{0:T(512)}, f32[2304]{0:T(1024)}, f32[3,3,3,2,768]{4,3,2,1,0:T(2,128)}, /*index=...) custom-call(bf16[576,384]{1,0:T(8,128)(2,1)} %bitcast.63, ...), custom_call_target="tpu_custom_call" | custom-call | flops 8999999488 | tf_op jit(solution)/shard_map/pallas_call | solution.py:68
  (180 shorter events, 57.4 us)
Async XLA Ops:
  7.4 26.2 %collective-permute-start.4 = (bf16[576,384]{1,0:T(8,128)(2,1)}, bf16[576,384]{1,0:T(8,128)(2,1)S(1)}, u32[]{:S(2)}, u32[]{:S(2)}) collective-permute-start(bf16[576,384]{1,0:T(8,128)(2,1)} %get-tuple-element.111.refs_0_), channel_id=1, source_target_pairs={{0,1},{1,0},{2,3},{3,2},{4,5},{5,4},{6,7},{7,6},{8,9},{9,8},{10,11... | collective-permute-start | bytes 1327112 | tf_op jit(solution)/shard_map/ppermute | solution.py:974
  17.7 17.3 %collective-permute-start.5 = (bf16[576,384]{1,0:T(8,128)(2,1)S(1)}, bf16[576,384]{1,0:T(8,128)(2,1)S(1)}, u32[]{:S(2)}, u32[]{:S(2)}) collective-permute-start(bf16[576,384]{1,0:T(8,128)(2,1)S(1)} %collective-permute-done.refs_1_), channel_id=1, source_target_pairs={{0,1},{1,0},{2,3},{3,2},{4,5},{5,4},{6,7},{7,6},{8,9},{9,8},{10,11... | collective-permute-start | bytes 1327112 | tf_op jit(solution)/shard_map/ppermute | solution.py:974
  17.8 17.2 %collective-permute-start.6 = (bf16[576,384]{1,0:T(8,128)(2,1)S(1)}, bf16[576,384]{1,0:T(8,128)(2,1)S(1)}, u32[]{:S(2)}, u32[]{:S(2)}) collective-permute-start(bf16[576,384]{1,0:T(8,128)(2,1)S(1)} %collective-permute-done.1.refs_2_), channel_id=1, source_target_pairs={{0,1},{1,0},{2,3},{3,2},{4,5},{5,4},{6,7},{7,6},{8,9},{9,8},{10,11... | collective-permute-start | bytes 1327112 | tf_op jit(solution)/shard_map/ppermute | solution.py:974
  27.8 25.7 %all-to-all-start = ((bf16[8,128,384]{2,1,0:T(8,128)(2,1)}), bf16[8,128,384]{2,1,0:T(8,128)(2,1)S(1)}, u32[]{:S(2)}, u32[]{:S(2)}) async-start(bf16[8,128,384]{2,1,0:T(8,128)(2,1)} %get-tuple-element.123), calls=%async_computation | async-start | bytes 1572864 | tf_op jit(solution)/shard_map/all_to_all | solution.py:997
  31.5 21.1 %collective-permute-start.9 = (bf16[144,1152]{1,0:T(8,128)(2,1)S(1)}, bf16[144,1152]{1,0:T(8,128)(2,1)}, u32[]{:S(2)}, u32[]{:S(2)}) collective-permute-start(bf16[144,1152]{1,0:T(8,128)(2,1)S(1)} %copy-done.24), channel_id=1, source_target_pairs={{0,2},{1,3},{2,0},{3,1},{4,6},{5,7},{6,4},{7,5},{8,10},{9,11},{10,... | collective-permute-start | bytes 995336 | tf_op jit(solution)/shard_map/ppermute | solution.py:974
  33.5 19.1 %collective-permute-start.10 = (bf16[144,1152]{1,0:T(8,128)(2,1)S(1)}, bf16[144,1152]{1,0:T(8,128)(2,1)}, u32[]{:S(2)}, u32[]{:S(2)}) collective-permute-start(bf16[144,1152]{1,0:T(8,128)(2,1)S(1)} %copy-done.24), channel_id=1, source_target_pairs={{0,4},{4,0},{1,5},{5,1},{2,6},{6,2},{3,7},{7,3},{8,12},{12,8},{9,1... | collective-permute-start | bytes 995336 | tf_op jit(solution)/shard_map/ppermute | solution.py:973
  35.0 17.6 %collective-permute-start.11 = (bf16[144,1152]{1,0:T(8,128)(2,1)S(1)}, bf16[144,1152]{1,0:T(8,128)(2,1)S(1)}, u32[]{:S(2)}, u32[]{:S(2)}) collective-permute-start(bf16[144,1152]{1,0:T(8,128)(2,1)S(1)} %copy-done.24), channel_id=1, source_target_pairs={{0,1},{1,0},{2,3},{3,2},{4,5},{5,4},{6,7},{7,6},{8,9},{9,8},{10,11... | collective-permute-start | bytes 995336 | tf_op jit(solution)/shard_map/ppermute | solution.py:974
  71.5 19.0 %collective-permute-start.12 = (bf16[80,1152]{1,0:T(8,128)(2,1)S(1)}, bf16[80,1152]{1,0:T(8,128)(2,1)S(1)}, u32[]{:S(2)}, u32[]{:S(2)}) collective-permute-start(bf16[80,1152]{1,0:T(8,128)(2,1)S(1)} %slice.31), channel_id=1, source_target_pairs={{0,4},{4,0},{1,5},{5,1},{2,6},{6,2},{3,7},{7,3},{8,12},{12,8},{9,1... | collective-permute-start | bytes 552968 | tf_op jit(solution)/shard_map/ppermute | solution.py:973
  90.5 19.7 %collective-permute-start.14 = (bf16[144,1536]{1,0:T(8,128)(2,1)}, bf16[144,1536]{1,0:T(8,128)(2,1)S(1)}, u32[]{:S(2)}, u32[]{:S(2)}) collective-permute-start(bf16[144,1536]{1,0:T(8,128)(2,1)} %get-tuple-element.146.refs_10_), channel_id=1, source_target_pairs={{0,2},{1,3},{2,0},{3,1},{4,6},{5,7},{6,4},{7,5},{8,10},{9,11},{10,... | collective-permute-start | bytes 1327112 | tf_op jit(solution)/shard_map/ppermute | solution.py:974
  90.7 19.9 %collective-permute-start.15 = (bf16[144,1536]{1,0:T(8,128)(2,1)}, bf16[144,1536]{1,0:T(8,128)(2,1)S(1)}, u32[]{:S(2)}, u32[]{:S(2)}) collective-permute-start(bf16[144,1536]{1,0:T(8,128)(2,1)} %get-tuple-element.146.refs_10_), channel_id=1, source_target_pairs={{0,4},{4,0},{1,5},{5,1},{2,6},{6,2},{3,7},{7,3},{8,12},{12,8},{9,1... | collective-permute-start | bytes 1327112 | tf_op jit(solution)/shard_map/ppermute | solution.py:973
  91.2 19.4 %collective-permute-start.16 = (bf16[144,1536]{1,0:T(8,128)(2,1)}, bf16[144,1536]{1,0:T(8,128)(2,1)S(1)}, u32[]{:S(2)}, u32[]{:S(2)}) collective-permute-start(bf16[144,1536]{1,0:T(8,128)(2,1)} %get-tuple-element.146.refs_10_), channel_id=1, source_target_pairs={{0,1},{1,0},{2,3},{3,2},{4,5},{5,4},{6,7},{7,6},{8,9},{9,8},{10,11... | collective-permute-start | bytes 1327112 | tf_op jit(solution)/shard_map/ppermute | solution.py:974
  91.2 44.6 %collective-permute-start.17 = (bf16[144,1152]{1,0:T(8,128)(2,1)}, bf16[144,1152]{1,0:T(8,128)(2,1)}, u32[]{:S(2)}, u32[]{:S(2)}) collective-permute-start(bf16[144,1152]{1,0:T(8,128)(2,1)} %collective-permute-done.9.refs_1_), channel_id=1, source_target_pairs={{0,1},{1,0},{2,3},{3,2},{4,5},{5,4},{6,7},{7,6},{8,9},{9,8},{10,11... | collective-permute-start | bytes 995336 | tf_op jit(solution)/shard_map/ppermute | solution.py:974
  91.7 44.2 %collective-permute-start.18 = (bf16[144,1152]{1,0:T(8,128)(2,1)}, bf16[144,1152]{1,0:T(8,128)(2,1)}, u32[]{:S(2)}, u32[]{:S(2)}) collective-permute-start(bf16[144,1152]{1,0:T(8,128)(2,1)} %collective-permute-done.10.refs_2_), channel_id=1, source_target_pairs={{0,1},{1,0},{2,3},{3,2},{4,5},{5,4},{6,7},{7,6},{8,9},{9,8},{10,11... | collective-permute-start | bytes 995336 | tf_op jit(solution)/shard_map/ppermute | solution.py:974
  106.5 43.4 %all-to-all-start.3 = ((bf16[8,288,384]{2,1,0:T(8,128)(2,1)}), bf16[8,288,384]{2,1,0:T(8,128)(2,1)S(1)}, u32[]{:S(2)}, u32[]{:S(2)}) async-start(bf16[8,288,384]{2,1,0:T(8,128)(2,1)} %get-tuple-element.140), calls=%async_computation.3 | async-start | bytes 3538944 | tf_op jit(solution)/shard_map/all_to_all | solution.py:1118
  110.1 26.2 %collective-permute-start.20 = (bf16[64,1152]{1,0:T(8,128)(2,1)S(1)}, bf16[64,1152]{1,0:T(8,128)(2,1)}, u32[]{:S(2)}, u32[]{:S(2)}) collective-permute-start(bf16[64,1152]{1,0:T(8,128)(2,1)S(1)} %collective-permute-done.13.refs_4_), channel_id=1, source_target_pairs={{0,1},{1,0},{2,3},{3,2},{4,5},{5,4},{6,7},{7,6},{8,9},{9,8},{10,11... | collective-permute-start | bytes 442376 | tf_op jit(solution)/shard_map/ppermute | solution.py:974
  110.6 26.8 %collective-permute-start.21 = (bf16[80,1536]{1,0:T(8,128)(2,1)S(1)}, bf16[80,1536]{1,0:T(8,128)(2,1)S(1)}, u32[]{:S(2)}, u32[]{:S(2)}) collective-permute-start(bf16[80,1536]{1,0:T(8,128)(2,1)S(1)} %slice.33), channel_id=1, source_target_pairs={{0,4},{4,0},{1,5},{5,1},{2,6},{6,2},{3,7},{7,3},{8,12},{12,8},{9,1... | collective-permute-start | bytes 737288 | tf_op jit(solution)/shard_map/ppermute | solution.py:973
  112.4 24.1 %collective-permute-start.22 = (bf16[64,1536]{1,0:T(8,128)(2,1)S(1)}, bf16[64,1536]{1,0:T(8,128)(2,1)S(1)}, u32[]{:S(2)}, u32[]{:S(2)}) collective-permute-start(bf16[64,1536]{1,0:T(8,128)(2,1)S(1)} %slice.34), channel_id=1, source_target_pairs={{0,2},{1,3},{2,0},{3,1},{4,6},{5,7},{6,4},{7,5},{8,10},{9,11},{10,... | collective-permute-start | bytes 589832 | tf_op jit(solution)/shard_map/ppermute | solution.py:974
  160.1 27.3 %all-to-all-start.4 = ((bf16[8,240,384]{2,1,0:T(8,128)(2,1)}), bf16[8,240,384]{2,1,0:T(8,128)(2,1)S(1)}, u32[]{:S(2)}, u32[]{:S(2)}) async-start(bf16[8,240,384]{2,1,0:T(8,128)(2,1)} %get-tuple-element.161), calls=%async_computation.4 | async-start | bytes 2949120 | tf_op jit(solution)/shard_map/all_to_all | solution.py:1204
  164.7 21.3 %collective-permute-start.27 = (bf16[264,384]{1,0:T(8,128)(2,1)S(1)}, bf16[264,384]{1,0:T(8,128)(2,1)S(1)}, u32[]{:S(2)}, u32[]{:S(2)}) collective-permute-start(bf16[264,384]{1,0:T(8,128)(2,1)S(1)} %get-tuple-element.249), channel_id=1, source_target_pairs={{0,8},{8,0},{16,24},{24,16},{1,9},{9,1},{17,25},{25,17},{2,10},{10... | collective-permute-start | bytes 608264 | tf_op jit(solution)/shard_map/ppermute | solution.py:1198
  166.4 19.7 %collective-permute-start.28 = (bf16[264,384]{1,0:T(8,128)(2,1)S(1)}, bf16[264,384]{1,0:T(8,128)(2,1)S(1)}, u32[]{:S(2)}, u32[]{:S(2)}) collective-permute-start(bf16[264,384]{1,0:T(8,128)(2,1)S(1)} %get-tuple-element.248), channel_id=1, source_target_pairs={{0,16},{8,24},{16,0},{24,8},{1,17},{9,25},{17,1},{25,9},{2,18},{10... | collective-permute-start | bytes 608264 | tf_op jit(solution)/shard_map/ppermute | solution.py:1198
  169.0 18.5 %collective-permute-start.29 = (bf16[264,384]{1,0:T(8,128)(2,1)S(1)}, bf16[264,384]{1,0:T(8,128)(2,1)}, u32[]{:S(2)}, u32[]{:S(2)}) collective-permute-start(bf16[264,384]{1,0:T(8,128)(2,1)S(1)} %get-tuple-element.247), channel_id=1, source_target_pairs={{0,24},{8,16},{16,8},{24,0},{1,25},{9,17},{17,9},{25,1},{2,26},{10... | collective-permute-start | bytes 608264 | tf_op jit(solution)/shard_map/ppermute | solution.py:1198
  188.6 35.6 %all-to-all-start.5 = ((bf16[8,336,384]{2,1,0:T(8,128)(2,1)}), bf16[8,336,384]{2,1,0:T(8,128)(2,1)S(1)}, u32[]{:S(2)}, u32[]{:S(2)}) async-start(bf16[8,336,384]{2,1,0:T(8,128)(2,1)} %get-tuple-element.165), calls=%async_computation.5 | async-start | bytes 4128768 | tf_op jit(solution)/shard_map/all_to_all | solution.py:1232
  205.1 19.0 %collective-permute-start.33 = (bf16[2,96,384]{2,1,0:T(8,128)(2,1)S(1)}, bf16[2,96,384]{2,1,0:T(8,128)(2,1)S(1)}, u32[]{:S(2)}, u32[]{:S(2)}) collective-permute-start(bf16[2,96,384]{2,1,0:T(8,128)(2,1)S(1)} %get-tuple-element.245), channel_id=1, source_target_pairs={{0,8},{8,0},{16,24},{24,16},{1,9},{9,1},{17,25},{25,17},{2,10},{10... | collective-permute-start | bytes 442376 | tf_op jit(solution)/shard_map/ppermute | solution.py:1198
  206.4 17.8 %collective-permute-start.34 = (bf16[2,96,384]{2,1,0:T(8,128)(2,1)S(1)}, bf16[2,96,384]{2,1,0:T(8,128)(2,1)S(1)}, u32[]{:S(2)}, u32[]{:S(2)}) collective-permute-start(bf16[2,96,384]{2,1,0:T(8,128)(2,1)S(1)} %get-tuple-element.244), channel_id=1, source_target_pairs={{0,16},{8,24},{16,0},{24,8},{1,17},{9,25},{17,1},{25,9},{2,18},{10... | collective-permute-start | bytes 442376 | tf_op jit(solution)/shard_map/ppermute | solution.py:1198
  (57 other events, 505.3 us)

commit v6 on v5

--- a/solution.py
+++ b/solution.py
@@ -995,8 +995,6 @@
     x6a, x6b, x3, x5 = across(x2, x4, cells_all // 2)
     x7a, x7b = last(x6a, x6b)
     y2 = lax.all_to_all(pay2, G, 0, 0, tiled=True)
-    early, x7a = lax.optimization_barrier((early, x7a))
-    e2, e4, e1 = near(early)
     cut = -(-per_q // 32) * 16
     taps = lax.dynamic_slice_in_dim(conv_kv.reshape(2, 27, width), member * hd, hd, 2)
     taps = jnp.pad(taps, ((0, 0), (0, 5), (0, LANE - hd)))
@@ -1038,8 +1036,6 @@
     place[2] = local % HALF
     place = jnp.asarray(place)
     wide = 384
-    kc, e2, e4, e1 = lax.optimization_barrier((kc, e2, e4, e1))
-    e6a, e6b, e3, e5 = across(e2, e4, cut)
     k_all, v_all, qt_all, o_all, l_all, joined = call(
         functools.partial(attend_kernel, hdims),
         (
@@ -1061,6 +1057,8 @@
         us=16,
         away=(0, 1),
     )
+    early, joined = lax.optimization_barrier((early, joined))
+    e2, e4, e1 = near(early)
     joined_rows = lax.all_to_all(joined.reshape(HEADS, per_q, LANE), G, 0, 0, tiled=True)
     k_all, joined_rows = lax.optimization_barrier((k_all, joined_rows))
     kt_all = call(turn_kernel, shape((BACK, KEYS), bf), (k_all,), smem=0, us=4)
@@ -1110,7 +1108,8 @@
         cost_estimate=cost(14),
     )(joined_rows, early, w_proj, w_short, b_proj, b_short, norm2_gain, norm2_bias, w_fc1, b_fc1, w_fc2, b_fc2)
     dj_head = lax.all_to_all(dj, G, 0, 0, tiled=True).reshape(queries, LANE)
-    keep, e6a, e6b = lax.optimization_barrier((keep, e6a, e6b))
+    keep, e2, e4, e1 = lax.optimization_barrier((keep, e2, e4, e1))
+    e6a, e6b, e3, e5 = across(e2, e4, cut)
     k2, k4, k1 = near(keep)
     e7a, e7b = last(e6a, e6b)
     output = output.transpose(1, 2, 0, 3)

time: 244 us -> 243 us (level)
    unnamed x82 -> x86, local copies, waits for them, and re-layouts: 13.1 us -> 12.5 us
  transfers between devices with their start and end apart: 43 -> 43, of which waited for: 8 -> 7; matrix products, arithmetic and copies ran while one was open for 4% -> 3% of each run, Pallas kernels for 42% -> 42%
where the time goes in v6:
time: 243 us; the launch traced here: 239 us
  Pallas kernels  123 us (51%)
  starting transfers between devices  62.7 us (26%)
  waiting for transfers between devices  18.7 us (8%)
  local copies, waits for them, and re-layouts  18.2 us (7%)
  blocking collectives  12.4 us (5%)
  between operations  2.96 us (1%)
    pallas_call x10, Pallas kernels, call(): pl.pallas_call(kernel, out_shape=outs, in_specs=specs, out_specs=tuple((p...  78.2 us
    pallas_call x1, Pallas kernels, body(): pl.pallas_call(functools.partial(conv_back_kernel, hdims), out_shape=(sha...  16.9 us
    pallas_call x1, Pallas kernels, body(): pl.pallas_call(functools.partial(conv_kernel, hdims), out_shape=(shape((C...  16.7 us
    unnamed x86, local copies, waits for them, and re-layouts  12.5 us
    all_gather x1, blocking collectives, body(): late_full = lax.all_gather(late, G, axis=0)  12.4 us
    ppermute x21, starting transfers between devices, swap(): lax.ppermute(value, 'height', [(i, i ^ bit) for i in range(n_height)])  11.8 us
    pallas_call x1, Pallas kernels, body(): pl.pallas_call(functools.partial(mlp_kernel, (width, hd)), grid=(HEADS //...  11.5 us
    ppermute x6, starting transfers between devices, swap(): lax.ppermute(value, 'tm', [(i, i ^ 1) for i in range(lax.axis_size('tm'))])  9.24 us
  transfers between devices with their start and end apart: 43, of which 7 were waited for; matrix products, arithmetic and copies ran while one was open for 3% of the time, Pallas kernels for 42%

profile of v6, /device:TPU:0, one launch (start us, length us, event | category | flops | bytes accessed | tf_op | source)
XLA Modules:
  0.0 239.0 jit_solution(14275015774023741931)
XLA Ops:
  2.9 2.9 %collective-permute-start = (bf16[576,384]{1,0:T(8,128)(2,1)}, bf16[576,384]{1,0:T(8,128)(2,1)S(1)}, u32[]{:S(2)}, u32[]{:S(2)}) collective-permute-start(bf16[576,384]{1,0:T(8,128)(2,1)} %get-tuple-element.108.refs_0_), channel_id=1, source_target_pairs={{0,2},{1,3},{2,0},{3,1},{4,6},{5,7},{6,4},{7,5},{8,10},{9,11},{10,... | collective-permute-start | bytes 1327112 | tf_op jit(solution)/shard_map/ppermute | solution.py:974
  9.6 4.6 %shard_map.401 = (bf16[8,128,384]{2,1,0:T(8,128)(2,1)}, bf16[144,1152]{1,0:T(8,128)(2,1)}) custom-call(bf16[2,2,4,6,24,768]{5,4,3,2,1,0:T(8,128)(2,1)} %bitcast.60, f32[2,2,2,768]{3,2,1,0:T(2,128)} %c_ref.1, bf16[4,3,12,768]{3,2,1,0:T(8,128)(2,1)} %bitcast.55, f32[144,384]{1,0:T(8,128)} %get-tuple-element.109.mx_ref.refs_2_), custom_call_target="tpu_custom_call" | custom-call | flops 5000000000 | tf_op jit(solution)/shard_map/pallas_call | solution.py:68
  21.7 4.1 %collective-permute-done.2.refs_3_ = bf16[288,384]{1,0:T(8,128)(2,1)S(1)} collective-permute-done((bf16[288,384]{1,0:T(8,128)(2,1)S(1)}, bf16[288,384]{1,0:T(8,128)(2,1)S(1)}, u32[]{:S(2)}, u32[]{:S(2)}) %collective-permute-start.2) | collective-permute-done | bytes 221216 | tf_op jit(solution)/shard_map/ppermute | solution.py:973
  27.7 3.7 %all-to-all-start = ((bf16[8,128,384]{2,1,0:T(8,128)(2,1)}), bf16[8,128,384]{2,1,0:T(8,128)(2,1)S(1)}, u32[]{:S(2)}, u32[]{:S(2)}) async-start(bf16[8,128,384]{2,1,0:T(8,128)(2,1)} %get-tuple-element.116), calls=%async_computation | async-start | bytes 1572864 | tf_op jit(solution)/shard_map/all_to_all | solution.py:997
  32.5 16.7 %shard_map.402 = (bf16[3200,256]{1,0:T(8,128)(2,1)}, bf16[3200,128]{1,0:T(8,128)(2,1)}, bf16[1152,128]{1,0:T(8,128)(2,1)}, f32[5064,128]{1,0:T(8,128)}, f32[5064,128]{1,0:T(8,128)}) custom-call(s32[5]{0:T(128)} %stack.16.meta, f32[32,256]{1,0:T(8,128)} %pad_maximum_fusion.1.w_ref, f32[1,384]{1,0:T(1,128)} %bitcast.59, ...), custom_call_target="tpu_custom_call" | custom-call | flops 17999998976 | tf_op jit(solution)/shard_map/pallas_call | solution.py:1007
  50.1 12.4 %shard_map.403 = (bf16[4864,256]{1,0:T(8,128)(2,1)}, bf16[4864,128]{1,0:T(8,128)(2,1)}, bf16[256,1152]{1,0:T(8,128)(2,1)}, f32[96,1152]{1,0:T(8,128)}, f32[1,1152]{1,0:T(1,128)}, /*index=5*/bf16[1152,128]{1,0:T(8,128)(2,1)}) custom-call(s32[5]{0:T(128)} %stack.16.meta, bf16[3200,256]{1,0:T(8,128)(2,1)} %get-tuple-element.113.kc_ref, ...), custom_call_target="tpu_custom_call" | custom-call | flops 16000000000 | tf_op jit(solution)/shard_map/pallas_call | solution.py:68
  62.5 4.6 %all-to-all-start.1 = ((bf16[8,144,128]{2,1,0:T(8,128)(2,1)}), bf16[8,144,128]{2,1,0:T(8,128)(2,1)S(1)}, u32[]{:S(2)}, u32[]{:S(2)}) async-start(bf16[8,144,128]{2,1,0:T(8,128)(2,1)} %bitcast.52), calls=%async_computation.1 | async-start | bytes 589824 | tf_op jit(solution)/shard_map/all_to_all | solution.py:1062
  70.7 4.1 %all-to-all-done.1.j_ref = bf16[8,144,128]{2,1,0:T(8,128)(2,1)S(1)} async-done(((bf16[8,144,128]{2,1,0:T(8,128)(2,1)}), bf16[8,144,128]{2,1,0:T(8,128)(2,1)S(1)}, u32[]{:S(2)}, u32[]{:S(2)}) %all-to-all-start.1) | async-done | bytes 294944 | tf_op jit(solution)/shard_map/all_to_all | solution.py:1062
  75.6 11.5 %shard_map.404 = (bf16[4,3,12,768]{3,2,1,0:T(8,128)(2,1)}, bf16[144,1536]{1,0:T(8,128)(2,1)}, bf16[8,288,384]{2,1,0:T(8,128)(2,1)}, bf16[8,144,128]{2,1,0:T(8,128)(2,1)}, f32[144,384]{1,0:T(8,128)}) custom-call(bf16[8,144,128]{2,1,0:T(8,128)(2,1)} %copy-done.8, bf16[144,1152]{1,0:T(8,128)(2,1)} %get-tuple-element.122.early_ref.refs_0_, ...), custom_call_target="tpu_custom_call" | custom-call | flops 14000000000 | tf_op jit(solution)/shard_map/pallas_call | solution.py:1068
  88.3 3.7 %all-to-all-start.2 = ((bf16[8,144,128]{2,1,0:T(8,128)(2,1)}), bf16[8,144,128]{2,1,0:T(8,128)(2,1)S(1)}, u32[]{:S(2)}, u32[]{:S(2)}) async-start(bf16[8,144,128]{2,1,0:T(8,128)(2,1)} %get-tuple-element.124), calls=%async_computation.2 | async-start | bytes 589824 | tf_op jit(solution)/shard_map/all_to_all | solution.py:1110
  95.7 3.5 %shard_map.405.kt_in = bf16[144,4864]{1,0:T(8,128)(2,1)} custom-call(bf16[4864,256]{1,0:T(8,128)(2,1)} %get-tuple-element.125.k_ref.k_in), custom_call_target="tpu_custom_call" | custom-call | flops 4000000000 | tf_op jit(solution)/shard_map/pallas_call | solution.py:68
  99.2 4.7 %all-to-all-done.2 = bf16[8,144,128]{2,1,0:T(8,128)(2,1)S(1)} async-done(((bf16[8,144,128]{2,1,0:T(8,128)(2,1)}), bf16[8,144,128]{2,1,0:T(8,128)(2,1)S(1)}, u32[]{:S(2)}, u32[]{:S(2)}) %all-to-all-start.2) | async-done | bytes 294944 | tf_op jit(solution)/shard_map/all_to_all | solution.py:1110
  104.6 3.6 %all-to-all-start.3 = ((bf16[8,288,384]{2,1,0:T(8,128)(2,1)}), bf16[8,288,384]{2,1,0:T(8,128)(2,1)S(1)}, u32[]{:S(2)}, u32[]{:S(2)}) async-start(bf16[8,288,384]{2,1,0:T(8,128)(2,1)} %get-tuple-element.136), calls=%async_computation.3 | async-start | bytes 3538944 | tf_op jit(solution)/shard_map/all_to_all | solution.py:1117
  113.6 21.7 %shard_map.406 = (f32[3200,128]{1,0:T(8,128)}, f32[3200,128]{1,0:T(8,128)}, bf16[8,144,384]{2,1,0:T(8,128)(2,1)}, f32[1152,128]{1,0:T(8,128)}, f32[24,32]{1,0:T(8,128)}) custom-call(bf16[256,1152]{1,0:T(8,128)(2,1)} %get-tuple-element.129.qt_ref, bf16[1152,128]{1,0:T(8,128)(2,1)} %get-tuple-element.115.q_ref, f32[96,1152]{1,0:T(8,128)} %get-tuple-element.130.o_ref, ...), custom_call_target="tpu_custom_call" | custom-call | flops 24999999488 | tf_op jit(solution)/shard_map/pallas_call | solution.py:68
  136.6 10.8 %shard_map.407.conv_ref = f32[16,384]{1,0:T(8,128)} custom-call(f32[5064,128]{1,0:T(8,128)} %get-tuple-element.141.mk_in, f32[5064,128]{1,0:T(8,128)} %get-tuple-element.142.mv_in, f32[3200,128]{1,0:T(8,128)} %get-tuple-element.152.dk_in.dk_ref, f32[3200,128]{1,0:T(8,128)} %get-tuple-element.143.dv_in.dv_ref), custom_call_target="tpu_custom_call" | custom-call | flops 12000000000 | tf_op jit(solution)/shard_map/pallas_call | solution.py:68
  150.2 9.0 %shard_map.408 = (bf16[768,384]{1,0:T(8,128)(2,1)}, bf16[8,240,384]{2,1,0:T(8,128)(2,1)}, bf16[192,384]{1,0:T(8,128)(2,1)}, bf16[96,384]{1,0:T(8,128)(2,1)}) custom-call(s32[5]{0:T(128)} %stack.16.meta, bf16[8,288,384]{2,1,0:T(8,128)(2,1)} %copy-done.4, bf16[1152,128]{1,0:T(8,128)(2,1)} %get-tuple-element.120.j_ref, ...), custom_call_target="tpu_custom_call" | custom-call | flops 8999999488 | tf_op jit(solution)/shard_map/pallas_call | solution.py:68
  159.2 3.7 %all-to-all-start.4 = ((bf16[8,240,384]{2,1,0:T(8,128)(2,1)}), bf16[8,240,384]{2,1,0:T(8,128)(2,1)S(1)}, u32[]{:S(2)}, u32[]{:S(2)}) async-start(bf16[8,240,384]{2,1,0:T(8,128)(2,1)} %get-tuple-element.155), calls=%async_computation.4 | async-start | bytes 2949120 | tf_op jit(solution)/shard_map/all_to_all | solution.py:1203
  168.3 16.9 %shard_map.409 = (bf16[8,336,384]{2,1,0:T(8,128)(2,1)}, f32[8,384]{1,0:T(8,128)}) custom-call(s32[5]{0:T(128)} %stack.16.meta, f32[3200,128]{1,0:T(8,128)} %get-tuple-element.152.dk_in.dk_ref, f32[3200,128]{1,0:T(8,128)} %get-tuple-element.143.dv_in.dv_ref, f32[1152,128]{1,0:T(8,128)} %get-tuple-element.153.pq_ref, f32[32,256]{1,0:T(8,128)} %pad_maximum_fusion.1.w_ref, ...), custom_call_target="tpu_custom_call" | custom-call | flops 17999998976 | tf_op jit(solution)/shard_map/pallas_call | solution.py:1211
  187.7 4.1 %all-to-all-start.5 = ((bf16[8,336,384]{2,1,0:T(8,128)(2,1)}), bf16[8,336,384]{2,1,0:T(8,128)(2,1)S(1)}, u32[]{:S(2)}, u32[]{:S(2)}) async-start(bf16[8,336,384]{2,1,0:T(8,128)(2,1)} %get-tuple-element.159), calls=%async_computation.5 | async-start | bytes 4128768 | tf_op jit(solution)/shard_map/all_to_all | solution.py:1231
  193.6 4.3 %shard_map.410 = bf16[40,384]{1,0:T(8,128)(2,1)} custom-call(f32[16,384]{1,0:T(8,128)} %shard_map.407.conv_ref, f32[8,384]{1,0:T(8,128)} %get-tuple-element.161.stat_ref, f32[24,32]{1,0:T(8,128)} %get-tuple-element.162.small_ref, bf16[2,2,4,6,24,768]{5,4,3,2,1,0:T(8,128)(2,1)} %bitcast.61, bf16[8,240,384]{2,1,0:T(8,128)(2,1)} %copy-done.2), custom_call_target="tpu_custom_call" | custom-call | flops 5000000000 | tf_op jit(solution)/shard_map/pallas_call | solution.py:68
  197.9 3.7 %collective-permute-start.32 = (bf16[40,384]{1,0:T(8,128)(2,1)}, bf16[40,384]{1,0:T(8,128)(2,1)S(1)}, u32[]{:S(2)}, u32[]{:S(2)}) collective-permute-start(bf16[40,384]{1,0:T(8,128)(2,1)} %shard_map.410), channel_id=1, source_target_pairs={{0,24},{8,16},{16,8},{24,0},{1,25},{9,17},{17,9},{25,1},{2,26},{10... | collective-permute-start | bytes 92168 | tf_op jit(solution)/shard_map/ppermute | solution.py:1190
  210.9 12.4 %all-gather = f32[320,384]{1,0:T(8,128)} all-gather(f32[40,384]{1,0:T(8,128)S(1)} %add_add_fusion), channel_id=2, replica_groups=mesh['clip'=4,'tm'=2,'height'=4] {'tm','height'}, dimensions={0}, use_global_device_ids=true | all-gather | bytes 552960 | tf_op jit(solution)/shard_map/all_gather | solution.py:1269
  224.4 4.9 %all-to-all-start.6 = ((bf16[4,72,384]{2,1,0:T(8,128)(2,1)}), bf16[4,72,384]{2,1,0:T(8,128)(2,1)S(1)}, u32[]{:S(2)}, u32[]{:S(2)}) async-start(bf16[4,72,384]{2,1,0:T(8,128)(2,1)} %reshape_reshape.3), calls=%async_computation.6 | async-start | bytes 442368 | tf_op jit(solution)/shard_map/all_to_all | solution.py:1274
  229.3 7.6 %shard_map.412 = (bf16[576,384]{1,0:T(8,128)(2,1)}, f32[384]{0:T(512)}, f32[384]{0:T(512)}, f32[2304]{0:T(1024)}, f32[3,3,3,2,768]{4,3,2,1,0:T(2,128)}, /*index=...) custom-call(bf16[576,384]{1,0:T(8,128)(2,1)} %bitcast.63, ...), custom_call_target="tpu_custom_call" | custom-call | flops 8999999488 | tf_op jit(solution)/shard_map/pallas_call | solution.py:68
  (184 shorter events, 56.9 us)
Async XLA Ops:
  7.4 24.1 %collective-permute-start.4 = (bf16[576,384]{1,0:T(8,128)(2,1)}, bf16[576,384]{1,0:T(8,128)(2,1)S(1)}, u32[]{:S(2)}, u32[]{:S(2)}) collective-permute-start(bf16[576,384]{1,0:T(8,128)(2,1)} %get-tuple-element.108.refs_0_), channel_id=1, source_target_pairs={{0,1},{1,0},{2,3},{3,2},{4,5},{5,4},{6,7},{7,6},{8,9},{9,8},{10,11... | collective-permute-start | bytes 1327112 | tf_op jit(solution)/shard_map/ppermute | solution.py:974
  27.7 21.5 %all-to-all-start = ((bf16[8,128,384]{2,1,0:T(8,128)(2,1)}), bf16[8,128,384]{2,1,0:T(8,128)(2,1)S(1)}, u32[]{:S(2)}, u32[]{:S(2)}) async-start(bf16[8,128,384]{2,1,0:T(8,128)(2,1)} %get-tuple-element.116), calls=%async_computation | async-start | bytes 1572864 | tf_op jit(solution)/shard_map/all_to_all | solution.py:997
  67.2 19.9 %collective-permute-start.9 = (bf16[144,1152]{1,0:T(8,128)(2,1)S(1)}, bf16[144,1152]{1,0:T(8,128)(2,1)S(1)}, u32[]{:S(2)}, u32[]{:S(2)}) collective-permute-start(bf16[144,1152]{1,0:T(8,128)(2,1)S(1)} %copy-done.24), channel_id=1, source_target_pairs={{0,2},{1,3},{2,0},{3,1},{4,6},{5,7},{6,4},{7,5},{8,10},{9,11},{10,... | collective-permute-start | bytes 995336 | tf_op jit(solution)/shard_map/ppermute | solution.py:974
  69.2 17.8 %collective-permute-start.10 = (bf16[144,1152]{1,0:T(8,128)(2,1)S(1)}, bf16[144,1152]{1,0:T(8,128)(2,1)S(1)}, u32[]{:S(2)}, u32[]{:S(2)}) collective-permute-start(bf16[144,1152]{1,0:T(8,128)(2,1)S(1)} %copy-done.24), channel_id=1, source_target_pairs={{0,4},{4,0},{1,5},{5,1},{2,6},{6,2},{3,7},{7,3},{8,12},{12,8},{9,1... | collective-permute-start | bytes 995336 | tf_op jit(solution)/shard_map/ppermute | solution.py:973
  70.7 16.4 %collective-permute-start.11 = (bf16[144,1152]{1,0:T(8,128)(2,1)S(1)}, bf16[144,1152]{1,0:T(8,128)(2,1)S(1)}, u32[]{:S(2)}, u32[]{:S(2)}) collective-permute-start(bf16[144,1152]{1,0:T(8,128)(2,1)S(1)} %copy-done.24), channel_id=1, source_target_pairs={{0,1},{1,0},{2,3},{3,2},{4,5},{5,4},{6,7},{7,6},{8,9},{9,8},{10,11... | collective-permute-start | bytes 995336 | tf_op jit(solution)/shard_map/ppermute | solution.py:974
  87.1 21.6 %collective-permute-start.12 = (bf16[144,1536]{1,0:T(8,128)(2,1)}, bf16[144,1536]{1,0:T(8,128)(2,1)S(1)}, u32[]{:S(2)}, u32[]{:S(2)}) collective-permute-start(bf16[144,1536]{1,0:T(8,128)(2,1)} %get-tuple-element.140.refs_10_), channel_id=1, source_target_pairs={{0,2},{1,3},{2,0},{3,1},{4,6},{5,7},{6,4},{7,5},{8,10},{9,11},{10,... | collective-permute-start | bytes 1327112 | tf_op jit(solution)/shard_map/ppermute | solution.py:974
  87.4 21.5 %collective-permute-start.13 = (bf16[144,1536]{1,0:T(8,128)(2,1)}, bf16[144,1536]{1,0:T(8,128)(2,1)}, u32[]{:S(2)}, u32[]{:S(2)}) collective-permute-start(bf16[144,1536]{1,0:T(8,128)(2,1)} %get-tuple-element.140.refs_10_), channel_id=1, source_target_pairs={{0,4},{4,0},{1,5},{5,1},{2,6},{6,2},{3,7},{7,3},{8,12},{12,8},{9,1... | collective-permute-start | bytes 1327112 | tf_op jit(solution)/shard_map/ppermute | solution.py:973
  88.3 21.0 %collective-permute-start.14 = (bf16[144,1536]{1,0:T(8,128)(2,1)}, bf16[144,1536]{1,0:T(8,128)(2,1)}, u32[]{:S(2)}, u32[]{:S(2)}) collective-permute-start(bf16[144,1536]{1,0:T(8,128)(2,1)} %get-tuple-element.140.refs_10_), channel_id=1, source_target_pairs={{0,1},{1,0},{2,3},{3,2},{4,5},{5,4},{6,7},{7,6},{8,9},{9,8},{10,11... | collective-permute-start | bytes 1327112 | tf_op jit(solution)/shard_map/ppermute | solution.py:974
  88.3 15.6 %all-to-all-start.2 = ((bf16[8,144,128]{2,1,0:T(8,128)(2,1)}), bf16[8,144,128]{2,1,0:T(8,128)(2,1)S(1)}, u32[]{:S(2)}, u32[]{:S(2)}) async-start(bf16[8,144,128]{2,1,0:T(8,128)(2,1)} %get-tuple-element.124), calls=%async_computation.2 | async-start | bytes 589824 | tf_op jit(solution)/shard_map/all_to_all | solution.py:1110
  92.1 19.9 %collective-permute-start.15 = (bf16[80,1152]{1,0:T(8,128)(2,1)S(1)}, bf16[80,1152]{1,0:T(8,128)(2,1)}, u32[]{:S(2)}, u32[]{:S(2)}) collective-permute-start(bf16[80,1152]{1,0:T(8,128)(2,1)S(1)} %slice.31), channel_id=1, source_target_pairs={{0,4},{4,0},{1,5},{5,1},{2,6},{6,2},{3,7},{7,3},{8,12},{12,8},{9,1... | collective-permute-start | bytes 552968 | tf_op jit(solution)/shard_map/ppermute | solution.py:973
  94.2 14.1 %collective-permute-start.16 = (bf16[64,1152]{1,0:T(8,128)(2,1)S(1)}, bf16[64,1152]{1,0:T(8,128)(2,1)}, u32[]{:S(2)}, u32[]{:S(2)}) collective-permute-start(bf16[64,1152]{1,0:T(8,128)(2,1)S(1)} %slice.32), channel_id=1, source_target_pairs={{0,2},{1,3},{2,0},{3,1},{4,6},{5,7},{6,4},{7,5},{8,10},{9,11},{10,... | collective-permute-start | bytes 442376 | tf_op jit(solution)/shard_map/ppermute | solution.py:974
  104.6 43.6 %all-to-all-start.3 = ((bf16[8,288,384]{2,1,0:T(8,128)(2,1)}), bf16[8,288,384]{2,1,0:T(8,128)(2,1)S(1)}, u32[]{:S(2)}, u32[]{:S(2)}) async-start(bf16[8,288,384]{2,1,0:T(8,128)(2,1)} %get-tuple-element.136), calls=%async_computation.3 | async-start | bytes 3538944 | tf_op jit(solution)/shard_map/all_to_all | solution.py:1117
  108.2 27.2 %collective-permute-start.17 = (bf16[144,1152]{1,0:T(8,128)(2,1)S(1)}, bf16[144,1152]{1,0:T(8,128)(2,1)S(1)}, u32[]{:S(2)}, u32[]{:S(2)}) collective-permute-start(bf16[144,1152]{1,0:T(8,128)(2,1)S(1)} %collective-permute-done.9.refs_1_), channel_id=1, source_target_pairs={{0,1},{1,0},{2,3},{3,2},{4,5},{5,4},{6,7},{7,6},{8,9},{9,8},{10,11... | collective-permute-start | bytes 995336 | tf_op jit(solution)/shard_map/ppermute | solution.py:974
  108.7 27.3 %collective-permute-start.18 = (bf16[144,1152]{1,0:T(8,128)(2,1)S(1)}, bf16[144,1152]{1,0:T(8,128)(2,1)S(1)}, u32[]{:S(2)}, u32[]{:S(2)}) collective-permute-start(bf16[144,1152]{1,0:T(8,128)(2,1)S(1)} %collective-permute-done.10.refs_2_), channel_id=1, source_target_pairs={{0,1},{1,0},{2,3},{3,2},{4,5},{5,4},{6,7},{7,6},{8,9},{9,8},{10,11... | collective-permute-start | bytes 995336 | tf_op jit(solution)/shard_map/ppermute | solution.py:974
  108.9 26.4 %collective-permute-start.20 = (bf16[64,1152]{1,0:T(8,128)(2,1)}, bf16[64,1152]{1,0:T(8,128)(2,1)}, u32[]{:S(2)}, u32[]{:S(2)}) collective-permute-start(bf16[64,1152]{1,0:T(8,128)(2,1)} %collective-permute-done.16.refs_4_), channel_id=1, source_target_pairs={{0,1},{1,0},{2,3},{3,2},{4,5},{5,4},{6,7},{7,6},{8,9},{9,8},{10,11... | collective-permute-start | bytes 442376 | tf_op jit(solution)/shard_map/ppermute | solution.py:974
  109.3 27.2 %collective-permute-start.21 = (bf16[80,1536]{1,0:T(8,128)(2,1)S(1)}, bf16[80,1536]{1,0:T(8,128)(2,1)S(1)}, u32[]{:S(2)}, u32[]{:S(2)}) collective-permute-start(bf16[80,1536]{1,0:T(8,128)(2,1)S(1)} %slice.33), channel_id=1, source_target_pairs={{0,4},{4,0},{1,5},{5,1},{2,6},{6,2},{3,7},{7,3},{8,12},{12,8},{9,1... | collective-permute-start | bytes 737288 | tf_op jit(solution)/shard_map/ppermute | solution.py:973
  112.0 24.0 %collective-permute-start.22 = (bf16[64,1536]{1,0:T(8,128)(2,1)S(1)}, bf16[64,1536]{1,0:T(8,128)(2,1)S(1)}, u32[]{:S(2)}, u32[]{:S(2)}) collective-permute-start(bf16[64,1536]{1,0:T(8,128)(2,1)S(1)} %slice.34), channel_id=1, source_target_pairs={{0,2},{1,3},{2,0},{3,1},{4,6},{5,7},{6,4},{7,5},{8,10},{9,11},{10,... | collective-permute-start | bytes 589832 | tf_op jit(solution)/shard_map/ppermute | solution.py:974
  159.2 27.4 %all-to-all-start.4 = ((bf16[8,240,384]{2,1,0:T(8,128)(2,1)}), bf16[8,240,384]{2,1,0:T(8,128)(2,1)S(1)}, u32[]{:S(2)}, u32[]{:S(2)}) async-start(bf16[8,240,384]{2,1,0:T(8,128)(2,1)} %get-tuple-element.155), calls=%async_computation.4 | async-start | bytes 2949120 | tf_op jit(solution)/shard_map/all_to_all | solution.py:1203
  163.9 21.4 %collective-permute-start.27 = (bf16[264,384]{1,0:T(8,128)(2,1)S(1)}, bf16[264,384]{1,0:T(8,128)(2,1)S(1)}, u32[]{:S(2)}, u32[]{:S(2)}) collective-permute-start(bf16[264,384]{1,0:T(8,128)(2,1)S(1)} %get-tuple-element.243), channel_id=1, source_target_pairs={{0,8},{8,0},{16,24},{24,16},{1,9},{9,1},{17,25},{25,17},{2,10},{10... | collective-permute-start | bytes 608264 | tf_op jit(solution)/shard_map/ppermute | solution.py:1197
  165.5 19.7 %collective-permute-start.28 = (bf16[264,384]{1,0:T(8,128)(2,1)S(1)}, bf16[264,384]{1,0:T(8,128)(2,1)S(1)}, u32[]{:S(2)}, u32[]{:S(2)}) collective-permute-start(bf16[264,384]{1,0:T(8,128)(2,1)S(1)} %get-tuple-element.242), channel_id=1, source_target_pairs={{0,16},{8,24},{16,0},{24,8},{1,17},{9,25},{17,1},{25,9},{2,18},{10... | collective-permute-start | bytes 608264 | tf_op jit(solution)/shard_map/ppermute | solution.py:1197
  168.1 18.5 %collective-permute-start.29 = (bf16[264,384]{1,0:T(8,128)(2,1)S(1)}, bf16[264,384]{1,0:T(8,128)(2,1)}, u32[]{:S(2)}, u32[]{:S(2)}) collective-permute-start(bf16[264,384]{1,0:T(8,128)(2,1)S(1)} %get-tuple-element.241), channel_id=1, source_target_pairs={{0,24},{8,16},{16,8},{24,0},{1,25},{9,17},{17,9},{25,1},{2,26},{10... | collective-permute-start | bytes 608264 | tf_op jit(solution)/shard_map/ppermute | solution.py:1197
  187.7 35.6 %all-to-all-start.5 = ((bf16[8,336,384]{2,1,0:T(8,128)(2,1)}), bf16[8,336,384]{2,1,0:T(8,128)(2,1)S(1)}, u32[]{:S(2)}, u32[]{:S(2)}) async-start(bf16[8,336,384]{2,1,0:T(8,128)(2,1)} %get-tuple-element.159), calls=%async_computation.5 | async-start | bytes 4128768 | tf_op jit(solution)/shard_map/all_to_all | solution.py:1231
  204.2 19.0 %collective-permute-start.33 = (bf16[2,96,384]{2,1,0:T(8,128)(2,1)S(1)}, bf16[2,96,384]{2,1,0:T(8,128)(2,1)S(1)}, u32[]{:S(2)}, u32[]{:S(2)}) collective-permute-start(bf16[2,96,384]{2,1,0:T(8,128)(2,1)S(1)} %get-tuple-element.239), channel_id=1, source_target_pairs={{0,8},{8,0},{16,24},{24,16},{1,9},{9,1},{17,25},{25,17},{2,10},{10... | collective-permute-start | bytes 442376 | tf_op jit(solution)/shard_map/ppermute | solution.py:1197
  205.5 17.8 %collective-permute-start.34 = (bf16[2,96,384]{2,1,0:T(8,128)(2,1)S(1)}, bf16[2,96,384]{2,1,0:T(8,128)(2,1)S(1)}, u32[]{:S(2)}, u32[]{:S(2)}) collective-permute-start(bf16[2,96,384]{2,1,0:T(8,128)(2,1)S(1)} %get-tuple-element.238), channel_id=1, source_target_pairs={{0,16},{8,24},{16,0},{24,8},{1,17},{9,25},{17,1},{25,9},{2,18},{10... | collective-permute-start | bytes 442376 | tf_op jit(solution)/shard_map/ppermute | solution.py:1197
  (59 other events, 476.4 us)
